TPU v7x, 512 devices: a whole 4x8x8 slice. The times are simulated.
512 devices in a mesh: dom: 64 (over z_lo, y, core), sub: 8 (over z_hi, x).
Axes of the slice: x: 4, y: 8, z: 8 (z_hi: 2, z_lo: 4; z = z_hi * 4 + z_lo), core: 2. Of those that a mesh axis runs over, the one named last changes fastest.
Arguments:
- embeddings: float32 [131072, 256], P(('dom', 'sub')), may hold values from -1.5 to 1.5
- row_accum: float32 [131072], P(('dom', 'sub')), may hold values from 0.05 to 5
- relations: float32 [8, 256, 256], replicated, may hold values from -0.375 to 0.375
- rel_accum: float32 [8, 256], replicated, may hold values from 0.05 to 5
- matching: int32 [64], replicated, may hold values from 0 to 63, each once
- src_rows: int32 [262144], P(('dom', 'sub')), may hold values from 0 to 255
- dst_rows: int32 [262144], P(('dom', 'sub')), may hold values from 0 to 2047
- rel_ids: int32 [262144], P(('dom', 'sub')), may hold values from 0 to 7
- neg_rows: int32 [512, 512], P(('dom', 'sub')), may hold values from 0 to 2047
Outputs:
- new_embeddings: float32 [131072, 256], P(('dom', 'sub'))
- new_row_accum: float32 [131072], P(('dom', 'sub'))
- new_relations: float32 [8, 256, 256], replicated
- new_rel_accum: float32 [8, 256], replicated
Inputs may be any that keep to these rules, and one draw needn't show every extreme that they name: matching is a permutation of the partitions 0 to 64 - 1.
All inputs are finite; a program needn't handle non-finite values.
Results may differ from a plain program's by a relative error of at most 0.0073.
Values may be sent and summed in bfloat16 or wider, within the bound.
No kernel may reach another device: no remote copies, remote signals or barrier semaphores. Data moves between devices by JAX's collectives and lax.ppermute only.
A program may use at most 64 MiB of HBM per device.

v0:
```python
import jax
import jax.numpy as jnp
from jax import lax
from jax.sharding import PartitionSpec as P

learn_rate = 0.1


def refresh(grad_part, weight_part, accum_part):
    accum_next = accum_part + jnp.mean(grad_part * grad_part, axis=-1)
    return (weight_part - learn_rate * grad_part / jnp.sqrt(accum_next)[:, None], accum_next)


def body(
    embeddings, row_accum, relations, rel_accum, matching, src_rows, dst_rows, rel_ids, neg_rows
):
    dom_size = lax.axis_size("dom")
    row_count, width = embeddings.shape
    piece_rows = row_count // dom_size
    rel_count = relations.shape[0]
    edge_count = src_rows.shape[0]
    span_count, neg_count = neg_rows.shape
    own_b = embeddings.astype(jnp.bfloat16)
    spread_rows = lax.all_to_all(
        own_b.reshape(dom_size, piece_rows, width), "dom", split_axis=0, concat_axis=0, tiled=True
    )
    routed = jnp.take(spread_rows, matching, axis=0)
    partner_slice = lax.all_to_all(routed, "dom", split_axis=0, concat_axis=0, tiled=True).reshape(
        row_count, width
    )
    wanted = jnp.concatenate([dst_rows, neg_rows.reshape(-1)])
    shard_rows = lax.all_gather(partner_slice, "sub", axis=0, tiled=True)
    columns = lax.iota(jnp.int32, shard_rows.shape[0])
    onehot = (wanted[:, None] == columns[None, :]).astype(jnp.bfloat16)
    selected = jnp.dot(onehot, shard_rows, preferred_element_type=jnp.float32).astype(jnp.bfloat16)
    dst_b = selected[:edge_count]
    negs_b = selected[edge_count:].reshape(span_count, neg_count, width)
    local_ids = lax.iota(jnp.int32, row_count)
    src_onehot = (src_rows[:, None] == local_ids[None, :]).astype(jnp.bfloat16)
    src_b = jnp.dot(src_onehot, own_b, preferred_element_type=jnp.float32).astype(jnp.bfloat16)
    rel_b = relations.astype(jnp.bfloat16)
    rel_mask = (rel_ids[:, None] == lax.iota(jnp.int32, rel_count)[None, :]).astype(jnp.bfloat16)
    forward_stack = jnp.transpose(rel_b, (0, 2, 1)).reshape(rel_count * width, width)
    masked_src = (rel_mask[:, :, None] * src_b[:, None, :]).reshape(edge_count, rel_count * width)
    trans = jnp.dot(masked_src, forward_stack, preferred_element_type=jnp.float32).astype(
        jnp.bfloat16
    )
    pos_score = jnp.sum(trans.astype(jnp.float32) * dst_b.astype(jnp.float32), axis=-1)
    trans_c = trans.reshape(span_count, neg_count, width)
    neg_score = jnp.einsum("cni,cmi->cnm", trans_c, negs_b, preferred_element_type=jnp.float32)
    g_pos = -jax.nn.sigmoid(-pos_score)
    g_neg = jax.nn.sigmoid(neg_score).astype(jnp.bfloat16)
    pulled = jnp.einsum("cnm,cmi->cni", g_neg, negs_b, preferred_element_type=jnp.float32).reshape(
        edge_count, width
    )
    g_trans = (g_pos[:, None] * dst_b.astype(jnp.float32) + pulled).astype(jnp.bfloat16)
    g_dst = (g_pos[:, None] * trans.astype(jnp.float32)).astype(jnp.bfloat16)
    g_negrow = jnp.einsum(
        "cnm,cni->cmi", g_neg, trans_c, preferred_element_type=jnp.float32
    ).astype(jnp.bfloat16)
    backward_stack = jnp.transpose(rel_b, (1, 0, 2)).reshape(width, rel_count * width)
    pulled_back = jnp.dot(g_trans, backward_stack, preferred_element_type=jnp.float32).reshape(
        edge_count, rel_count, width
    )
    g_src = jnp.sum(pulled_back * rel_mask.astype(jnp.float32)[:, :, None], axis=1).astype(
        jnp.bfloat16
    )
    masked_grad = (rel_mask[:, :, None] * g_trans[:, None, :]).reshape(
        edge_count, rel_count * width
    )
    rel_term = lax.dot_general(
        masked_grad, src_b, (((0,), (0,)), ((), ())), preferred_element_type=jnp.float32
    )
    own_grad = lax.dot_general(
        src_onehot, g_src, (((0,), (0,)), ((), ())), preferred_element_type=jnp.float32
    )
    grad_rows = jnp.concatenate([g_dst, g_negrow.reshape(-1, width)], axis=0)
    targets = lax.iota(jnp.int32, row_count * lax.axis_size("sub"))
    onehot = (targets[:, None] == wanted[None, :]).astype(jnp.bfloat16)
    partner_grad = lax.psum_scatter(
        jnp.dot(onehot, grad_rows, preferred_element_type=jnp.float32).astype(jnp.bfloat16),
        "sub",
        scatter_dimension=0,
        tiled=True,
    ).astype(jnp.float32)
    spread_grads = lax.all_to_all(
        partner_grad.reshape(dom_size, piece_rows, width).astype(jnp.bfloat16),
        "dom",
        split_axis=0,
        concat_axis=0,
        tiled=True,
    ).astype(jnp.float32)
    slots = lax.iota(jnp.int32, dom_size)
    inverse = jnp.sum(jnp.where(matching[None, :] == slots[:, None], slots[None, :], 0), axis=1)
    returned = (
        lax.all_to_all(
            jnp.take(spread_grads, inverse, axis=0).astype(jnp.bfloat16),
            "dom",
            split_axis=0,
            concat_axis=0,
            tiled=True,
        )
        .astype(jnp.float32)
        .reshape(row_count, width)
    )
    row_grad = own_grad + returned
    new_row_accum = row_accum + jnp.mean(row_grad * row_grad, axis=-1)
    new_embeddings = embeddings - learn_rate * row_grad / jnp.sqrt(new_row_accum)[:, None]
    rel_flat = relations.reshape(rel_count * width, width)
    accum_flat = rel_accum.reshape(rel_count * width)
    summed = lax.psum(rel_term, ("dom", "sub"))
    new_rel, new_racc = refresh(summed, rel_flat, accum_flat)
    return (
        new_embeddings,
        new_row_accum,
        new_rel.reshape(rel_count, width, width),
        new_racc.reshape(rel_count, width),
    )


def solution(mesh):
    placed = (
        P(("dom", "sub"), None),
        P(("dom", "sub")),
        P(),
        P(),
        P(),
        P(("dom", "sub")),
        P(("dom", "sub")),
        P(("dom", "sub")),
        P(("dom", "sub"), None),
    )
    return jax.shard_map(
        body,
        mesh=mesh,
        in_specs=placed,
        out_specs=(P(("dom", "sub"), None), P(("dom", "sub")), P(), P()),
        check_vma=False,
    )
```

profile of v0, /device:TPU:1, one launch (start us, length us, event | category | flops | bytes accessed | tf_op | source)
XLA Modules:
  0.0 525.6 jit_solution(14680909028433447135)
XLA Ops:
  7.2 1.1 convert_element_type.76
  8.3 0.7 reshape.162
  9.0 14.6 %all-to-all-start = ((bf16[64,4,256]{2,1,0:T(4,128)(2,1)}), bf16[64,4,256]{2,1,0:T(4,128)(2,1)S(1)}, u32[]{:S(2)}, u32[]{:S(2)}) async-start(bf16[64,4,256]{2,1,0:T(4,128)(2,1)} %reshape.162), calls=%async_computation | async-start | bytes 262144 | tf_op jit(solution)/shard_map/all_to_all | solution.py:24
  23.6 0.0 all-gather.2.cloned.1.call-start
  23.6 0.7 compare_select_fusion.2
  24.3 0.7 compare_and_fusion.1
  25.0 8.7 %all-to-all-done = bf16[64,4,256]{2,1,0:T(4,128)(2,1)S(1)} async-done(((bf16[64,4,256]{2,1,0:T(4,128)(2,1)}), bf16[64,4,256]{2,1,0:T(4,128)(2,1)S(1)}, u32[]{:S(2)}, u32[]{:S(2)}) %all-to-all-start) | async-done | bytes 131104 | tf_op jit(solution)/shard_map/all_to_all | solution.py:24
  33.7 0.7 gather_fusion
  34.4 0.1 broadcast_select_fusion
  34.5 14.7 %all_to_all.20 = bf16[64,4,256]{2,1,0:T(4,128)(2,1)S(1)} all-to-all(bf16[64,4,256]{2,1,0:T(4,128)(2,1)S(1)} %broadcast_select_fusion), channel_id=1, replica_groups=mesh['dom'=64,'sub'=8] {'dom'}, dimensions={0} | all-to-all | bytes 262144 | tf_op jit(solution)/shard_map/all_to_all | solution.py:28
  49.2 0.7 reshape.163
  50.0 0.0 reduce-scatter.2.cloned.1.call-start
  50.0 0.3 convolution_convert_fusion.1
  50.3 0.9 copy.27
  51.2 0.6 copy.28
  51.8 62.8 %all-gather.2.cloned.1.call-done = bf16[2048,256]{1,0:T(8,128)(2,1)} async-done(((bf16[256,256]{1,0:T(8,128)(2,1)}), bf16[2048,256]{1,0:T(8,128)(2,1)}) %all-gather.2.cloned.1.call-update) | async-done | bytes 1048592 | tf_op jit(solution)/shard_map/all_gather | solution.py:32
  114.7 2.8 fusion.11
  117.4 0.9 fusion.24
  118.3 0.5 fusion.10
  118.8 0.3 convolution_convert_fusion
  119.2 0.4 copy-done.11
  119.6 0.1 fusion.23
  119.7 2.6 fusion.4
  122.3 0.0 reduce-scatter.2.cloned.1.call-update
  122.4 0.0 all-reduce.2.cloned.1.call-start
  122.4 2.2 fusion.15
  124.6 1.8 copy.34
  126.4 1.1 broadcast_multiply_fusion
  127.5 2.0 fusion.41
  129.6 0.9 copy-done.1
  130.5 0.8 copy.33
  131.3 0.1 select_reduce_fusion
  131.5 2.0 multiply_reduce_fusion
  133.5 77.8 %reduce-scatter.2.cloned.1.call-done = bf16[256,256]{1,0:T(8,128)(2,1)} async-done(((bf16[2048,256]{1,0:T(8,128)(2,1)}), bf16[256,256]{1,0:T(8,128)(2,1)}) %reduce-scatter.2.cloned.1.call-update) | async-done | bytes 131088 | tf_op jit(solution)/shard_map/reduce_scatter | solution.py:80
  211.3 1.6 convert_element_type.90
  212.9 9.8 %all-to-all-start.2 = ((bf16[64,4,256]{2,1,0:T(4,128)(2,1)}), bf16[64,4,256]{2,1,0:T(4,128)(2,1)S(1)}, u32[]{:S(2)}, u32[]{:S(2)}) async-start(bf16[64,4,256]{2,1,0:T(4,128)(2,1)} %convert_element_type.90), calls=%async_computation.3 | async-start | bytes 262144 | tf_op jit(solution)/shard_map/all_to_all | solution.py:86
  222.7 271.4 %all-reduce.2.cloned.1.call-done = f32[2048,256]{1,0:T(8,128)} async-done(((f32[2048,256]{1,0:T(8,128)}), f32[2048,256]{1,0:T(8,128)}) %all-reduce.2.cloned.1.call-update) | async-done | bytes 2097168 | tf_op jit(solution)/shard_map/psum | solution.py:111
  494.1 1.9 multiply_reduce_fusion.1
  496.1 0.7 gather_fusion.1
  496.8 0.8 select_convert_fusion
  497.6 9.4 %all-to-all-start.3 = ((bf16[64,4,256]{2,1,0:T(4,128)(2,1)}), bf16[64,4,256]{2,1,0:T(4,128)(2,1)S(1)}, u32[]{:S(2)}, u32[]{:S(2)}) async-start(bf16[64,4,256]{2,1,0:T(4,128)(2,1)} %select_convert_fusion), calls=%async_computation.4 | async-start | bytes 262144 | tf_op jit(solution)/shard_map/all_to_all | solution.py:96
  507.0 3.5 bitcast_subtract_fusion
  510.5 0.6 add.72
  511.1 5.9 %all-to-all-done.3 = bf16[64,4,256]{2,1,0:T(4,128)(2,1)S(1)} async-done(((bf16[64,4,256]{2,1,0:T(4,128)(2,1)}), bf16[64,4,256]{2,1,0:T(4,128)(2,1)S(1)}, u32[]{:S(2)}, u32[]{:S(2)}) %all-to-all-start.3) | async-done | bytes 131104 | tf_op jit(solution)/shard_map/all_to_all | solution.py:96
  517.1 0.1 copy.32
  517.2 0.4 multiply_reduce_fusion.2
  517.6 0.6 fusion.40
  518.2 0.8 copy.35
  (39 shorter events, 0.2 us)
Async XLA Ops:
  7.2 42.9 %copy-start.5 = (s32[512]{0:T(512)S(1)}, s32[512]{0:T(512)}, u32[]{:S(2)}) copy-start(s32[512]{0:T(512)} %param.14) | copy-start | bytes 6148
  7.2 44.0 %copy-start = (f32[8,256,256]{2,1,0:T(8,128)S(1)}, f32[8,256,256]{2,1,0:T(8,128)}, u32[]{:S(2)}) copy-start(f32[8,256,256]{2,1,0:T(8,128)} %param.11) | copy-start | bytes 6291460
  9.0 24.7 %all-to-all-start = ((bf16[64,4,256]{2,1,0:T(4,128)(2,1)}), bf16[64,4,256]{2,1,0:T(4,128)(2,1)S(1)}, u32[]{:S(2)}, u32[]{:S(2)}) async-start(bf16[64,4,256]{2,1,0:T(4,128)(2,1)} %reshape.162), calls=%async_computation | async-start | bytes 262144 | tf_op jit(solution)/shard_map/all_to_all | solution.py:24
  23.6 91.1 %all-gather.2.cloned.1.call-start = ((), (), s32[]{:S(2)}) async-start(), calls=%async_computation.5 | async-start | bytes 1179648 | tf_op jit(solution)/shard_map/all_gather | solution.py:32
  49.9 1.8 copy-start.6
  49.9 1.8 copy-start.7
  49.9 1.8 copy-start.8
  50.0 161.3 %reduce-scatter.2.cloned.1.call-start = ((), (), s32[]{:S(2)}) async-start(), calls=%async_computation.6 | async-start | bytes 1179648 | tf_op jit(solution)/shard_map/reduce_scatter | solution.py:80
  114.7 2.8 copy-start.3
  117.4 0.9 copy-start.12
  118.8 0.8 copy-start.11
  122.4 371.8 %all-reduce.2.cloned.1.call-start = ((), (), s32[]{:S(2)}) async-start(), calls=%async_computation.7 | async-start | bytes 4194304 | tf_op jit(solution)/shard_map/psum | solution.py:111
  129.5 0.9 copy-start.1
  129.5 1.8 copy-start.4
  129.5 1.8 copy-start.10
  212.9 283.2 %all-to-all-start.2 = ((bf16[64,4,256]{2,1,0:T(4,128)(2,1)}), bf16[64,4,256]{2,1,0:T(4,128)(2,1)S(1)}, u32[]{:S(2)}, u32[]{:S(2)}) async-start(bf16[64,4,256]{2,1,0:T(4,128)(2,1)} %convert_element_type.90), calls=%async_computation.3 | async-start | bytes 262144 | tf_op jit(solution)/shard_map/all_to_all | solution.py:86
  497.6 19.5 %all-to-all-start.3 = ((bf16[64,4,256]{2,1,0:T(4,128)(2,1)}), bf16[64,4,256]{2,1,0:T(4,128)(2,1)S(1)}, u32[]{:S(2)}, u32[]{:S(2)}) async-start(bf16[64,4,256]{2,1,0:T(4,128)(2,1)} %select_convert_fusion), calls=%async_computation.4 | async-start | bytes 262144 | tf_op jit(solution)/shard_map/all_to_all | solution.py:96
  507.0 10.6 %copy-start.9 = (f32[256]{0:T(256)S(1)}, f32[256]{0:T(256)}, u32[]{:S(2)}) copy-start(f32[256]{0:T(256)} %param.10) | copy-start | bytes 3076
  507.0 11.2 %copy-start.2 = (f32[256,256]{0,1:T(8,128)S(1)}, f32[256,256]{0,1:T(8,128)}, u32[]{:S(2)}) copy-start(f32[256,256]{0,1:T(8,128)} %copy.33) | copy-start | bytes 786436
Sparse Core Ops, SparseCore 0:
  50.1 64.5 all-gather.1
  122.5 88.7 reduce-scatter.1
  217.6 276.5 all-reduce.1
where the time goes:
time: 526 us
  waiting for transfers between devices  427 us (81%)
  starting transfers between devices  33.9 us (6%)
  blocking collectives  14.7 us (3%)
  between operations  14 us (3%)
  matrix products  13.9 us (3%)
  other arithmetic  11.4 us (2%)
  local copies, waits for them, and re-layouts  10.8 us (2%)
    psum x1, waiting for transfers between devices, body(): summed = lax.psum(rel_term, ('dom', 'sub'))  271 us
    reduce_scatter x1, waiting for transfers between devices, body(): lax.psum_scatter(jnp.dot(onehot, grad_rows, preferred_element_type=jnp.fl...  77.8 us
    all_gather x1, waiting for transfers between devices, body(): shard_rows = lax.all_gather(partner_slice, 'sub', axis=0, tiled=True)  62.8 us
    all_to_all x1, blocking collectives, body(): lax.all_to_all(routed, 'dom', split_axis=0, concat_axis=0, tiled=True)  14.7 us
    all_to_all x1, starting transfers between devices, body(): lax.all_to_all(own_b.reshape(dom_size, piece_rows, width), 'dom', split_a...  14.6 us
  transfers between devices with their start and end apart: 6, of which 5 were waited for; matrix products, arithmetic and copies ran while one was open for 4% of the time, Pallas kernels for 0%

commit v1 on v0

v1 whole, which is shorter than its diff:
```python
import jax
import jax.numpy as jnp
from jax import lax
from jax.sharding import Mesh, PartitionSpec as P

learn_rate = 0.1
AXES = ("zlo", "y", "core", "zhi", "x")
DOM = ("zlo", "y", "core")
SUB = ("zhi", "x")
bf16 = jnp.bfloat16
f32 = jnp.float32


def swap(value, axis):
    return lax.ppermute(value, axis, [(0, 1), (1, 0)])


def spread(value, axis):
    return lax.all_to_all(value, axis, split_axis=0, concat_axis=0, tiled=True)


def to_pieces(block):
    return block.reshape(32, 8, 2, 128).transpose(2, 0, 1, 3).reshape(64, 8, 128)


def from_pieces(pieces):
    return pieces.reshape(2, 32, 8, 128).transpose(1, 2, 0, 3).reshape(256, 256)


def body(
    embeddings, row_accum, relations, rel_accum, matching, src_rows, dst_rows, rel_ids, neg_rows
):
    core = lax.axis_index("core")
    zhi = lax.axis_index("zhi")
    own_b = embeddings.astype(bf16)
    index = jnp.stack([src_rows, rel_ids, dst_rows, neg_rows.reshape(-1)])
    other_b = swap(own_b, "zhi")
    other_index = swap(index, "zhi")

    arrived = spread(to_pieces(own_b), DOM)
    routed = jnp.take(arrived, matching, axis=0)
    partner_slice = spread(routed, DOM)
    rows4 = spread(jnp.broadcast_to(partner_slice[None], (4, 64, 8, 128)), "x")
    rows = rows4.reshape(4, 2, 256, 128).transpose(0, 2, 1, 3).reshape(1024, 256)

    rel_b = relations.astype(bf16)
    both = jnp.stack([index, other_index])
    src_i, rel_i = both[:, 0], both[:, 1]
    dst_i, neg_i = both[:, 2] - zhi * 1024, both[:, 3] - zhi * 1024
    local = lax.iota(jnp.int32, 256)
    src_hot = (src_i[:, :, None] == local).astype(bf16)
    source = jnp.einsum(
        "ser,srj->sej", src_hot, jnp.stack([own_b, other_b]), preferred_element_type=f32
    ).astype(bf16)
    slots = lax.iota(jnp.int32, 8)
    mask = (rel_i[:, :, None] == slots).astype(bf16)
    masked_src = (mask[:, :, :, None] * source[:, :, None, :]).reshape(1024, 2048)
    trans = jnp.dot(
        masked_src, rel_b.transpose(0, 2, 1).reshape(2048, 256), preferred_element_type=f32
    ).astype(bf16)
    wide = lax.iota(jnp.int32, 1024)
    counts = jnp.sum((neg_i[:, :, None] == wide).astype(f32), axis=1)

    score = jnp.dot(trans, rows.T, preferred_element_type=f32).reshape(2, 512, 1024)
    sig = jax.nn.sigmoid(score)
    hit = dst_i[:, :, None] == wide
    weight = counts[:, None, :] * sig + jnp.where(hit, sig - 1.0, 0.0)
    weight = weight.astype(bf16).reshape(1024, 1024)
    g_trans = jnp.dot(weight, rows, preferred_element_type=f32).astype(bf16)
    g_rows = lax.dot_general(weight, trans, (((0,), (0,)), ((), ())), preferred_element_type=f32)
    masked_g = (mask.reshape(1024, 8)[:, :, None] * g_trans[:, None, :]).reshape(1024, 2048)
    rel_grad = lax.dot_general(
        masked_g, source.reshape(1024, 256), (((0,), (0,)), ((), ())), preferred_element_type=f32
    ).reshape(2, 1024, 256)
    g_src = jnp.dot(masked_g, rel_b.reshape(2048, 256), preferred_element_type=f32)
    own = jnp.einsum(
        "ser,sej->srj", src_hot, g_src.astype(bf16).reshape(2, 512, 256), preferred_element_type=f32
    )
    own_here = own[0] + swap(own[1].astype(bf16), "zhi").astype(f32)

    kept = lax.dynamic_index_in_dim(rel_grad, core, 0, keepdims=False)
    given = lax.dynamic_index_in_dim(rel_grad, 1 - core, 0, keepdims=False)
    half = (kept + swap(given.astype(bf16), "core").astype(f32)).astype(bf16)
    out = jnp.stack(
        [g_rows.astype(bf16).reshape(4, 256, 256), half.reshape(4, 256, 256)], axis=1
    )
    got = jnp.sum(spread(out, "x").astype(f32), axis=0).astype(bf16)
    pieces = jnp.concatenate([to_pieces(got[0]), to_pieces(got[1])], axis=1)
    mid = spread(pieces, DOM)
    spots = lax.iota(jnp.int32, 64)
    inverse = jnp.sum(jnp.where(matching[None, :] == spots[:, None], spots[None, :], 0), axis=1)
    row_mid = jnp.take(mid[:, :8], inverse, axis=0)
    rel_mid = jnp.sum(mid[:, 8:].astype(f32).reshape(32, 2, 8, 128), axis=0)
    rel_mid = (rel_mid + swap(rel_mid, "zhi")).astype(bf16)
    rel_out = jnp.broadcast_to(rel_mid[None], (32, 2, 8, 128)).reshape(64, 8, 128)
    last = spread(jnp.concatenate([row_mid, rel_out], axis=1), DOM)
    returned = from_pieces(last[:, :8]).astype(f32)
    rel_one = from_pieces(last[:, 8:])
    rel_four = spread(jnp.broadcast_to(rel_one[None], (4, 256, 256)), "x")
    rel_rest = swap(rel_four, "core")
    first = jnp.where(core == 0, rel_four, rel_rest)
    second = jnp.where(core == 0, rel_rest, rel_four)
    total = jnp.concatenate([first, second], axis=0).astype(f32)

    row_grad = own_here + returned
    new_row_accum = row_accum + jnp.mean(row_grad * row_grad, axis=-1)
    new_embeddings = embeddings - learn_rate * row_grad / jnp.sqrt(new_row_accum)[:, None]
    new_rel_accum = rel_accum + jnp.mean(total * total, axis=-1)
    new_relations = relations - learn_rate * total / jnp.sqrt(new_rel_accum)[:, :, None]
    return new_embeddings, new_row_accum, new_relations, new_rel_accum


def solution(mesh):
    fine = Mesh(mesh.devices.reshape(4, 8, 2, 2, 4), AXES)
    placed = (
        P(AXES, None),
        P(AXES),
        P(),
        P(),
        P(),
        P(AXES),
        P(AXES),
        P(AXES),
        P(AXES, None),
    )
    return jax.shard_map(
        body,
        mesh=fine,
        in_specs=placed,
        out_specs=(P(AXES, None), P(AXES), P(), P()),
        check_vma=False,
    )
```

time: 526 us -> 186 us (0.35)
  waiting for transfers between devices: 427 us -> 48.3 us
  starting transfers between devices: 33.9 us -> 80.6 us
  blocking collectives: 14.7 us -> 0 us
  between operations: 14 us -> 1.15 us
  other arithmetic: 11.4 us -> 22.6 us
    psum x1 -> x0, waiting for transfers between devices: 271 us -> none  [body(): summed = lax.psum(rel_term, ('dom', 'sub'))]
    reduce_scatter x1 -> x0, waiting for transfers between devices: 77.8 us -> none  [body(): lax.psum_scatter(jnp.dot(onehot, grad_rows, preferred_element_type=jnp.fl...]
    all_gather x1 -> x0, waiting for transfers between devices: 62.8 us -> none  [body(): shard_rows = lax.all_gather(partner_slice, 'sub', axis=0, tiled=True)]
    ppermute x0 -> x6, starting transfers between devices: none -> 35.4 us  [swap(): return lax.ppermute(value, axis, [(0, 1), (1, 0)])]
    all_to_all x3 -> x7, waiting for transfers between devices: 14.6 us -> 48 us  [spread(): return lax.all_to_all(value, axis, split_axis=0, concat_axis=0, tiled=True)]
    all_to_all x1 -> x0, blocking collectives: 14.7 us -> none  [body(): lax.all_to_all(routed, 'dom', split_axis=0, concat_axis=0, tiled=True)]
    all_to_all x3 -> x7, starting transfers between devices: 33.8 us -> 45.1 us  [spread(): return lax.all_to_all(value, axis, split_axis=0, concat_axis=0, tiled=True)]
    mul x1 -> x3, other arithmetic: 1.11 us -> 6.87 us  [the longest x1 3.51 us: body(): mask[:, :, :, None] * source[:, :, None, :]]
  transfers between devices with their start and end apart: 6 -> 13, of which waited for: 5 -> 8; matrix products, arithmetic and copies ran while one was open for 4% -> 17% of each run, Pallas kernels for 0% -> 0%
where the time goes in v1:
time: 186 us; the launch traced here: 184 us
  starting transfers between devices  80.6 us (43%)
  waiting for transfers between devices  48.3 us (26%)
  other arithmetic  22.6 us (12%)
  matrix products  18 us (10%)
  local copies, waits for them, and re-layouts  13.2 us (7%)
    all_to_all x7, waiting for transfers between devices, spread(): return lax.all_to_all(value, axis, split_axis=0, concat_axis=0, tiled=True)  48 us
    all_to_all x7, starting transfers between devices, spread(): return lax.all_to_all(value, axis, split_axis=0, concat_axis=0, tiled=True)  45.1 us
    ppermute x6, starting transfers between devices, swap(): return lax.ppermute(value, axis, [(0, 1), (1, 0)])  35.4 us
    unnamed x23, local copies, waits for them, and re-layouts  7.57 us
    dot_general x1, matrix products, body(): jnp.dot(trans, rows.T, preferred_element_type=f32).reshape(2, 512, 1024)  5.37 us
    dot_general x1, matrix products, body(): jnp.dot(masked_src, rel_b.transpose(0, 2, 1).reshape(2048, 256), preferre...  4.28 us
  transfers between devices with their start and end apart: 13, of which 8 were waited for; matrix products, arithmetic and copies ran while one was open for 17% of the time, Pallas kernels for 0%

profile of v1, /device:TPU:1, one launch (start us, length us, event | category | flops | bytes accessed | tf_op | source)
XLA Modules:
  0.0 183.9 jit_solution(12647199212685975150)
XLA Ops:
  0.6 0.7 fusion.28
  1.4 11.5 %collective-permute-start = (s32[4,512]{1,0:T(4,128)S(1)}, s32[4,512]{1,0:T(4,128)S(1)}, u32[]{:S(2)}, u32[]{:S(2)}) collective-permute-start(s32[4,512]{1,0:T(4,128)S(1)} %get-tuple-element.42), channel_id=1, source_target_pairs={{0,4},{4,0},{1,5},{5,1},{2,6},{6,2},{3,7},{7,3},{8,12},{12,8},{9,1... | collective-permute-start | bytes 24584 | tf_op jit(solution)/shard_map/ppermute | solution.py:15
  12.9 1.0 convert_element_type.84
  13.8 1.9 %collective-permute-start.1 = (bf16[256,256]{1,0:T(8,128)(2,1)S(1)}, bf16[256,256]{1,0:T(8,128)(2,1)S(1)}, u32[]{:S(2)}, u32[]{:S(2)}) collective-permute-start(bf16[256,256]{1,0:T(8,128)(2,1)S(1)} %convert_element_type.84), channel_id=1, source_target_pairs={{0,4},{4,0},{1,5},{5,1},{2,6},{6,2},{3,7},{7,3},{8,12},{12,8},{9,1... | collective-permute-start | bytes 393224 | tf_op jit(solution)/shard_map/ppermute | solution.py:15
  15.8 1.0 convert_bitcast_fusion.1
  16.7 0.7 copy.58
  17.4 11.3 %all-to-all-start = ((bf16[64,8,128]{2,1,0:T(8,128)(2,1)}), bf16[64,8,128]{2,1,0:T(8,128)(2,1)S(1)}, u32[]{:S(2)}, u32[]{:S(2)}) async-start(bf16[64,8,128]{2,1,0:T(8,128)(2,1)} %bitcast.13), calls=%async_computation | async-start | bytes 262144 | tf_op jit(solution)/shard_map/all_to_all | solution.py:19
  28.7 1.0 convert_bitcast_fusion.2
  30.4 0.7 compare_and_fusion.1
  31.0 1.8 copy.57
  33.1 3.0 %fusion = f32[2,512,1024]{2,1,0:T(8,128)} fusion(s32[2,512]{1,0:T(2,128)S(1)} %bitcast.132), kind=kOutput, calls=%fused_computation.2 | output fusion | flops 2099711 | bytes 4198400 | tf_op jit(solution)/shard_map/mul | solution.py:67
  36.5 2.3 %all-to-all-done = bf16[64,8,128]{2,1,0:T(8,128)(2,1)S(1)} async-done(((bf16[64,8,128]{2,1,0:T(8,128)(2,1)}), bf16[64,8,128]{2,1,0:T(8,128)(2,1)S(1)}, u32[]{:S(2)}, u32[]{:S(2)}) %all-to-all-start) | async-done | bytes 131104 | tf_op jit(solution)/shard_map/all_to_all | solution.py:19
  39.5 0.8 broadcast_select_fusion.3
  40.2 8.4 %all-to-all-start.1 = ((bf16[64,8,128]{2,1,0:T(8,128)(2,1)}), bf16[64,8,128]{2,1,0:T(8,128)(2,1)S(1)}, u32[]{:S(2)}, u32[]{:S(2)}) async-start(bf16[64,8,128]{2,1,0:T(8,128)(2,1)} %broadcast_select_fusion.3), calls=%async_computation.1 | async-start | bytes 262144 | tf_op jit(solution)/shard_map/all_to_all | solution.py:19
  48.7 3.5 %broadcast_multiply_fusion.1 = bf16[2,512,8,256]{3,2,1,0:T(8,128)(2,1)S(1)} fusion(bf16[2,512,256]{2,1,0:T(8,128)(2,1)S(1)} %convolution_convert_fusion.2, bf16[2,512,8]{2,1,0:T(8,128)(2,1)S(1)} %fusion.14), kind=kLoop, calls=%fused_computation.14 | loop fusion | flops 2097152 | bytes 4734976 | tf_op jit(solution)/shard_map/mul | solution.py:57
  52.2 3.4 %copy.80 = bf16[128,8,8,256]{3,1,2,0:T(8,128)(2,1)} copy(bf16[128,8,8,256]{3,2,1,0:T(8,128)(2,1)S(1)} %bitcast.115) | data formatting | bytes 8388608
  55.6 3.1 %all-to-all-done.1 = bf16[64,8,128]{2,1,0:T(8,128)(2,1)S(1)} async-done(((bf16[64,8,128]{2,1,0:T(8,128)(2,1)}), bf16[64,8,128]{2,1,0:T(8,128)(2,1)S(1)}, u32[]{:S(2)}, u32[]{:S(2)}) %all-to-all-start.1) | async-done | bytes 131104 | tf_op jit(solution)/shard_map/all_to_all | solution.py:19
  58.7 0.9 broadcast_in_dim.33
  59.6 4.0 %all-to-all-start.2 = ((bf16[4,64,8,128]{3,2,1,0:T(8,128)(2,1)}), bf16[4,64,8,128]{3,2,1,0:T(8,128)(2,1)S(1)}, u32[]{:S(2)}, u32[]{:S(2)}) async-start(bf16[4,64,8,128]{3,2,1,0:T(8,128)(2,1)} %broadcast_in_dim.33), calls=%async_computation.2 | async-start | bytes 1048576 | tf_op jit(solution)/shard_map/all_to_all | solution.py:19
  63.6 4.3 %convolution_convert_fusion.3 = bf16[1024,256]{1,0:T(8,128)(2,1)} fusion(bf16[1024,2048]{1,0:T(8,128)(2,1)} %bitcast.117, bf16[2048,256]{1,0:T(8,128)(2,1)S(1)} %bitcast.121), kind=kOutput, calls=%fused_computation.21 | convolution fusion | flops 1074003968 | bytes 5767168 | tf_op jit(solution)/shard_map/dot_general | solution.py:58
  67.9 4.6 %all-to-all-done.2 = bf16[4,64,8,128]{3,2,1,0:T(8,128)(2,1)S(1)} async-done(((bf16[4,64,8,128]{3,2,1,0:T(8,128)(2,1)}), bf16[4,64,8,128]{3,2,1,0:T(8,128)(2,1)S(1)}, u32[]{:S(2)}, u32[]{:S(2)}) %all-to-all-start.2) | async-done | bytes 524320 | tf_op jit(solution)/shard_map/all_to_all | solution.py:19
  73.4 5.4 %add_convert_fusion = bf16[2,512,1024]{2,1,0:T(8,128)(2,1)} fusion(f32[2,512,1024]{2,1,0:T(8,128)} %fusion, bf16[2,512,256]{2,1,0:T(8,128)(2,1)} %bitcast.139, bf16[1024,256,1]{1,0,2:T(8,128)(2,1)S(1)} %reshape.171, s32[2,512]{1,0:T(2,128)S(1)} %bitcast.134), kind=kOutput, calls=%fused_computation.3 | convolution fusion | flops 546308096 | bytes 7344128 | tf_op jit(solution)/shard_map/dot_general | solution.py:64
  78.8 2.3 %convolution_convert_fusion.1 = bf16[1024,256]{1,0:T(8,128)(2,1)S(1)} fusion(bf16[1024,1024]{1,0:T(8,128)(2,1)} %bitcast.16, bf16[128,8,2,128]{3,2,1,0:T(2,128)(2,1)S(1)} %bitcast.119), kind=kOutput, calls=%fused_computation.18 | convolution fusion | flops 537133056 | bytes 3145728 | tf_op jit(solution)/shard_map/dot_general | solution.py:69
  81.6 1.3 fusion.33
  82.9 1.3 copy-done.2
  84.3 3.5 %collective-permute-start.3 = (bf16[1024,256]{1,0:T(8,128)(2,1)S(1)}, bf16[1024,256]{1,0:T(8,128)(2,1)S(1)}, u32[]{:S(2)}, u32[]{:S(2)}) collective-permute-start(bf16[1024,256]{1,0:T(8,128)(2,1)S(1)} %fusion.9), channel_id=1, source_target_pairs={{0,8},{8,0},{1,9},{9,1},{2,10},{10,2},{3,11},{11,3},{4,12},{12,4},... | collective-permute-start | bytes 1572872 | tf_op jit(solution)/shard_map/ppermute | solution.py:15
  87.8 2.6 %convolution_convert_fusion = bf16[1024,256]{1,0:T(8,128)(2,1)S(1)} fusion(bf16[1024,1024]{1,0:T(8,128)(2,1)} %bitcast.16, bf16[1024,256]{1,0:T(8,128)(2,1)} %convolution_convert_fusion.3), kind=kOutput, calls=%fused_computation.17 | convolution fusion | flops 537133056 | bytes 3145728 | tf_op jit(solution)/shard_map/dot_general | solution.py:70
  90.5 1.1 pad_maximum_fusion
  91.6 3.5 %all-to-all-start.3 = ((bf16[4,2,256,256]{3,2,1,0:T(8,128)(2,1)}), bf16[4,2,256,256]{3,2,1,0:T(8,128)(2,1)S(1)}, u32[]{:S(2)}, u32[]{:S(2)}) async-start(bf16[4,2,256,256]{3,2,1,0:T(8,128)(2,1)} %pad_maximum_fusion), calls=%async_computation.3 | async-start | bytes 2097152 | tf_op jit(solution)/shard_map/all_to_all | solution.py:19
  95.4 15.0 %all-to-all-done.3 = bf16[4,2,256,256]{3,2,1,0:T(8,128)(2,1)S(1)} async-done(((bf16[4,2,256,256]{3,2,1,0:T(8,128)(2,1)}), bf16[4,2,256,256]{3,2,1,0:T(8,128)(2,1)S(1)}, u32[]{:S(2)}, u32[]{:S(2)}) %all-to-all-start.3) | async-done | bytes 1048608 | tf_op jit(solution)/shard_map/all_to_all | solution.py:19
  110.7 0.7 pad_maximum_fusion.2
  111.4 8.0 %all-to-all-start.4 = ((bf16[64,16,128]{2,1,0:T(8,128)(2,1)}), bf16[64,16,128]{2,1,0:T(8,128)(2,1)S(1)}, u32[]{:S(2)}, u32[]{:S(2)}) async-start(bf16[64,16,128]{2,1,0:T(8,128)(2,1)} %pad_maximum_fusion.2), calls=%async_computation.4 | async-start | bytes 524288 | tf_op jit(solution)/shard_map/all_to_all | solution.py:19
  119.5 12.2 %all-to-all-done.4 = bf16[64,16,128]{2,1,0:T(8,128)(2,1)S(1)} async-done(((bf16[64,16,128]{2,1,0:T(8,128)(2,1)}), bf16[64,16,128]{2,1,0:T(8,128)(2,1)S(1)}, u32[]{:S(2)}, u32[]{:S(2)}) %all-to-all-start.4) | async-done | bytes 262176 | tf_op jit(solution)/shard_map/all_to_all | solution.py:19
  131.8 7.5 %collective-permute-start.4 = (f32[2,8,128]{2,1,0:T(8,128)S(1)}, f32[2,8,128]{2,1,0:T(8,128)S(1)}, u32[]{:S(2)}, u32[]{:S(2)}) collective-permute-start(f32[2,8,128]{2,1,0:T(8,128)S(1)} %convert_reduce_fusion.1), channel_id=1, source_target_pairs={{0,4},{4,0},{1,5},{5,1},{2,6},{6,2},{3,7},{7,3},{8,12},{12,8},{9,1... | collective-permute-start | bytes 24584 | tf_op jit(solution)/shard_map/ppermute | solution.py:15
  140.4 0.7 pad_maximum_fusion.3
  141.2 6.3 %all-to-all-start.5 = ((bf16[64,16,128]{2,1,0:T(8,128)(2,1)}), bf16[64,16,128]{2,1,0:T(8,128)(2,1)S(1)}, u32[]{:S(2)}, u32[]{:S(2)}) async-start(bf16[64,16,128]{2,1,0:T(8,128)(2,1)} %pad_maximum_fusion.3), calls=%async_computation.5 | async-start | bytes 524288 | tf_op jit(solution)/shard_map/all_to_all | solution.py:19
  147.5 1.3 fusion.6
  149.4 10.4 %all-to-all-done.5 = bf16[64,16,128]{2,1,0:T(8,128)(2,1)S(1)} async-done(((bf16[64,16,128]{2,1,0:T(8,128)(2,1)}), bf16[64,16,128]{2,1,0:T(8,128)(2,1)S(1)}, u32[]{:S(2)}, u32[]{:S(2)}) %all-to-all-start.5) | async-done | bytes 262176 | tf_op jit(solution)/shard_map/all_to_all | solution.py:19
  159.9 0.8 broadcast_in_dim.39
  160.7 3.5 %all-to-all-start.6 = ((bf16[4,256,256]{2,1,0:T(8,128)(2,1)}), bf16[4,256,256]{2,1,0:T(8,128)(2,1)S(1)}, u32[]{:S(2)}, u32[]{:S(2)}) async-start(bf16[4,256,256]{2,1,0:T(8,128)(2,1)} %broadcast_in_dim.39), calls=%async_computation.6 | async-start | bytes 1048576 | tf_op jit(solution)/shard_map/all_to_all | solution.py:19
  164.2 0.7 fusion.20
  164.9 7.5 %collective-permute-start.2 = (bf16[256,256]{0,1:T(8,128)(2,1)}, bf16[256,256]{0,1:T(8,128)(2,1)}, u32[]{:S(2)}, u32[]{:S(2)}) collective-permute-start(bf16[256,256]{0,1:T(8,128)(2,1)} %fusion.20), channel_id=1, source_target_pairs={{0,4},{4,0},{1,5},{5,1},{2,6},{6,2},{3,7},{7,3},{8,12},{12,8},{9,1... | collective-permute-start | bytes 393224 | tf_op jit(solution)/shard_map/ppermute | solution.py:15
  172.9 3.5 %collective-permute-start.5 = (bf16[4,256,256]{2,1,0:T(8,128)(2,1)S(1)}, bf16[4,256,256]{2,1,0:T(8,128)(2,1)}, u32[]{:S(2)}, u32[]{:S(2)}) collective-permute-start(bf16[4,256,256]{2,1,0:T(8,128)(2,1)S(1)} %all-to-all-done.6), channel_id=1, source_target_pairs={{0,8},{8,0},{1,9},{9,1},{2,10},{10,2},{3,11},{11,3},{4,12},{12,4},... | collective-permute-start | bytes 1572872 | tf_op jit(solution)/shard_map/ppermute | solution.py:15
  176.5 1.1 multiply_reduce_fusion
  178.2 1.1 divide_subtract_fusion
  179.2 0.8 copy.72
  180.1 1.1 broadcast_select_fusion.1
  182.2 1.7 fusion.3
  (61 shorter events, 7.8 us)
Async XLA Ops:
  1.4 31.5 %collective-permute-start = (s32[4,512]{1,0:T(4,128)S(1)}, s32[4,512]{1,0:T(4,128)S(1)}, u32[]{:S(2)}, u32[]{:S(2)}) collective-permute-start(s32[4,512]{1,0:T(4,128)S(1)} %get-tuple-element.42), channel_id=1, source_target_pairs={{0,4},{4,0},{1,5},{5,1},{2,6},{6,2},{3,7},{7,3},{8,12},{12,8},{9,1... | collective-permute-start | bytes 24584 | tf_op jit(solution)/shard_map/ppermute | solution.py:15
  13.8 22.3 %collective-permute-start.1 = (bf16[256,256]{1,0:T(8,128)(2,1)S(1)}, bf16[256,256]{1,0:T(8,128)(2,1)S(1)}, u32[]{:S(2)}, u32[]{:S(2)}) collective-permute-start(bf16[256,256]{1,0:T(8,128)(2,1)S(1)} %convert_element_type.84), channel_id=1, source_target_pairs={{0,4},{4,0},{1,5},{5,1},{2,6},{6,2},{3,7},{7,3},{8,12},{12,8},{9,1... | collective-permute-start | bytes 393224 | tf_op jit(solution)/shard_map/ppermute | solution.py:15
  17.4 21.4 %all-to-all-start = ((bf16[64,8,128]{2,1,0:T(8,128)(2,1)}), bf16[64,8,128]{2,1,0:T(8,128)(2,1)S(1)}, u32[]{:S(2)}, u32[]{:S(2)}) async-start(bf16[64,8,128]{2,1,0:T(8,128)(2,1)} %bitcast.13), calls=%async_computation | async-start | bytes 262144 | tf_op jit(solution)/shard_map/all_to_all | solution.py:19
  40.2 18.5 %all-to-all-start.1 = ((bf16[64,8,128]{2,1,0:T(8,128)(2,1)}), bf16[64,8,128]{2,1,0:T(8,128)(2,1)S(1)}, u32[]{:S(2)}, u32[]{:S(2)}) async-start(bf16[64,8,128]{2,1,0:T(8,128)(2,1)} %broadcast_select_fusion.3), calls=%async_computation.1 | async-start | bytes 262144 | tf_op jit(solution)/shard_map/all_to_all | solution.py:19
  59.6 12.9 %all-to-all-start.2 = ((bf16[4,64,8,128]{3,2,1,0:T(8,128)(2,1)}), bf16[4,64,8,128]{3,2,1,0:T(8,128)(2,1)S(1)}, u32[]{:S(2)}, u32[]{:S(2)}) async-start(bf16[4,64,8,128]{3,2,1,0:T(8,128)(2,1)} %broadcast_in_dim.33), calls=%async_computation.2 | async-start | bytes 1048576 | tf_op jit(solution)/shard_map/all_to_all | solution.py:19
  82.9 1.3 copy-start.2
  84.3 6.1 %collective-permute-start.3 = (bf16[1024,256]{1,0:T(8,128)(2,1)S(1)}, bf16[1024,256]{1,0:T(8,128)(2,1)S(1)}, u32[]{:S(2)}, u32[]{:S(2)}) collective-permute-start(bf16[1024,256]{1,0:T(8,128)(2,1)S(1)} %fusion.9), channel_id=1, source_target_pairs={{0,8},{8,0},{1,9},{9,1},{2,10},{10,2},{3,11},{11,3},{4,12},{12,4},... | collective-permute-start | bytes 1572872 | tf_op jit(solution)/shard_map/ppermute | solution.py:15
  87.8 2.6 %copy-start.3 = (f32[2,1024,256]{2,1,0:T(8,128)S(1)}, f32[2,1024,256]{2,1,0:T(8,128)}, u32[]{:S(2)}) copy-start(f32[2,1024,256]{2,1,0:T(8,128)} %copy-done.2) | copy-start | bytes 6291460
  90.4 4.8 %copy-start.1 = (f32[256,256]{1,0:T(8,128)S(1)}, f32[256,256]{1,0:T(8,128)}, u32[]{:S(2)}) copy-start(f32[256,256]{1,0:T(8,128)} %param.11) | copy-start | bytes 786436
  90.4 4.9 %copy-start.7 = (s32[64]{0:T(128)S(1)}, s32[64]{0:T(128)}, u32[]{:S(2)}) copy-start(s32[64]{0:T(128)} %param.15) | copy-start | bytes 772
  91.6 18.7 %all-to-all-start.3 = ((bf16[4,2,256,256]{3,2,1,0:T(8,128)(2,1)}), bf16[4,2,256,256]{3,2,1,0:T(8,128)(2,1)S(1)}, u32[]{:S(2)}, u32[]{:S(2)}) async-start(bf16[4,2,256,256]{3,2,1,0:T(8,128)(2,1)} %pad_maximum_fusion), calls=%async_computation.3 | async-start | bytes 2097152 | tf_op jit(solution)/shard_map/all_to_all | solution.py:19
  111.4 20.3 %all-to-all-start.4 = ((bf16[64,16,128]{2,1,0:T(8,128)(2,1)}), bf16[64,16,128]{2,1,0:T(8,128)(2,1)S(1)}, u32[]{:S(2)}, u32[]{:S(2)}) async-start(bf16[64,16,128]{2,1,0:T(8,128)(2,1)} %pad_maximum_fusion.2), calls=%async_computation.4 | async-start | bytes 524288 | tf_op jit(solution)/shard_map/all_to_all | solution.py:19
  131.8 8.6 %collective-permute-start.4 = (f32[2,8,128]{2,1,0:T(8,128)S(1)}, f32[2,8,128]{2,1,0:T(8,128)S(1)}, u32[]{:S(2)}, u32[]{:S(2)}) collective-permute-start(f32[2,8,128]{2,1,0:T(8,128)S(1)} %convert_reduce_fusion.1), channel_id=1, source_target_pairs={{0,4},{4,0},{1,5},{5,1},{2,6},{6,2},{3,7},{7,3},{8,12},{12,8},{9,1... | collective-permute-start | bytes 24584 | tf_op jit(solution)/shard_map/ppermute | solution.py:15
  141.2 18.6 %all-to-all-start.5 = ((bf16[64,16,128]{2,1,0:T(8,128)(2,1)}), bf16[64,16,128]{2,1,0:T(8,128)(2,1)S(1)}, u32[]{:S(2)}, u32[]{:S(2)}) async-start(bf16[64,16,128]{2,1,0:T(8,128)(2,1)} %pad_maximum_fusion.3), calls=%async_computation.5 | async-start | bytes 524288 | tf_op jit(solution)/shard_map/all_to_all | solution.py:19
  148.8 28.8 %copy-start.6 = (f32[256]{0:T(256)S(1)}, f32[256]{0:T(256)}, u32[]{:S(2)}) copy-start(f32[256]{0:T(256)} %param.12) | copy-start | bytes 3076
  149.4 23.0 %copy-start.4 = (f32[2,256,256]{1,2,0:T(8,128)}, f32[2,256,256]{1,2,0:T(8,128)S(1)}, u32[]{:S(2)}) copy-start(f32[2,256,256]{1,2,0:T(8,128)S(1)} %fusion.8) | copy-start | bytes 1572868
  159.8 21.7 %copy-start.5 = (f32[8,256]{1,0:T(8,128)S(1)}, f32[8,256]{1,0:T(8,128)}, u32[]{:S(2)}) copy-start(f32[8,256]{1,0:T(8,128)} %param.14) | copy-start | bytes 24580
  159.9 22.3 %copy-start = (f32[8,256,256]{2,1,0:T(8,128)S(1)}, f32[8,256,256]{2,1,0:T(8,128)}, u32[]{:S(2)}) copy-start(f32[8,256,256]{2,1,0:T(8,128)} %param.13) | copy-start | bytes 6291460
  160.7 12.2 %all-to-all-start.6 = ((bf16[4,256,256]{2,1,0:T(8,128)(2,1)}), bf16[4,256,256]{2,1,0:T(8,128)(2,1)S(1)}, u32[]{:S(2)}, u32[]{:S(2)}) async-start(bf16[4,256,256]{2,1,0:T(8,128)(2,1)} %broadcast_in_dim.39), calls=%async_computation.6 | async-start | bytes 1048576 | tf_op jit(solution)/shard_map/all_to_all | solution.py:19
  164.9 11.6 %collective-permute-start.2 = (bf16[256,256]{0,1:T(8,128)(2,1)}, bf16[256,256]{0,1:T(8,128)(2,1)}, u32[]{:S(2)}, u32[]{:S(2)}) collective-permute-start(bf16[256,256]{0,1:T(8,128)(2,1)} %fusion.20), channel_id=1, source_target_pairs={{0,4},{4,0},{1,5},{5,1},{2,6},{6,2},{3,7},{7,3},{8,12},{12,8},{9,1... | collective-permute-start | bytes 393224 | tf_op jit(solution)/shard_map/ppermute | solution.py:15
  172.9 7.1 %collective-permute-start.5 = (bf16[4,256,256]{2,1,0:T(8,128)(2,1)S(1)}, bf16[4,256,256]{2,1,0:T(8,128)(2,1)}, u32[]{:S(2)}, u32[]{:S(2)}) collective-permute-start(bf16[4,256,256]{2,1,0:T(8,128)(2,1)S(1)} %all-to-all-done.6), channel_id=1, source_target_pairs={{0,8},{8,0},{1,9},{9,1},{2,10},{10,2},{3,11},{11,3},{4,12},{12,4},... | collective-permute-start | bytes 1572872 | tf_op jit(solution)/shard_map/ppermute | solution.py:15

commit v2 on v1

v2 whole, which is shorter than its diff:
```python
import functools

import jax
import jax.numpy as jnp
from jax import lax
from jax.experimental import pallas as pl
from jax.experimental.pallas import tpu as pltpu
from jax.sharding import Mesh, PartitionSpec as P

learn_rate = 0.1
AXES = ("zlo", "y", "core", "zhi", "x")
DOM = ("zlo", "y", "core")
bf16 = jnp.bfloat16
f32 = jnp.float32
VMEM = pl.BlockSpec(memory_space=pltpu.VMEM)
SMEM = pl.BlockSpec(memory_space=pltpu.SMEM)
NN = (((1,), (0,)), ((), ()))
NT = (((1,), (1,)), ((), ()))


def shape(dims, dtype):
    return jax.ShapeDtypeStruct(dims, dtype)


def dot(a, b, dims=NN):
    return lax.dot_general(a, b, dims, preferred_element_type=f32)


def call(kernel, outs, scalars, args, flops=0, moved=0, scratch=()):
    return pl.pallas_call(
        kernel,
        out_shape=outs,
        in_specs=[SMEM] * scalars + [VMEM] * (len(args) - scalars),
        out_specs=jax.tree.map(lambda _: VMEM, outs),
        scratch_shapes=list(scratch),
        compiler_params=pltpu.CompilerParams(vmem_limit_bytes=40 * 1024 * 1024),
        cost_estimate=pl.CostEstimate(flops=flops, bytes_accessed=moved, transcendentals=0),
    )(*args)


def swap(value, axis):
    return lax.ppermute(value, axis, [(0, 1), (1, 0)])


def spread(value, axis):
    return lax.all_to_all(value, axis, split_axis=0, concat_axis=0, tiled=True)


def pack_kernel(emb, src, rel, dst, neg, pieces, pack):
    for h in range(2):
        pieces[h * 32 : (h + 1) * 32] = emb[:, h * 128 : (h + 1) * 128].reshape(32, 8, 128).astype(bf16)
    pack[0:256, :] = emb[...].astype(bf16)
    wide = jnp.concatenate([src[...], rel[...], dst[...], neg[...]], axis=0)
    high = wide // 256
    low = (wide - high * 256).astype(f32)
    both = jnp.concatenate([high.astype(f32), low], axis=0)
    pack[256:272, :] = jnp.concatenate([both[:, :256], both[:, 256:]], axis=0).astype(bf16)


def indices(pack):
    part = pack[256:272, :].astype(f32)
    both = jnp.concatenate([part[0:8], part[8:16]], axis=1)
    return both[0:4] * 256.0 + both[4:8]


def columns(value):
    return jnp.concatenate([value, value], axis=0).T


def lane_ids(rows, width):
    return lax.broadcasted_iota(jnp.int32, (rows, width), 1).astype(f32)


def trans_kernel(zhi, own, other, rel, trans, source, rel_b, counts):
    for r in range(8):
        rel_b[r] = rel[r].astype(bf16)
    base = (zhi[0] * 1024).astype(f32)
    ids = lane_ids(512, 256)
    for s, pack in enumerate((own, other)):
        index = indices(pack)
        column = columns(index)
        hot = (column[:, 0:1] == ids).astype(f32).astype(bf16)
        rows = dot(hot, pack[0:256, :])
        source[s * 512 : (s + 1) * 512, :] = rows.astype(bf16)
        total = jnp.zeros((512, 256), f32)
        for r in range(8):
            masked = jnp.where(column[:, 1:2] == float(r), rows, 0.0).astype(bf16)
            total = total + dot(masked, rel_b[r], NT)
        trans[s * 512 : (s + 1) * 512, :] = total.astype(bf16)
        hits = (column[:, 3:4] - base == lane_ids(512, 1024)).astype(f32)
        counts[s : s + 1, :] = jnp.sum(hits, axis=0, keepdims=True)
    counts[2:8, :] = jnp.zeros((6, 1024), f32)


def score_kernel(
    place, rows4, trans, source, counts, own, other, weight, g_trans, kept, given, rows
):
    core = place[0]
    base = (place[1] * 1024).astype(f32)
    for k in range(4):
        rows[k * 256 : (k + 1) * 256, :] = jnp.concatenate([rows4[k, 0], rows4[k, 1]], axis=1)
    index = [indices(own), indices(other)]
    ids = lane_ids(256, 1024)
    for b in range(4):
        s = b // 2
        column = columns(index[s])[(b % 2) * 256 : (b % 2 + 1) * 256]
        span = slice(b * 256, (b + 1) * 256)
        score = dot(trans[span, :], rows[...], NT)
        sig = 1.0 / (1.0 + jnp.exp(-score))
        count = counts[s : s + 1, :]
        hit = column[:, 2:3] - base == ids
        part = jnp.where(hit, (count + 1.0) * sig - 1.0, count * sig).astype(bf16)
        weight[span, :] = part
        g_trans[span, :] = dot(part, rows[...]).astype(bf16)
    turned = g_trans[...].astype(f32).T
    kinds = jnp.concatenate([index[0][1:2], index[1][1:2]], axis=1)
    for r in range(8):
        wanted = r + 4 * core if r < 4 else r - 4 * core
        masked = jnp.where(kinds == wanted.astype(f32), turned, 0.0).astype(bf16)
        grad = dot(masked, source[...]).astype(bf16)
        if r < 4:
            kept[r * 256 : (r + 1) * 256, :] = grad
        else:
            given[(r - 4) * 256 : (r - 3) * 256, :] = grad


def back_kernel(weight, trans, g_trans, rel_b, own, other, g_rows, own_here, own_there):
    turned = trans[...].astype(f32).T.astype(bf16)
    for k in range(4):
        part = dot(turned, weight[:, k * 256 : (k + 1) * 256])
        g_rows[k] = part.T.astype(bf16)
    sub_ids = lax.broadcasted_iota(jnp.int32, (256, 512), 0).astype(f32)
    for s, pack in enumerate((own, other)):
        index = indices(pack)
        column = columns(index)
        grad = g_trans[s * 512 : (s + 1) * 512, :].astype(f32)
        total = jnp.zeros((512, 256), f32)
        for r in range(8):
            masked = jnp.where(column[:, 1:2] == float(r), grad, 0.0).astype(bf16)
            total = total + dot(masked, rel_b[r])
        hot = (index[0:1, :] == sub_ids).astype(f32).astype(bf16)
        mine = dot(hot, total.astype(bf16))
        if s == 0:
            own_here[...] = mine
        else:
            own_there[...] = mine.astype(bf16)


def join_kernel(g_rows, kept, came, out):
    for k in range(4):
        out[k, 0:256, :] = g_rows[k]
        span = slice(k * 256, (k + 1) * 256)
        out[k, 256:512, :] = (kept[span, :].astype(f32) + came[span, :].astype(f32)).astype(bf16)


def pieces_kernel(got, out):
    for h in range(2):
        half = slice(h * 128, (h + 1) * 128)
        total = got[0, :, half].astype(f32)
        for k in range(1, 4):
            total = total + got[k, :, half].astype(f32)
        both = total.reshape(2, 32, 8, 128)
        out[h * 32 : (h + 1) * 32] = jnp.concatenate([both[0], both[1]], axis=1).astype(bf16)


def middle_kernel(mid, rel_sum):
    for c in range(2):
        total = jnp.zeros((8, 128), f32)
        for k in range(32):
            total = total + mid[2 * k + c].astype(f32)[8:16]
        rel_sum[c] = total


def route_kernel(matching, mid, rel_sum, rel_came, out):
    rel = [rel_sum[c] + rel_came[c] for c in range(2)]
    for d in range(64):
        target = matching[d]
        tail = jnp.where(target % 2 == 0, rel[0], rel[1])
        out[target] = jnp.concatenate([mid[d].astype(f32)[0:8], tail], axis=0).astype(bf16)


def rel_kernel(last, out):
    for h in range(2):
        part = last[h * 32 : (h + 1) * 32].astype(f32)[:, 8:16].reshape(256, 128).astype(bf16)
        for k in range(4):
            out[k, :, h * 128 : (h + 1) * 128] = part


def to_row(column):
    return jnp.broadcast_to(column, (256, 128)).T[0:1]


def to_column(row):
    return jnp.broadcast_to(row, (128, 256)).T[:, 0:1]


def rows_kernel(emb, accum, own_here, own_came, last, new_emb, new_accum):
    halves = [
        last[h * 32 : (h + 1) * 32].astype(f32)[:, 0:8].reshape(256, 128) for h in range(2)
    ]
    grad = own_here[...] + own_came[...].astype(f32) + jnp.concatenate(halves, axis=1)
    total = to_column(accum[...]) + jnp.mean(grad * grad, axis=1, keepdims=True)
    new_emb[...] = emb[...] - learn_rate * grad / jnp.sqrt(total)
    new_accum[...] = to_row(total)


def update_kernel(place, rel, accum, four, rest, new_rel, new_accum):
    core = place[0]
    old = jnp.concatenate([accum[...], accum[...]], axis=0)
    ordered = jnp.where(core == 0, old[0:8], old[4:12])
    column = ordered.T
    totals = []
    for r in range(8):
        target = r + 4 * core if r < 4 else r - 4 * core
        grad = (four[r] if r < 4 else rest[r - 4]).astype(f32)
        total = column[:, r : r + 1] + jnp.mean(grad * grad, axis=1, keepdims=True)
        new_rel[target] = rel[target] - learn_rate * grad / jnp.sqrt(total)
        totals.append(total)
    rows = jnp.concatenate(totals, axis=1).T
    twice = jnp.concatenate([rows, rows], axis=0)
    new_accum[...] = jnp.where(core == 0, twice[0:8], twice[4:12])


def body(
    embeddings, row_accum, relations, rel_accum, matching, src_rows, dst_rows, rel_ids, neg_rows
):
    core = lax.axis_index("core").astype(jnp.int32)
    zhi = lax.axis_index("zhi").astype(jnp.int32)
    place = jnp.stack([core, zhi])
    line = lambda v: v.reshape(1, 512)
    pieces, pack = call(
        pack_kernel,
        (shape((64, 8, 128), bf16), shape((272, 256), bf16)),
        0,
        (embeddings, line(src_rows), line(rel_ids), line(dst_rows), line(neg_rows)),
    )
    arrived = spread(pieces, DOM)
    routed = jnp.take(arrived, matching, axis=0)
    other = swap(pack, "zhi")
    partner_slice = spread(routed, DOM)
    other, routed = lax.optimization_barrier((other, routed))
    trans, source, rel_b, counts = call(
        trans_kernel,
        (
            shape((1024, 256), bf16),
            shape((1024, 256), bf16),
            shape((8, 256, 256), bf16),
            shape((8, 1024), f32),
        ),
        1,
        (zhi.reshape(1), pack, other, relations),
        flops=1_300_000_000,
        moved=4_000_000,
    )
    rows4 = spread(jnp.broadcast_to(partner_slice[None], (4, 64, 8, 128)), "x")
    weight, g_trans, kept, given = call(
        score_kernel,
        (
            shape((1024, 1024), bf16),
            shape((1024, 256), bf16),
            shape((1024, 256), bf16),
            shape((1024, 256), bf16),
        ),
        1,
        (place, rows4.reshape(4, 2, 256, 128), trans, source, counts, pack, other),
        flops=2_200_000_000,
        moved=4_000_000,
        scratch=[pltpu.VMEM((1024, 256), bf16)],
    )
    came = swap(given, "core")
    g_rows, own_here, own_there = call(
        back_kernel,
        (shape((4, 256, 256), bf16), shape((256, 256), f32), shape((256, 256), bf16)),
        0,
        (weight, trans, g_trans, rel_b, pack, other),
        flops=1_700_000_000,
        moved=4_000_000,
    )
    own_came = swap(own_there, "zhi")
    joined = call(join_kernel, shape((4, 512, 256), bf16), 0, (g_rows, kept, came), moved=2_000_000)
    got = spread(joined, "x")
    mid = spread(call(pieces_kernel, shape((64, 16, 128), bf16), 0, (got,), moved=1_000_000), DOM)
    rel_sum = call(middle_kernel, shape((2, 8, 128), f32), 0, (mid,), moved=256_000)
    rel_came = swap(rel_sum, "zhi")
    routed_back = call(
        route_kernel,
        shape((64, 16, 128), bf16),
        1,
        (matching, mid, rel_sum, rel_came),
        moved=512_000,
    )
    last = spread(routed_back, DOM)
    rel_four = spread(call(rel_kernel, shape((4, 256, 256), bf16), 0, (last,), moved=512_000), "x")
    new_embeddings, new_row_accum = call(
        rows_kernel,
        (shape((256, 256), f32), shape((1, 256), f32)),
        0,
        (embeddings, row_accum.reshape(1, 256), own_here, own_came, last),
        flops=1_000_000,
        moved=1_000_000,
    )
    rel_rest = swap(rel_four, "core")
    new_relations, new_rel_accum = call(
        update_kernel,
        (shape((8, 256, 256), f32), shape((8, 256), f32)),
        1,
        (place, relations, rel_accum, rel_four, rel_rest),
        moved=5_000_000,
    )
    return new_embeddings, new_row_accum.reshape(256), new_relations, new_rel_accum


def solution(mesh):
    fine = Mesh(mesh.devices.reshape(4, 8, 2, 2, 4), AXES)
    placed = (
        P(AXES, None),
        P(AXES),
        P(),
        P(),
        P(),
        P(AXES),
        P(AXES),
        P(AXES),
        P(AXES, None),
    )
    return jax.shard_map(
        body,
        mesh=fine,
        in_specs=placed,
        out_specs=(P(AXES, None), P(AXES), P(), P()),
        check_vma=False,
    )
```

time: 186 us -> 177 us (0.952)
  blocking collectives: 0 us -> 84 us
  starting transfers between devices: 80.6 us -> 48 us
  waiting for transfers between devices: 48.3 us -> 16.8 us
  other arithmetic: 22.6 us -> 1.54 us
  matrix products: 18 us -> 0 us
  Pallas kernels: 0 us -> 15.7 us
  local copies, waits for them, and re-layouts: 13.2 us -> 8.18 us
    all_to_all x0 -> x5, blocking collectives: none -> 84 us  [spread(): return lax.all_to_all(value, axis, split_axis=0, concat_axis=0, tiled=True)]
    all_to_all x7 -> x2, waiting for transfers between devices: 48 us -> 8.75 us  [spread(): return lax.all_to_all(value, axis, split_axis=0, concat_axis=0, tiled=True)]
    all_to_all x7 -> x2, starting transfers between devices: 45.1 us -> 18.6 us  [spread(): return lax.all_to_all(value, axis, split_axis=0, concat_axis=0, tiled=True)]
    dot_general x8 -> x0, matrix products: 18 us -> none  [the longest x1 5.37 us: body(): jnp.dot(trans, rows.T, preferred_element_type=f32).reshape(2, 512, 1024)]
    pallas_call x0 -> x11, Pallas kernels: none -> 15.7 us  [call(): pl.pallas_call(kernel, out_shape=outs, in_specs=[SMEM] * scalars + [VMEM]...]
    ppermute x6 -> x5, waiting for transfers between devices: 0.27 us -> 8.06 us  [swap(): return lax.ppermute(value, axis, [(0, 1), (1, 0)])]
    mul x3 -> x0, other arithmetic: 6.87 us -> none  [the longest x1 3.51 us: body(): mask[:, :, :, None] * source[:, :, None, :]]
    ppermute x6 -> x5, starting transfers between devices: 35.4 us -> 29.4 us  [swap(): return lax.ppermute(value, axis, [(0, 1), (1, 0)])]
  transfers between devices with their start and end apart: 13 -> 7, of which waited for: 8 -> 4; matrix products, arithmetic and copies ran while one was open for 17% -> 1% of each run, Pallas kernels for 0% -> 4%
where the time goes in v2:
time: 177 us; the launch traced here: 175 us
  blocking collectives  84 us (47%)
  starting transfers between devices  48 us (27%)
  waiting for transfers between devices  16.8 us (9%)
  Pallas kernels  15.7 us (9%)
  local copies, waits for them, and re-layouts  8.18 us (5%)
    all_to_all x5, blocking collectives, spread(): return lax.all_to_all(value, axis, split_axis=0, concat_axis=0, tiled=True)  84 us
    ppermute x5, starting transfers between devices, swap(): return lax.ppermute(value, axis, [(0, 1), (1, 0)])  29.4 us
    all_to_all x2, starting transfers between devices, spread(): return lax.all_to_all(value, axis, split_axis=0, concat_axis=0, tiled=True)  18.6 us
    pallas_call x11, Pallas kernels, call(): pl.pallas_call(kernel, out_shape=outs, in_specs=[SMEM] * scalars + [VMEM]...  15.7 us
    all_to_all x2, waiting for transfers between devices, spread(): return lax.all_to_all(value, axis, split_axis=0, concat_axis=0, tiled=True)  8.75 us
    ppermute x5, waiting for transfers between devices, swap(): return lax.ppermute(value, axis, [(0, 1), (1, 0)])  8.06 us
    unnamed x28, local copies, waits for them, and re-layouts  6.67 us
  transfers between devices with their start and end apart: 7, of which 4 were waited for; matrix products, arithmetic and copies ran while one was open for 1% of the time, Pallas kernels for 4%

profile of v2, /device:TPU:1, one launch (start us, length us, event | category | flops | bytes accessed | tf_op | source)
XLA Modules:
  0.0 175.1 jit_solution(15905676706533474516)
XLA Ops:
  0.6 0.0 copy-start.1
  0.7 1.1 copy-done.1
  1.7 0.7 copy-done.4
  2.4 0.7 copy-done.5
  3.1 0.7 copy-done.6
  3.8 0.7 copy-done.7
  4.5 0.7 shard_map.120
  5.1 14.6 %all-to-all-start = ((bf16[64,8,128]{2,1,0:T(8,128)(2,1)}), bf16[64,8,128]{2,1,0:T(8,128)(2,1)S(1)}, u32[]{:S(2)}, u32[]{:S(2)}) async-start(bf16[64,8,128]{2,1,0:T(8,128)(2,1)} %get-tuple-element.22), calls=%async_computation | async-start | bytes 262144 | tf_op jit(solution)/shard_map/all_to_all | solution.py:46
  19.7 0.7 compare_select_fusion
  20.4 0.7 compare_and_fusion
  21.1 8.7 %all-to-all-done = bf16[64,8,128]{2,1,0:T(8,128)(2,1)S(1)} async-done(((bf16[64,8,128]{2,1,0:T(8,128)(2,1)}), bf16[64,8,128]{2,1,0:T(8,128)(2,1)S(1)}, u32[]{:S(2)}, u32[]{:S(2)}) %all-to-all-start) | async-done | bytes 131104 | tf_op jit(solution)/shard_map/all_to_all | solution.py:46
  29.8 0.6 gather_fusion
  30.5 0.1 broadcast_select_fusion
  30.6 14.7 %all_to_all.35 = bf16[64,8,128]{2,1,0:T(8,128)(2,1)S(1)} all-to-all(bf16[64,8,128]{2,1,0:T(8,128)(2,1)S(1)} %broadcast_select_fusion), channel_id=1, replica_groups=mesh['zlo'=4,'y'=8,'core'=2,'zhi'=2,'x'=4] {'zlo','y','core'}, dimensions={0} | all-to-all | bytes 262144 | tf_op jit(solution)/shard_map/all_to_all | solution.py:46
  45.3 0.9 broadcast_in_dim.21
  46.2 4.0 %all-to-all-start.2 = ((bf16[4,64,8,128]{3,2,1,0:T(8,128)(2,1)}), bf16[4,64,8,128]{3,2,1,0:T(8,128)(2,1)S(1)}, u32[]{:S(2)}, u32[]{:S(2)}) async-start(bf16[4,64,8,128]{3,2,1,0:T(8,128)(2,1)} %broadcast_in_dim.21), calls=%async_computation.2 | async-start | bytes 1048576 | tf_op jit(solution)/shard_map/all_to_all | solution.py:46
  50.2 7.9 %collective-permute-start = (bf16[272,256]{1,0:T(8,128)(2,1)S(1)}, bf16[272,256]{1,0:T(8,128)(2,1)S(1)}, u32[]{:S(2)}, u32[]{:S(2)}) collective-permute-start(bf16[272,256]{1,0:T(8,128)(2,1)S(1)} %get-tuple-element.23.own), channel_id=1, source_target_pairs={{0,4},{4,0},{1,5},{5,1},{2,6},{6,2},{3,7},{7,3},{8,12},{12,8},{9,1... | collective-permute-start | bytes 417800 | tf_op jit(solution)/shard_map/ppermute | solution.py:42
  58.2 0.1 pad_add_fusion.place
  58.2 3.3 %collective-permute-done.other = bf16[272,256]{1,0:T(8,128)(2,1)S(1)} collective-permute-done((bf16[272,256]{1,0:T(8,128)(2,1)S(1)}, bf16[272,256]{1,0:T(8,128)(2,1)S(1)}, u32[]{:S(2)}, u32[]{:S(2)}) %collective-permute-start) | collective-permute-done | bytes 139296 | tf_op jit(solution)/shard_map/ppermute | solution.py:42
  61.5 2.5 %shard_map.121 = (bf16[1024,256]{1,0:T(8,128)(2,1)S(1)}, bf16[1024,256]{1,0:T(8,128)(2,1)S(1)}, bf16[8,256,256]{2,1,0:T(8,128)(2,1)S(1)}, f32[8,1024]{1,0:T(8,128)S(1)}) custom-call(s32[1]{0:T(128)} %bitcast.2.zhi, bf16[272,256]{1,0:T(8,128)(2,1)S(1)} %get-tuple-element.23.own, bf16[272,256]{1,0:T(8,128)(2,1)S(1)} %collective-permute-done.other, ...), custom_call_target="tpu_custom_call" | custom-call | flops 1300000000 | bytes 4000000 | tf_op jit(solution)/shard_map/pallas_call | solution.py:30
  64.0 0.0 copy-start.10
  64.0 1.0 copy-done.10
  65.0 0.8 copy-done.12
  65.8 0.0 all-to-all-done.2
  65.8 1.0 copy-done.13
  66.9 3.6 %shard_map.122 = (bf16[1024,1024]{1,0:T(8,128)(2,1)S(1)}, bf16[1024,256]{1,0:T(8,128)(2,1)S(1)}, bf16[1024,256]{1,0:T(8,128)(2,1)S(1)}, bf16[1024,256]{1,0:T(8,128)(2,1)S(1)}) custom-call(s32[2]{0:T(128)S(1)} %pad_add_fusion.place, bf16[4,2,256,128]{3,2,1,0:T(8,128)(2,1)S(1)} %bitcast.8, bf16[1024,256]{1,0:T(8,128)(2,1)S(1)} %get-tuple-element.25.trans, ...), custom_call_target="tpu_custom_call" | custom-call | flops 2200000000 | bytes 4000000 | tf_op jit(solution)/shard_map/pallas_call | solution.py:30
  70.5 3.2 %collective-permute-start.2 = (bf16[1024,256]{1,0:T(8,128)(2,1)S(1)}, bf16[1024,256]{1,0:T(8,128)(2,1)S(1)}, u32[]{:S(2)}, u32[]{:S(2)}) collective-permute-start(bf16[1024,256]{1,0:T(8,128)(2,1)S(1)} %get-tuple-element.35), channel_id=1, source_target_pairs={{0,8},{8,0},{1,9},{9,1},{2,10},{10,2},{3,11},{11,3},{4,12},{12,4},... | collective-permute-start | bytes 1572872 | tf_op jit(solution)/shard_map/ppermute | solution.py:42
  73.7 3.4 %shard_map.123 = (bf16[4,256,256]{2,1,0:T(8,128)(2,1)S(1)}, f32[256,256]{1,0:T(8,128)S(1)}, bf16[256,256]{1,0:T(8,128)(2,1)S(1)}) custom-call(bf16[1024,1024]{1,0:T(8,128)(2,1)S(1)} %get-tuple-element.28.weight, bf16[1024,256]{1,0:T(8,128)(2,1)S(1)} %get-tuple-element.25.trans, bf16[1024,256]{1,0:T(8,128)(2,1)S(1)} %get-tuple-element.29.g_trans, ...), custom_call_target="tpu_custom_call" | custom-call | flops 1700000000 | bytes 4000000 | tf_op jit(solution)/shard_map/pallas_call | solution.py:30
  77.1 0.0 collective-permute-done.2.came
  77.1 0.1 shard_map.124
  77.3 0.0 copy-start.9
  77.3 19.0 %all_to_all.36.got = bf16[4,512,256]{2,1,0:T(8,128)(2,1)S(1)} all-to-all(bf16[4,512,256]{2,1,0:T(8,128)(2,1)S(1)} %shard_map.124), channel_id=1, replica_groups=mesh['zlo'=4,'y'=8,'core'=2,'zhi'=2,'x'=4] {'x'}, dimensions={0} | all-to-all | bytes 2097152 | tf_op jit(solution)/shard_map/all_to_all | solution.py:46
  96.3 0.1 shard_map.125
  96.4 0.0 copy-start.2
  96.4 0.0 copy-start.8
  96.4 20.7 %all_to_all.37.mid = bf16[64,16,128]{2,1,0:T(8,128)(2,1)S(1)} all-to-all(bf16[64,16,128]{2,1,0:T(8,128)(2,1)S(1)} %shard_map.125), channel_id=1, replica_groups=mesh['zlo'=4,'y'=8,'core'=2,'zhi'=2,'x'=4] {'zlo','y','core'}, dimensions={0} | all-to-all | bytes 524288 | tf_op jit(solution)/shard_map/all_to_all | solution.py:46
  117.2 7.3 %collective-permute-start.3 = (f32[2,8,128]{2,1,0:T(8,128)S(1)}, f32[2,8,128]{2,1,0:T(8,128)S(1)}, u32[]{:S(2)}, u32[]{:S(2)}) collective-permute-start(f32[2,8,128]{2,1,0:T(8,128)S(1)} %shard_map.126.rel_sum), channel_id=1, source_target_pairs={{0,4},{4,0},{1,5},{5,1},{2,6},{6,2},{3,7},{7,3},{8,12},{12,8},{9,1... | collective-permute-start | bytes 24584 | tf_op jit(solution)/shard_map/ppermute | solution.py:42
  124.5 1.0 collective-permute-done.3.rel_came
  125.5 0.8 shard_map.127
  126.3 18.7 %all_to_all.38.last = bf16[64,16,128]{2,1,0:T(8,128)(2,1)S(1)} all-to-all(bf16[64,16,128]{2,1,0:T(8,128)(2,1)S(1)} %shard_map.127), channel_id=1, replica_groups=mesh['zlo'=4,'y'=8,'core'=2,'zhi'=2,'x'=4] {'zlo','y','core'}, dimensions={0} | all-to-all | bytes 524288 | tf_op jit(solution)/shard_map/all_to_all | solution.py:46
  144.9 0.1 shard_map.129
  145.0 10.9 %all_to_all.39.four = bf16[4,256,256]{2,1,0:T(8,128)(2,1)S(1)} all-to-all(bf16[4,256,256]{2,1,0:T(8,128)(2,1)S(1)} %shard_map.129), channel_id=1, replica_groups=mesh['zlo'=4,'y'=8,'core'=2,'zhi'=2,'x'=4] {'x'}, dimensions={0} | all-to-all | bytes 1048576 | tf_op jit(solution)/shard_map/all_to_all | solution.py:46
  155.9 3.8 %collective-permute-start.4 = (bf16[4,256,256]{2,1,0:T(8,128)(2,1)S(1)}, bf16[4,256,256]{2,1,0:T(8,128)(2,1)S(1)}, u32[]{:S(2)}, u32[]{:S(2)}) collective-permute-start(bf16[4,256,256]{2,1,0:T(8,128)(2,1)S(1)} %all_to_all.39.four), channel_id=1, source_target_pairs={{0,8},{8,0},{1,9},{9,1},{2,10},{10,2},{3,11},{11,3},{4,12},{12,4},... | collective-permute-start | bytes 1572872 | tf_op jit(solution)/shard_map/ppermute | solution.py:42
  159.7 7.1 %collective-permute-start.1 = (bf16[256,256]{1,0:T(8,128)(2,1)S(1)}, bf16[256,256]{1,0:T(8,128)(2,1)S(1)}, u32[]{:S(2)}, u32[]{:S(2)}) collective-permute-start(bf16[256,256]{1,0:T(8,128)(2,1)S(1)} %get-tuple-element.32), channel_id=1, source_target_pairs={{0,4},{4,0},{1,5},{5,1},{2,6},{6,2},{3,7},{7,3},{8,12},{12,8},{9,1... | collective-permute-start | bytes 393224 | tf_op jit(solution)/shard_map/ppermute | solution.py:42
  166.9 3.8 %collective-permute-done.1.own_came = bf16[256,256]{1,0:T(8,128)(2,1)S(1)} collective-permute-done((bf16[256,256]{1,0:T(8,128)(2,1)S(1)}, bf16[256,256]{1,0:T(8,128)(2,1)S(1)}, u32[]{:S(2)}, u32[]{:S(2)}) %collective-permute-start.1) | collective-permute-done | bytes 131104 | tf_op jit(solution)/shard_map/ppermute | solution.py:42
  170.7 1.0 shard_map.128
  171.7 0.0 collective-permute-done.4.rest
  171.7 3.4 %shard_map.130 = (f32[8,256,256]{2,1,0:T(8,128)}, f32[8,256]{1,0:T(8,128)}) custom-call(s32[2]{0:T(128)S(1)} %pad_add_fusion.place, f32[8,256,256]{2,1,0:T(8,128)S(1)} %copy-done, f32[8,256]{1,0:T(8,128)S(1)} %copy-done.3, bf16[4,256,256]{2,1,0:T(8,128)(2,1)S(1)} %all_to_all.39.four, bf16[4,256,256]{2,1,0:T(8,128)(2,1)S(1)} %collective-permute-done.4.rest), custom_call_target="tpu_custom_call" | custom-call | bytes 5000000 | tf_op jit(solution)/shard_map/pallas_call | solution.py:30
  (17 shorter events, 0.1 us)
Async XLA Ops:
  0.6 60.9 %copy-start = (f32[8,256,256]{2,1,0:T(8,128)S(1)}, f32[8,256,256]{2,1,0:T(8,128)}, u32[]{:S(2)}) copy-start(f32[8,256,256]{2,1,0:T(8,128)} %rel.3) | copy-start | bytes 6291460
  0.6 1.1 copy-start.1
  1.7 0.7 copy-start.4
  2.4 0.7 copy-start.5
  3.1 0.7 copy-start.6
  3.8 0.7 copy-start.7
  5.1 24.7 %all-to-all-start = ((bf16[64,8,128]{2,1,0:T(8,128)(2,1)}), bf16[64,8,128]{2,1,0:T(8,128)(2,1)S(1)}, u32[]{:S(2)}, u32[]{:S(2)}) async-start(bf16[64,8,128]{2,1,0:T(8,128)(2,1)} %get-tuple-element.22), calls=%async_computation | async-start | bytes 262144 | tf_op jit(solution)/shard_map/all_to_all | solution.py:46
  46.2 19.6 %all-to-all-start.2 = ((bf16[4,64,8,128]{3,2,1,0:T(8,128)(2,1)}), bf16[4,64,8,128]{3,2,1,0:T(8,128)(2,1)S(1)}, u32[]{:S(2)}, u32[]{:S(2)}) async-start(bf16[4,64,8,128]{3,2,1,0:T(8,128)(2,1)} %broadcast_in_dim.21), calls=%async_computation.2 | async-start | bytes 1048576 | tf_op jit(solution)/shard_map/all_to_all | solution.py:46
  50.2 11.3 %collective-permute-start = (bf16[272,256]{1,0:T(8,128)(2,1)S(1)}, bf16[272,256]{1,0:T(8,128)(2,1)S(1)}, u32[]{:S(2)}, u32[]{:S(2)}) collective-permute-start(bf16[272,256]{1,0:T(8,128)(2,1)S(1)} %get-tuple-element.23.own), channel_id=1, source_target_pairs={{0,4},{4,0},{1,5},{5,1},{2,6},{6,2},{3,7},{7,3},{8,12},{12,8},{9,1... | collective-permute-start | bytes 417800 | tf_op jit(solution)/shard_map/ppermute | solution.py:42
  64.0 1.0 copy-start.10
  65.0 0.8 copy-start.12
  65.8 1.0 copy-start.13
  66.9 6.9 %copy-start.11 = (bf16[8,256,256]{2,1,0:T(8,128)(2,1)S(1)}, bf16[8,256,256]{2,1,0:T(8,128)(2,1)}, u32[]{:S(2)}) copy-start(bf16[8,256,256]{2,1,0:T(8,128)(2,1)} %copy-done.10) | copy-start | bytes 3145732
  70.5 6.6 %collective-permute-start.2 = (bf16[1024,256]{1,0:T(8,128)(2,1)S(1)}, bf16[1024,256]{1,0:T(8,128)(2,1)S(1)}, u32[]{:S(2)}, u32[]{:S(2)}) collective-permute-start(bf16[1024,256]{1,0:T(8,128)(2,1)S(1)} %get-tuple-element.35), channel_id=1, source_target_pairs={{0,8},{8,0},{1,9},{9,1},{2,10},{10,2},{3,11},{11,3},{4,12},{12,4},... | collective-permute-start | bytes 1572872 | tf_op jit(solution)/shard_map/ppermute | solution.py:42
  77.3 48.2 %copy-start.9 = (s32[64]{0:T(128)S(1)}, s32[64]{0:T(128)}, u32[]{:S(2)}) copy-start(s32[64]{0:T(128)} %matching.1) | copy-start | bytes 772
  96.4 74.3 %copy-start.2 = (f32[256,256]{1,0:T(8,128)S(1)}, f32[256,256]{1,0:T(8,128)}, u32[]{:S(2)}) copy-start(f32[256,256]{1,0:T(8,128)} %emb.3) | copy-start | bytes 786436
  96.4 74.3 %copy-start.8 = (f32[256]{0:T(256)S(1)}, f32[256]{0:T(256)}, u32[]{:S(2)}) copy-start(f32[256]{0:T(256)} %param.10) | copy-start | bytes 3076
  117.1 54.6 %copy-start.3 = (f32[8,256]{1,0:T(8,128)S(1)}, f32[8,256]{1,0:T(8,128)}, u32[]{:S(2)}) copy-start(f32[8,256]{1,0:T(8,128)} %accum.1) | copy-start | bytes 24580
  117.2 8.3 %collective-permute-start.3 = (f32[2,8,128]{2,1,0:T(8,128)S(1)}, f32[2,8,128]{2,1,0:T(8,128)S(1)}, u32[]{:S(2)}, u32[]{:S(2)}) collective-permute-start(f32[2,8,128]{2,1,0:T(8,128)S(1)} %shard_map.126.rel_sum), channel_id=1, source_target_pairs={{0,4},{4,0},{1,5},{5,1},{2,6},{6,2},{3,7},{7,3},{8,12},{12,8},{9,1... | collective-permute-start | bytes 24584 | tf_op jit(solution)/shard_map/ppermute | solution.py:42
  155.9 15.8 %collective-permute-start.4 = (bf16[4,256,256]{2,1,0:T(8,128)(2,1)S(1)}, bf16[4,256,256]{2,1,0:T(8,128)(2,1)S(1)}, u32[]{:S(2)}, u32[]{:S(2)}) collective-permute-start(bf16[4,256,256]{2,1,0:T(8,128)(2,1)S(1)} %all_to_all.39.four), channel_id=1, source_target_pairs={{0,8},{8,0},{1,9},{9,1},{2,10},{10,2},{3,11},{11,3},{4,12},{12,4},... | collective-permute-start | bytes 1572872 | tf_op jit(solution)/shard_map/ppermute | solution.py:42
  159.7 10.9 %collective-permute-start.1 = (bf16[256,256]{1,0:T(8,128)(2,1)S(1)}, bf16[256,256]{1,0:T(8,128)(2,1)S(1)}, u32[]{:S(2)}, u32[]{:S(2)}) collective-permute-start(bf16[256,256]{1,0:T(8,128)(2,1)S(1)} %get-tuple-element.32), channel_id=1, source_target_pairs={{0,4},{4,0},{1,5},{5,1},{2,6},{6,2},{3,7},{7,3},{8,12},{12,8},{9,1... | collective-permute-start | bytes 393224 | tf_op jit(solution)/shard_map/ppermute | solution.py:42

commit v3 on v2

--- a/solution.py
+++ b/solution.py
@@ -26,14 +26,14 @@
     return lax.dot_general(a, b, dims, preferred_element_type=f32)
 
 
-def call(kernel, outs, scalars, args, flops=0, moved=0, scratch=()):
+def call(kernel, outs, scalars, args, flops=0, moved=0, scratch=(), space=8):
     return pl.pallas_call(
         kernel,
         out_shape=outs,
         in_specs=[SMEM] * scalars + [VMEM] * (len(args) - scalars),
         out_specs=jax.tree.map(lambda _: VMEM, outs),
         scratch_shapes=list(scratch),
-        compiler_params=pltpu.CompilerParams(vmem_limit_bytes=40 * 1024 * 1024),
+        compiler_params=pltpu.CompilerParams(vmem_limit_bytes=space * 1024 * 1024),
         cost_estimate=pl.CostEstimate(flops=flops, bytes_accessed=moved, transcendentals=0),
     )(*args)
 
@@ -46,15 +46,23 @@
     return lax.all_to_all(value, axis, split_axis=0, concat_axis=0, tiled=True)
 
 
-def pack_kernel(emb, src, rel, dst, neg, pieces, pack):
+def first_kernel(emb, pieces):
     for h in range(2):
         pieces[h * 32 : (h + 1) * 32] = emb[:, h * 128 : (h + 1) * 128].reshape(32, 8, 128).astype(bf16)
+
+
+def pack_kernel(emb, src, rel, dst, neg, pack):
     pack[0:256, :] = emb[...].astype(bf16)
     wide = jnp.concatenate([src[...], rel[...], dst[...], neg[...]], axis=0)
     high = wide // 256
     low = (wide - high * 256).astype(f32)
     both = jnp.concatenate([high.astype(f32), low], axis=0)
     pack[256:272, :] = jnp.concatenate([both[:, :256], both[:, 256:]], axis=0).astype(bf16)
+
+
+def take_kernel(matching, arrived, routed):
+    for d in range(64):
+        routed[d] = arrived[matching[d]]
 
 
 def indices(pack):
@@ -200,25 +208,49 @@
     ]
     grad = own_here[...] + own_came[...].astype(f32) + jnp.concatenate(halves, axis=1)
     total = to_column(accum[...]) + jnp.mean(grad * grad, axis=1, keepdims=True)
-    new_emb[...] = emb[...] - learn_rate * grad / jnp.sqrt(total)
+    new_emb[...] = emb[...] - grad * (learn_rate / jnp.sqrt(total))
     new_accum[...] = to_row(total)
 
 
-def update_kernel(place, rel, accum, four, rest, new_rel, new_accum):
-    core = place[0]
+def update_kernel(place, rel, accum, grads, *rest):
+    if len(rest) == 6:
+        core, (seen, held, new_rel, new_accum, block, sem) = 1 - place[0], rest
+    else:
+        core, (new_rel, new_accum, block, sem) = place[0], rest
     old = jnp.concatenate([accum[...], accum[...]], axis=0)
-    ordered = jnp.where(core == 0, old[0:8], old[4:12])
-    column = ordered.T
+    column = jnp.where(core == 0, old[0:8], old[4:12]).T
     totals = []
-    for r in range(8):
-        target = r + 4 * core if r < 4 else r - 4 * core
-        grad = (four[r] if r < 4 else rest[r - 4]).astype(f32)
+    for r in range(4):
+        grad = grads[r].astype(f32)
         total = column[:, r : r + 1] + jnp.mean(grad * grad, axis=1, keepdims=True)
-        new_rel[target] = rel[target] - learn_rate * grad / jnp.sqrt(total)
+        block[r] = rel[4 * core + r] - grad * (learn_rate / jnp.sqrt(total))
         totals.append(total)
-    rows = jnp.concatenate(totals, axis=1).T
-    twice = jnp.concatenate([rows, rows], axis=0)
-    new_accum[...] = jnp.where(core == 0, twice[0:8], twice[4:12])
+    copy = pltpu.make_async_copy(block, new_rel.at[pl.ds(4 * core, 4)], sem)
+    copy.start()
+    rows = jnp.concatenate(totals + totals, axis=1).T
+    if len(rest) == 6:
+        first = jnp.concatenate([held[...], held[...]], axis=0)
+        mixed = jnp.concatenate([rows[0:4], first[0:4]], axis=0)
+        turned = jnp.concatenate([first[0:4], rows[0:4]], axis=0)
+        new_accum[...] = jnp.where(core == 0, mixed, turned)
+    else:
+        new_accum[...] = rows
+    copy.wait()
+
+
+def update_half(place, relations, rel_accum, grads, before=None):
+    given = (place, relations, rel_accum, grads) + (before or ())
+    specs = [SMEM, VMEM, VMEM, VMEM] + ([pl.BlockSpec(memory_space=pl.ANY), VMEM] if before else [])
+    return pl.pallas_call(
+        update_kernel,
+        out_shape=(shape((8, 256, 256), f32), shape((8, 256), f32)),
+        in_specs=specs,
+        out_specs=(pl.BlockSpec(memory_space=pl.ANY), VMEM),
+        scratch_shapes=[pltpu.VMEM((4, 256, 256), f32), pltpu.SemaphoreType.DMA],
+        input_output_aliases={4: 0} if before else {},
+        compiler_params=pltpu.CompilerParams(vmem_limit_bytes=8 * 1024 * 1024),
+        cost_estimate=pl.CostEstimate(flops=0, bytes_accessed=3_000_000, transcendentals=0),
+    )(*given)
 
 
 def body(
@@ -228,17 +260,20 @@
     zhi = lax.axis_index("zhi").astype(jnp.int32)
     place = jnp.stack([core, zhi])
     line = lambda v: v.reshape(1, 512)
-    pieces, pack = call(
+    pieces = call(first_kernel, shape((64, 8, 128), bf16), 0, (embeddings,), moved=400_000)
+    arrived = spread(pieces, DOM)
+    pack = call(
         pack_kernel,
-        (shape((64, 8, 128), bf16), shape((272, 256), bf16)),
+        shape((272, 256), bf16),
         0,
         (embeddings, line(src_rows), line(rel_ids), line(dst_rows), line(neg_rows)),
-    )
-    arrived = spread(pieces, DOM)
-    routed = jnp.take(arrived, matching, axis=0)
+        flops=2_000_000_000,
+        moved=400_000,
+    )
     other = swap(pack, "zhi")
+    routed = call(take_kernel, shape((64, 8, 128), bf16), 1, (matching, arrived), moved=400_000)
+    other, routed = lax.optimization_barrier((other, routed))
     partner_slice = spread(routed, DOM)
-    other, routed = lax.optimization_barrier((other, routed))
     trans, source, rel_b, counts = call(
         trans_kernel,
         (
@@ -250,6 +285,7 @@
         1,
         (zhi.reshape(1), pack, other, relations),
         flops=1_300_000_000,
+        space=16,
         moved=4_000_000,
     )
     rows4 = spread(jnp.broadcast_to(partner_slice[None], (4, 64, 8, 128)), "x")
@@ -264,6 +300,7 @@
         1,
         (place, rows4.reshape(4, 2, 256, 128), trans, source, counts, pack, other),
         flops=2_200_000_000,
+        space=20,
         moved=4_000_000,
         scratch=[pltpu.VMEM((1024, 256), bf16)],
     )
@@ -274,11 +311,13 @@
         0,
         (weight, trans, g_trans, rel_b, pack, other),
         flops=1_700_000_000,
+        space=16,
         moved=4_000_000,
     )
     own_came = swap(own_there, "zhi")
     joined = call(join_kernel, shape((4, 512, 256), bf16), 0, (g_rows, kept, came), moved=2_000_000)
     got = spread(joined, "x")
+    own_came, got = lax.optimization_barrier((own_came, got))
     mid = spread(call(pieces_kernel, shape((64, 16, 128), bf16), 0, (got,), moved=1_000_000), DOM)
     rel_sum = call(middle_kernel, shape((2, 8, 128), f32), 0, (mid,), moved=256_000)
     rel_came = swap(rel_sum, "zhi")
@@ -300,13 +339,8 @@
         moved=1_000_000,
     )
     rel_rest = swap(rel_four, "core")
-    new_relations, new_rel_accum = call(
-        update_kernel,
-        (shape((8, 256, 256), f32), shape((8, 256), f32)),
-        1,
-        (place, relations, rel_accum, rel_four, rel_rest),
-        moved=5_000_000,
-    )
+    half = update_half(place, relations, rel_accum, rel_four)
+    new_relations, new_rel_accum = update_half(place, relations, rel_accum, rel_rest, half)
     return new_embeddings, new_row_accum.reshape(256), new_relations, new_rel_accum
 
 

time: 177 us -> 169 us (0.955)
  blocking collectives: 84 us -> 69.8 us
  starting transfers between devices: 48 us -> 51.7 us
  Pallas kernels: 15.7 us -> 18.2 us
    all_to_all x5 -> x4, blocking collectives: 84 us -> 69.8 us  [spread(): return lax.all_to_all(value, axis, split_axis=0, concat_axis=0, tiled=True)]
    pallas_call x0 -> x2, Pallas kernels: none -> 5.38 us  [update_half(): pl.pallas_call(update_kernel, out_shape=(shape((8, 256, 256), f32), shape...]
    all_to_all x2 -> x3, starting transfers between devices: 18.6 us -> 22.1 us  [spread(): return lax.all_to_all(value, axis, split_axis=0, concat_axis=0, tiled=True)]
    pallas_call x11 -> x12, Pallas kernels: 15.7 us -> 12.9 us  [call(): pl.pallas_call(kernel, out_shape=outs, in_specs=[SMEM] * scalars + [VMEM]...]
    unnamed x28 -> x36, local copies, waits for them, and re-layouts: 6.67 us -> 8.51 us
    all_to_all x2 -> x3, waiting for transfers between devices: 8.75 us -> 8.65 us  [spread(): return lax.all_to_all(value, axis, split_axis=0, concat_axis=0, tiled=True)]
  transfers between devices with their start and end apart: 7 -> 8, of which waited for: 4 -> 5; matrix products, arithmetic and copies ran while one was open for 1% -> 0% of each run, Pallas kernels for 4% -> 6%
where the time goes in v3:
time: 169 us; the launch traced here: 168 us
  blocking collectives  69.8 us (41%)
  starting transfers between devices  51.7 us (31%)
  Pallas kernels  18.2 us (11%)
  waiting for transfers between devices  17.4 us (10%)
  local copies, waits for them, and re-layouts  9.37 us (6%)
    all_to_all x4, blocking collectives, spread(): return lax.all_to_all(value, axis, split_axis=0, concat_axis=0, tiled=True)  69.8 us
    ppermute x5, starting transfers between devices, swap(): return lax.ppermute(value, axis, [(0, 1), (1, 0)])  29.6 us
    all_to_all x3, starting transfers between devices, spread(): return lax.all_to_all(value, axis, split_axis=0, concat_axis=0, tiled=True)  22.1 us
    pallas_call x12, Pallas kernels, call(): pl.pallas_call(kernel, out_shape=outs, in_specs=[SMEM] * scalars + [VMEM]...  12.9 us
    ppermute x5, waiting for transfers between devices, swap(): return lax.ppermute(value, axis, [(0, 1), (1, 0)])  8.79 us
    all_to_all x3, waiting for transfers between devices, spread(): return lax.all_to_all(value, axis, split_axis=0, concat_axis=0, tiled=True)  8.65 us
    unnamed x36, local copies, waits for them, and re-layouts  8.51 us
    pallas_call x2, Pallas kernels, update_half(): pl.pallas_call(update_kernel, out_shape=(shape((8, 256, 256), f32), shape...  5.38 us
  transfers between devices with their start and end apart: 8, of which 5 were waited for; matrix products, arithmetic and copies ran while one was open for 0% of the time, Pallas kernels for 6%

profile of v3, /device:TPU:1, one launch (start us, length us, event | category | flops | bytes accessed | tf_op | source)
XLA Modules:
  0.0 167.7 jit_solution(2183585649370833888)
XLA Ops:
  0.6 0.0 copy-start.2
  0.6 0.9 copy-done.2
  1.6 0.7 shard_map.121
  2.3 14.6 %all-to-all-start = ((bf16[64,8,128]{2,1,0:T(8,128)(2,1)}), bf16[64,8,128]{2,1,0:T(8,128)(2,1)S(1)}, u32[]{:S(2)}, u32[]{:S(2)}) async-start(bf16[64,8,128]{2,1,0:T(8,128)(2,1)} %shard_map.121), calls=%async_computation | async-start | bytes 262144 | tf_op jit(solution)/shard_map/all_to_all | solution.py:46
  16.8 0.0 copy-start.8
  16.9 0.7 copy-done.8
  17.5 0.7 copy-done.9
  18.2 0.7 copy-done.10
  18.9 0.7 copy-done.11
  19.6 0.0 copy-start
  19.6 8.1 %collective-permute-start = (bf16[272,256]{1,0:T(8,128)(2,1)S(1)}, bf16[272,256]{1,0:T(8,128)(2,1)S(1)}, u32[]{:S(2)}, u32[]{:S(2)}) collective-permute-start(bf16[272,256]{1,0:T(8,128)(2,1)S(1)} %shard_map.120.own), channel_id=1, source_target_pairs={{0,4},{4,0},{1,5},{5,1},{2,6},{6,2},{3,7},{7,3},{8,12},{12,8},{9,1... | collective-permute-start | bytes 417800 | tf_op jit(solution)/shard_map/ppermute | solution.py:42
  27.7 0.6 shard_map.122
  28.3 3.5 %collective-permute-done.other = bf16[272,256]{1,0:T(8,128)(2,1)S(1)} collective-permute-done((bf16[272,256]{1,0:T(8,128)(2,1)S(1)}, bf16[272,256]{1,0:T(8,128)(2,1)S(1)}, u32[]{:S(2)}, u32[]{:S(2)}) %collective-permute-start) | collective-permute-done | bytes 139296 | tf_op jit(solution)/shard_map/ppermute | solution.py:42
  31.9 22.6 %all_to_all.35 = bf16[64,8,128]{2,1,0:T(8,128)(2,1)S(1)} all-to-all(bf16[64,8,128]{2,1,0:T(8,128)(2,1)S(1)} %shard_map.122), channel_id=1, replica_groups=mesh['zlo'=4,'y'=8,'core'=2,'zhi'=2,'x'=4] {'zlo','y','core'}, dimensions={0} | all-to-all | bytes 262144 | tf_op jit(solution)/shard_map/all_to_all | solution.py:46
  54.5 0.9 broadcast_in_dim.2
  55.3 4.0 %all-to-all-start.2 = ((bf16[4,64,8,128]{3,2,1,0:T(8,128)(2,1)}), bf16[4,64,8,128]{3,2,1,0:T(8,128)(2,1)S(1)}, u32[]{:S(2)}, u32[]{:S(2)}) async-start(bf16[4,64,8,128]{3,2,1,0:T(8,128)(2,1)} %broadcast_in_dim.2), calls=%async_computation.2 | async-start | bytes 1048576 | tf_op jit(solution)/shard_map/all_to_all | solution.py:46
  59.4 0.1 pad_add_fusion.place
  59.4 2.5 %shard_map.123 = (bf16[1024,256]{1,0:T(8,128)(2,1)S(1)}, bf16[1024,256]{1,0:T(8,128)(2,1)S(1)}, bf16[8,256,256]{2,1,0:T(8,128)(2,1)S(1)}, f32[8,1024]{1,0:T(8,128)S(1)}) custom-call(s32[1]{0:T(128)} %bitcast.2.zhi, bf16[272,256]{1,0:T(8,128)(2,1)S(1)} %shard_map.120.own, bf16[272,256]{1,0:T(8,128)(2,1)S(1)} %collective-permute-done.other, ...), custom_call_target="tpu_custom_call" | custom-call | flops 1300000000 | bytes 4000000 | tf_op jit(solution)/shard_map/pallas_call | solution.py:30
  61.9 0.0 copy-start.12
  61.9 1.0 copy-done.12
  62.9 0.8 copy-done.16
  63.7 4.6 %all-to-all-done.2 = bf16[4,64,8,128]{3,2,1,0:T(8,128)(2,1)S(1)} async-done(((bf16[4,64,8,128]{3,2,1,0:T(8,128)(2,1)}), bf16[4,64,8,128]{3,2,1,0:T(8,128)(2,1)S(1)}, u32[]{:S(2)}, u32[]{:S(2)}) %all-to-all-start.2) | async-done | bytes 524320 | tf_op jit(solution)/shard_map/all_to_all | solution.py:46
  68.2 1.0 copy-done.17
  69.3 3.6 %shard_map.124 = (bf16[1024,1024]{1,0:T(8,128)(2,1)S(1)}, bf16[1024,256]{1,0:T(8,128)(2,1)S(1)}, bf16[1024,256]{1,0:T(8,128)(2,1)S(1)}, bf16[1024,256]{1,0:T(8,128)(2,1)S(1)}) custom-call(s32[2]{0:T(128)S(1)} %pad_add_fusion.place, bf16[4,2,256,128]{3,2,1,0:T(8,128)(2,1)S(1)} %bitcast.8, bf16[1024,256]{1,0:T(8,128)(2,1)S(1)} %get-tuple-element.27.trans, ...), custom_call_target="tpu_custom_call" | custom-call | flops 2200000000 | bytes 4000000 | tf_op jit(solution)/shard_map/pallas_call | solution.py:30
  72.9 3.5 %collective-permute-start.2 = (bf16[1024,256]{1,0:T(8,128)(2,1)S(1)}, bf16[1024,256]{1,0:T(8,128)(2,1)S(1)}, u32[]{:S(2)}, u32[]{:S(2)}) collective-permute-start(bf16[1024,256]{1,0:T(8,128)(2,1)S(1)} %get-tuple-element.37), channel_id=1, source_target_pairs={{0,8},{8,0},{1,9},{9,1},{2,10},{10,2},{3,11},{11,3},{4,12},{12,4},... | collective-permute-start | bytes 1572872 | tf_op jit(solution)/shard_map/ppermute | solution.py:42
  76.3 1.0 copy-done.15
  77.4 3.4 %shard_map.125 = (bf16[4,256,256]{2,1,0:T(8,128)(2,1)S(1)}, f32[256,256]{1,0:T(8,128)S(1)}, bf16[256,256]{1,0:T(8,128)(2,1)S(1)}) custom-call(bf16[1024,1024]{1,0:T(8,128)(2,1)S(1)} %get-tuple-element.30.weight, bf16[1024,256]{1,0:T(8,128)(2,1)S(1)} %copy-done.15, bf16[1024,256]{1,0:T(8,128)(2,1)S(1)} %get-tuple-element.31.g_trans, ...), custom_call_target="tpu_custom_call" | custom-call | flops 1700000000 | bytes 4000000 | tf_op jit(solution)/shard_map/pallas_call | solution.py:30
  80.8 0.0 copy-start.7
  80.8 0.1 shard_map.126
  80.9 0.0 copy-start.1
  80.9 1.0 copy-done.1
  81.9 3.5 %all-to-all-start.3 = ((bf16[4,512,256]{2,1,0:T(8,128)(2,1)}), bf16[4,512,256]{2,1,0:T(8,128)(2,1)S(1)}, u32[]{:S(2)}, u32[]{:S(2)}) async-start(bf16[4,512,256]{2,1,0:T(8,128)(2,1)} %copy-done.1), calls=%async_computation.3 | async-start | bytes 2097152 | tf_op jit(solution)/shard_map/all_to_all | solution.py:46
  85.4 7.0 %collective-permute-start.1 = (bf16[256,256]{1,0:T(8,128)(2,1)}, bf16[256,256]{1,0:T(8,128)(2,1)S(1)}, u32[]{:S(2)}, u32[]{:S(2)}) collective-permute-start(bf16[256,256]{1,0:T(8,128)(2,1)} %copy-done.7), channel_id=1, source_target_pairs={{0,4},{4,0},{1,5},{5,1},{2,6},{6,2},{3,7},{7,3},{8,12},{12,8},{9,1... | collective-permute-start | bytes 393224 | tf_op jit(solution)/shard_map/ppermute | solution.py:42
  92.4 4.1 %collective-permute-done.1.own_came = bf16[256,256]{1,0:T(8,128)(2,1)S(1)} collective-permute-done((bf16[256,256]{1,0:T(8,128)(2,1)}, bf16[256,256]{1,0:T(8,128)(2,1)S(1)}, u32[]{:S(2)}, u32[]{:S(2)}) %collective-permute-start.1) | collective-permute-done | bytes 131104 | tf_op jit(solution)/shard_map/ppermute | solution.py:42
  96.6 4.1 %all-to-all-done.3.got = bf16[4,512,256]{2,1,0:T(8,128)(2,1)S(1)} async-done(((bf16[4,512,256]{2,1,0:T(8,128)(2,1)}), bf16[4,512,256]{2,1,0:T(8,128)(2,1)S(1)}, u32[]{:S(2)}, u32[]{:S(2)}) %all-to-all-start.3) | async-done | bytes 1048608 | tf_op jit(solution)/shard_map/all_to_all | solution.py:46
  100.7 0.1 shard_map.127
  100.8 0.0 copy-start.3
  100.8 17.3 %all_to_all.36.mid = bf16[64,16,128]{2,1,0:T(8,128)(2,1)S(1)} all-to-all(bf16[64,16,128]{2,1,0:T(8,128)(2,1)S(1)} %shard_map.127), channel_id=1, replica_groups=mesh['zlo'=4,'y'=8,'core'=2,'zhi'=2,'x'=4] {'zlo','y','core'}, dimensions={0} | all-to-all | bytes 524288 | tf_op jit(solution)/shard_map/all_to_all | solution.py:46
  118.2 7.2 %collective-permute-start.3 = (f32[2,8,128]{2,1,0:T(8,128)S(1)}, f32[2,8,128]{2,1,0:T(8,128)S(1)}, u32[]{:S(2)}, u32[]{:S(2)}) collective-permute-start(f32[2,8,128]{2,1,0:T(8,128)S(1)} %shard_map.128.rel_sum), channel_id=1, source_target_pairs={{0,4},{4,0},{1,5},{5,1},{2,6},{6,2},{3,7},{7,3},{8,12},{12,8},{9,1... | collective-permute-start | bytes 24584 | tf_op jit(solution)/shard_map/ppermute | solution.py:42
  125.4 1.1 collective-permute-done.3.rel_came
  126.5 0.8 shard_map.129
  127.3 18.7 %all_to_all.37.last = bf16[64,16,128]{2,1,0:T(8,128)(2,1)S(1)} all-to-all(bf16[64,16,128]{2,1,0:T(8,128)(2,1)S(1)} %shard_map.129), channel_id=1, replica_groups=mesh['zlo'=4,'y'=8,'core'=2,'zhi'=2,'x'=4] {'zlo','y','core'}, dimensions={0} | all-to-all | bytes 524288 | tf_op jit(solution)/shard_map/all_to_all | solution.py:46
  146.0 0.1 shard_map.131
  146.0 11.2 %all_to_all.38.grads = bf16[4,256,256]{2,1,0:T(8,128)(2,1)S(1)} all-to-all(bf16[4,256,256]{2,1,0:T(8,128)(2,1)S(1)} %shard_map.131), channel_id=1, replica_groups=mesh['zlo'=4,'y'=8,'core'=2,'zhi'=2,'x'=4] {'x'}, dimensions={0} | all-to-all | bytes 1048576 | tf_op jit(solution)/shard_map/all_to_all | solution.py:46
  157.3 3.9 %collective-permute-start.4 = (bf16[4,256,256]{2,1,0:T(8,128)(2,1)S(1)}, bf16[4,256,256]{2,1,0:T(8,128)(2,1)S(1)}, u32[]{:S(2)}, u32[]{:S(2)}) collective-permute-start(bf16[4,256,256]{2,1,0:T(8,128)(2,1)S(1)} %all_to_all.38.grads), channel_id=1, source_target_pairs={{0,8},{8,0},{1,9},{9,1},{2,10},{10,2},{3,11},{11,3},{4,12},{12,4},... | collective-permute-start | bytes 1572872 | tf_op jit(solution)/shard_map/ppermute | solution.py:42
  161.1 1.0 shard_map.130
  162.2 2.4 %shard_map.132 = (f32[8,256,256]{2,1,0:T(8,128)}, f32[8,256]{1,0:T(8,128)S(1)}) custom-call(s32[2]{0:T(128)S(1)} %pad_add_fusion.place, f32[8,256,256]{2,1,0:T(8,128)S(1)} %copy-done, f32[8,256]{1,0:T(8,128)S(1)} %copy-done.4, bf16[4,256,256]{2,1,0:T(8,128)(2,1)S(1)} %all_to_all.38.grads), custom_call_target="tpu_custom_call" | custom-call | bytes 3000000 | tf_op jit(solution)/shard_map/pallas_call | solution.py:244
  164.6 3.0 %shard_map.133 = (f32[8,256,256]{2,1,0:T(8,128)}, f32[8,256]{1,0:T(8,128)}) custom-call(s32[2]{0:T(128)S(1)} %pad_add_fusion.place, f32[8,256,256]{2,1,0:T(8,128)S(1)} %copy-done, f32[8,256]{1,0:T(8,128)S(1)} %copy-done.4, bf16[4,256,256]{2,1,0:T(8,128)(2,1)S(1)} %collective-permute-done.4.grads, ...), custom_call_target="tpu_custom_call", output_to_operand_aliasing={{0}: (4, {})} | custom-call | bytes 3000000 | tf_op jit(solution)/shard_map/pallas_call | solution.py:244
  (24 shorter events, 0.1 us)
Async XLA Ops:
  0.6 1.0 copy-start.2
  2.3 25.5 %all-to-all-start = ((bf16[64,8,128]{2,1,0:T(8,128)(2,1)}), bf16[64,8,128]{2,1,0:T(8,128)(2,1)S(1)}, u32[]{:S(2)}, u32[]{:S(2)}) async-start(bf16[64,8,128]{2,1,0:T(8,128)(2,1)} %shard_map.121), calls=%async_computation | async-start | bytes 262144 | tf_op jit(solution)/shard_map/all_to_all | solution.py:46
  16.8 0.7 copy-start.8
  17.5 0.7 copy-start.9
  18.2 0.7 copy-start.10
  18.9 0.7 copy-start.11
  19.6 8.1 %copy-start.5 = (s32[64]{0:T(128)S(1)}, s32[64]{0:T(128)}, u32[]{:S(2)}) copy-start(s32[64]{0:T(128)} %matching.3) | copy-start | bytes 772
  19.6 39.8 %copy-start = (f32[8,256,256]{2,1,0:T(8,128)S(1)}, f32[8,256,256]{2,1,0:T(8,128)}, u32[]{:S(2)}) copy-start(f32[8,256,256]{2,1,0:T(8,128)} %rel.5) | copy-start | bytes 6291460
  19.6 12.3 %collective-permute-start = (bf16[272,256]{1,0:T(8,128)(2,1)S(1)}, bf16[272,256]{1,0:T(8,128)(2,1)S(1)}, u32[]{:S(2)}, u32[]{:S(2)}) collective-permute-start(bf16[272,256]{1,0:T(8,128)(2,1)S(1)} %shard_map.120.own), channel_id=1, source_target_pairs={{0,4},{4,0},{1,5},{5,1},{2,6},{6,2},{3,7},{7,3},{8,12},{12,8},{9,1... | collective-permute-start | bytes 417800 | tf_op jit(solution)/shard_map/ppermute | solution.py:42
  55.3 12.9 %all-to-all-start.2 = ((bf16[4,64,8,128]{3,2,1,0:T(8,128)(2,1)}), bf16[4,64,8,128]{3,2,1,0:T(8,128)(2,1)S(1)}, u32[]{:S(2)}, u32[]{:S(2)}) async-start(bf16[4,64,8,128]{3,2,1,0:T(8,128)(2,1)} %broadcast_in_dim.2), calls=%async_computation.2 | async-start | bytes 1048576 | tf_op jit(solution)/shard_map/all_to_all | solution.py:46
  61.9 1.0 copy-start.12
  62.9 0.8 copy-start.16
  63.7 9.2 %copy-start.14 = (bf16[1024,256]{1,0:T(8,128)(2,1)}, bf16[1024,256]{1,0:T(8,128)(2,1)S(1)}, u32[]{:S(2)}) copy-start(bf16[1024,256]{1,0:T(8,128)(2,1)S(1)} %get-tuple-element.27.trans) | copy-start | bytes 1572868
  68.2 1.0 copy-start.17
  69.3 7.0 %copy-start.13 = (bf16[8,256,256]{2,1,0:T(8,128)(2,1)S(1)}, bf16[8,256,256]{2,1,0:T(8,128)(2,1)}, u32[]{:S(2)}) copy-start(bf16[8,256,256]{2,1,0:T(8,128)(2,1)} %copy-done.12) | copy-start | bytes 3145732
  72.9 7.9 %collective-permute-start.2 = (bf16[1024,256]{1,0:T(8,128)(2,1)S(1)}, bf16[1024,256]{1,0:T(8,128)(2,1)S(1)}, u32[]{:S(2)}, u32[]{:S(2)}) collective-permute-start(bf16[1024,256]{1,0:T(8,128)(2,1)S(1)} %get-tuple-element.37), channel_id=1, source_target_pairs={{0,8},{8,0},{1,9},{9,1},{2,10},{10,2},{3,11},{11,3},{4,12},{12,4},... | collective-permute-start | bytes 1572872 | tf_op jit(solution)/shard_map/ppermute | solution.py:42
  76.3 1.0 copy-start.15
  80.8 4.7 %copy-start.7 = (bf16[256,256]{1,0:T(8,128)(2,1)}, bf16[256,256]{1,0:T(8,128)(2,1)S(1)}, u32[]{:S(2)}) copy-start(bf16[256,256]{1,0:T(8,128)(2,1)S(1)} %get-tuple-element.34) | copy-start | bytes 393220
  80.9 1.0 copy-start.1
  81.9 18.8 %all-to-all-start.3 = ((bf16[4,512,256]{2,1,0:T(8,128)(2,1)}), bf16[4,512,256]{2,1,0:T(8,128)(2,1)S(1)}, u32[]{:S(2)}, u32[]{:S(2)}) async-start(bf16[4,512,256]{2,1,0:T(8,128)(2,1)} %copy-done.1), calls=%async_computation.3 | async-start | bytes 2097152 | tf_op jit(solution)/shard_map/all_to_all | solution.py:46
  85.4 11.2 %collective-permute-start.1 = (bf16[256,256]{1,0:T(8,128)(2,1)}, bf16[256,256]{1,0:T(8,128)(2,1)S(1)}, u32[]{:S(2)}, u32[]{:S(2)}) collective-permute-start(bf16[256,256]{1,0:T(8,128)(2,1)} %copy-done.7), channel_id=1, source_target_pairs={{0,4},{4,0},{1,5},{5,1},{2,6},{6,2},{3,7},{7,3},{8,12},{12,8},{9,1... | collective-permute-start | bytes 393224 | tf_op jit(solution)/shard_map/ppermute | solution.py:42
  100.8 60.3 %copy-start.3 = (f32[256,256]{1,0:T(8,128)S(1)}, f32[256,256]{1,0:T(8,128)}, u32[]{:S(2)}) copy-start(f32[256,256]{1,0:T(8,128)} %emb.5) | copy-start | bytes 786436
  100.8 60.3 %copy-start.6 = (f32[256]{0:T(256)S(1)}, f32[256]{0:T(256)}, u32[]{:S(2)}) copy-start(f32[256]{0:T(256)} %param.10) | copy-start | bytes 3076
  118.2 44.0 %copy-start.4 = (f32[8,256]{1,0:T(8,128)S(1)}, f32[8,256]{1,0:T(8,128)}, u32[]{:S(2)}) copy-start(f32[8,256]{1,0:T(8,128)} %accum.3) | copy-start | bytes 24580
  118.2 8.3 %collective-permute-start.3 = (f32[2,8,128]{2,1,0:T(8,128)S(1)}, f32[2,8,128]{2,1,0:T(8,128)S(1)}, u32[]{:S(2)}, u32[]{:S(2)}) collective-permute-start(f32[2,8,128]{2,1,0:T(8,128)S(1)} %shard_map.128.rel_sum), channel_id=1, source_target_pairs={{0,4},{4,0},{1,5},{5,1},{2,6},{6,2},{3,7},{7,3},{8,12},{12,8},{9,1... | collective-permute-start | bytes 24584 | tf_op jit(solution)/shard_map/ppermute | solution.py:42
  157.3 7.3 %collective-permute-start.4 = (bf16[4,256,256]{2,1,0:T(8,128)(2,1)S(1)}, bf16[4,256,256]{2,1,0:T(8,128)(2,1)S(1)}, u32[]{:S(2)}, u32[]{:S(2)}) collective-permute-start(bf16[4,256,256]{2,1,0:T(8,128)(2,1)S(1)} %all_to_all.38.grads), channel_id=1, source_target_pairs={{0,8},{8,0},{1,9},{9,1},{2,10},{10,2},{3,11},{11,3},{4,12},{12,4},... | collective-permute-start | bytes 1572872 | tf_op jit(solution)/shard_map/ppermute | solution.py:42

commit v4 on v3

v4 whole, which is shorter than its diff:
```python
import jax
import jax.numpy as jnp
from jax import lax
from jax.experimental import pallas as pl
from jax.experimental.pallas import tpu as pltpu
from jax.sharding import Mesh, PartitionSpec as P

learn_rate = 0.1
AXES = ("zlo", "y", "core", "zhi", "x")
DOM = ("zlo", "y", "core")
DOM_Z = DOM + ("zhi",)
bf16 = jnp.bfloat16
f32 = jnp.float32
VMEM = pl.BlockSpec(memory_space=pltpu.VMEM)
SMEM = pl.BlockSpec(memory_space=pltpu.SMEM)
NN = (((1,), (0,)), ((), ()))
NT = (((1,), (1,)), ((), ()))


def shape(dims, dtype):
    return jax.ShapeDtypeStruct(dims, dtype)


def dot(a, b, dims=NN):
    return lax.dot_general(a, b, dims, preferred_element_type=f32)


def call(kernel, outs, scalars, args, flops=0, moved=0, scratch=(), space=8):
    return pl.pallas_call(
        kernel,
        out_shape=outs,
        in_specs=[SMEM] * scalars + [VMEM] * (len(args) - scalars),
        out_specs=jax.tree.map(lambda _: VMEM, outs),
        scratch_shapes=list(scratch),
        compiler_params=pltpu.CompilerParams(vmem_limit_bytes=space * 1024 * 1024),
        cost_estimate=pl.CostEstimate(flops=flops, bytes_accessed=moved, transcendentals=0),
    )(*args)


def swap(value, axis):
    return lax.ppermute(value, axis, [(0, 1), (1, 0)])


def spread(value, axis):
    return lax.all_to_all(value, axis, split_axis=0, concat_axis=0, tiled=True)


def first_kernel(emb, pieces):
    for h in range(2):
        pieces[h * 32 : (h + 1) * 32] = emb[:, h * 128 : (h + 1) * 128].reshape(32, 8, 128).astype(bf16)


def pack_kernel(emb, src, rel, dst, neg, out):
    wide = jnp.concatenate([src[...], rel[...], dst[...], neg[...]], axis=0)
    high = wide // 256
    low = (wide - high * 256).astype(f32)
    both = jnp.concatenate([high.astype(f32), low], axis=0)
    index = jnp.concatenate([both[:, :256], both[:, 256:]], axis=0).astype(bf16)
    out[0:256, :] = emb[...].astype(bf16)
    out[256:272, :] = index


def take_kernel(matching, arrived, routed):
    for d in range(64):
        piece = arrived[matching[d]]
        routed[d, 0] = piece
        routed[d, 1] = piece


def indices(part):
    part = part.astype(f32)
    both = jnp.concatenate([part[0:8], part[8:16]], axis=1)
    return both[0:4] * 256.0 + both[4:8]


def columns(value):
    return jnp.concatenate([value, value], axis=0).T


def lane_ids(rows, width):
    return lax.broadcasted_iota(jnp.int32, (rows, width), 1)


def row_ids(x, rows):
    ids = lane_ids(rows, 512)
    return (ids + jnp.where(ids >= 256, 768, 0) + x * 256).astype(f32)


def trans_kernel(place, pack0, pack1, pack2, pack3, rel, trans, source, rel_b, counts, known):
    packs = (pack0, pack1, pack2, pack3)
    for r in range(8):
        rel_b[r] = rel[r].astype(bf16)
    ids = lane_ids(512, 256).astype(f32)
    wide = row_ids(place[2], 512)
    for s in range(4):
        index = indices(packs[s][256:272, :])
        known[s * 4 : (s + 1) * 4, :] = index
        column = columns(index)
        hot = (column[:, 0:1] == ids).astype(f32).astype(bf16)
        rows = dot(hot, packs[s][0:256, :])
        source[s * 512 : (s + 1) * 512, :] = rows.astype(bf16)
        total = jnp.zeros((512, 256), f32)
        for r in range(8):
            masked = jnp.where(column[:, 1:2] == float(r), rows, 0.0).astype(bf16)
            total = total + dot(masked, rel_b[r], NT)
        trans[s * 512 : (s + 1) * 512, :] = total.astype(bf16)
        hits = (column[:, 3:4] == wide).astype(f32)
        counts[s : s + 1, :] = jnp.sum(hits, axis=0, keepdims=True)
    counts[4:8, :] = jnp.zeros((4, 512), f32)


def score_kernel(
    place, rows_in, trans, source, counts, known, weight, g_trans, kept, given, rows
):
    core = place[0]
    for z in range(2):
        both = rows_in[:, z].reshape(2, 256, 128)
        rows[z * 256 : (z + 1) * 256, :] = jnp.concatenate([both[0], both[1]], axis=1)
    index = [known[s * 4 : (s + 1) * 4, :] for s in range(4)]
    ids = row_ids(place[2], 256)
    for b in range(8):
        s = b // 2
        column = columns(index[s])[(b % 2) * 256 : (b % 2 + 1) * 256]
        span = slice(b * 256, (b + 1) * 256)
        score = dot(trans[span, :], rows[...], NT)
        sig = 1.0 / (1.0 + jnp.exp(-score))
        count = counts[s : s + 1, :]
        hit = column[:, 2:3] == ids
        part = jnp.where(hit, (count + 1.0) * sig - 1.0, count * sig).astype(bf16)
        weight[span, :] = part
        g_trans[span, :] = dot(part, rows[...]).astype(bf16)
    turned = g_trans[...].astype(f32).T
    kinds = jnp.concatenate([part[1:2] for part in index], axis=1)
    for r in range(8):
        wanted = r + 4 * core if r < 4 else r - 4 * core
        masked = jnp.where(kinds == wanted.astype(f32), turned, 0.0).astype(bf16)
        grad = dot(masked, source[...]).astype(bf16)
        if r < 4:
            kept[r * 256 : (r + 1) * 256, :] = grad
        else:
            given[(r - 4) * 256 : (r - 3) * 256, :] = grad


def back_kernel(place, weight, trans, g_trans, rel_b, known, g_rows, own):
    turned = trans[...].astype(f32).T.astype(bf16)
    for z in range(2):
        part = dot(turned, weight[:, z * 256 : (z + 1) * 256])
        g_rows[z] = part.T.astype(bf16)
    sub_ids = lax.broadcasted_iota(jnp.int32, (256, 512), 0).astype(f32)
    for s in range(4):
        index = known[s * 4 : (s + 1) * 4, :]
        column = columns(index)
        grad = g_trans[s * 512 : (s + 1) * 512, :].astype(f32)
        total = jnp.zeros((512, 256), f32)
        for r in range(8):
            masked = jnp.where(column[:, 1:2] == float(r), grad, 0.0).astype(bf16)
            total = total + dot(masked, rel_b[r])
        hot = (index[0:1, :] == sub_ids).astype(f32).astype(bf16)
        own[(place[2] + s) % 4] = dot(hot, total.astype(bf16)).astype(bf16)


def join_kernel(own, kept, came, out):
    for k in range(4):
        out[k, 0:256, :] = own[k]
        span = slice(k * 256, (k + 1) * 256)
        out[k, 256:512, :] = (kept[span, :].astype(f32) + came[span, :].astype(f32)).astype(bf16)


def upper(tiles):
    return lax.broadcasted_iota(jnp.int32, tiles, len(tiles) - 2) % 8 < 4


def halves_swapped(tiles):
    return jnp.concatenate([tiles[:, 4:8], tiles[:, 0:4]], axis=1)


def pieces_kernel(got, g_rows, out, own_here):
    first = upper((32, 8, 128))
    for h in range(2):
        half = slice(h * 128, (h + 1) * 128)
        total = got[0, :, half].astype(f32)
        for k in range(1, 4):
            total = total + got[k, :, half].astype(f32)
        own_here[:, half] = total[0:256]
        rel = total[256:512].reshape(32, 8, 128)
        turned = halves_swapped(rel)
        near = g_rows[0, :, half].astype(f32).reshape(32, 8, 128)
        far = g_rows[1, :, half].astype(f32).reshape(32, 8, 128)
        span = slice(h * 32, (h + 1) * 32)
        out[span, 0] = jnp.concatenate(
            [jnp.where(first, near, far), jnp.where(first, rel, turned)], axis=1
        ).astype(bf16)
        out[span, 1] = jnp.concatenate(
            [jnp.where(first, far, near), jnp.where(first, turned, rel)], axis=1
        ).astype(bf16)


def route_kernel(place, matching, mid, out, sums):
    rel = [jnp.zeros((8, 128), f32), jnp.zeros((8, 128), f32)]
    for d in range(64):
        both = mid[d, 0].astype(f32) + mid[d, 1].astype(f32)
        sums[d] = both[0:8]
        rel[d % 2] = rel[d % 2] + both[8:16]
    first = upper((8, 128))
    near = first == (place[1] == 0)
    for d in range(64):
        target = matching[d]
        tail = jnp.where(target % 2 == 0, rel[0], rel[1])
        out[target, 0] = jnp.where(near, sums[d], tail).astype(bf16)
        out[target, 1] = jnp.where(near, tail, sums[d]).astype(bf16)


def rel_kernel(place, last, out):
    first = upper((32, 8, 128))
    for h in range(2):
        even = last[h * 32 : (h + 1) * 32, 0].astype(f32)
        odd = last[h * 32 : (h + 1) * 32, 1].astype(f32)
        straight = jnp.where(first, even, odd)
        crossed = halves_swapped(jnp.where(first, odd, even))
        part = jnp.where(place[1] == 0, crossed, straight).reshape(256, 128).astype(bf16)
        for k in range(4):
            out[k, :, h * 128 : (h + 1) * 128] = part


def to_row(column):
    return jnp.broadcast_to(column, (256, 128)).T[0:1]


def to_column(row):
    return jnp.broadcast_to(row, (128, 256)).T[:, 0:1]


def rows_kernel(place, emb, accum, own_here, last, new_emb, new_accum):
    first = upper((64, 8, 128)) == (place[1] == 0)
    rows = jnp.where(first, last[:, 0].astype(f32), last[:, 1].astype(f32))
    halves = [rows[h * 32 : (h + 1) * 32].reshape(256, 128) for h in range(2)]
    grad = own_here[...] + jnp.concatenate(halves, axis=1)
    total = to_column(accum[...]) + jnp.mean(grad * grad, axis=1, keepdims=True)
    new_emb[...] = emb[...] - grad * (learn_rate / jnp.sqrt(total))
    new_accum[...] = to_row(total)


def update_kernel(place, rel, accum, grads, *rest):
    if len(rest) == 6:
        core, (seen, held, new_rel, new_accum, block, sem) = 1 - place[0], rest
    else:
        core, (new_rel, new_accum, block, sem) = place[0], rest
    old = jnp.concatenate([accum[...], accum[...]], axis=0)
    column = jnp.where(core == 0, old[0:8], old[4:12]).T
    totals = []
    for r in range(4):
        grad = grads[r].astype(f32)
        total = column[:, r : r + 1] + jnp.mean(grad * grad, axis=1, keepdims=True)
        block[r] = rel[4 * core + r] - grad * (learn_rate / jnp.sqrt(total))
        totals.append(total)
    copy = pltpu.make_async_copy(block, new_rel.at[pl.ds(4 * core, 4)], sem)
    copy.start()
    rows = jnp.concatenate(totals + totals, axis=1).T
    if len(rest) == 6:
        first = jnp.concatenate([held[...], held[...]], axis=0)
        mixed = jnp.concatenate([rows[0:4], first[0:4]], axis=0)
        turned = jnp.concatenate([first[0:4], rows[0:4]], axis=0)
        new_accum[...] = jnp.where(core == 0, mixed, turned)
    else:
        new_accum[...] = rows
    copy.wait()


def update_half(place, relations, rel_accum, grads, before=None):
    given = (place, relations, rel_accum, grads) + (before or ())
    specs = [SMEM, VMEM, VMEM, VMEM] + ([pl.BlockSpec(memory_space=pl.ANY), VMEM] if before else [])
    return pl.pallas_call(
        update_kernel,
        out_shape=(shape((8, 256, 256), f32), shape((8, 256), f32)),
        in_specs=specs,
        out_specs=(pl.BlockSpec(memory_space=pl.ANY), VMEM),
        scratch_shapes=[pltpu.VMEM((4, 256, 256), f32), pltpu.SemaphoreType.DMA],
        input_output_aliases={4: 0} if before else {},
        compiler_params=pltpu.CompilerParams(vmem_limit_bytes=8 * 1024 * 1024),
        cost_estimate=pl.CostEstimate(flops=0, bytes_accessed=3_000_000, transcendentals=0),
    )(*given)


def body(
    embeddings, row_accum, relations, rel_accum, matching, src_rows, dst_rows, rel_ids, neg_rows
):
    place = jnp.stack([lax.axis_index(name) for name in ("core", "zhi", "x")]).astype(jnp.int32)
    line = lambda v: v.reshape(1, 512)
    pieces = call(first_kernel, shape((64, 8, 128), bf16), 0, (embeddings,), moved=400_000)
    arrived = spread(pieces, DOM)
    pack = call(
        pack_kernel,
        shape((272, 256), bf16),
        0,
        (embeddings, line(src_rows), line(rel_ids), line(dst_rows), line(neg_rows)),
        flops=2_000_000_000,
        moved=400_000,
    )
    packs = [pack] + [
        lax.ppermute(pack, "x", [(i, (i - k) % 4) for i in range(4)]) for k in range(1, 4)
    ]
    packs[1], packs[3], arrived = lax.optimization_barrier((packs[1], packs[3], arrived))
    routed = call(take_kernel, shape((64, 2, 8, 128), bf16), 1, (matching, arrived), moved=400_000)
    rows_in = spread(routed.reshape(128, 8, 128), DOM_Z).reshape(64, 2, 8, 128)
    trans, source, rel_b, counts, known = call(
        trans_kernel,
        (
            shape((2048, 256), bf16),
            shape((2048, 256), bf16),
            shape((8, 256, 256), bf16),
            shape((8, 512), f32),
            shape((16, 512), f32),
        ),
        1,
        (place, *packs, relations),
        flops=2_500_000_000,
        moved=6_000_000,
        space=16,
    )
    weight, g_trans, kept, given = call(
        score_kernel,
        (
            shape((2048, 512), bf16),
            shape((2048, 256), bf16),
            shape((1024, 256), bf16),
            shape((1024, 256), bf16),
        ),
        1,
        (place, rows_in, trans, source, counts, known),
        flops=3_200_000_000,
        moved=6_000_000,
        scratch=[pltpu.VMEM((512, 256), bf16)],
        space=20,
    )
    came = swap(given, "core")
    g_rows, own = call(
        back_kernel,
        (shape((2, 256, 256), bf16), shape((4, 256, 256), bf16)),
        1,
        (place, weight, trans, g_trans, rel_b, known),
        flops=3_000_000_000,
        moved=6_000_000,
        space=16,
    )
    joined = call(join_kernel, shape((4, 512, 256), bf16), 0, (own, kept, came), moved=2_000_000)
    got = spread(joined, "x")
    out, own_here = call(
        pieces_kernel,
        (shape((64, 2, 16, 128), bf16), shape((256, 256), f32)),
        0,
        (got, g_rows),
        moved=2_000_000,
    )
    mid = spread(out.reshape(128, 16, 128), DOM_Z).reshape(64, 2, 16, 128)
    routed_back = call(
        route_kernel,
        shape((64, 2, 8, 128), bf16),
        2,
        (place, matching, mid),
        moved=512_000,
        scratch=[pltpu.VMEM((64, 8, 128), f32)],
    )
    last = spread(routed_back.reshape(128, 8, 128), DOM_Z).reshape(64, 2, 8, 128)
    rel_four = spread(
        call(rel_kernel, shape((4, 256, 256), bf16), 1, (place, last), moved=512_000), "x"
    )
    new_embeddings, new_row_accum = call(
        rows_kernel,
        (shape((256, 256), f32), shape((1, 256), f32)),
        1,
        (place, embeddings, row_accum.reshape(1, 256), own_here, last),
        flops=1_000_000,
        moved=1_000_000,
    )
    rel_rest = swap(rel_four, "core")
    half = update_half(place, relations, rel_accum, rel_four)
    new_relations, new_rel_accum = update_half(place, relations, rel_accum, rel_rest, half)
    return new_embeddings, new_row_accum.reshape(256), new_relations, new_rel_accum


def solution(mesh):
    fine = Mesh(mesh.devices.reshape(4, 8, 2, 2, 4), AXES)
    placed = (
        P(AXES, None),
        P(AXES),
        P(),
        P(),
        P(),
        P(AXES),
        P(AXES),
        P(AXES),
        P(AXES, None),
    )
    return jax.shard_map(
        body,
        mesh=fine,
        in_specs=placed,
        out_specs=(P(AXES, None), P(AXES), P(), P()),
        check_vma=False,
    )
```

time: 169 us -> 177 us (1.047)
  blocking collectives: 69.8 us -> 83 us
  waiting for transfers between devices: 17.4 us -> 6.23 us
  Pallas kernels: 18.2 us -> 26.6 us
  starting transfers between devices: 51.7 us -> 49.7 us
    ppermute x5 -> x2, starting transfers between devices: 29.6 us -> 8.31 us  [swap(): return lax.ppermute(value, axis, [(0, 1), (1, 0)])]
    all_to_all x4, blocking collectives: 69.8 us -> 83 us  [spread(): return lax.all_to_all(value, axis, split_axis=0, concat_axis=0, tiled=True)]
    ppermute x0 -> x3, starting transfers between devices: none -> 11 us  [body(): lax.ppermute(pack, 'x', [(i, (i - k) % 4) for i in range(4)])]
    ppermute x5 -> x2, waiting for transfers between devices: 8.79 us -> 0.01 us  [swap(): return lax.ppermute(value, axis, [(0, 1), (1, 0)])]
    all_to_all x3 -> x2, waiting for transfers between devices: 8.65 us -> 0.01 us  [spread(): return lax.all_to_all(value, axis, split_axis=0, concat_axis=0, tiled=True)]
    pallas_call x12 -> x11, Pallas kernels: 12.9 us -> 21.2 us  [call(): pl.pallas_call(kernel, out_shape=outs, in_specs=[SMEM] * scalars + [VMEM]...]
    all_to_all x3 -> x2, starting transfers between devices: 22.1 us -> 30.4 us  [spread(): return lax.all_to_all(value, axis, split_axis=0, concat_axis=0, tiled=True)]
    ppermute x0 -> x3, waiting for transfers between devices: none -> 6.22 us  [body(): lax.ppermute(pack, 'x', [(i, (i - k) % 4) for i in range(4)])]
  transfers between devices with their start and end apart: 8 -> 7, of which waited for: 5 -> 3; matrix products, arithmetic and copies ran while one was open for 0% -> 0% of each run, Pallas kernels for 6% -> 8%
where the time goes in v4:
time: 177 us
  blocking collectives  83 us (47%)
  starting transfers between devices  49.7 us (28%)
  Pallas kernels  26.6 us (15%)
  local copies, waits for them, and re-layouts  10 us (6%)
  waiting for transfers between devices  6.23 us (4%)
    all_to_all x4, blocking collectives, spread(): return lax.all_to_all(value, axis, split_axis=0, concat_axis=0, tiled=True)  83 us
    all_to_all x2, starting transfers between devices, spread(): return lax.all_to_all(value, axis, split_axis=0, concat_axis=0, tiled=True)  30.4 us
    pallas_call x11, Pallas kernels, call(): pl.pallas_call(kernel, out_shape=outs, in_specs=[SMEM] * scalars + [VMEM]...  21.2 us
    ppermute x3, starting transfers between devices, body(): lax.ppermute(pack, 'x', [(i, (i - k) % 4) for i in range(4)])  11 us
    unnamed x36, local copies, waits for them, and re-layouts  10 us
    ppermute x2, starting transfers between devices, swap(): return lax.ppermute(value, axis, [(0, 1), (1, 0)])  8.31 us
    ppermute x3, waiting for transfers between devices, body(): lax.ppermute(pack, 'x', [(i, (i - k) % 4) for i in range(4)])  6.22 us
    pallas_call x2, Pallas kernels, update_half(): pl.pallas_call(update_kernel, out_shape=(shape((8, 256, 256), f32), shape...  5.38 us
  transfers between devices with their start and end apart: 7, of which 3 were waited for; matrix products, arithmetic and copies ran while one was open for 0% of the time, Pallas kernels for 8%

profile of v4, /device:TPU:1, one launch (start us, length us, event | category | flops | bytes accessed | tf_op | source)
XLA Modules:
  0.0 176.6 jit_solution(5561976787787977380)
XLA Ops:
  0.6 0.0 copy-start.1
  0.6 0.9 copy-done.1
  1.6 0.7 shard_map.121
  2.3 14.6 %all-to-all-start = ((bf16[64,8,128]{2,1,0:T(8,128)(2,1)}), bf16[64,8,128]{2,1,0:T(8,128)(2,1)S(1)}, u32[]{:S(2)}, u32[]{:S(2)}) async-start(bf16[64,8,128]{2,1,0:T(8,128)(2,1)} %shard_map.121), calls=%async_computation | async-start | bytes 262144 | tf_op jit(solution)/shard_map/all_to_all | solution.py:45
  16.8 0.0 copy-start.2
  16.9 0.9 copy-done.2
  17.8 0.7 copy-done.7
  18.5 0.7 copy-done.8
  19.2 0.7 copy-done.9
  19.8 0.7 copy-done.10
  20.6 3.3 %collective-permute-start.1 = (bf16[272,256]{1,0:T(8,128)(2,1)S(1)}, bf16[272,256]{1,0:T(8,128)(2,1)S(1)}, u32[]{:S(2)}, u32[]{:S(2)}) collective-permute-start(bf16[272,256]{1,0:T(8,128)(2,1)S(1)} %shard_map.120.pack0), channel_id=1, source_target_pairs={{0,1},{1,2},{2,3},{3,0},{4,5},{5,6},{6,7},{7,4},{8,9},{9,10},{10,1... | collective-permute-start | bytes 417800 | tf_op jit(solution)/shard_map/ppermute | solution.py:300
  23.8 3.4 %collective-permute-start = (bf16[272,256]{1,0:T(8,128)(2,1)S(1)}, bf16[272,256]{1,0:T(8,128)(2,1)S(1)}, u32[]{:S(2)}, u32[]{:S(2)}) collective-permute-start(bf16[272,256]{1,0:T(8,128)(2,1)S(1)} %shard_map.120.pack0), channel_id=1, source_target_pairs={{0,3},{1,0},{2,1},{3,2},{4,7},{5,4},{6,5},{7,6},{8,11},{9,8},{10,9... | collective-permute-start | bytes 417800 | tf_op jit(solution)/shard_map/ppermute | solution.py:300
  27.2 1.4 collective-permute-done.1.pack3
  28.6 1.6 collective-permute-done.pack1
  30.2 0.0 all-to-all-done.arrived
  30.2 1.3 shard_map.122
  31.5 15.8 %all-to-all-start.1 = ((bf16[128,8,128]{2,1,0:T(8,128)(2,1)}), bf16[128,8,128]{2,1,0:T(8,128)(2,1)S(1)}, u32[]{:S(2)}, u32[]{:S(2)}) async-start(bf16[128,8,128]{2,1,0:T(8,128)(2,1)} %bitcast.7), calls=%async_computation.1 | async-start | bytes 524288 | tf_op jit(solution)/shard_map/all_to_all | solution.py:45
  47.3 4.4 %collective-permute-start.2 = (bf16[272,256]{1,0:T(8,128)(2,1)S(1)}, bf16[272,256]{1,0:T(8,128)(2,1)S(1)}, u32[]{:S(2)}, u32[]{:S(2)}) collective-permute-start(bf16[272,256]{1,0:T(8,128)(2,1)S(1)} %shard_map.120.pack0), channel_id=1, source_target_pairs={{0,2},{1,3},{2,0},{3,1},{4,6},{5,7},{6,4},{7,5},{8,10},{9,11},{10,... | collective-permute-start | bytes 417800 | tf_op jit(solution)/shard_map/ppermute | solution.py:300
  51.7 0.1 pad_add_fusion.place
  51.8 3.2 %collective-permute-done.2.pack2 = bf16[272,256]{1,0:T(8,128)(2,1)S(1)} collective-permute-done((bf16[272,256]{1,0:T(8,128)(2,1)S(1)}, bf16[272,256]{1,0:T(8,128)(2,1)S(1)}, u32[]{:S(2)}, u32[]{:S(2)}) %collective-permute-start.2) | collective-permute-done | bytes 139296 | tf_op jit(solution)/shard_map/ppermute | solution.py:300
  55.0 4.5 %shard_map.123 = (bf16[2048,256]{1,0:T(8,128)(2,1)S(1)}, bf16[2048,256]{1,0:T(8,128)(2,1)S(1)}, bf16[8,256,256]{2,1,0:T(8,128)(2,1)S(1)}, f32[8,512]{1,0:T(8,128)S(1)}, f32[16,512]{1,0:T(8,128)S(1)}) custom-call(s32[3]{0:T(128)S(1)} %pad_add_fusion.place, bf16[272,256]{1,0:T(8,128)(2,1)S(1)} %shard_map.120.pack0, ...), custom_call_target="tpu_custom_call" | custom-call | flops 2500000000 | bytes 6000000 | tf_op jit(solution)/shard_map/pallas_call | solution.py:29
  59.5 0.0 copy-start.11
  59.5 1.0 copy-done.11
  60.5 1.0 copy-done.14
  61.5 1.0 copy-done.16
  62.4 0.0 all-to-all-done.1
  62.4 1.2 copy-done.12
  63.7 1.2 copy-done.17
  64.9 4.9 %shard_map.124 = (bf16[2048,512]{1,0:T(8,128)(2,1)S(1)}, bf16[2048,256]{1,0:T(8,128)(2,1)S(1)}, bf16[1024,256]{1,0:T(8,128)(2,1)S(1)}, bf16[1024,256]{1,0:T(8,128)(2,1)S(1)}) custom-call(s32[3]{0:T(128)S(1)} %pad_add_fusion.place, bf16[64,2,8,128]{3,2,1,0:T(8,128)(2,1)S(1)} %bitcast.19, bf16[2048,256]{1,0:T(8,128)(2,1)S(1)} %copy-done.12, ...), custom_call_target="tpu_custom_call" | custom-call | flops 3200000000 | bytes 6000000 | tf_op jit(solution)/shard_map/pallas_call | solution.py:29
  69.8 3.9 %collective-permute-start.3 = (bf16[1024,256]{1,0:T(8,128)(2,1)S(1)}, bf16[1024,256]{1,0:T(8,128)(2,1)S(1)}, u32[]{:S(2)}, u32[]{:S(2)}) collective-permute-start(bf16[1024,256]{1,0:T(8,128)(2,1)S(1)} %get-tuple-element.38), channel_id=1, source_target_pairs={{0,8},{8,0},{1,9},{9,1},{2,10},{10,2},{3,11},{11,3},{4,12},{12,4},... | collective-permute-start | bytes 1572872 | tf_op jit(solution)/shard_map/ppermute | solution.py:41
  73.7 6.5 %shard_map.125 = (bf16[2,256,256]{2,1,0:T(8,128)(2,1)S(1)}, bf16[4,256,256]{2,1,0:T(8,128)(2,1)S(1)}) custom-call(s32[3]{0:T(128)S(1)} %pad_add_fusion.place, bf16[2048,512]{1,0:T(8,128)(2,1)S(1)} %get-tuple-element.33.weight, bf16[2048,256]{1,0:T(8,128)(2,1)S(1)} %copy-done.13, bf16[2048,256]{1,0:T(8,128)(2,1)S(1)} %get-tuple-element.34.g_trans, ...), custom_call_target="tpu_custom_call" | custom-call | flops 3000000000 | bytes 6000000 | tf_op jit(solution)/shard_map/pallas_call | solution.py:29
  80.2 0.0 collective-permute-done.3.came
  80.2 0.1 shard_map.126
  80.4 18.7 %all_to_all.30.got = bf16[4,512,256]{2,1,0:T(8,128)(2,1)S(1)} all-to-all(bf16[4,512,256]{2,1,0:T(8,128)(2,1)S(1)} %shard_map.126), channel_id=1, replica_groups=mesh['zlo'=4,'y'=8,'core'=2,'zhi'=2,'x'=4] {'x'}, dimensions={0} | all-to-all | bytes 2097152 | tf_op jit(solution)/shard_map/all_to_all | solution.py:45
  99.0 0.2 shard_map.127
  99.3 0.0 copy-start.3
  99.3 0.0 copy-start.6
  99.3 33.2 %all_to_all.31 = bf16[128,16,128]{2,1,0:T(8,128)(2,1)S(1)} all-to-all(bf16[128,16,128]{2,1,0:T(8,128)(2,1)S(1)} %bitcast.18), channel_id=1, replica_groups=mesh['zlo'=4,'y'=8,'core'=2,'zhi'=2,'x'=4] {'zlo','y','core','zhi'}, dimensions={0} | all-to-all | bytes 1048576 | tf_op jit(solution)/shard_map/all_to_all | solution.py:45
  132.5 0.8 shard_map.128
  133.3 20.8 %all_to_all.32 = bf16[128,8,128]{2,1,0:T(8,128)(2,1)S(1)} all-to-all(bf16[128,8,128]{2,1,0:T(8,128)(2,1)S(1)} %bitcast.17), channel_id=1, replica_groups=mesh['zlo'=4,'y'=8,'core'=2,'zhi'=2,'x'=4] {'zlo','y','core','zhi'}, dimensions={0} | all-to-all | bytes 524288 | tf_op jit(solution)/shard_map/all_to_all | solution.py:45
  154.1 0.6 shard_map.130
  154.7 10.3 %all_to_all.33.grads = bf16[4,256,256]{2,1,0:T(8,128)(2,1)S(1)} all-to-all(bf16[4,256,256]{2,1,0:T(8,128)(2,1)S(1)} %shard_map.130), channel_id=1, replica_groups=mesh['zlo'=4,'y'=8,'core'=2,'zhi'=2,'x'=4] {'x'}, dimensions={0} | all-to-all | bytes 1048576 | tf_op jit(solution)/shard_map/all_to_all | solution.py:45
  165.1 4.4 %collective-permute-start.4 = (bf16[4,256,256]{2,1,0:T(8,128)(2,1)S(1)}, bf16[4,256,256]{2,1,0:T(8,128)(2,1)S(1)}, u32[]{:S(2)}, u32[]{:S(2)}) collective-permute-start(bf16[4,256,256]{2,1,0:T(8,128)(2,1)S(1)} %all_to_all.33.grads), channel_id=1, source_target_pairs={{0,8},{8,0},{1,9},{9,1},{2,10},{10,2},{3,11},{11,3},{4,12},{12,4},... | collective-permute-start | bytes 1572872 | tf_op jit(solution)/shard_map/ppermute | solution.py:41
  169.5 0.0 copy-done.3
  169.5 1.6 shard_map.129
  171.1 2.4 %shard_map.131 = (f32[8,256,256]{2,1,0:T(8,128)}, f32[8,256]{1,0:T(8,128)S(1)}) custom-call(s32[3]{0:T(128)S(1)} %pad_add_fusion.place, f32[8,256,256]{2,1,0:T(8,128)S(1)} %copy-done, f32[8,256]{1,0:T(8,128)S(1)} %copy-done.4, bf16[4,256,256]{2,1,0:T(8,128)(2,1)S(1)} %all_to_all.33.grads), custom_call_target="tpu_custom_call" | custom-call | bytes 3000000 | tf_op jit(solution)/shard_map/pallas_call | solution.py:272
  173.5 0.0 collective-permute-done.4.grads
  173.5 3.0 %shard_map.132 = (f32[8,256,256]{2,1,0:T(8,128)}, f32[8,256]{1,0:T(8,128)}) custom-call(s32[3]{0:T(128)S(1)} %pad_add_fusion.place, f32[8,256,256]{2,1,0:T(8,128)S(1)} %copy-done, f32[8,256]{1,0:T(8,128)S(1)} %copy-done.4, bf16[4,256,256]{2,1,0:T(8,128)(2,1)S(1)} %collective-permute-done.4.grads, ...), custom_call_target="tpu_custom_call", output_to_operand_aliasing={{0}: (4, {})} | custom-call | bytes 3000000 | tf_op jit(solution)/shard_map/pallas_call | solution.py:272
  (20 shorter events, 0.1 us)
Async XLA Ops:
  0.6 1.0 copy-start.1
  2.3 27.9 %all-to-all-start = ((bf16[64,8,128]{2,1,0:T(8,128)(2,1)}), bf16[64,8,128]{2,1,0:T(8,128)(2,1)S(1)}, u32[]{:S(2)}, u32[]{:S(2)}) async-start(bf16[64,8,128]{2,1,0:T(8,128)(2,1)} %shard_map.121), calls=%async_computation | async-start | bytes 262144 | tf_op jit(solution)/shard_map/all_to_all | solution.py:45
  16.8 1.0 copy-start.2
  17.8 0.7 copy-start.7
  18.5 0.7 copy-start.8
  19.2 0.7 copy-start.9
  19.8 0.7 copy-start.10
  20.5 9.7 %copy-start.5 = (s32[64]{0:T(128)S(1)}, s32[64]{0:T(128)}, u32[]{:S(2)}) copy-start(s32[64]{0:T(128)} %matching.3) | copy-start | bytes 772
  20.5 34.5 %copy-start = (f32[8,256,256]{2,1,0:T(8,128)S(1)}, f32[8,256,256]{2,1,0:T(8,128)}, u32[]{:S(2)}) copy-start(f32[8,256,256]{2,1,0:T(8,128)} %rel.5) | copy-start | bytes 6291460
  20.6 8.0 %collective-permute-start.1 = (bf16[272,256]{1,0:T(8,128)(2,1)S(1)}, bf16[272,256]{1,0:T(8,128)(2,1)S(1)}, u32[]{:S(2)}, u32[]{:S(2)}) collective-permute-start(bf16[272,256]{1,0:T(8,128)(2,1)S(1)} %shard_map.120.pack0), channel_id=1, source_target_pairs={{0,1},{1,2},{2,3},{3,0},{4,5},{5,6},{6,7},{7,4},{8,9},{9,10},{10,1... | collective-permute-start | bytes 417800 | tf_op jit(solution)/shard_map/ppermute | solution.py:300
  23.8 6.4 %collective-permute-start = (bf16[272,256]{1,0:T(8,128)(2,1)S(1)}, bf16[272,256]{1,0:T(8,128)(2,1)S(1)}, u32[]{:S(2)}, u32[]{:S(2)}) collective-permute-start(bf16[272,256]{1,0:T(8,128)(2,1)S(1)} %shard_map.120.pack0), channel_id=1, source_target_pairs={{0,3},{1,0},{2,1},{3,2},{4,7},{5,4},{6,5},{7,6},{8,11},{9,8},{10,9... | collective-permute-start | bytes 417800 | tf_op jit(solution)/shard_map/ppermute | solution.py:300
  31.5 30.9 %all-to-all-start.1 = ((bf16[128,8,128]{2,1,0:T(8,128)(2,1)}), bf16[128,8,128]{2,1,0:T(8,128)(2,1)S(1)}, u32[]{:S(2)}, u32[]{:S(2)}) async-start(bf16[128,8,128]{2,1,0:T(8,128)(2,1)} %bitcast.7), calls=%async_computation.1 | async-start | bytes 524288 | tf_op jit(solution)/shard_map/all_to_all | solution.py:45
  47.3 7.7 %collective-permute-start.2 = (bf16[272,256]{1,0:T(8,128)(2,1)S(1)}, bf16[272,256]{1,0:T(8,128)(2,1)S(1)}, u32[]{:S(2)}, u32[]{:S(2)}) collective-permute-start(bf16[272,256]{1,0:T(8,128)(2,1)S(1)} %shard_map.120.pack0), channel_id=1, source_target_pairs={{0,2},{1,3},{2,0},{3,1},{4,6},{5,7},{6,4},{7,5},{8,10},{9,11},{10,... | collective-permute-start | bytes 417800 | tf_op jit(solution)/shard_map/ppermute | solution.py:300
  59.5 1.0 copy-start.11
  60.5 1.0 copy-start.14
  61.5 1.0 copy-start.16
  62.4 1.2 copy-start.12
  63.7 1.2 copy-start.17
  64.9 8.8 %copy-start.13 = (bf16[2048,256]{1,0:T(8,128)(2,1)S(1)}, bf16[2048,256]{1,0:T(8,128)(2,1)}, u32[]{:S(2)}) copy-start(bf16[2048,256]{1,0:T(8,128)(2,1)} %copy-done.11) | copy-start | bytes 3145732
  64.9 8.8 %copy-start.15 = (bf16[8,256,256]{2,1,0:T(8,128)(2,1)S(1)}, bf16[8,256,256]{2,1,0:T(8,128)(2,1)}, u32[]{:S(2)}) copy-start(bf16[8,256,256]{2,1,0:T(8,128)(2,1)} %copy-done.14) | copy-start | bytes 3145732
  69.8 10.4 %collective-permute-start.3 = (bf16[1024,256]{1,0:T(8,128)(2,1)S(1)}, bf16[1024,256]{1,0:T(8,128)(2,1)S(1)}, u32[]{:S(2)}, u32[]{:S(2)}) collective-permute-start(bf16[1024,256]{1,0:T(8,128)(2,1)S(1)} %get-tuple-element.38), channel_id=1, source_target_pairs={{0,8},{8,0},{1,9},{9,1},{2,10},{10,2},{3,11},{11,3},{4,12},{12,4},... | collective-permute-start | bytes 1572872 | tf_op jit(solution)/shard_map/ppermute | solution.py:41
  99.3 70.2 %copy-start.3 = (f32[256,256]{1,0:T(8,128)S(1)}, f32[256,256]{1,0:T(8,128)}, u32[]{:S(2)}) copy-start(f32[256,256]{1,0:T(8,128)} %emb.5) | copy-start | bytes 786436
  99.3 70.2 %copy-start.6 = (f32[256]{0:T(256)S(1)}, f32[256]{0:T(256)}, u32[]{:S(2)}) copy-start(f32[256]{0:T(256)} %param.10) | copy-start | bytes 3076
  132.5 38.6 %copy-start.4 = (f32[8,256]{1,0:T(8,128)S(1)}, f32[8,256]{1,0:T(8,128)}, u32[]{:S(2)}) copy-start(f32[8,256]{1,0:T(8,128)} %accum.3) | copy-start | bytes 24580
  165.1 8.4 %collective-permute-start.4 = (bf16[4,256,256]{2,1,0:T(8,128)(2,1)S(1)}, bf16[4,256,256]{2,1,0:T(8,128)(2,1)S(1)}, u32[]{:S(2)}, u32[]{:S(2)}) collective-permute-start(bf16[4,256,256]{2,1,0:T(8,128)(2,1)S(1)} %all_to_all.33.grads), channel_id=1, source_target_pairs={{0,8},{8,0},{1,9},{9,1},{2,10},{10,2},{3,11},{11,3},{4,12},{12,4},... | collective-permute-start | bytes 1572872 | tf_op jit(solution)/shard_map/ppermute | solution.py:41

commit v5 on v4

v5 whole, which is shorter than its diff:
```python
import jax
import jax.numpy as jnp
from jax import lax
from jax.experimental import pallas as pl
from jax.experimental.pallas import tpu as pltpu
from jax.sharding import Mesh, PartitionSpec as P

learn_rate = 0.1
AXES = ("zlo", "y", "core", "zhi", "x")
DOM = ("zlo", "y", "core")
DOM_Z = DOM + ("zhi",)
bf16 = jnp.bfloat16
f32 = jnp.float32
VMEM = pl.BlockSpec(memory_space=pltpu.VMEM)
ANY = pl.BlockSpec(memory_space=pltpu.HBM)
SMEM = pl.BlockSpec(memory_space=pltpu.SMEM)
NN = (((1,), (0,)), ((), ()))
NT = (((1,), (1,)), ((), ()))


def shape(dims, dtype):
    return jax.ShapeDtypeStruct(dims, dtype)


def dot(a, b, dims=NN):
    return lax.dot_general(a, b, dims, preferred_element_type=f32)


def call(kernel, outs, scalars, args, flops=0, moved=0, scratch=(), space=8, far=(), far_outs=()):
    specs = [SMEM] * scalars + [ANY if k in far else VMEM for k in range(scalars, len(args))]
    many = isinstance(outs, tuple)
    return pl.pallas_call(
        kernel,
        out_shape=outs,
        in_specs=specs,
        out_specs=tuple(ANY if k in far_outs else VMEM for k in range(len(outs))) if many else VMEM,
        scratch_shapes=list(scratch),
        compiler_params=pltpu.CompilerParams(vmem_limit_bytes=space * 1024 * 1024),
        cost_estimate=pl.CostEstimate(flops=flops, bytes_accessed=moved, transcendentals=0),
    )(*args)


def swap(value, axis):
    return lax.ppermute(value, axis, [(0, 1), (1, 0)])


def spread(value, axis):
    return lax.all_to_all(value, axis, split_axis=0, concat_axis=0, tiled=True)


def first_kernel(emb, src, rel, dst, neg, pieces, pack, rows, index, sems):
    copies = [pltpu.make_async_copy(emb, rows, sems.at[0])]
    for k, part in enumerate((src, rel, dst, neg)):
        copies.append(pltpu.make_async_copy(part, index.at[k], sems.at[k + 1]))
    for copy in copies:
        copy.start()
    for copy in copies:
        copy.wait()
    wide = jnp.concatenate([index[k] for k in range(4)], axis=0)
    high = wide // 256
    low = (wide - high * 256).astype(f32)
    both = jnp.concatenate([high.astype(f32), low], axis=0)
    pack[256:272, :] = jnp.concatenate([both[:, :256], both[:, 256:]], axis=0).astype(bf16)
    pack[0:256, :] = rows[...].astype(bf16)
    for h in range(2):
        half = rows[:, h * 128 : (h + 1) * 128]
        pieces[h * 32 : (h + 1) * 32] = half.reshape(32, 8, 128).astype(bf16)


def take_kernel(matching, arrived, routed):
    for d in range(64):
        piece = arrived[matching[d]]
        routed[d, 0] = piece
        routed[d, 1] = piece


def indices(part):
    part = part.astype(f32)
    both = jnp.concatenate([part[0:8], part[8:16]], axis=1)
    return both[0:4] * 256.0 + both[4:8]


def columns(value):
    return jnp.concatenate([value, value], axis=0).T


def lane_ids(rows, width):
    return lax.broadcasted_iota(jnp.int32, (rows, width), 1)


def row_ids(x, rows):
    ids = lane_ids(rows, 512)
    return (ids + jnp.where(ids >= 256, 768, 0) + x * 256).astype(f32)


def by_relation(kinds, rows):
    parts = [jnp.where(kinds == float(r), rows, 0.0).astype(bf16) for r in range(8)]
    return jnp.concatenate(parts, axis=1)


def trans_kernel(place, packs, rel, counts, known, *rest):
    outs, (trans, source, *rel_b), sems = rest[: len(rest) // 2], rest[len(rest) // 2 : -1], rest[-1]
    stack = jnp.concatenate([rel[r].astype(bf16) for r in range(8)], axis=1)
    copies = []
    if rel_b:
        for r in range(8):
            rel_b[0][r] = rel[r].astype(bf16)
        copies.append(pltpu.make_async_copy(rel_b[0], outs[2], sems.at[2]))
        copies[-1].start()
    ids = lane_ids(512, 256).astype(f32)
    wide = row_ids(place[2], 512)
    for s in range(2):
        index = indices(packs[s * 272 + 256 : s * 272 + 272, :])
        known[s * 4 : (s + 1) * 4, :] = index
        column = columns(index)
        hot = (column[:, 0:1] == ids).astype(f32).astype(bf16)
        rows = dot(hot, packs[s * 272 : s * 272 + 256, :])
        source[s * 512 : (s + 1) * 512, :] = rows.astype(bf16)
        trans[s * 512 : (s + 1) * 512, :] = dot(by_relation(column[:, 1:2], rows), stack, NT).astype(bf16)
        hits = (column[:, 3:4] == wide).astype(f32)
        counts[s : s + 1, :] = jnp.sum(hits, axis=0, keepdims=True)
    counts[2:8, :] = jnp.zeros((6, 512), f32)
    for k, held in enumerate((trans, source)):
        copies.append(pltpu.make_async_copy(held, outs[k], sems.at[k]))
        copies[-1].start()
    for copy in copies:
        copy.wait()


def score_kernel(
    place, rows_in, counts0, counts1, known0, known1, trans0, trans1, source0, source1,
    weight, g_trans, kept, given, rows, trans, source, sems
):
    copies = []
    for k, (part, held) in enumerate(
        ((trans0, trans), (trans1, trans), (source0, source), (source1, source))
    ):
        span = pl.ds((k % 2) * 1024, 1024)
        copies.append(pltpu.make_async_copy(part, held.at[span, :], sems.at[k]))
        copies[-1].start()
    core = place[0]
    for z in range(2):
        both = rows_in[:, z].reshape(2, 256, 128)
        rows[z * 256 : (z + 1) * 256, :] = jnp.concatenate([both[0], both[1]], axis=1)
    index = [known[s * 4 : (s + 1) * 4, :] for known in (known0, known1) for s in range(2)]
    ids = row_ids(place[2], 256)
    for b in range(8):
        if b % 4 == 0:
            copies[b // 4].wait()
        s = b // 2
        column = columns(index[s])[(b % 2) * 256 : (b % 2 + 1) * 256]
        span = slice(b * 256, (b + 1) * 256)
        score = dot(trans[span, :], rows[...], NT)
        sig = 1.0 / (1.0 + jnp.exp(-score))
        count = (counts0, counts1)[s // 2][s % 2 : s % 2 + 1, :]
        hit = column[:, 2:3] == ids
        part = jnp.where(hit, (count + 1.0) * sig - 1.0, count * sig).astype(bf16)
        weight[span, :] = part
        g_trans[span, :] = dot(part, rows[...]).astype(bf16)
    turned = g_trans[...].astype(f32).T
    kinds = jnp.concatenate([part[1:2] for part in index], axis=1)
    copies[2].wait()
    copies[3].wait()
    for r in range(8):
        wanted = r + 4 * core if r < 4 else r - 4 * core
        masked = jnp.where(kinds == wanted.astype(f32), turned, 0.0).astype(bf16)
        grad = dot(masked, source[...]).astype(bf16)
        if r < 4:
            kept[r * 256 : (r + 1) * 256, :] = grad
        else:
            given[(r - 4) * 256 : (r - 3) * 256, :] = grad


def back_kernel(
    place, weight, g_trans, known0, known1, trans0, trans1, rel_in, mine, theirs, own,
    trans, rel_b, sems
):
    copies = [pltpu.make_async_copy(rel_in, rel_b, sems.at[2])]
    for k, part in enumerate((trans0, trans1)):
        span = pl.ds(k * 1024, 1024)
        copies.append(pltpu.make_async_copy(part, trans.at[span, :], sems.at[k]))
    for copy in copies:
        copy.start()
    sub_ids = lax.broadcasted_iota(jnp.int32, (256, 512), 0).astype(f32)
    copies[0].wait()
    stack = rel_b[...].reshape(2048, 256)
    for s in range(4):
        index = (known0, known1)[s // 2][(s % 2) * 4 : (s % 2 + 1) * 4, :]
        grad = g_trans[s * 512 : (s + 1) * 512, :].astype(f32)
        total = dot(by_relation(columns(index)[:, 1:2], grad), stack)
        hot = (index[0:1, :] == sub_ids).astype(f32).astype(bf16)
        own[place[2] ^ s] = dot(hot, total.astype(bf16)).astype(bf16)
    copies[1].wait()
    copies[2].wait()
    turned = trans[...].astype(f32).T.astype(bf16)
    near = dot(turned, weight[:, 0:256]).T
    far = dot(turned, weight[:, 256:512]).T
    mine[...] = jnp.where(place[1] == 0, near, far)
    theirs[...] = jnp.where(place[1] == 0, far, near).astype(bf16)


def join_kernel(own, kept, came, out):
    for k in range(4):
        out[k, 0:256, :] = own[k]
        span = slice(k * 256, (k + 1) * 256)
        out[k, 256:512, :] = (kept[span, :].astype(f32) + came[span, :].astype(f32)).astype(bf16)


def upper(tiles):
    return lax.broadcasted_iota(jnp.int32, tiles, len(tiles) - 2) % 8 < 4


def pieces_kernel(got, mine, came, out, own_here):
    first = upper((32, 8, 128))
    for h in range(2):
        half = slice(h * 128, (h + 1) * 128)
        total = got[0, :, half].astype(f32)
        for k in range(1, 4):
            total = total + got[k, :, half].astype(f32)
        own_here[:, half] = total[0:256]
        rel = total[256:512].reshape(32, 8, 128)
        rows = (mine[:, half] + came[:, half].astype(f32)).reshape(32, 8, 128)
        span = slice(h * 32, (h + 1) * 32)
        out[span, 0] = jnp.where(first, rows, rel).astype(bf16)
        out[span, 1] = jnp.where(first, rel, rows).astype(bf16)


def route_kernel(place, matching, mid, out):
    rel = [jnp.zeros((8, 128), f32), jnp.zeros((8, 128), f32)]
    for d in range(64):
        rel[d % 2] = rel[d % 2] + (mid[d, 0].astype(f32) + mid[d, 1].astype(f32))
    near = upper((8, 128)) == (place[1] == 0)
    for d in range(64):
        target = matching[d]
        tail = jnp.where(target % 2 == 0, rel[0], rel[1])
        for z in range(2):
            out[target, z] = jnp.where(near, mid[d, z].astype(f32), tail).astype(bf16)


def rel_kernel(last, out):
    first = upper((32, 8, 128))
    for h in range(2):
        even = last[h * 32 : (h + 1) * 32, 0].astype(f32)
        odd = last[h * 32 : (h + 1) * 32, 1].astype(f32)
        part = jnp.where(first, odd, even).reshape(256, 128).astype(bf16)
        for k in range(4):
            out[k, :, h * 128 : (h + 1) * 128] = part


def to_row(column):
    return jnp.broadcast_to(column, (256, 128)).T[0:1]


def to_column(row):
    return jnp.broadcast_to(row, (128, 256)).T[:, 0:1]


def rows_kernel(emb, accum, own_here, last, new_emb, new_accum):
    first = upper((64, 8, 128))
    rows = jnp.where(first, last[:, 0].astype(f32), last[:, 1].astype(f32))
    halves = [rows[h * 32 : (h + 1) * 32].reshape(256, 128) for h in range(2)]
    grad = own_here[...] + jnp.concatenate(halves, axis=1)
    total = to_column(accum[...]) + jnp.mean(grad * grad, axis=1, keepdims=True)
    new_emb[...] = emb[...] - grad * (learn_rate / jnp.sqrt(total))
    new_accum[...] = to_row(total)


def update_kernel(place, rel, accum, grads, *rest):
    if len(rest) == 6:
        core, (seen, held, new_rel, new_accum, block, sem) = 1 - place[0], rest
    else:
        core, (new_rel, new_accum, block, sem) = place[0], rest
    old = jnp.concatenate([accum[...], accum[...]], axis=0)
    column = jnp.where(core == 0, old[0:8], old[4:12]).T
    totals = []
    for r in range(4):
        grad = grads[r].astype(f32)
        total = column[:, r : r + 1] + jnp.mean(grad * grad, axis=1, keepdims=True)
        block[r] = rel[4 * core + r] - grad * (learn_rate / jnp.sqrt(total))
        totals.append(total)
    copy = pltpu.make_async_copy(block, new_rel.at[pl.ds(4 * core, 4)], sem)
    copy.start()
    rows = jnp.concatenate(totals + totals, axis=1).T
    if len(rest) == 6:
        first = jnp.concatenate([held[...], held[...]], axis=0)
        mixed = jnp.concatenate([rows[0:4], first[0:4]], axis=0)
        turned = jnp.concatenate([first[0:4], rows[0:4]], axis=0)
        new_accum[...] = jnp.where(core == 0, mixed, turned)
    else:
        new_accum[...] = rows
    copy.wait()


def update_half(place, relations, rel_accum, grads, before=None):
    given = (place, relations, rel_accum, grads) + (before or ())
    specs = [SMEM, VMEM, VMEM, VMEM] + ([ANY, VMEM] if before else [])
    return pl.pallas_call(
        update_kernel,
        out_shape=(shape((8, 256, 256), f32), shape((8, 256), f32)),
        in_specs=specs,
        out_specs=(ANY, VMEM),
        scratch_shapes=[pltpu.VMEM((4, 256, 256), f32), pltpu.SemaphoreType.DMA],
        input_output_aliases={4: 0} if before else {},
        compiler_params=pltpu.CompilerParams(vmem_limit_bytes=62 * 1024 * 1024),
        cost_estimate=pl.CostEstimate(flops=0, bytes_accessed=3_000_000, transcendentals=0),
    )(*given)


def body(
    embeddings, row_accum, relations, rel_accum, matching, src_rows, dst_rows, rel_ids, neg_rows
):
    place = jnp.stack([lax.axis_index(name) for name in ("core", "zhi", "x")]).astype(jnp.int32)
    line = lambda v: v.reshape(1, 512)
    block = shape((1024, 256), bf16)
    pieces, pack = call(
        first_kernel,
        (shape((64, 8, 128), bf16), shape((272, 256), bf16)),
        0,
        (embeddings, line(src_rows), line(rel_ids), line(dst_rows), line(neg_rows)),
        moved=800_000,
        far=(0, 1, 2, 3, 4),
        space=62,
        scratch=[
            pltpu.VMEM((256, 256), f32),
            pltpu.VMEM((4, 1, 512), jnp.int32),
            pltpu.SemaphoreType.DMA((5,)),
        ],
    )
    arrived = spread(pieces, DOM)
    near = jnp.concatenate([pack, lax.ppermute(pack, "x", [(i, i ^ 1) for i in range(4)])], axis=0)
    near, arrived = lax.optimization_barrier((near, arrived))
    routed = call(take_kernel, shape((64, 2, 8, 128), bf16), 1, (matching, arrived), moved=400_000)
    rows_in = spread(routed.reshape(128, 8, 128), DOM_Z).reshape(64, 2, 8, 128)
    away = lax.ppermute(near, "x", [(i, i ^ 2) for i in range(4)])
    held = [pltpu.VMEM((1024, 256), bf16)] * 2
    counts0, known0, trans0, source0, rel_b = call(
        trans_kernel,
        (shape((8, 512), f32), shape((8, 512), f32), block, block, shape((8, 256, 256), bf16)),
        1,
        (place, near, relations),
        flops=1_300_000_000,
        moved=6_000_000,
        far_outs=(2, 3, 4),
        scratch=held + [pltpu.VMEM((8, 256, 256), bf16), pltpu.SemaphoreType.DMA((3,))],
        space=62,
    )
    counts1, known1, trans1, source1 = call(
        trans_kernel,
        (shape((8, 512), f32), shape((8, 512), f32), block, block),
        1,
        (place, away, relations),
        flops=1_300_000_000,
        moved=5_000_000,
        far_outs=(2, 3),
        scratch=held + [pltpu.SemaphoreType.DMA((2,))],
        space=62,
    )
    weight, g_trans, kept, given = call(
        score_kernel,
        (shape((2048, 512), bf16), shape((2048, 256), bf16), block, block),
        1,
        (place, rows_in, counts0, counts1, known0, known1, trans0, trans1, source0, source1),
        flops=3_200_000_000,
        moved=6_000_000,
        far=(6, 7, 8, 9),
        scratch=[
            pltpu.VMEM((512, 256), bf16),
            pltpu.VMEM((2048, 256), bf16),
            pltpu.VMEM((2048, 256), bf16),
            pltpu.SemaphoreType.DMA((4,)),
        ],
        space=56,
    )
    came = swap(given, "core")
    mine, theirs, own = call(
        back_kernel,
        (shape((256, 256), f32), shape((256, 256), bf16), shape((4, 256, 256), bf16)),
        1,
        (place, weight, g_trans, known0, known1, trans0, trans1, rel_b),
        flops=3_000_000_000,
        moved=6_000_000,
        far=(5, 6, 7),
        scratch=[
            pltpu.VMEM((2048, 256), bf16),
            pltpu.VMEM((8, 256, 256), bf16),
            pltpu.SemaphoreType.DMA((3,)),
        ],
        space=56,
    )
    rows_came = swap(theirs, "zhi")
    joined = call(join_kernel, shape((4, 512, 256), bf16), 0, (own, kept, came), moved=2_000_000)
    got = spread(joined, "x")
    out, own_here = call(
        pieces_kernel,
        (shape((64, 2, 8, 128), bf16), shape((256, 256), f32)),
        0,
        (got, mine, rows_came),
        moved=2_000_000,
    )
    mid = spread(out.reshape(128, 8, 128), DOM_Z).reshape(64, 2, 8, 128)
    routed_back = call(
        route_kernel, shape((64, 2, 8, 128), bf16), 2, (place, matching, mid), moved=512_000
    )
    last = spread(routed_back.reshape(128, 8, 128), DOM_Z).reshape(64, 2, 8, 128)
    rel_four = spread(
        call(rel_kernel, shape((4, 256, 256), bf16), 0, (last,), moved=512_000), "x"
    )
    new_embeddings, new_row_accum = call(
        rows_kernel,
        (shape((256, 256), f32), shape((1, 256), f32)),
        0,
        (embeddings, row_accum.reshape(1, 256), own_here, last),
        flops=1_000_000,
        moved=1_000_000,
    )
    new_embeddings, rel_four = lax.optimization_barrier((new_embeddings, rel_four))
    rel_rest = swap(rel_four, "core")
    half = update_half(place, relations, rel_accum, rel_four)
    new_relations, new_rel_accum = update_half(place, relations, rel_accum, rel_rest, half)
    return new_embeddings, new_row_accum.reshape(256), new_relations, new_rel_accum


def solution(mesh):
    fine = Mesh(mesh.devices.reshape(4, 8, 2, 2, 4), AXES)
    placed = (
        P(AXES, None),
        P(AXES),
        P(),
        P(),
        P(),
        P(AXES),
        P(AXES),
        P(AXES),
        P(AXES, None),
    )
    return jax.shard_map(
        body,
        mesh=fine,
        in_specs=placed,
        out_specs=(P(AXES, None), P(AXES), P(), P()),
        check_vma=False,
    )
```

time: 177 us -> 181 us (1.023)
  blocking collectives: 83 us -> 48.3 us
  Pallas kernels: 26.6 us -> 45.1 us
  waiting for transfers between devices: 6.23 us -> 23.4 us
  starting transfers between devices: 49.7 us -> 56.2 us
  local copies, waits for them, and re-layouts: 10 us -> 3.9 us
    all_to_all x4 -> x2, blocking collectives: 83 us -> 48.3 us  [spread(): return lax.all_to_all(value, axis, split_axis=0, concat_axis=0, tiled=True)]
    all_to_all x2 -> x4, waiting for transfers between devices: 0.01 us -> 20 us  [spread(): return lax.all_to_all(value, axis, split_axis=0, concat_axis=0, tiled=True)]
    pallas_call x11, Pallas kernels: 21.2 us -> 36.8 us  [call(): pl.pallas_call(kernel, out_shape=outs, in_specs=specs, out_specs=tuple((A...]
    ppermute x2 -> x3, starting transfers between devices: 8.31 us -> 15.4 us  [swap(): return lax.ppermute(value, axis, [(0, 1), (1, 0)])]
    ppermute x3 -> x2, waiting for transfers between devices: 6.22 us -> 0.01 us  [the longest x1 0.01 us: body(): away = lax.ppermute(near, 'x', [(i, i ^ 2) for i in range(4)])]
    unnamed x36 -> x28, local copies, waits for them, and re-layouts: 10 us -> 3.9 us
    ppermute x2 -> x3, waiting for transfers between devices: 0.01 us -> 3.4 us  [swap(): return lax.ppermute(value, axis, [(0, 1), (1, 0)])]
    pallas_call x2, Pallas kernels: 5.38 us -> 8.3 us  [update_half(): pl.pallas_call(update_kernel, out_shape=(shape((8, 256, 256), f32), shape...]
  transfers between devices with their start and end apart: 7 -> 9, of which waited for: 3 -> 4; matrix products, arithmetic and copies ran while one was open for 0% -> 1% of each run, Pallas kernels for 8% -> 15%
where the time goes in v5:
time: 181 us; the launch traced here: 180 us
  starting transfers between devices  56.2 us (31%)
  blocking collectives  48.3 us (27%)
  Pallas kernels  45.1 us (25%)
  waiting for transfers between devices  23.4 us (13%)
  local copies, waits for them, and re-layouts  3.9 us (2%)
    all_to_all x2, blocking collectives, spread(): return lax.all_to_all(value, axis, split_axis=0, concat_axis=0, tiled=True)  48.3 us
    pallas_call x11, Pallas kernels, call(): pl.pallas_call(kernel, out_shape=outs, in_specs=specs, out_specs=tuple((A...  36.8 us
    all_to_all x4, starting transfers between devices, spread(): return lax.all_to_all(value, axis, split_axis=0, concat_axis=0, tiled=True)  32.5 us
    all_to_all x4, waiting for transfers between devices, spread(): return lax.all_to_all(value, axis, split_axis=0, concat_axis=0, tiled=True)  20 us
    ppermute x3, starting transfers between devices, swap(): return lax.ppermute(value, axis, [(0, 1), (1, 0)])  15.4 us
    pallas_call x2, Pallas kernels, update_half(): pl.pallas_call(update_kernel, out_shape=(shape((8, 256, 256), f32), shape...  8.3 us
    ppermute x1, starting transfers between devices, body(): away = lax.ppermute(near, 'x', [(i, i ^ 2) for i in range(4)])  4.36 us
    ppermute x1, starting transfers between devices, body(): lax.ppermute(pack, 'x', [(i, i ^ 1) for i in range(4)])  3.95 us
  transfers between devices with their start and end apart: 9, of which 4 were waited for; matrix products, arithmetic and copies ran while one was open for 1% of the time, Pallas kernels for 15%

profile of v5, /device:TPU:1, one launch (start us, length us, event | category | flops | bytes accessed | tf_op | source)
XLA Modules:
  0.0 179.7 jit_solution(5020656157725613743)
XLA Ops:
  0.6 1.7 shard_map.120
  2.4 3.9 %collective-permute-start = (bf16[272,256]{1,0:T(8,128)(2,1)}, bf16[272,256]{1,0:T(8,128)(2,1)S(1)}, u32[]{:S(2)}, u32[]{:S(2)}) collective-permute-start(bf16[272,256]{1,0:T(8,128)(2,1)} %get-tuple-element.34), channel_id=1, source_target_pairs={{0,1},{1,0},{2,3},{3,2},{4,5},{5,4},{6,7},{7,6},{8,9},{9,8},{10,11... | collective-permute-start | bytes 417800 | tf_op jit(solution)/shard_map/ppermute | solution.py:330
  6.3 14.0 %all-to-all-start = ((bf16[64,8,128]{2,1,0:T(8,128)(2,1)}), bf16[64,8,128]{2,1,0:T(8,128)(2,1)S(1)}, u32[]{:S(2)}, u32[]{:S(2)}) async-start(bf16[64,8,128]{2,1,0:T(8,128)(2,1)} %get-tuple-element.35), calls=%async_computation | async-start | bytes 262144 | tf_op jit(solution)/shard_map/all_to_all | solution.py:48
  20.4 0.0 collective-permute-done
  20.4 0.9 pad_maximum_fusion.packs
  21.3 0.0 copy-start.10
  21.3 9.1 %all-to-all-done.arrived = bf16[64,8,128]{2,1,0:T(8,128)(2,1)S(1)} async-done(((bf16[64,8,128]{2,1,0:T(8,128)(2,1)}), bf16[64,8,128]{2,1,0:T(8,128)(2,1)S(1)}, u32[]{:S(2)}, u32[]{:S(2)}) %all-to-all-start) | async-done | bytes 131104 | tf_op jit(solution)/shard_map/all_to_all | solution.py:48
  30.4 0.7 copy-done.5
  31.1 1.3 shard_map.121
  32.4 11.2 %all-to-all-start.1 = ((bf16[128,8,128]{2,1,0:T(8,128)(2,1)}), bf16[128,8,128]{2,1,0:T(8,128)(2,1)S(1)}, u32[]{:S(2)}, u32[]{:S(2)}) async-start(bf16[128,8,128]{2,1,0:T(8,128)(2,1)} %bitcast.7), calls=%async_computation.1 | async-start | bytes 524288 | tf_op jit(solution)/shard_map/all_to_all | solution.py:48
  43.6 4.4 %collective-permute-start.1 = (bf16[544,256]{1,0:T(8,128)(2,1)S(1)}, bf16[544,256]{1,0:T(8,128)(2,1)S(1)}, u32[]{:S(2)}, u32[]{:S(2)}) collective-permute-start(bf16[544,256]{1,0:T(8,128)(2,1)S(1)} %pad_maximum_fusion.packs), channel_id=1, source_target_pairs={{0,2},{1,3},{2,0},{3,1},{4,6},{5,7},{6,4},{7,5},{8,10},{9,11},{10,... | collective-permute-start | bytes 835592 | tf_op jit(solution)/shard_map/ppermute | solution.py:334
  47.9 0.7 pad_add_fusion.place
  48.6 0.0 copy-done.10
  48.6 6.0 %shard_map.122 = (f32[8,512]{1,0:T(8,128)}, f32[8,512]{1,0:T(8,128)}, bf16[1024,256]{1,0:T(8,128)(2,1)}, bf16[1024,256]{1,0:T(8,128)(2,1)}, bf16[8,256,256]{2,1,0:T(8,128)(2,1)}) custom-call(s32[3]{0:T(128)} %pad_add_fusion.place, bf16[544,256]{1,0:T(8,128)(2,1)} %copy-done.10, f32[8,256,256]{2,1,0:T(8,128)} %rel.7), custom_call_target="tpu_custom_call" | custom-call | flops 1300000000 | bytes 6000000 | tf_op jit(solution)/shard_map/pallas_call | solution.py:32
  54.6 0.0 collective-permute-done.1.packs
  54.6 0.0 copy-start.12
  54.7 0.7 copy-done.12
  55.4 5.6 %shard_map.123 = (f32[8,512]{1,0:T(8,128)}, f32[8,512]{1,0:T(8,128)}, bf16[1024,256]{1,0:T(8,128)(2,1)}, bf16[1024,256]{1,0:T(8,128)(2,1)}) custom-call(s32[3]{0:T(128)} %pad_add_fusion.place, bf16[544,256]{1,0:T(8,128)(2,1)} %copy-done.12, f32[8,256,256]{2,1,0:T(8,128)} %rel.7), custom_call_target="tpu_custom_call" | custom-call | flops 1300000000 | bytes 5000000 | tf_op jit(solution)/shard_map/pallas_call | solution.py:32
  61.0 0.0 all-to-all-done.1
  61.0 0.0 copy-start.11
  61.0 0.7 copy-done.11
  61.7 7.7 %shard_map.124 = (bf16[2048,512]{1,0:T(8,128)(2,1)}, bf16[2048,256]{1,0:T(8,128)(2,1)}, bf16[1024,256]{1,0:T(8,128)(2,1)}, bf16[1024,256]{1,0:T(8,128)(2,1)}) custom-call(s32[3]{0:T(128)} %pad_add_fusion.place, bf16[64,2,8,128]{3,2,1,0:T(8,128)(2,1)} %bitcast.20, f32[8,512]{1,0:T(8,128)} %get-tuple-element.38.counts0, f32[8,512]{1,0:T(8,128)} %get-tuple-element.39.counts1, ...), custom_call_target="tpu_custom_call" | custom-call | flops 3200000000 | bytes 6000000 | tf_op jit(solution)/shard_map/pallas_call | solution.py:32
  69.4 3.5 %collective-permute-start.2 = (bf16[1024,256]{1,0:T(8,128)(2,1)}, bf16[1024,256]{1,0:T(8,128)(2,1)S(1)}, u32[]{:S(2)}, u32[]{:S(2)}) collective-permute-start(bf16[1024,256]{1,0:T(8,128)(2,1)} %get-tuple-element.51), channel_id=1, source_target_pairs={{0,8},{8,0},{1,9},{9,1},{2,10},{10,2},{3,11},{11,3},{4,12},{12,4},... | collective-permute-start | bytes 1572872 | tf_op jit(solution)/shard_map/ppermute | solution.py:44
  72.9 10.5 %shard_map.125 = (f32[256,256]{1,0:T(8,128)}, bf16[256,256]{1,0:T(8,128)(2,1)}, bf16[4,256,256]{2,1,0:T(8,128)(2,1)}) custom-call(s32[3]{0:T(128)} %pad_add_fusion.place, bf16[2048,512]{1,0:T(8,128)(2,1)} %get-tuple-element.46.weight, bf16[2048,256]{1,0:T(8,128)(2,1)} %get-tuple-element.47.g_trans, f32[8,512]{1,0:T(8,128)} %get-tuple-element.40.known0, ...), custom_call_target="tpu_custom_call" | custom-call | flops 3000000000 | bytes 6000000 | tf_op jit(solution)/shard_map/pallas_call | solution.py:32
  83.5 0.0 collective-permute-done.2.came
  83.5 1.0 copy-done.2
  84.5 1.1 shard_map.126
  85.6 3.8 %all-to-all-start.2 = ((bf16[4,512,256]{2,1,0:T(8,128)(2,1)}), bf16[4,512,256]{2,1,0:T(8,128)(2,1)S(1)}, u32[]{:S(2)}, u32[]{:S(2)}) async-start(bf16[4,512,256]{2,1,0:T(8,128)(2,1)} %shard_map.126), calls=%async_computation.2 | async-start | bytes 2097152 | tf_op jit(solution)/shard_map/all_to_all | solution.py:48
  89.5 7.2 %collective-permute-start.3 = (bf16[256,256]{1,0:T(8,128)(2,1)S(1)}, bf16[256,256]{1,0:T(8,128)(2,1)S(1)}, u32[]{:S(2)}, u32[]{:S(2)}) collective-permute-start(bf16[256,256]{1,0:T(8,128)(2,1)S(1)} %copy-done.13), channel_id=1, source_target_pairs={{0,4},{4,0},{1,5},{5,1},{2,6},{6,2},{3,7},{7,3},{8,12},{12,8},{9,1... | collective-permute-start | bytes 393224 | tf_op jit(solution)/shard_map/ppermute | solution.py:44
  96.7 3.4 %collective-permute-done.3.came = bf16[256,256]{1,0:T(8,128)(2,1)S(1)} collective-permute-done((bf16[256,256]{1,0:T(8,128)(2,1)S(1)}, bf16[256,256]{1,0:T(8,128)(2,1)S(1)}, u32[]{:S(2)}, u32[]{:S(2)}) %collective-permute-start.3) | collective-permute-done | bytes 131104 | tf_op jit(solution)/shard_map/ppermute | solution.py:44
  100.1 4.3 %all-to-all-done.2.got = bf16[4,512,256]{2,1,0:T(8,128)(2,1)S(1)} async-done(((bf16[4,512,256]{2,1,0:T(8,128)(2,1)}), bf16[4,512,256]{2,1,0:T(8,128)(2,1)S(1)}, u32[]{:S(2)}, u32[]{:S(2)}) %all-to-all-start.2) | async-done | bytes 1048608 | tf_op jit(solution)/shard_map/all_to_all | solution.py:48
  104.4 0.2 shard_map.127
  104.6 28.0 %all_to_all.30 = bf16[128,8,128]{2,1,0:T(8,128)(2,1)S(1)} all-to-all(bf16[128,8,128]{2,1,0:T(8,128)(2,1)S(1)} %bitcast.18), channel_id=1, replica_groups=mesh['zlo'=4,'y'=8,'core'=2,'zhi'=2,'x'=4] {'zlo','y','core','zhi'}, dimensions={0} | all-to-all | bytes 524288 | tf_op jit(solution)/shard_map/all_to_all | solution.py:48
  132.6 0.0 copy-done.6
  132.6 0.8 shard_map.128
  133.4 20.3 %all_to_all.31 = bf16[128,8,128]{2,1,0:T(8,128)(2,1)S(1)} all-to-all(bf16[128,8,128]{2,1,0:T(8,128)(2,1)S(1)} %bitcast.17), channel_id=1, replica_groups=mesh['zlo'=4,'y'=8,'core'=2,'zhi'=2,'x'=4] {'zlo','y','core','zhi'}, dimensions={0} | all-to-all | bytes 524288 | tf_op jit(solution)/shard_map/all_to_all | solution.py:48
  153.7 0.9 shard_map.130
  154.6 3.5 %all-to-all-start.5 = ((bf16[4,256,256]{2,1,0:T(8,128)(2,1)}), bf16[4,256,256]{2,1,0:T(8,128)(2,1)S(1)}, u32[]{:S(2)}, u32[]{:S(2)}) async-start(bf16[4,256,256]{2,1,0:T(8,128)(2,1)} %shard_map.130), calls=%async_computation.5 | async-start | bytes 1048576 | tf_op jit(solution)/shard_map/all_to_all | solution.py:48
  158.1 0.0 copy-done
  158.1 0.0 copy-done.7
  158.1 1.0 shard_map.129
  159.1 6.6 %all-to-all-done.5.grads = bf16[4,256,256]{2,1,0:T(8,128)(2,1)S(1)} async-done(((bf16[4,256,256]{2,1,0:T(8,128)(2,1)}), bf16[4,256,256]{2,1,0:T(8,128)(2,1)S(1)}, u32[]{:S(2)}, u32[]{:S(2)}) %all-to-all-start.5) | async-done | bytes 524320 | tf_op jit(solution)/shard_map/all_to_all | solution.py:48
  165.7 4.7 %collective-permute-start.4 = (bf16[4,256,256]{2,1,0:T(8,128)(2,1)S(1)}, bf16[4,256,256]{2,1,0:T(8,128)(2,1)S(1)}, u32[]{:S(2)}, u32[]{:S(2)}) collective-permute-start(bf16[4,256,256]{2,1,0:T(8,128)(2,1)S(1)} %all-to-all-done.5.grads), channel_id=1, source_target_pairs={{0,8},{8,0},{1,9},{9,1},{2,10},{10,2},{3,11},{11,3},{4,12},{12,4},... | collective-permute-start | bytes 1572872 | tf_op jit(solution)/shard_map/ppermute | solution.py:44
  170.4 4.2 %shard_map.131 = (f32[8,256,256]{2,1,0:T(8,128)}, f32[8,256]{1,0:T(8,128)}) custom-call(s32[3]{0:T(128)} %pad_add_fusion.place, f32[8,256,256]{2,1,0:T(8,128)} %rel.7, f32[8,256]{1,0:T(8,128)} %accum.3, bf16[4,256,256]{2,1,0:T(8,128)(2,1)} %copy-done.8), custom_call_target="tpu_custom_call" | custom-call | bytes 3000000 | tf_op jit(solution)/shard_map/pallas_call | solution.py:297
  174.6 0.0 collective-permute-done.4.grads
  174.6 0.0 copy-start.9
  174.6 0.8 copy-done.9
  175.4 4.1 %shard_map.132 = (f32[8,256,256]{2,1,0:T(8,128)}, f32[8,256]{1,0:T(8,128)}) custom-call(s32[3]{0:T(128)} %pad_add_fusion.place, f32[8,256,256]{2,1,0:T(8,128)} %rel.7, f32[8,256]{1,0:T(8,128)} %accum.3, bf16[4,256,256]{2,1,0:T(8,128)(2,1)} %copy-done.9, f32[8,256,256]{2,1,0:T(8,128)} %get-tuple-element.60.rest_0_, ...), custom_call_target="tpu_custom_call", output_to_operand_aliasing={{0}: (4, {})} | custom-call | bytes 3000000 | tf_op jit(solution)/shard_map/pallas_call | solution.py:297
  (15 shorter events, 0.0 us)
Async XLA Ops:
  2.4 18.0 %collective-permute-start = (bf16[272,256]{1,0:T(8,128)(2,1)}, bf16[272,256]{1,0:T(8,128)(2,1)S(1)}, u32[]{:S(2)}, u32[]{:S(2)}) collective-permute-start(bf16[272,256]{1,0:T(8,128)(2,1)} %get-tuple-element.34), channel_id=1, source_target_pairs={{0,1},{1,0},{2,3},{3,2},{4,5},{5,4},{6,7},{7,6},{8,9},{9,8},{10,11... | collective-permute-start | bytes 417800 | tf_op jit(solution)/shard_map/ppermute | solution.py:330
  6.3 24.1 %all-to-all-start = ((bf16[64,8,128]{2,1,0:T(8,128)(2,1)}), bf16[64,8,128]{2,1,0:T(8,128)(2,1)S(1)}, u32[]{:S(2)}, u32[]{:S(2)}) async-start(bf16[64,8,128]{2,1,0:T(8,128)(2,1)} %get-tuple-element.35), calls=%async_computation | async-start | bytes 262144 | tf_op jit(solution)/shard_map/all_to_all | solution.py:48
  21.3 27.3 %copy-start.10 = (bf16[544,256]{1,0:T(8,128)(2,1)}, bf16[544,256]{1,0:T(8,128)(2,1)S(1)}, u32[]{:S(2)}) copy-start(bf16[544,256]{1,0:T(8,128)(2,1)S(1)} %pad_maximum_fusion.packs) | copy-start | bytes 835588
  30.4 0.7 copy-start.5
  32.4 28.6 %all-to-all-start.1 = ((bf16[128,8,128]{2,1,0:T(8,128)(2,1)}), bf16[128,8,128]{2,1,0:T(8,128)(2,1)S(1)}, u32[]{:S(2)}, u32[]{:S(2)}) async-start(bf16[128,8,128]{2,1,0:T(8,128)(2,1)} %bitcast.7), calls=%async_computation.1 | async-start | bytes 524288 | tf_op jit(solution)/shard_map/all_to_all | solution.py:48
  43.6 11.1 %collective-permute-start.1 = (bf16[544,256]{1,0:T(8,128)(2,1)S(1)}, bf16[544,256]{1,0:T(8,128)(2,1)S(1)}, u32[]{:S(2)}, u32[]{:S(2)}) collective-permute-start(bf16[544,256]{1,0:T(8,128)(2,1)S(1)} %pad_maximum_fusion.packs), channel_id=1, source_target_pairs={{0,2},{1,3},{2,0},{3,1},{4,6},{5,7},{6,4},{7,5},{8,10},{9,11},{10,... | collective-permute-start | bytes 835592 | tf_op jit(solution)/shard_map/ppermute | solution.py:334
  54.6 0.7 copy-start.12
  61.0 0.7 copy-start.11
  69.4 14.1 %collective-permute-start.2 = (bf16[1024,256]{1,0:T(8,128)(2,1)}, bf16[1024,256]{1,0:T(8,128)(2,1)S(1)}, u32[]{:S(2)}, u32[]{:S(2)}) collective-permute-start(bf16[1024,256]{1,0:T(8,128)(2,1)} %get-tuple-element.51), channel_id=1, source_target_pairs={{0,8},{8,0},{1,9},{9,1},{2,10},{10,2},{3,11},{11,3},{4,12},{12,4},... | collective-permute-start | bytes 1572872 | tf_op jit(solution)/shard_map/ppermute | solution.py:44
  72.9 10.6 %copy-start.1 = (bf16[1024,256]{1,0:T(8,128)(2,1)S(1)}, bf16[1024,256]{1,0:T(8,128)(2,1)}, u32[]{:S(2)}) copy-start(bf16[1024,256]{1,0:T(8,128)(2,1)} %get-tuple-element.50.kept) | copy-start | bytes 1572868
  83.5 1.0 copy-start.2
  84.5 5.0 %copy-start.13 = (bf16[256,256]{1,0:T(8,128)(2,1)S(1)}, bf16[256,256]{1,0:T(8,128)(2,1)}, u32[]{:S(2)}) copy-start(bf16[256,256]{1,0:T(8,128)(2,1)} %get-tuple-element.53) | copy-start | bytes 393220
  84.5 19.9 %copy-start.3 = (f32[256,256]{1,0:T(8,128)S(1)}, f32[256,256]{1,0:T(8,128)}, u32[]{:S(2)}) copy-start(f32[256,256]{1,0:T(8,128)} %get-tuple-element.52.mine) | copy-start | bytes 786436
  85.6 47.0 %copy-start.4 = (s32[3]{0:T(128)S(1)}, s32[3]{0:T(128)}, u32[]{:S(2)}) copy-start(s32[3]{0:T(128)} %pad_add_fusion.place) | copy-start | bytes 40
  85.6 47.0 %copy-start.6 = (s32[64]{0:T(128)S(1)}, s32[64]{0:T(128)}, u32[]{:S(2)}) copy-start(s32[64]{0:T(128)} %matching.3) | copy-start | bytes 772
  85.6 18.8 %all-to-all-start.2 = ((bf16[4,512,256]{2,1,0:T(8,128)(2,1)}), bf16[4,512,256]{2,1,0:T(8,128)(2,1)S(1)}, u32[]{:S(2)}, u32[]{:S(2)}) async-start(bf16[4,512,256]{2,1,0:T(8,128)(2,1)} %shard_map.126), calls=%async_computation.2 | async-start | bytes 2097152 | tf_op jit(solution)/shard_map/all_to_all | solution.py:48
  89.5 10.6 %collective-permute-start.3 = (bf16[256,256]{1,0:T(8,128)(2,1)S(1)}, bf16[256,256]{1,0:T(8,128)(2,1)S(1)}, u32[]{:S(2)}, u32[]{:S(2)}) collective-permute-start(bf16[256,256]{1,0:T(8,128)(2,1)S(1)} %copy-done.13), channel_id=1, source_target_pairs={{0,4},{4,0},{1,5},{5,1},{2,6},{6,2},{3,7},{7,3},{8,12},{12,8},{9,1... | collective-permute-start | bytes 393224 | tf_op jit(solution)/shard_map/ppermute | solution.py:44
  104.4 53.7 %copy-start = (f32[256,256]{1,0:T(8,128)S(1)}, f32[256,256]{1,0:T(8,128)}, u32[]{:S(2)}) copy-start(f32[256,256]{1,0:T(8,128)} %emb.3) | copy-start | bytes 786436
  104.4 53.7 %copy-start.7 = (f32[256]{0:T(256)S(1)}, f32[256]{0:T(256)}, u32[]{:S(2)}) copy-start(f32[256]{0:T(256)} %param.10) | copy-start | bytes 3076
  154.6 11.1 %all-to-all-start.5 = ((bf16[4,256,256]{2,1,0:T(8,128)(2,1)}), bf16[4,256,256]{2,1,0:T(8,128)(2,1)S(1)}, u32[]{:S(2)}, u32[]{:S(2)}) async-start(bf16[4,256,256]{2,1,0:T(8,128)(2,1)} %shard_map.130), calls=%async_computation.5 | async-start | bytes 1048576 | tf_op jit(solution)/shard_map/all_to_all | solution.py:48
  165.7 4.7 %copy-start.8 = (bf16[4,256,256]{2,1,0:T(8,128)(2,1)}, bf16[4,256,256]{2,1,0:T(8,128)(2,1)S(1)}, u32[]{:S(2)}) copy-start(bf16[4,256,256]{2,1,0:T(8,128)(2,1)S(1)} %all-to-all-done.5.grads) | copy-start | bytes 1572868
  165.7 8.9 %collective-permute-start.4 = (bf16[4,256,256]{2,1,0:T(8,128)(2,1)S(1)}, bf16[4,256,256]{2,1,0:T(8,128)(2,1)S(1)}, u32[]{:S(2)}, u32[]{:S(2)}) collective-permute-start(bf16[4,256,256]{2,1,0:T(8,128)(2,1)S(1)} %all-to-all-done.5.grads), channel_id=1, source_target_pairs={{0,8},{8,0},{1,9},{9,1},{2,10},{10,2},{3,11},{11,3},{4,12},{12,4},... | collective-permute-start | bytes 1572872 | tf_op jit(solution)/shard_map/ppermute | solution.py:44
  174.6 0.8 copy-start.9

commit v6 on v5

--- a/solution.py
+++ b/solution.py
@@ -98,15 +98,10 @@
     return jnp.concatenate(parts, axis=1)
 
 
-def trans_kernel(place, packs, rel, counts, known, *rest):
-    outs, (trans, source, *rel_b), sems = rest[: len(rest) // 2], rest[len(rest) // 2 : -1], rest[-1]
+def trans_kernel(place, packs, rel, counts, known, trans, source, *rel_b):
     stack = jnp.concatenate([rel[r].astype(bf16) for r in range(8)], axis=1)
-    copies = []
-    if rel_b:
-        for r in range(8):
-            rel_b[0][r] = rel[r].astype(bf16)
-        copies.append(pltpu.make_async_copy(rel_b[0], outs[2], sems.at[2]))
-        copies[-1].start()
+    for r in range(8) if rel_b else ():
+        rel_b[0][r] = rel[r].astype(bf16)
     ids = lane_ids(512, 256).astype(f32)
     wide = row_ids(place[2], 512)
     for s in range(2):
@@ -120,24 +115,12 @@
         hits = (column[:, 3:4] == wide).astype(f32)
         counts[s : s + 1, :] = jnp.sum(hits, axis=0, keepdims=True)
     counts[2:8, :] = jnp.zeros((6, 512), f32)
-    for k, held in enumerate((trans, source)):
-        copies.append(pltpu.make_async_copy(held, outs[k], sems.at[k]))
-        copies[-1].start()
-    for copy in copies:
-        copy.wait()
 
 
 def score_kernel(
     place, rows_in, counts0, counts1, known0, known1, trans0, trans1, source0, source1,
-    weight, g_trans, kept, given, rows, trans, source, sems
+    weight, g_trans, kept, given, rows
 ):
-    copies = []
-    for k, (part, held) in enumerate(
-        ((trans0, trans), (trans1, trans), (source0, source), (source1, source))
-    ):
-        span = pl.ds((k % 2) * 1024, 1024)
-        copies.append(pltpu.make_async_copy(part, held.at[span, :], sems.at[k]))
-        copies[-1].start()
     core = place[0]
     for z in range(2):
         both = rows_in[:, z].reshape(2, 256, 128)
@@ -145,12 +128,11 @@
     index = [known[s * 4 : (s + 1) * 4, :] for known in (known0, known1) for s in range(2)]
     ids = row_ids(place[2], 256)
     for b in range(8):
-        if b % 4 == 0:
-            copies[b // 4].wait()
         s = b // 2
         column = columns(index[s])[(b % 2) * 256 : (b % 2 + 1) * 256]
+        trans = (trans0, trans1)[b // 4][(b % 4) * 256 : (b % 4 + 1) * 256, :]
         span = slice(b * 256, (b + 1) * 256)
-        score = dot(trans[span, :], rows[...], NT)
+        score = dot(trans, rows[...], NT)
         sig = 1.0 / (1.0 + jnp.exp(-score))
         count = (counts0, counts1)[s // 2][s % 2 : s % 2 + 1, :]
         hit = column[:, 2:3] == ids
@@ -159,90 +141,76 @@
         g_trans[span, :] = dot(part, rows[...]).astype(bf16)
     turned = g_trans[...].astype(f32).T
     kinds = jnp.concatenate([part[1:2] for part in index], axis=1)
-    copies[2].wait()
-    copies[3].wait()
+    source = jnp.concatenate([source0[...], source1[...]], axis=0)
     for r in range(8):
         wanted = r + 4 * core if r < 4 else r - 4 * core
         masked = jnp.where(kinds == wanted.astype(f32), turned, 0.0).astype(bf16)
-        grad = dot(masked, source[...]).astype(bf16)
+        grad = dot(masked, source).astype(bf16)
         if r < 4:
-            kept[r * 256 : (r + 1) * 256, :] = grad
+            kept[r] = grad
         else:
-            given[(r - 4) * 256 : (r - 3) * 256, :] = grad
-
-
-def back_kernel(
-    place, weight, g_trans, known0, known1, trans0, trans1, rel_in, mine, theirs, own,
-    trans, rel_b, sems
-):
-    copies = [pltpu.make_async_copy(rel_in, rel_b, sems.at[2])]
-    for k, part in enumerate((trans0, trans1)):
-        span = pl.ds(k * 1024, 1024)
-        copies.append(pltpu.make_async_copy(part, trans.at[span, :], sems.at[k]))
-    for copy in copies:
-        copy.start()
+            given[r - 4] = grad
+
+
+def partner_kernel(weight, trans0, trans1, g_rows):
+    turned = jnp.concatenate([t[...].astype(f32).T.astype(bf16) for t in (trans0, trans1)], axis=1)
+    for z in range(2):
+        g_rows[z] = dot(turned, weight[:, z * 256 : (z + 1) * 256]).T.astype(bf16)
+
+
+def own_kernel(g_trans, known0, known1, rel_b, own0, *others):
     sub_ids = lax.broadcasted_iota(jnp.int32, (256, 512), 0).astype(f32)
-    copies[0].wait()
     stack = rel_b[...].reshape(2048, 256)
     for s in range(4):
         index = (known0, known1)[s // 2][(s % 2) * 4 : (s % 2 + 1) * 4, :]
         grad = g_trans[s * 512 : (s + 1) * 512, :].astype(f32)
         total = dot(by_relation(columns(index)[:, 1:2], grad), stack)
         hot = (index[0:1, :] == sub_ids).astype(f32).astype(bf16)
-        own[place[2] ^ s] = dot(hot, total.astype(bf16)).astype(bf16)
-    copies[1].wait()
-    copies[2].wait()
-    turned = trans[...].astype(f32).T.astype(bf16)
-    near = dot(turned, weight[:, 0:256]).T
-    far = dot(turned, weight[:, 256:512]).T
-    mine[...] = jnp.where(place[1] == 0, near, far)
-    theirs[...] = jnp.where(place[1] == 0, far, near).astype(bf16)
-
-
-def join_kernel(own, kept, came, out):
+        mine = dot(hot, total.astype(bf16))
+        if s == 0:
+            own0[...] = mine
+        else:
+            others[s - 1][...] = mine.astype(bf16)
+
+
+def join_kernel(kept, came, out):
     for k in range(4):
-        out[k, 0:256, :] = own[k]
-        span = slice(k * 256, (k + 1) * 256)
-        out[k, 256:512, :] = (kept[span, :].astype(f32) + came[span, :].astype(f32)).astype(bf16)
-
-
-def upper(tiles):
-    return lax.broadcasted_iota(jnp.int32, tiles, len(tiles) - 2) % 8 < 4
-
-
-def pieces_kernel(got, mine, came, out, own_here):
-    first = upper((32, 8, 128))
+        out[k] = (kept[k].astype(f32) + came[k].astype(f32)).astype(bf16)
+
+
+def pieces_kernel(got, g_rows, out):
     for h in range(2):
         half = slice(h * 128, (h + 1) * 128)
-        total = got[0, :, half].astype(f32)
+        rel = got[0, :, half].astype(f32)
         for k in range(1, 4):
-            total = total + got[k, :, half].astype(f32)
-        own_here[:, half] = total[0:256]
-        rel = total[256:512].reshape(32, 8, 128)
-        rows = (mine[:, half] + came[:, half].astype(f32)).reshape(32, 8, 128)
-        span = slice(h * 32, (h + 1) * 32)
-        out[span, 0] = jnp.where(first, rows, rel).astype(bf16)
-        out[span, 1] = jnp.where(first, rel, rows).astype(bf16)
-
-
-def route_kernel(place, matching, mid, out):
-    rel = [jnp.zeros((8, 128), f32), jnp.zeros((8, 128), f32)]
+            rel = rel + got[k, :, half].astype(f32)
+        for p, part in enumerate((g_rows[0, :, half].astype(f32), g_rows[1, :, half].astype(f32), rel)):
+            tiles = part.reshape(32, 8, 128)
+            for z in range(2):
+                out[h * 32 : (h + 1) * 32, z, p] = tiles[:, z * 4 : (z + 1) * 4].astype(bf16)
+
+
+def route_kernel(matching, mid, out):
+    rel = [jnp.zeros((4, 128), f32), jnp.zeros((4, 128), f32)]
     for d in range(64):
-        rel[d % 2] = rel[d % 2] + (mid[d, 0].astype(f32) + mid[d, 1].astype(f32))
-    near = upper((8, 128)) == (place[1] == 0)
+        rel[d % 2] = rel[d % 2] + (mid[d, 0, 2].astype(f32) + mid[d, 1, 2].astype(f32))
     for d in range(64):
         target = matching[d]
-        tail = jnp.where(target % 2 == 0, rel[0], rel[1])
+        tail = jnp.where(target % 2 == 0, rel[0], rel[1]).astype(bf16)
         for z in range(2):
-            out[target, z] = jnp.where(near, mid[d, z].astype(f32), tail).astype(bf16)
+            out[target, z, 0] = (mid[d, 0, z].astype(f32) + mid[d, 1, z].astype(f32)).astype(bf16)
+            out[target, z, 1] = tail
+
+
+def whole(last, h, p):
+    span = slice(h * 32, (h + 1) * 32)
+    parts = [last[span, z, p].astype(f32) for z in range(2)]
+    return jnp.concatenate(parts, axis=1).reshape(256, 128)
 
 
 def rel_kernel(last, out):
-    first = upper((32, 8, 128))
     for h in range(2):
-        even = last[h * 32 : (h + 1) * 32, 0].astype(f32)
-        odd = last[h * 32 : (h + 1) * 32, 1].astype(f32)
-        part = jnp.where(first, odd, even).reshape(256, 128).astype(bf16)
+        part = whole(last, h, 1).astype(bf16)
         for k in range(4):
             out[k, :, h * 128 : (h + 1) * 128] = part
 
@@ -255,11 +223,10 @@
     return jnp.broadcast_to(row, (128, 256)).T[:, 0:1]
 
 
-def rows_kernel(emb, accum, own_here, last, new_emb, new_accum):
-    first = upper((64, 8, 128))
-    rows = jnp.where(first, last[:, 0].astype(f32), last[:, 1].astype(f32))
-    halves = [rows[h * 32 : (h + 1) * 32].reshape(256, 128) for h in range(2)]
-    grad = own_here[...] + jnp.concatenate(halves, axis=1)
+def rows_kernel(emb, accum, own0, own1, own2, own3, last, new_emb, new_accum):
+    grad = own0[...] + jnp.concatenate([whole(last, 0, 0), whole(last, 1, 0)], axis=1)
+    for own in (own1, own2, own3):
+        grad = grad + own[...].astype(f32)
     total = to_column(accum[...]) + jnp.mean(grad * grad, axis=1, keepdims=True)
     new_emb[...] = emb[...] - grad * (learn_rate / jnp.sqrt(total))
     new_accum[...] = to_row(total)
@@ -301,7 +268,7 @@
         out_specs=(ANY, VMEM),
         scratch_shapes=[pltpu.VMEM((4, 256, 256), f32), pltpu.SemaphoreType.DMA],
         input_output_aliases={4: 0} if before else {},
-        compiler_params=pltpu.CompilerParams(vmem_limit_bytes=62 * 1024 * 1024),
+        compiler_params=pltpu.CompilerParams(vmem_limit_bytes=8 * 1024 * 1024),
         cost_estimate=pl.CostEstimate(flops=0, bytes_accessed=3_000_000, transcendentals=0),
     )(*given)
 
@@ -328,11 +295,6 @@
     )
     arrived = spread(pieces, DOM)
     near = jnp.concatenate([pack, lax.ppermute(pack, "x", [(i, i ^ 1) for i in range(4)])], axis=0)
-    near, arrived = lax.optimization_barrier((near, arrived))
-    routed = call(take_kernel, shape((64, 2, 8, 128), bf16), 1, (matching, arrived), moved=400_000)
-    rows_in = spread(routed.reshape(128, 8, 128), DOM_Z).reshape(64, 2, 8, 128)
-    away = lax.ppermute(near, "x", [(i, i ^ 2) for i in range(4)])
-    held = [pltpu.VMEM((1024, 256), bf16)] * 2
     counts0, known0, trans0, source0, rel_b = call(
         trans_kernel,
         (shape((8, 512), f32), shape((8, 512), f32), block, block, shape((8, 256, 256), bf16)),
@@ -340,10 +302,12 @@
         (place, near, relations),
         flops=1_300_000_000,
         moved=6_000_000,
-        far_outs=(2, 3, 4),
-        scratch=held + [pltpu.VMEM((8, 256, 256), bf16), pltpu.SemaphoreType.DMA((3,))],
-        space=62,
-    )
+        space=16,
+    )
+    trans0, arrived = lax.optimization_barrier((trans0, arrived))
+    routed = call(take_kernel, shape((64, 2, 8, 128), bf16), 1, (matching, arrived), moved=400_000)
+    rows_in = spread(routed.reshape(128, 8, 128), DOM_Z).reshape(64, 2, 8, 128)
+    away = lax.ppermute(near, "x", [(i, i ^ 2) for i in range(4)])
     counts1, known1, trans1, source1 = call(
         trans_kernel,
         (shape((8, 512), f32), shape((8, 512), f32), block, block),
@@ -351,65 +315,64 @@
         (place, away, relations),
         flops=1_300_000_000,
         moved=5_000_000,
-        far_outs=(2, 3),
-        scratch=held + [pltpu.SemaphoreType.DMA((2,))],
-        space=62,
-    )
+        space=16,
+    )
+    four = shape((4, 256, 256), bf16)
     weight, g_trans, kept, given = call(
         score_kernel,
-        (shape((2048, 512), bf16), shape((2048, 256), bf16), block, block),
+        (shape((2048, 512), bf16), shape((2048, 256), bf16), four, four),
         1,
         (place, rows_in, counts0, counts1, known0, known1, trans0, trans1, source0, source1),
         flops=3_200_000_000,
         moved=6_000_000,
-        far=(6, 7, 8, 9),
-        scratch=[
-            pltpu.VMEM((512, 256), bf16),
-            pltpu.VMEM((2048, 256), bf16),
-            pltpu.VMEM((2048, 256), bf16),
-            pltpu.SemaphoreType.DMA((4,)),
-        ],
-        space=56,
+        scratch=[pltpu.VMEM((512, 256), bf16)],
+        space=20,
     )
     came = swap(given, "core")
-    mine, theirs, own = call(
-        back_kernel,
-        (shape((256, 256), f32), shape((256, 256), bf16), shape((4, 256, 256), bf16)),
+    g_rows = call(
+        partner_kernel,
+        shape((2, 256, 256), bf16),
+        0,
+        (weight, trans0, trans1),
+        flops=1_500_000_000,
+        moved=4_000_000,
+        space=16,
+    )
+    came, g_rows = lax.optimization_barrier((came, g_rows))
+    got = spread(call(join_kernel, four, 0, (kept, came), moved=1_500_000), "x")
+    one = shape((256, 256), bf16)
+    own0, *others = call(
+        own_kernel,
+        (shape((256, 256), f32), one, one, one),
+        0,
+        (g_trans, known0, known1, rel_b),
+        flops=3_000_000_000,
+        moved=4_000_000,
+        space=16,
+    )
+    *others, got = lax.optimization_barrier((*others, got))
+    others = [
+        lax.ppermute(part, "x", [(i, i ^ k) for i in range(4)]) for k, part in enumerate(others, 1)
+    ]
+    out = call(
+        pieces_kernel, shape((64, 2, 3, 4, 128), bf16), 0, (got, g_rows), moved=2_000_000
+    )
+    mid = spread(out.reshape(128, 3, 4, 128), DOM_Z)
+    *others, mid = lax.optimization_barrier((*others, mid))
+    routed_back = call(
+        route_kernel,
+        shape((64, 2, 2, 4, 128), bf16),
         1,
-        (place, weight, g_trans, known0, known1, trans0, trans1, rel_b),
-        flops=3_000_000_000,
-        moved=6_000_000,
-        far=(5, 6, 7),
-        scratch=[
-            pltpu.VMEM((2048, 256), bf16),
-            pltpu.VMEM((8, 256, 256), bf16),
-            pltpu.SemaphoreType.DMA((3,)),
-        ],
-        space=56,
-    )
-    rows_came = swap(theirs, "zhi")
-    joined = call(join_kernel, shape((4, 512, 256), bf16), 0, (own, kept, came), moved=2_000_000)
-    got = spread(joined, "x")
-    out, own_here = call(
-        pieces_kernel,
-        (shape((64, 2, 8, 128), bf16), shape((256, 256), f32)),
-        0,
-        (got, mine, rows_came),
-        moved=2_000_000,
-    )
-    mid = spread(out.reshape(128, 8, 128), DOM_Z).reshape(64, 2, 8, 128)
-    routed_back = call(
-        route_kernel, shape((64, 2, 8, 128), bf16), 2, (place, matching, mid), moved=512_000
-    )
-    last = spread(routed_back.reshape(128, 8, 128), DOM_Z).reshape(64, 2, 8, 128)
-    rel_four = spread(
-        call(rel_kernel, shape((4, 256, 256), bf16), 0, (last,), moved=512_000), "x"
-    )
+        (matching, mid.reshape(64, 2, 3, 4, 128)),
+        moved=512_000,
+    )
+    last = spread(routed_back.reshape(128, 2, 4, 128), DOM_Z).reshape(64, 2, 2, 4, 128)
+    rel_four = spread(call(rel_kernel, four, 0, (last,), moved=512_000), "x")
     new_embeddings, new_row_accum = call(
         rows_kernel,
         (shape((256, 256), f32), shape((1, 256), f32)),
         0,
-        (embeddings, row_accum.reshape(1, 256), own_here, last),
+        (embeddings, row_accum.reshape(1, 256), own0, *others, last),
         flops=1_000_000,
         moved=1_000_000,
     )

time: 181 us -> 173 us (0.956)
  starting transfers between devices: 56.2 us -> 77.7 us
  blocking collectives: 48.3 us -> 27.3 us
  Pallas kernels: 45.1 us -> 30 us
  local copies, waits for them, and re-layouts: 3.9 us -> 15.4 us
  waiting for transfers between devices: 23.4 us -> 20.1 us
    all_to_all x2 -> x1, blocking collectives: 48.3 us -> 27.3 us  [spread(): return lax.all_to_all(value, axis, split_axis=0, concat_axis=0, tiled=True)]
    all_to_all x4 -> x5, starting transfers between devices: 32.5 us -> 51.8 us  [spread(): return lax.all_to_all(value, axis, split_axis=0, concat_axis=0, tiled=True)]
    all_to_all x4 -> x5, waiting for transfers between devices: 20 us -> 5.47 us  [spread(): return lax.all_to_all(value, axis, split_axis=0, concat_axis=0, tiled=True)]
    pallas_call x11 -> x12, Pallas kernels: 36.8 us -> 24.6 us  [call(): pl.pallas_call(kernel, out_shape=outs, in_specs=specs, out_specs=tuple((A...]
    unnamed x28 -> x53, local copies, waits for them, and re-layouts: 3.9 us -> 15.4 us
    ppermute x0 -> x3, starting transfers between devices: none -> 9.58 us  [body(): lax.ppermute(part, 'x', [(i, i ^ k) for i in range(4)])]
    ppermute x3 -> x2, starting transfers between devices: 15.4 us -> 8.6 us  [swap(): return lax.ppermute(value, axis, [(0, 1), (1, 0)])]
    ppermute x1, waiting for transfers between devices: 0.01 us -> 6.01 us  [body(): away = lax.ppermute(near, 'x', [(i, i ^ 2) for i in range(4)])]
  transfers between devices with their start and end apart: 9 -> 12, of which waited for: 4 -> 7; matrix products, arithmetic and copies ran while one was open for 1% -> 1% of each run, Pallas kernels for 15% -> 9%
where the time goes in v6:
time: 173 us; the launch traced here: 172 us
  starting transfers between devices  77.7 us (45%)
  Pallas kernels  30 us (17%)
  blocking collectives  27.3 us (16%)
  waiting for transfers between devices  20.1 us (12%)
  local copies, waits for them, and re-layouts  15.4 us (9%)
    all_to_all x5, starting transfers between devices, spread(): return lax.all_to_all(value, axis, split_axis=0, concat_axis=0, tiled=True)  51.8 us
    all_to_all x1, blocking collectives, spread(): return lax.all_to_all(value, axis, split_axis=0, concat_axis=0, tiled=True)  27.3 us
    pallas_call x12, Pallas kernels, call(): pl.pallas_call(kernel, out_shape=outs, in_specs=specs, out_specs=tuple((A...  24.6 us
    unnamed x53, local copies, waits for them, and re-layouts  15.4 us
    ppermute x3, starting transfers between devices, body(): lax.ppermute(part, 'x', [(i, i ^ k) for i in range(4)])  9.58 us
    ppermute x2, starting transfers between devices, swap(): return lax.ppermute(value, axis, [(0, 1), (1, 0)])  8.6 us
    ppermute x1, waiting for transfers between devices, body(): away = lax.ppermute(near, 'x', [(i, i ^ 2) for i in range(4)])  6.01 us
    all_to_all x5, waiting for transfers between devices, spread(): return lax.all_to_all(value, axis, split_axis=0, concat_axis=0, tiled=True)  5.47 us
  transfers between devices with their start and end apart: 12, of which 7 were waited for; matrix products, arithmetic and copies ran while one was open for 1% of the time, Pallas kernels for 9%

profile of v6, /device:TPU:1, one launch (start us, length us, event | category | flops | bytes accessed | tf_op | source)
XLA Modules:
  0.0 171.7 jit_solution(10607459094633172519)
XLA Ops:
  0.6 1.7 %shard_map.120 = (bf16[64,8,128]{2,1,0:T(8,128)(2,1)}, bf16[272,256]{1,0:T(8,128)(2,1)}) custom-call(f32[256,256]{1,0:T(8,128)} %emb.3, s32[1,512]{1,0:T(1,128)} %bitcast.20, s32[1,512]{1,0:T(1,128)} %bitcast.21, s32[1,512]{1,0:T(1,128)} %bitcast.22, s32[1,512]{1,0:T(1,128)} %neg.1), custom_call_target="tpu_custom_call" | custom-call | bytes 800000 | tf_op jit(solution)/shard_map/pallas_call | solution.py:32
  2.4 14.6 %all-to-all-start = ((bf16[64,8,128]{2,1,0:T(8,128)(2,1)}), bf16[64,8,128]{2,1,0:T(8,128)(2,1)S(1)}, u32[]{:S(2)}, u32[]{:S(2)}) async-start(bf16[64,8,128]{2,1,0:T(8,128)(2,1)} %get-tuple-element.45), calls=%async_computation | async-start | bytes 262144 | tf_op jit(solution)/shard_map/all_to_all | solution.py:48
  17.0 3.1 %collective-permute-start = (bf16[272,256]{1,0:T(8,128)(2,1)}, bf16[272,256]{1,0:T(8,128)(2,1)S(1)}, u32[]{:S(2)}, u32[]{:S(2)}) collective-permute-start(bf16[272,256]{1,0:T(8,128)(2,1)} %get-tuple-element.43), channel_id=1, source_target_pairs={{0,1},{1,0},{2,3},{3,2},{4,5},{5,4},{6,7},{7,6},{8,9},{9,8},{10,11... | collective-permute-start | bytes 417800 | tf_op jit(solution)/shard_map/ppermute | solution.py:297
  20.1 0.9 constant_dynamic-update-slice_fusion.1
  21.1 2.8 %collective-permute-done = bf16[272,256]{1,0:T(8,128)(2,1)S(1)} collective-permute-done((bf16[272,256]{1,0:T(8,128)(2,1)}, bf16[272,256]{1,0:T(8,128)(2,1)S(1)}, u32[]{:S(2)}, u32[]{:S(2)}) %collective-permute-start) | collective-permute-done | bytes 139296 | tf_op jit(solution)/shard_map/ppermute | solution.py:297
  23.9 1.6 copy-done
  25.5 2.8 %shard_map.121 = (f32[8,512]{1,0:T(8,128)S(1)}, f32[8,512]{1,0:T(8,128)S(1)}, bf16[1024,256]{1,0:T(8,128)(2,1)S(1)}, bf16[1024,256]{1,0:T(8,128)(2,1)S(1)}, bf16[8,256,256]{2,1,0:T(8,128)(2,1)S(1)}) custom-call(s32[3]{0:T(128)S(1)} %pad_add_fusion.place, bf16[544,256]{1,0:T(8,128)(2,1)S(1)} %constant_dynamic-update-slice_fusion.packs, f32[8,256,256]{2,1,0:T(8,128)S(1)} %copy-done), custom_call_target="tpu_custom_call" | custom-call | flops 1300000000 | bytes 6000000 | tf_op jit(solution)/shard_map/pallas_call | solution.py:32
  28.3 1.0 copy-done.12
  29.3 0.8 copy-done.16
  30.2 1.3 shard_map.122
  31.5 15.5 %all-to-all-start.1 = ((bf16[128,8,128]{2,1,0:T(8,128)(2,1)}), bf16[128,8,128]{2,1,0:T(8,128)(2,1)S(1)}, u32[]{:S(2)}, u32[]{:S(2)}) async-start(bf16[128,8,128]{2,1,0:T(8,128)(2,1)} %bitcast.7), calls=%async_computation.1 | async-start | bytes 524288 | tf_op jit(solution)/shard_map/all_to_all | solution.py:48
  47.0 4.7 %collective-permute-start.1 = (bf16[544,256]{1,0:T(8,128)(2,1)S(1)}, bf16[544,256]{1,0:T(8,128)(2,1)S(1)}, u32[]{:S(2)}, u32[]{:S(2)}) collective-permute-start(bf16[544,256]{1,0:T(8,128)(2,1)S(1)} %constant_dynamic-update-slice_fusion.packs), channel_id=1, source_target_pairs={{0,2},{1,3},{2,0},{3,1},{4,6},{5,7},{6,4},{7,5},{8,10},{9,11},{10,... | collective-permute-start | bytes 835592 | tf_op jit(solution)/shard_map/ppermute | solution.py:310
  51.6 6.0 %collective-permute-done.1.packs = bf16[544,256]{1,0:T(8,128)(2,1)S(1)} collective-permute-done((bf16[544,256]{1,0:T(8,128)(2,1)S(1)}, bf16[544,256]{1,0:T(8,128)(2,1)S(1)}, u32[]{:S(2)}, u32[]{:S(2)}) %collective-permute-start.1) | collective-permute-done | bytes 278560 | tf_op jit(solution)/shard_map/ppermute | solution.py:310
  57.6 2.9 %shard_map.123 = (f32[8,512]{1,0:T(8,128)S(1)}, f32[8,512]{1,0:T(8,128)S(1)}, bf16[1024,256]{1,0:T(8,128)(2,1)S(1)}, bf16[1024,256]{1,0:T(8,128)(2,1)S(1)}) custom-call(s32[3]{0:T(128)S(1)} %pad_add_fusion.place, bf16[544,256]{1,0:T(8,128)(2,1)S(1)} %collective-permute-done.1.packs, f32[8,256,256]{2,1,0:T(8,128)S(1)} %copy-done.1), custom_call_target="tpu_custom_call" | custom-call | flops 1300000000 | bytes 5000000 | tf_op jit(solution)/shard_map/pallas_call | solution.py:32
  60.5 0.8 copy-done.14
  61.3 0.8 copy-done.18
  62.1 1.0 copy-done.15
  63.2 1.0 copy-done.17
  64.2 1.0 copy-done.19
  65.2 5.0 %shard_map.124 = (bf16[2048,512]{1,0:T(8,128)(2,1)S(1)}, bf16[2048,256]{1,0:T(8,128)(2,1)S(1)}, bf16[4,256,256]{2,1,0:T(8,128)(2,1)S(1)}, bf16[4,256,256]{2,1,0:T(8,128)(2,1)S(1)}) custom-call(s32[3]{0:T(128)S(1)} %pad_add_fusion.place, bf16[64,2,8,128]{3,2,1,0:T(8,128)(2,1)S(1)} %bitcast.18, f32[8,512]{1,0:T(8,128)S(1)} %get-tuple-element.47.counts0, ...), custom_call_target="tpu_custom_call" | custom-call | flops 3200000000 | bytes 6000000 | tf_op jit(solution)/shard_map/pallas_call | solution.py:32
  70.2 3.9 %collective-permute-start.2 = (bf16[4,256,256]{2,1,0:T(8,128)(2,1)S(1)}, bf16[4,256,256]{2,1,0:T(8,128)(2,1)S(1)}, u32[]{:S(2)}, u32[]{:S(2)}) collective-permute-start(bf16[4,256,256]{2,1,0:T(8,128)(2,1)S(1)} %get-tuple-element.62), channel_id=1, source_target_pairs={{0,8},{8,0},{1,9},{9,1},{2,10},{10,2},{3,11},{11,3},{4,12},{12,4},... | collective-permute-start | bytes 1572872 | tf_op jit(solution)/shard_map/ppermute | solution.py:44
  74.1 0.9 shard_map.126.g_rows
  75.5 0.9 shard_map.127
  76.4 4.0 %all-to-all-start.2 = ((bf16[4,256,256]{2,1,0:T(8,128)(2,1)}), bf16[4,256,256]{2,1,0:T(8,128)(2,1)S(1)}, u32[]{:S(2)}, u32[]{:S(2)}) async-start(bf16[4,256,256]{2,1,0:T(8,128)(2,1)} %shard_map.127), calls=%async_computation.2 | async-start | bytes 1048576 | tf_op jit(solution)/shard_map/all_to_all | solution.py:48
  80.4 1.2 copy-done.13
  81.6 1.2 copy-done.21
  82.9 0.7 copy-done.23
  83.6 0.7 copy-done.25
  84.3 5.4 %shard_map.125 = (f32[256,256]{1,0:T(8,128)S(1)}, bf16[256,256]{1,0:T(8,128)(2,1)S(1)}, bf16[256,256]{1,0:T(8,128)(2,1)S(1)}, bf16[256,256]{1,0:T(8,128)(2,1)S(1)}) custom-call(bf16[2048,256]{1,0:T(8,128)(2,1)S(1)} %copy-done.21, f32[8,512]{1,0:T(8,128)S(1)} %copy-done.23, f32[8,512]{1,0:T(8,128)S(1)} %copy-done.25, bf16[8,256,256]{2,1,0:T(8,128)(2,1)S(1)} %copy-done.13), custom_call_target="tpu_custom_call" | custom-call | flops 3000000000 | bytes 4000000 | tf_op jit(solution)/shard_map/pallas_call | solution.py:32
  89.8 0.9 shard_map.128
  90.7 14.2 %all-to-all-start.3 = ((bf16[128,3,4,128]{3,2,1,0:T(4,128)(2,1)}), bf16[128,3,4,128]{3,2,1,0:T(4,128)(2,1)S(1)}, u32[]{:S(2)}, u32[]{:S(2)}) async-start(bf16[128,3,4,128]{3,2,1,0:T(4,128)(2,1)} %bitcast.9), calls=%async_computation.3 | async-start | bytes 786432 | tf_op jit(solution)/shard_map/all_to_all | solution.py:48
  104.9 3.2 %collective-permute-start.3 = (bf16[256,256]{1,0:T(8,128)(2,1)}, bf16[256,256]{1,0:T(8,128)(2,1)S(1)}, u32[]{:S(2)}, u32[]{:S(2)}) collective-permute-start(bf16[256,256]{1,0:T(8,128)(2,1)} %copy-done.11), channel_id=1, source_target_pairs={{0,1},{1,0},{2,3},{3,2},{4,5},{5,4},{6,7},{7,6},{8,9},{9,8},{10,11... | collective-permute-start | bytes 393224 | tf_op jit(solution)/shard_map/ppermute | solution.py:355
  108.1 4.3 %collective-permute-start.4 = (bf16[256,256]{1,0:T(8,128)(2,1)S(1)}, bf16[256,256]{1,0:T(8,128)(2,1)S(1)}, u32[]{:S(2)}, u32[]{:S(2)}) collective-permute-start(bf16[256,256]{1,0:T(8,128)(2,1)S(1)} %get-tuple-element.66), channel_id=1, source_target_pairs={{0,2},{1,3},{2,0},{3,1},{4,6},{5,7},{6,4},{7,5},{8,10},{9,11},{10,... | collective-permute-start | bytes 393224 | tf_op jit(solution)/shard_map/ppermute | solution.py:355
  112.5 2.0 %collective-permute-start.5 = (bf16[256,256]{1,0:T(8,128)(2,1)}, bf16[256,256]{1,0:T(8,128)(2,1)S(1)}, u32[]{:S(2)}, u32[]{:S(2)}) collective-permute-start(bf16[256,256]{1,0:T(8,128)(2,1)} %copy-done.10), channel_id=1, source_target_pairs={{0,3},{1,2},{2,1},{3,0},{4,7},{5,6},{6,5},{7,4},{8,11},{9,10},{10,... | collective-permute-start | bytes 393224 | tf_op jit(solution)/shard_map/ppermute | solution.py:355
  114.5 1.9 %collective-permute-done.4.own2 = bf16[256,256]{1,0:T(8,128)(2,1)S(1)} collective-permute-done((bf16[256,256]{1,0:T(8,128)(2,1)S(1)}, bf16[256,256]{1,0:T(8,128)(2,1)S(1)}, u32[]{:S(2)}, u32[]{:S(2)}) %collective-permute-start.4) | collective-permute-done | bytes 131104 | tf_op jit(solution)/shard_map/ppermute | solution.py:355
  116.4 3.5 %collective-permute-done.5.own3 = bf16[256,256]{1,0:T(8,128)(2,1)S(1)} collective-permute-done((bf16[256,256]{1,0:T(8,128)(2,1)}, bf16[256,256]{1,0:T(8,128)(2,1)S(1)}, u32[]{:S(2)}, u32[]{:S(2)}) %collective-permute-start.5) | collective-permute-done | bytes 131104 | tf_op jit(solution)/shard_map/ppermute | solution.py:355
  119.9 1.4 all-to-all-done.3
  121.3 0.8 shard_map.129
  122.1 27.3 %all_to_all.30 = bf16[128,2,4,128]{3,2,1,0:T(4,128)(2,1)S(1)} all-to-all(bf16[128,2,4,128]{3,2,1,0:T(4,128)(2,1)S(1)} %bitcast.17), channel_id=1, replica_groups=mesh['zlo'=4,'y'=8,'core'=2,'zhi'=2,'x'=4] {'zlo','y','core','zhi'}, dimensions={0} | all-to-all | bytes 524288 | tf_op jit(solution)/shard_map/all_to_all | solution.py:48
  149.4 0.9 shard_map.131
  150.3 3.5 %all-to-all-start.5 = ((bf16[4,256,256]{2,1,0:T(8,128)(2,1)}), bf16[4,256,256]{2,1,0:T(8,128)(2,1)S(1)}, u32[]{:S(2)}, u32[]{:S(2)}) async-start(bf16[4,256,256]{2,1,0:T(8,128)(2,1)} %shard_map.131), calls=%async_computation.5 | async-start | bytes 1048576 | tf_op jit(solution)/shard_map/all_to_all | solution.py:48
  153.8 0.9 copy-done.4
  154.7 0.9 copy-done.6
  156.3 1.0 shard_map.130
  157.3 4.1 %all-to-all-done.5.grads = bf16[4,256,256]{2,1,0:T(8,128)(2,1)S(1)} async-done(((bf16[4,256,256]{2,1,0:T(8,128)(2,1)}), bf16[4,256,256]{2,1,0:T(8,128)(2,1)S(1)}, u32[]{:S(2)}, u32[]{:S(2)}) %all-to-all-start.5) | async-done | bytes 524320 | tf_op jit(solution)/shard_map/all_to_all | solution.py:48
  161.3 4.7 %collective-permute-start.6 = (bf16[4,256,256]{2,1,0:T(8,128)(2,1)S(1)}, bf16[4,256,256]{2,1,0:T(8,128)(2,1)S(1)}, u32[]{:S(2)}, u32[]{:S(2)}) collective-permute-start(bf16[4,256,256]{2,1,0:T(8,128)(2,1)S(1)} %all-to-all-done.5.grads), channel_id=1, source_target_pairs={{0,8},{8,0},{1,9},{9,1},{2,10},{10,2},{3,11},{11,3},{4,12},{12,4},... | collective-permute-start | bytes 1572872 | tf_op jit(solution)/shard_map/ppermute | solution.py:44
  166.1 2.4 %shard_map.132 = (f32[8,256,256]{2,1,0:T(8,128)}, f32[8,256]{1,0:T(8,128)S(1)}) custom-call(s32[3]{0:T(128)S(1)} %pad_add_fusion.place, f32[8,256,256]{2,1,0:T(8,128)S(1)} %copy-done.1, f32[8,256]{1,0:T(8,128)S(1)} %copy-done.7, bf16[4,256,256]{2,1,0:T(8,128)(2,1)S(1)} %all-to-all-done.5.grads), custom_call_target="tpu_custom_call" | custom-call | bytes 3000000 | tf_op jit(solution)/shard_map/pallas_call | solution.py:264
  168.5 3.0 %shard_map.133 = (f32[8,256,256]{2,1,0:T(8,128)}, f32[8,256]{1,0:T(8,128)}) custom-call(s32[3]{0:T(128)S(1)} %pad_add_fusion.place, f32[8,256,256]{2,1,0:T(8,128)S(1)} %copy-done.1, f32[8,256]{1,0:T(8,128)S(1)} %copy-done.7, bf16[4,256,256]{2,1,0:T(8,128)(2,1)S(1)} %collective-permute-done.6.grads, ...), custom_call_target="tpu_custom_call", output_to_operand_aliasing={{0}: (4, {})} | custom-call | bytes 3000000 | tf_op jit(solution)/shard_map/pallas_call | solution.py:264
  (46 shorter events, 1.3 us)
Async XLA Ops:
  2.4 27.8 %all-to-all-start = ((bf16[64,8,128]{2,1,0:T(8,128)(2,1)}), bf16[64,8,128]{2,1,0:T(8,128)(2,1)S(1)}, u32[]{:S(2)}, u32[]{:S(2)}) async-start(bf16[64,8,128]{2,1,0:T(8,128)(2,1)} %get-tuple-element.45), calls=%async_computation | async-start | bytes 262144 | tf_op jit(solution)/shard_map/all_to_all | solution.py:48
  17.0 6.9 %collective-permute-start = (bf16[272,256]{1,0:T(8,128)(2,1)}, bf16[272,256]{1,0:T(8,128)(2,1)S(1)}, u32[]{:S(2)}, u32[]{:S(2)}) collective-permute-start(bf16[272,256]{1,0:T(8,128)(2,1)} %get-tuple-element.43), channel_id=1, source_target_pairs={{0,1},{1,0},{2,3},{3,2},{4,5},{5,4},{6,7},{7,6},{8,9},{9,8},{10,11... | collective-permute-start | bytes 417800 | tf_op jit(solution)/shard_map/ppermute | solution.py:297
  23.9 1.6 copy-start
  25.5 4.7 %copy-start.8 = (s32[64]{0:T(128)S(1)}, s32[64]{0:T(128)}, u32[]{:S(2)}) copy-start(s32[64]{0:T(128)} %matching.3) | copy-start | bytes 772
  25.5 32.2 %copy-start.1 = (f32[8,256,256]{2,1,0:T(8,128)S(1)}, f32[8,256,256]{2,1,0:T(8,128)}, u32[]{:S(2)}) copy-start(f32[8,256,256]{2,1,0:T(8,128)} %rel.7) | copy-start | bytes 6291460
  28.3 1.0 copy-start.12
  29.3 0.8 copy-start.16
  30.1 32.0 %copy-start.22 = (f32[8,512]{1,0:T(8,128)}, f32[8,512]{1,0:T(8,128)S(1)}, u32[]{:S(2)}) copy-start(f32[8,512]{1,0:T(8,128)S(1)} %get-tuple-element.49.known0) | copy-start | bytes 49156
  31.5 30.6 %all-to-all-start.1 = ((bf16[128,8,128]{2,1,0:T(8,128)(2,1)}), bf16[128,8,128]{2,1,0:T(8,128)(2,1)S(1)}, u32[]{:S(2)}, u32[]{:S(2)}) async-start(bf16[128,8,128]{2,1,0:T(8,128)(2,1)} %bitcast.7), calls=%async_computation.1 | async-start | bytes 524288 | tf_op jit(solution)/shard_map/all_to_all | solution.py:48
  47.0 10.7 %collective-permute-start.1 = (bf16[544,256]{1,0:T(8,128)(2,1)S(1)}, bf16[544,256]{1,0:T(8,128)(2,1)S(1)}, u32[]{:S(2)}, u32[]{:S(2)}) collective-permute-start(bf16[544,256]{1,0:T(8,128)(2,1)S(1)} %constant_dynamic-update-slice_fusion.packs), channel_id=1, source_target_pairs={{0,2},{1,3},{2,0},{3,1},{4,6},{5,7},{6,4},{7,5},{8,10},{9,11},{10,... | collective-permute-start | bytes 835592 | tf_op jit(solution)/shard_map/ppermute | solution.py:310
  60.5 0.8 copy-start.14
  61.3 0.8 copy-start.18
  62.1 8.1 %copy-start.24 = (f32[8,512]{1,0:T(8,128)}, f32[8,512]{1,0:T(8,128)S(1)}, u32[]{:S(2)}) copy-start(f32[8,512]{1,0:T(8,128)S(1)} %get-tuple-element.50.known1) | copy-start | bytes 49156
  62.1 1.0 copy-start.15
  63.2 1.0 copy-start.17
  64.2 1.0 copy-start.19
  70.2 4.8 %copy-start.20 = (bf16[2048,256]{1,0:T(8,128)(2,1)}, bf16[2048,256]{1,0:T(8,128)(2,1)S(1)}, u32[]{:S(2)}) copy-start(bf16[2048,256]{1,0:T(8,128)(2,1)S(1)} %get-tuple-element.55.g_trans) | copy-start | bytes 3145732
  70.2 5.2 %collective-permute-start.2 = (bf16[4,256,256]{2,1,0:T(8,128)(2,1)S(1)}, bf16[4,256,256]{2,1,0:T(8,128)(2,1)S(1)}, u32[]{:S(2)}, u32[]{:S(2)}) collective-permute-start(bf16[4,256,256]{2,1,0:T(8,128)(2,1)S(1)} %get-tuple-element.62), channel_id=1, source_target_pairs={{0,8},{8,0},{1,9},{9,1},{2,10},{10,2},{3,11},{11,3},{4,12},{12,4},... | collective-permute-start | bytes 1572872 | tf_op jit(solution)/shard_map/ppermute | solution.py:44
  76.4 13.4 %all-to-all-start.2 = ((bf16[4,256,256]{2,1,0:T(8,128)(2,1)}), bf16[4,256,256]{2,1,0:T(8,128)(2,1)S(1)}, u32[]{:S(2)}, u32[]{:S(2)}) async-start(bf16[4,256,256]{2,1,0:T(8,128)(2,1)} %shard_map.127), calls=%async_computation.2 | async-start | bytes 1048576 | tf_op jit(solution)/shard_map/all_to_all | solution.py:48
  80.4 1.2 copy-start.13
  81.6 1.2 copy-start.21
  82.9 0.7 copy-start.23
  83.6 0.7 copy-start.25
  89.7 0.9 copy-start.11
  89.8 0.9 copy-start.10
  90.7 63.1 %copy-start.2 = (f32[256,256]{1,0:T(8,128)S(1)}, f32[256,256]{1,0:T(8,128)}, u32[]{:S(2)}) copy-start(f32[256,256]{1,0:T(8,128)} %emb.3) | copy-start | bytes 786436
  90.7 30.6 %all-to-all-start.3 = ((bf16[128,3,4,128]{3,2,1,0:T(4,128)(2,1)}), bf16[128,3,4,128]{3,2,1,0:T(4,128)(2,1)S(1)}, u32[]{:S(2)}, u32[]{:S(2)}) async-start(bf16[128,3,4,128]{3,2,1,0:T(4,128)(2,1)} %bitcast.9), calls=%async_computation.3 | async-start | bytes 786432 | tf_op jit(solution)/shard_map/all_to_all | solution.py:48
  104.9 9.6 %collective-permute-start.3 = (bf16[256,256]{1,0:T(8,128)(2,1)}, bf16[256,256]{1,0:T(8,128)(2,1)S(1)}, u32[]{:S(2)}, u32[]{:S(2)}) collective-permute-start(bf16[256,256]{1,0:T(8,128)(2,1)} %copy-done.11), channel_id=1, source_target_pairs={{0,1},{1,0},{2,3},{3,2},{4,5},{5,4},{6,7},{7,6},{8,9},{9,8},{10,11... | collective-permute-start | bytes 393224 | tf_op jit(solution)/shard_map/ppermute | solution.py:355
  108.1 8.3 %collective-permute-start.4 = (bf16[256,256]{1,0:T(8,128)(2,1)S(1)}, bf16[256,256]{1,0:T(8,128)(2,1)S(1)}, u32[]{:S(2)}, u32[]{:S(2)}) collective-permute-start(bf16[256,256]{1,0:T(8,128)(2,1)S(1)} %get-tuple-element.66), channel_id=1, source_target_pairs={{0,2},{1,3},{2,0},{3,1},{4,6},{5,7},{6,4},{7,5},{8,10},{9,11},{10,... | collective-permute-start | bytes 393224 | tf_op jit(solution)/shard_map/ppermute | solution.py:355
  112.5 7.4 %collective-permute-start.5 = (bf16[256,256]{1,0:T(8,128)(2,1)}, bf16[256,256]{1,0:T(8,128)(2,1)S(1)}, u32[]{:S(2)}, u32[]{:S(2)}) collective-permute-start(bf16[256,256]{1,0:T(8,128)(2,1)} %copy-done.10), channel_id=1, source_target_pairs={{0,3},{1,2},{2,1},{3,0},{4,7},{5,6},{6,5},{7,4},{8,11},{9,10},{10,... | collective-permute-start | bytes 393224 | tf_op jit(solution)/shard_map/ppermute | solution.py:355
  116.4 33.9 %copy-start.3 = (bf16[256,256]{1,0:T(8,128)(2,1)}, bf16[256,256]{1,0:T(8,128)(2,1)S(1)}, u32[]{:S(2)}) copy-start(bf16[256,256]{1,0:T(8,128)(2,1)S(1)} %collective-permute-done.4.own2) | copy-start | bytes 393220
  119.9 30.4 %copy-start.5 = (bf16[256,256]{1,0:T(8,128)(2,1)}, bf16[256,256]{1,0:T(8,128)(2,1)S(1)}, u32[]{:S(2)}) copy-start(bf16[256,256]{1,0:T(8,128)(2,1)S(1)} %collective-permute-done.5.own3) | copy-start | bytes 393220
  121.3 44.8 %copy-start.7 = (f32[8,256]{1,0:T(8,128)S(1)}, f32[8,256]{1,0:T(8,128)}, u32[]{:S(2)}) copy-start(f32[8,256]{1,0:T(8,128)} %accum.3) | copy-start | bytes 24580
  150.3 11.1 %all-to-all-start.5 = ((bf16[4,256,256]{2,1,0:T(8,128)(2,1)}), bf16[4,256,256]{2,1,0:T(8,128)(2,1)S(1)}, u32[]{:S(2)}, u32[]{:S(2)}) async-start(bf16[4,256,256]{2,1,0:T(8,128)(2,1)} %shard_map.131), calls=%async_computation.5 | async-start | bytes 1048576 | tf_op jit(solution)/shard_map/all_to_all | solution.py:48
  153.8 0.9 copy-start.4
  154.7 0.9 copy-start.6
  155.6 0.7 copy-start.9
  161.3 7.1 %collective-permute-start.6 = (bf16[4,256,256]{2,1,0:T(8,128)(2,1)S(1)}, bf16[4,256,256]{2,1,0:T(8,128)(2,1)S(1)}, u32[]{:S(2)}, u32[]{:S(2)}) collective-permute-start(bf16[4,256,256]{2,1,0:T(8,128)(2,1)S(1)} %all-to-all-done.5.grads), channel_id=1, source_target_pairs={{0,8},{8,0},{1,9},{9,1},{2,10},{10,2},{3,11},{11,3},{4,12},{12,4},... | collective-permute-start | bytes 1572872 | tf_op jit(solution)/shard_map/ppermute | solution.py:44

commit v7 on v6

--- a/solution.py
+++ b/solution.py
@@ -60,8 +60,10 @@
     high = wide // 256
     low = (wide - high * 256).astype(f32)
     both = jnp.concatenate([high.astype(f32), low], axis=0)
-    pack[256:272, :] = jnp.concatenate([both[:, :256], both[:, 256:]], axis=0).astype(bf16)
-    pack[0:256, :] = rows[...].astype(bf16)
+    index_b = jnp.concatenate([both[:, :256], both[:, 256:]], axis=0).astype(bf16)
+    for k in range(4):
+        pack[k, 256:272, :] = index_b
+        pack[k, 0:256, :] = rows[...].astype(bf16)
     for h in range(2):
         half = rows[:, h * 128 : (h + 1) * 128]
         pieces[h * 32 : (h + 1) * 32] = half.reshape(32, 8, 128).astype(bf16)
@@ -98,73 +100,71 @@
     return jnp.concatenate(parts, axis=1)
 
 
-def trans_kernel(place, packs, rel, counts, known, trans, source, *rel_b):
+def trans_kernel(place, packs, rel, counts, known, trans, source, rel_b):
     stack = jnp.concatenate([rel[r].astype(bf16) for r in range(8)], axis=1)
-    for r in range(8) if rel_b else ():
-        rel_b[0][r] = rel[r].astype(bf16)
+    for r in range(8):
+        rel_b[r] = rel[r].astype(bf16)
     ids = lane_ids(512, 256).astype(f32)
     wide = row_ids(place[2], 512)
-    for s in range(2):
-        index = indices(packs[s * 272 + 256 : s * 272 + 272, :])
-        known[s * 4 : (s + 1) * 4, :] = index
+    for s in range(4):
+        index = indices(packs[s, 256:272, :])
+        known[s * 8 : (s + 1) * 8, :] = jnp.concatenate([index, index], axis=0)
         column = columns(index)
         hot = (column[:, 0:1] == ids).astype(f32).astype(bf16)
-        rows = dot(hot, packs[s * 272 : s * 272 + 256, :])
+        rows = dot(hot, packs[s, 0:256, :])
         source[s * 512 : (s + 1) * 512, :] = rows.astype(bf16)
         trans[s * 512 : (s + 1) * 512, :] = dot(by_relation(column[:, 1:2], rows), stack, NT).astype(bf16)
         hits = (column[:, 3:4] == wide).astype(f32)
         counts[s : s + 1, :] = jnp.sum(hits, axis=0, keepdims=True)
-    counts[2:8, :] = jnp.zeros((6, 512), f32)
+    counts[4:8, :] = jnp.zeros((4, 512), f32)
 
 
 def score_kernel(
-    place, rows_in, counts0, counts1, known0, known1, trans0, trans1, source0, source1,
-    weight, g_trans, kept, given, rows
+    place, rows_in, counts, known, trans, source, weight, g_trans, kept, given, rows
 ):
     core = place[0]
     for z in range(2):
         both = rows_in[:, z].reshape(2, 256, 128)
         rows[z * 256 : (z + 1) * 256, :] = jnp.concatenate([both[0], both[1]], axis=1)
-    index = [known[s * 4 : (s + 1) * 4, :] for known in (known0, known1) for s in range(2)]
+    index = [known[s * 8 : s * 8 + 4, :] for s in range(4)]
     ids = row_ids(place[2], 256)
     for b in range(8):
         s = b // 2
         column = columns(index[s])[(b % 2) * 256 : (b % 2 + 1) * 256]
-        trans = (trans0, trans1)[b // 4][(b % 4) * 256 : (b % 4 + 1) * 256, :]
         span = slice(b * 256, (b + 1) * 256)
-        score = dot(trans, rows[...], NT)
+        score = dot(trans[span, :], rows[...], NT)
         sig = 1.0 / (1.0 + jnp.exp(-score))
-        count = (counts0, counts1)[s // 2][s % 2 : s % 2 + 1, :]
+        count = counts[s : s + 1, :]
         hit = column[:, 2:3] == ids
         part = jnp.where(hit, (count + 1.0) * sig - 1.0, count * sig).astype(bf16)
         weight[span, :] = part
         g_trans[span, :] = dot(part, rows[...]).astype(bf16)
     turned = g_trans[...].astype(f32).T
     kinds = jnp.concatenate([part[1:2] for part in index], axis=1)
-    source = jnp.concatenate([source0[...], source1[...]], axis=0)
     for r in range(8):
         wanted = r + 4 * core if r < 4 else r - 4 * core
         masked = jnp.where(kinds == wanted.astype(f32), turned, 0.0).astype(bf16)
-        grad = dot(masked, source).astype(bf16)
+        grad = dot(masked, source[...]).astype(bf16)
         if r < 4:
             kept[r] = grad
         else:
             given[r - 4] = grad
 
 
-def partner_kernel(weight, trans0, trans1, g_rows):
-    turned = jnp.concatenate([t[...].astype(f32).T.astype(bf16) for t in (trans0, trans1)], axis=1)
+def partner_kernel(weight, trans, g_rows):
+    turned = trans[...].astype(f32).T.astype(bf16)
     for z in range(2):
         g_rows[z] = dot(turned, weight[:, z * 256 : (z + 1) * 256]).T.astype(bf16)
 
 
-def own_kernel(g_trans, known0, known1, rel_b, own0, *others):
+def own_kernel(place, g_trans, known, rel_b, own0, *others):
     sub_ids = lax.broadcasted_iota(jnp.int32, (256, 512), 0).astype(f32)
     stack = rel_b[...].reshape(2048, 256)
     for s in range(4):
-        index = (known0, known1)[s // 2][(s % 2) * 4 : (s % 2 + 1) * 4, :]
-        grad = g_trans[s * 512 : (s + 1) * 512, :].astype(f32)
-        total = dot(by_relation(columns(index)[:, 1:2], grad), stack)
+        span = place[2] ^ s
+        index = known[pl.ds(pl.multiple_of(span * 8, 8), 8), :]
+        grad = g_trans[pl.ds(pl.multiple_of(span * 512, 512), 512), :].astype(f32)
+        total = dot(by_relation(columns(index[0:4])[:, 1:2], grad), stack)
         hot = (index[0:1, :] == sub_ids).astype(f32).astype(bf16)
         mine = dot(hot, total.astype(bf16))
         if s == 0:
@@ -278,10 +278,9 @@
 ):
     place = jnp.stack([lax.axis_index(name) for name in ("core", "zhi", "x")]).astype(jnp.int32)
     line = lambda v: v.reshape(1, 512)
-    block = shape((1024, 256), bf16)
     pieces, pack = call(
         first_kernel,
-        (shape((64, 8, 128), bf16), shape((272, 256), bf16)),
+        (shape((64, 8, 128), bf16), shape((4, 272, 256), bf16)),
         0,
         (embeddings, line(src_rows), line(rel_ids), line(dst_rows), line(neg_rows)),
         moved=800_000,
@@ -294,27 +293,23 @@
         ],
     )
     arrived = spread(pieces, DOM)
-    near = jnp.concatenate([pack, lax.ppermute(pack, "x", [(i, i ^ 1) for i in range(4)])], axis=0)
-    counts0, known0, trans0, source0, rel_b = call(
+    packs = spread(pack, "x")
+    routed = call(take_kernel, shape((64, 2, 8, 128), bf16), 1, (matching, arrived), moved=400_000)
+    routed, packs = lax.optimization_barrier((routed, packs))
+    rows_in = spread(routed.reshape(128, 8, 128), DOM_Z).reshape(64, 2, 8, 128)
+    counts, known, trans, source, rel_b = call(
         trans_kernel,
-        (shape((8, 512), f32), shape((8, 512), f32), block, block, shape((8, 256, 256), bf16)),
+        (
+            shape((8, 512), f32),
+            shape((32, 512), f32),
+            shape((2048, 256), bf16),
+            shape((2048, 256), bf16),
+            shape((8, 256, 256), bf16),
+        ),
         1,
-        (place, near, relations),
-        flops=1_300_000_000,
+        (place, packs, relations),
+        flops=2_600_000_000,
         moved=6_000_000,
-        space=16,
-    )
-    trans0, arrived = lax.optimization_barrier((trans0, arrived))
-    routed = call(take_kernel, shape((64, 2, 8, 128), bf16), 1, (matching, arrived), moved=400_000)
-    rows_in = spread(routed.reshape(128, 8, 128), DOM_Z).reshape(64, 2, 8, 128)
-    away = lax.ppermute(near, "x", [(i, i ^ 2) for i in range(4)])
-    counts1, known1, trans1, source1 = call(
-        trans_kernel,
-        (shape((8, 512), f32), shape((8, 512), f32), block, block),
-        1,
-        (place, away, relations),
-        flops=1_300_000_000,
-        moved=5_000_000,
         space=16,
     )
     four = shape((4, 256, 256), bf16)
@@ -322,7 +317,7 @@
         score_kernel,
         (shape((2048, 512), bf16), shape((2048, 256), bf16), four, four),
         1,
-        (place, rows_in, counts0, counts1, known0, known1, trans0, trans1, source0, source1),
+        (place, rows_in, counts, known, trans, source),
         flops=3_200_000_000,
         moved=6_000_000,
         scratch=[pltpu.VMEM((512, 256), bf16)],
@@ -333,7 +328,7 @@
         partner_kernel,
         shape((2, 256, 256), bf16),
         0,
-        (weight, trans0, trans1),
+        (weight, trans),
         flops=1_500_000_000,
         moved=4_000_000,
         space=16,
@@ -344,16 +339,15 @@
     own0, *others = call(
         own_kernel,
         (shape((256, 256), f32), one, one, one),
-        0,
-        (g_trans, known0, known1, rel_b),
+        1,
+        (place, g_trans, known, rel_b),
         flops=3_000_000_000,
         moved=4_000_000,
         space=16,
     )
     *others, got = lax.optimization_barrier((*others, got))
-    others = [
-        lax.ppermute(part, "x", [(i, i ^ k) for i in range(4)]) for k, part in enumerate(others, 1)
-    ]
+    away = lambda part, k: lax.ppermute(part, "x", [(i, i ^ k) for i in range(4)])
+    others[0], others[1] = away(others[0], 1), away(others[1], 2)
     out = call(
         pieces_kernel, shape((64, 2, 3, 4, 128), bf16), 0, (got, g_rows), moved=2_000_000
     )
@@ -366,7 +360,9 @@
         (matching, mid.reshape(64, 2, 3, 4, 128)),
         moved=512_000,
     )
+    others[2] = away(others[2], 3)
     last = spread(routed_back.reshape(128, 2, 4, 128), DOM_Z).reshape(64, 2, 2, 4, 128)
+    others[2], last = lax.optimization_barrier((others[2], last))
     rel_four = spread(call(rel_kernel, four, 0, (last,), moved=512_000), "x")
     new_embeddings, new_row_accum = call(
         rows_kernel,

time: 173 us -> 166 us (0.960)
  starting transfers between devices: 77.7 us -> 58.5 us
  waiting for transfers between devices: 20.1 us -> 37.9 us
  local copies, waits for them, and re-layouts: 15.4 us -> 12.3 us
  blocking collectives: 27.3 us -> 24.8 us
    all_to_all x5 -> x6, waiting for transfers between devices: 5.47 us -> 29.5 us  [spread(): return lax.all_to_all(value, axis, split_axis=0, concat_axis=0, tiled=True)]
    all_to_all x5 -> x6, starting transfers between devices: 51.8 us -> 39.1 us  [spread(): return lax.all_to_all(value, axis, split_axis=0, concat_axis=0, tiled=True)]
    ppermute x2 -> x0, waiting for transfers between devices: 8.77 us -> none  [the longest x1 6.01 us: body(): away = lax.ppermute(near, 'x', [(i, i ^ 2) for i in range(4)])]
    ppermute x2 -> x0, starting transfers between devices: 7.77 us -> none  [the longest x1 4.65 us: body(): away = lax.ppermute(near, 'x', [(i, i ^ 2) for i in range(4)])]
    unnamed x53 -> x42, local copies, waits for them, and re-layouts: 15.4 us -> 12.3 us
    all_to_all x1, blocking collectives: 27.3 us -> 24.8 us  [spread(): return lax.all_to_all(value, axis, split_axis=0, concat_axis=0, tiled=True)]
    ppermute x3, waiting for transfers between devices: 5.37 us -> 7.82 us  [body(): lax.ppermute(part, 'x', [(i, i ^ k) for i in range(4)])]
    pallas_call x12 -> x11, Pallas kernels: 24.6 us -> 24.7 us  [call(): pl.pallas_call(kernel, out_shape=outs, in_specs=specs, out_specs=tuple((A...]
  transfers between devices with their start and end apart: 12 -> 11, of which waited for: 7 -> 8; matrix products, arithmetic and copies ran while one was open for 1% -> 0% of each run, Pallas kernels for 9% -> 10%
where the time goes in v7:
time: 166 us; the launch traced here: 165 us
  starting transfers between devices  58.5 us (35%)
  waiting for transfers between devices  37.9 us (23%)
  Pallas kernels  30.1 us (18%)
  blocking collectives  24.8 us (15%)
  local copies, waits for them, and re-layouts  12.3 us (7%)
    all_to_all x6, starting transfers between devices, spread(): return lax.all_to_all(value, axis, split_axis=0, concat_axis=0, tiled=True)  39.1 us
    all_to_all x6, waiting for transfers between devices, spread(): return lax.all_to_all(value, axis, split_axis=0, concat_axis=0, tiled=True)  29.5 us
    all_to_all x1, blocking collectives, spread(): return lax.all_to_all(value, axis, split_axis=0, concat_axis=0, tiled=True)  24.8 us
    pallas_call x11, Pallas kernels, call(): pl.pallas_call(kernel, out_shape=outs, in_specs=specs, out_specs=tuple((A...  24.7 us
    unnamed x42, local copies, waits for them, and re-layouts  12.3 us
    ppermute x3, starting transfers between devices, body(): lax.ppermute(part, 'x', [(i, i ^ k) for i in range(4)])  11.1 us
    ppermute x2, starting transfers between devices, swap(): return lax.ppermute(value, axis, [(0, 1), (1, 0)])  8.39 us
    ppermute x3, waiting for transfers between devices, body(): lax.ppermute(part, 'x', [(i, i ^ k) for i in range(4)])  7.82 us
  transfers between devices with their start and end apart: 11, of which 8 were waited for; matrix products, arithmetic and copies ran while one was open for 0% of the time, Pallas kernels for 10%

profile of v7, /device:TPU:1, one launch (start us, length us, event | category | flops | bytes accessed | tf_op | source)
XLA Modules:
  0.0 164.7 jit_solution(5763529496424317310)
XLA Ops:
  0.6 1.9 %shard_map.120 = (bf16[64,8,128]{2,1,0:T(8,128)(2,1)}, bf16[4,272,256]{2,1,0:T(8,128)(2,1)}) custom-call(f32[256,256]{1,0:T(8,128)} %emb.3, s32[1,512]{1,0:T(1,128)} %bitcast.19, s32[1,512]{1,0:T(1,128)} %bitcast.20, s32[1,512]{1,0:T(1,128)} %bitcast.21, s32[1,512]{1,0:T(1,128)} %neg.1), custom_call_target="tpu_custom_call" | custom-call | bytes 800000 | tf_op jit(solution)/shard_map/pallas_call | solution.py:32
  2.5 24.8 %all_to_all.35.arrived = bf16[64,8,128]{2,1,0:T(8,128)(2,1)S(1)} all-to-all(bf16[64,8,128]{2,1,0:T(8,128)(2,1)} %get-tuple-element.41), channel_id=1, replica_groups=mesh['zlo'=4,'y'=8,'core'=2,'zhi'=2,'x'=4] {'zlo','y','core'}, dimensions={0} | all-to-all | bytes 262144 | tf_op jit(solution)/shard_map/all_to_all | solution.py:48
  27.4 4.0 %all-to-all-start.1 = ((bf16[4,272,256]{2,1,0:T(8,128)(2,1)}), bf16[4,272,256]{2,1,0:T(8,128)(2,1)S(1)}, u32[]{:S(2)}, u32[]{:S(2)}) async-start(bf16[4,272,256]{2,1,0:T(8,128)(2,1)} %get-tuple-element.42), calls=%async_computation.1 | async-start | bytes 1114112 | tf_op jit(solution)/shard_map/all_to_all | solution.py:48
  31.4 0.7 copy-done.7
  32.0 1.3 shard_map.121
  33.3 7.3 %all-to-all-done.1.packs = bf16[4,272,256]{2,1,0:T(8,128)(2,1)S(1)} async-done(((bf16[4,272,256]{2,1,0:T(8,128)(2,1)}), bf16[4,272,256]{2,1,0:T(8,128)(2,1)S(1)}, u32[]{:S(2)}, u32[]{:S(2)}) %all-to-all-start.1) | async-done | bytes 557088 | tf_op jit(solution)/shard_map/all_to_all | solution.py:48
  40.6 12.3 %all-to-all-start.2 = ((bf16[128,8,128]{2,1,0:T(8,128)(2,1)}), bf16[128,8,128]{2,1,0:T(8,128)(2,1)S(1)}, u32[]{:S(2)}, u32[]{:S(2)}) async-start(bf16[128,8,128]{2,1,0:T(8,128)(2,1)} %bitcast.7), calls=%async_computation.2 | async-start | bytes 524288 | tf_op jit(solution)/shard_map/all_to_all | solution.py:48
  52.9 0.1 pad_add_fusion.place
  53.0 4.4 %shard_map.122 = (f32[8,512]{1,0:T(8,128)S(1)}, f32[32,512]{1,0:T(8,128)S(1)}, bf16[2048,256]{1,0:T(8,128)(2,1)S(1)}, bf16[2048,256]{1,0:T(8,128)(2,1)S(1)}, bf16[8,256,256]{2,1,0:T(8,128)(2,1)S(1)}) custom-call(s32[3]{0:T(128)S(1)} %pad_add_fusion.place, bf16[4,272,256]{2,1,0:T(8,128)(2,1)S(1)} %all-to-all-done.1.packs, f32[8,256,256]{2,1,0:T(8,128)S(1)} %copy-done), custom_call_target="tpu_custom_call" | custom-call | flops 2600000000 | bytes 6000000 | tf_op jit(solution)/shard_map/pallas_call | solution.py:32
  57.4 0.0 copy-start.13
  57.4 1.0 copy-done.13
  58.4 1.0 copy-done.15
  59.4 1.0 copy-done.17
  60.3 6.7 %all-to-all-done.2 = bf16[128,8,128]{2,1,0:T(8,128)(2,1)S(1)} async-done(((bf16[128,8,128]{2,1,0:T(8,128)(2,1)}), bf16[128,8,128]{2,1,0:T(8,128)(2,1)S(1)}, u32[]{:S(2)}, u32[]{:S(2)}) %all-to-all-start.2) | async-done | bytes 262176 | tf_op jit(solution)/shard_map/all_to_all | solution.py:48
  67.0 1.2 copy-done.14
  68.2 1.2 copy-done.18
  69.5 5.0 %shard_map.123 = (bf16[2048,512]{1,0:T(8,128)(2,1)S(1)}, bf16[2048,256]{1,0:T(8,128)(2,1)S(1)}, bf16[4,256,256]{2,1,0:T(8,128)(2,1)S(1)}, bf16[4,256,256]{2,1,0:T(8,128)(2,1)S(1)}) custom-call(s32[3]{0:T(128)S(1)} %pad_add_fusion.place, bf16[64,2,8,128]{3,2,1,0:T(8,128)(2,1)S(1)} %bitcast.17, f32[8,512]{1,0:T(8,128)S(1)} %get-tuple-element.45.counts, ...), custom_call_target="tpu_custom_call" | custom-call | flops 3200000000 | bytes 6000000 | tf_op jit(solution)/shard_map/pallas_call | solution.py:32
  74.4 3.5 %collective-permute-start = (bf16[4,256,256]{2,1,0:T(8,128)(2,1)S(1)}, bf16[4,256,256]{2,1,0:T(8,128)(2,1)S(1)}, u32[]{:S(2)}, u32[]{:S(2)}) collective-permute-start(bf16[4,256,256]{2,1,0:T(8,128)(2,1)S(1)} %get-tuple-element.56), channel_id=1, source_target_pairs={{0,8},{8,0},{1,9},{9,1},{2,10},{10,2},{3,11},{11,3},{4,12},{12,4},... | collective-permute-start | bytes 1572872 | tf_op jit(solution)/shard_map/ppermute | solution.py:44
  78.0 0.9 shard_map.125.g_rows
  78.8 0.6 collective-permute-done.came
  79.5 0.9 shard_map.126
  80.4 3.6 %all-to-all-start.3 = ((bf16[4,256,256]{2,1,0:T(8,128)(2,1)}), bf16[4,256,256]{2,1,0:T(8,128)(2,1)S(1)}, u32[]{:S(2)}, u32[]{:S(2)}) async-start(bf16[4,256,256]{2,1,0:T(8,128)(2,1)} %shard_map.126), calls=%async_computation.3 | async-start | bytes 1048576 | tf_op jit(solution)/shard_map/all_to_all | solution.py:48
  84.1 1.2 copy-done.16
  85.3 1.2 copy-done.20
  86.5 6.0 %shard_map.124 = (f32[256,256]{1,0:T(8,128)S(1)}, bf16[256,256]{1,0:T(8,128)(2,1)S(1)}, bf16[256,256]{1,0:T(8,128)(2,1)S(1)}, bf16[256,256]{1,0:T(8,128)(2,1)S(1)}) custom-call(s32[3]{0:T(128)S(1)} %pad_add_fusion.place, bf16[2048,256]{1,0:T(8,128)(2,1)S(1)} %copy-done.20, f32[32,512]{1,0:T(8,128)S(1)} %get-tuple-element.46.known, ...), custom_call_target="tpu_custom_call" | custom-call | flops 3000000000 | bytes 4000000 | tf_op jit(solution)/shard_map/pallas_call | solution.py:32
  92.6 0.6 copy-done.11
  93.2 0.6 copy-done.12
  93.9 0.9 shard_map.127
  94.8 5.7 %all-to-all-start.4 = ((bf16[128,3,4,128]{3,2,1,0:T(4,128)(2,1)}), bf16[128,3,4,128]{3,2,1,0:T(4,128)(2,1)S(1)}, u32[]{:S(2)}, u32[]{:S(2)}) async-start(bf16[128,3,4,128]{3,2,1,0:T(4,128)(2,1)} %bitcast.9), calls=%async_computation.4 | async-start | bytes 786432 | tf_op jit(solution)/shard_map/all_to_all | solution.py:48
  100.5 3.4 %collective-permute-start.1 = (bf16[256,256]{1,0:T(8,128)(2,1)}, bf16[256,256]{1,0:T(8,128)(2,1)S(1)}, u32[]{:S(2)}, u32[]{:S(2)}) collective-permute-start(bf16[256,256]{1,0:T(8,128)(2,1)} %copy-done.12), channel_id=1, source_target_pairs={{0,1},{1,0},{2,3},{3,2},{4,5},{5,4},{6,7},{7,6},{8,9},{9,8},{10,11... | collective-permute-start | bytes 393224 | tf_op jit(solution)/shard_map/ppermute | solution.py:349
  103.9 4.3 %collective-permute-start.2 = (bf16[256,256]{1,0:T(8,128)(2,1)}, bf16[256,256]{1,0:T(8,128)(2,1)S(1)}, u32[]{:S(2)}, u32[]{:S(2)}) collective-permute-start(bf16[256,256]{1,0:T(8,128)(2,1)} %copy-done.11), channel_id=1, source_target_pairs={{0,2},{1,3},{2,0},{3,1},{4,6},{5,7},{6,4},{7,5},{8,10},{9,11},{10,... | collective-permute-start | bytes 393224 | tf_op jit(solution)/shard_map/ppermute | solution.py:349
  108.2 3.8 %collective-permute-done.2.own2 = bf16[256,256]{1,0:T(8,128)(2,1)S(1)} collective-permute-done((bf16[256,256]{1,0:T(8,128)(2,1)}, bf16[256,256]{1,0:T(8,128)(2,1)S(1)}, u32[]{:S(2)}, u32[]{:S(2)}) %collective-permute-start.2) | collective-permute-done | bytes 131104 | tf_op jit(solution)/shard_map/ppermute | solution.py:349
  112.0 4.9 %all-to-all-done.4 = bf16[128,3,4,128]{3,2,1,0:T(4,128)(2,1)S(1)} async-done(((bf16[128,3,4,128]{3,2,1,0:T(4,128)(2,1)}), bf16[128,3,4,128]{3,2,1,0:T(4,128)(2,1)S(1)}, u32[]{:S(2)}, u32[]{:S(2)}) %all-to-all-start.4) | async-done | bytes 393248 | tf_op jit(solution)/shard_map/all_to_all | solution.py:48
  117.0 1.5 shard_map.128
  118.5 9.9 %all-to-all-start.5 = ((bf16[128,2,4,128]{3,2,1,0:T(4,128)(2,1)}), bf16[128,2,4,128]{3,2,1,0:T(4,128)(2,1)S(1)}, u32[]{:S(2)}, u32[]{:S(2)}) async-start(bf16[128,2,4,128]{3,2,1,0:T(4,128)(2,1)} %bitcast.11), calls=%async_computation.5 | async-start | bytes 524288 | tf_op jit(solution)/shard_map/all_to_all | solution.py:48
  128.4 3.4 %collective-permute-start.3 = (bf16[256,256]{1,0:T(8,128)(2,1)}, bf16[256,256]{1,0:T(8,128)(2,1)S(1)}, u32[]{:S(2)}, u32[]{:S(2)}) collective-permute-start(bf16[256,256]{1,0:T(8,128)(2,1)} %copy-done.10), channel_id=1, source_target_pairs={{0,3},{1,2},{2,1},{3,0},{4,7},{5,6},{6,5},{7,4},{8,11},{9,10},{10,... | collective-permute-start | bytes 393224 | tf_op jit(solution)/shard_map/ppermute | solution.py:349
  131.8 4.0 %collective-permute-done.3.own3 = bf16[256,256]{1,0:T(8,128)(2,1)S(1)} collective-permute-done((bf16[256,256]{1,0:T(8,128)(2,1)}, bf16[256,256]{1,0:T(8,128)(2,1)S(1)}, u32[]{:S(2)}, u32[]{:S(2)}) %collective-permute-start.3) | collective-permute-done | bytes 131104 | tf_op jit(solution)/shard_map/ppermute | solution.py:349
  135.8 6.7 %all-to-all-done.5 = bf16[128,2,4,128]{3,2,1,0:T(4,128)(2,1)S(1)} async-done(((bf16[128,2,4,128]{3,2,1,0:T(4,128)(2,1)}), bf16[128,2,4,128]{3,2,1,0:T(4,128)(2,1)S(1)}, u32[]{:S(2)}, u32[]{:S(2)}) %all-to-all-start.5) | async-done | bytes 262176 | tf_op jit(solution)/shard_map/all_to_all | solution.py:48
  142.5 0.9 shard_map.130
  143.4 3.5 %all-to-all-start.6 = ((bf16[4,256,256]{2,1,0:T(8,128)(2,1)}), bf16[4,256,256]{2,1,0:T(8,128)(2,1)S(1)}, u32[]{:S(2)}, u32[]{:S(2)}) async-start(bf16[4,256,256]{2,1,0:T(8,128)(2,1)} %shard_map.130), calls=%async_computation.6 | async-start | bytes 1048576 | tf_op jit(solution)/shard_map/all_to_all | solution.py:48
  146.9 0.9 copy-done.3
  147.8 0.9 copy-done.5
  148.7 0.7 copy-done.9
  149.3 1.0 shard_map.129
  150.4 3.9 %all-to-all-done.6.grads = bf16[4,256,256]{2,1,0:T(8,128)(2,1)S(1)} async-done(((bf16[4,256,256]{2,1,0:T(8,128)(2,1)}), bf16[4,256,256]{2,1,0:T(8,128)(2,1)S(1)}, u32[]{:S(2)}, u32[]{:S(2)}) %all-to-all-start.6) | async-done | bytes 524320 | tf_op jit(solution)/shard_map/all_to_all | solution.py:48
  154.2 4.9 %collective-permute-start.4 = (bf16[4,256,256]{2,1,0:T(8,128)(2,1)S(1)}, bf16[4,256,256]{2,1,0:T(8,128)(2,1)S(1)}, u32[]{:S(2)}, u32[]{:S(2)}) collective-permute-start(bf16[4,256,256]{2,1,0:T(8,128)(2,1)S(1)} %all-to-all-done.6.grads), channel_id=1, source_target_pairs={{0,8},{8,0},{1,9},{9,1},{2,10},{10,2},{3,11},{11,3},{4,12},{12,4},... | collective-permute-start | bytes 1572872 | tf_op jit(solution)/shard_map/ppermute | solution.py:44
  159.2 2.4 %shard_map.131 = (f32[8,256,256]{2,1,0:T(8,128)}, f32[8,256]{1,0:T(8,128)S(1)}) custom-call(s32[3]{0:T(128)S(1)} %pad_add_fusion.place, f32[8,256,256]{2,1,0:T(8,128)S(1)} %copy-done, f32[8,256]{1,0:T(8,128)S(1)} %copy-done.6, bf16[4,256,256]{2,1,0:T(8,128)(2,1)S(1)} %all-to-all-done.6.grads), custom_call_target="tpu_custom_call" | custom-call | bytes 3000000 | tf_op jit(solution)/shard_map/pallas_call | solution.py:264
  161.6 3.0 %shard_map.132 = (f32[8,256,256]{2,1,0:T(8,128)}, f32[8,256]{1,0:T(8,128)}) custom-call(s32[3]{0:T(128)S(1)} %pad_add_fusion.place, f32[8,256,256]{2,1,0:T(8,128)S(1)} %copy-done, f32[8,256]{1,0:T(8,128)S(1)} %copy-done.6, bf16[4,256,256]{2,1,0:T(8,128)(2,1)S(1)} %collective-permute-done.4.grads, ...), custom_call_target="tpu_custom_call", output_to_operand_aliasing={{0}: (4, {})} | custom-call | bytes 3000000 | tf_op jit(solution)/shard_map/pallas_call | solution.py:264
  (31 shorter events, 0.1 us)
Async XLA Ops:
  2.5 50.5 %copy-start = (f32[8,256,256]{2,1,0:T(8,128)S(1)}, f32[8,256,256]{2,1,0:T(8,128)}, u32[]{:S(2)}) copy-start(f32[8,256,256]{2,1,0:T(8,128)} %rel.5) | copy-start | bytes 6291460
  27.4 13.2 %all-to-all-start.1 = ((bf16[4,272,256]{2,1,0:T(8,128)(2,1)}), bf16[4,272,256]{2,1,0:T(8,128)(2,1)S(1)}, u32[]{:S(2)}, u32[]{:S(2)}) async-start(bf16[4,272,256]{2,1,0:T(8,128)(2,1)} %get-tuple-element.42), calls=%async_computation.1 | async-start | bytes 1114112 | tf_op jit(solution)/shard_map/all_to_all | solution.py:48
  31.4 0.7 copy-start.7
  40.6 26.4 %all-to-all-start.2 = ((bf16[128,8,128]{2,1,0:T(8,128)(2,1)}), bf16[128,8,128]{2,1,0:T(8,128)(2,1)S(1)}, u32[]{:S(2)}, u32[]{:S(2)}) async-start(bf16[128,8,128]{2,1,0:T(8,128)(2,1)} %bitcast.7), calls=%async_computation.2 | async-start | bytes 524288 | tf_op jit(solution)/shard_map/all_to_all | solution.py:48
  57.4 1.0 copy-start.13
  58.4 1.0 copy-start.15
  59.4 1.0 copy-start.17
  67.0 1.2 copy-start.14
  68.2 1.2 copy-start.18
  74.4 4.4 %copy-start.19 = (bf16[2048,256]{1,0:T(8,128)(2,1)}, bf16[2048,256]{1,0:T(8,128)(2,1)S(1)}, u32[]{:S(2)}) copy-start(bf16[2048,256]{1,0:T(8,128)(2,1)S(1)} %get-tuple-element.49.g_trans) | copy-start | bytes 3145732
  74.4 5.0 %collective-permute-start = (bf16[4,256,256]{2,1,0:T(8,128)(2,1)S(1)}, bf16[4,256,256]{2,1,0:T(8,128)(2,1)S(1)}, u32[]{:S(2)}, u32[]{:S(2)}) collective-permute-start(bf16[4,256,256]{2,1,0:T(8,128)(2,1)S(1)} %get-tuple-element.56), channel_id=1, source_target_pairs={{0,8},{8,0},{1,9},{9,1},{2,10},{10,2},{3,11},{11,3},{4,12},{12,4},... | collective-permute-start | bytes 1572872 | tf_op jit(solution)/shard_map/ppermute | solution.py:44
  80.4 12.8 %all-to-all-start.3 = ((bf16[4,256,256]{2,1,0:T(8,128)(2,1)}), bf16[4,256,256]{2,1,0:T(8,128)(2,1)S(1)}, u32[]{:S(2)}, u32[]{:S(2)}) async-start(bf16[4,256,256]{2,1,0:T(8,128)(2,1)} %shard_map.126), calls=%async_computation.3 | async-start | bytes 1048576 | tf_op jit(solution)/shard_map/all_to_all | solution.py:48
  84.1 1.2 copy-start.16
  85.3 1.2 copy-start.20
  86.5 30.4 %copy-start.8 = (s32[64]{0:T(128)S(1)}, s32[64]{0:T(128)}, u32[]{:S(2)}) copy-start(s32[64]{0:T(128)} %matching.3) | copy-start | bytes 772
  92.6 0.7 copy-start.11
  93.2 0.7 copy-start.12
  93.2 1.6 copy-start.10
  94.8 52.1 %copy-start.1 = (f32[256,256]{1,0:T(8,128)S(1)}, f32[256,256]{1,0:T(8,128)}, u32[]{:S(2)}) copy-start(f32[256,256]{1,0:T(8,128)} %emb.3) | copy-start | bytes 786436
  94.8 22.2 %all-to-all-start.4 = ((bf16[128,3,4,128]{3,2,1,0:T(4,128)(2,1)}), bf16[128,3,4,128]{3,2,1,0:T(4,128)(2,1)S(1)}, u32[]{:S(2)}, u32[]{:S(2)}) async-start(bf16[128,3,4,128]{3,2,1,0:T(4,128)(2,1)} %bitcast.9), calls=%async_computation.4 | async-start | bytes 786432 | tf_op jit(solution)/shard_map/all_to_all | solution.py:48
  100.5 7.7 %collective-permute-start.1 = (bf16[256,256]{1,0:T(8,128)(2,1)}, bf16[256,256]{1,0:T(8,128)(2,1)S(1)}, u32[]{:S(2)}, u32[]{:S(2)}) collective-permute-start(bf16[256,256]{1,0:T(8,128)(2,1)} %copy-done.12), channel_id=1, source_target_pairs={{0,1},{1,0},{2,3},{3,2},{4,5},{5,4},{6,7},{7,6},{8,9},{9,8},{10,11... | collective-permute-start | bytes 393224 | tf_op jit(solution)/shard_map/ppermute | solution.py:349
  103.9 8.1 %collective-permute-start.2 = (bf16[256,256]{1,0:T(8,128)(2,1)}, bf16[256,256]{1,0:T(8,128)(2,1)S(1)}, u32[]{:S(2)}, u32[]{:S(2)}) collective-permute-start(bf16[256,256]{1,0:T(8,128)(2,1)} %copy-done.11), channel_id=1, source_target_pairs={{0,2},{1,3},{2,0},{3,1},{4,6},{5,7},{6,4},{7,5},{8,10},{9,11},{10,... | collective-permute-start | bytes 393224 | tf_op jit(solution)/shard_map/ppermute | solution.py:349
  112.0 31.4 %copy-start.2 = (bf16[256,256]{1,0:T(8,128)(2,1)}, bf16[256,256]{1,0:T(8,128)(2,1)S(1)}, u32[]{:S(2)}) copy-start(bf16[256,256]{1,0:T(8,128)(2,1)S(1)} %collective-permute-done.2.own2) | copy-start | bytes 393220
  117.0 42.2 %copy-start.6 = (f32[8,256]{1,0:T(8,128)S(1)}, f32[8,256]{1,0:T(8,128)}, u32[]{:S(2)}) copy-start(f32[8,256]{1,0:T(8,128)} %accum.3) | copy-start | bytes 24580
  118.5 24.0 %all-to-all-start.5 = ((bf16[128,2,4,128]{3,2,1,0:T(4,128)(2,1)}), bf16[128,2,4,128]{3,2,1,0:T(4,128)(2,1)S(1)}, u32[]{:S(2)}, u32[]{:S(2)}) async-start(bf16[128,2,4,128]{3,2,1,0:T(4,128)(2,1)} %bitcast.11), calls=%async_computation.5 | async-start | bytes 524288 | tf_op jit(solution)/shard_map/all_to_all | solution.py:48
  128.4 7.4 %collective-permute-start.3 = (bf16[256,256]{1,0:T(8,128)(2,1)}, bf16[256,256]{1,0:T(8,128)(2,1)S(1)}, u32[]{:S(2)}, u32[]{:S(2)}) collective-permute-start(bf16[256,256]{1,0:T(8,128)(2,1)} %copy-done.10), channel_id=1, source_target_pairs={{0,3},{1,2},{2,1},{3,0},{4,7},{5,6},{6,5},{7,4},{8,11},{9,10},{10,... | collective-permute-start | bytes 393224 | tf_op jit(solution)/shard_map/ppermute | solution.py:349
  135.8 7.5 %copy-start.4 = (bf16[256,256]{1,0:T(8,128)(2,1)}, bf16[256,256]{1,0:T(8,128)(2,1)S(1)}, u32[]{:S(2)}) copy-start(bf16[256,256]{1,0:T(8,128)(2,1)S(1)} %collective-permute-done.3.own3) | copy-start | bytes 393220
  143.4 10.9 %all-to-all-start.6 = ((bf16[4,256,256]{2,1,0:T(8,128)(2,1)}), bf16[4,256,256]{2,1,0:T(8,128)(2,1)S(1)}, u32[]{:S(2)}, u32[]{:S(2)}) async-start(bf16[4,256,256]{2,1,0:T(8,128)(2,1)} %shard_map.130), calls=%async_computation.6 | async-start | bytes 1048576 | tf_op jit(solution)/shard_map/all_to_all | solution.py:48
  146.9 0.9 copy-start.3
  147.8 0.9 copy-start.5
  148.7 0.7 copy-start.9
  154.2 7.3 %collective-permute-start.4 = (bf16[4,256,256]{2,1,0:T(8,128)(2,1)S(1)}, bf16[4,256,256]{2,1,0:T(8,128)(2,1)S(1)}, u32[]{:S(2)}, u32[]{:S(2)}) collective-permute-start(bf16[4,256,256]{2,1,0:T(8,128)(2,1)S(1)} %all-to-all-done.6.grads), channel_id=1, source_target_pairs={{0,8},{8,0},{1,9},{9,1},{2,10},{10,2},{3,11},{11,3},{4,12},{12,4},... | collective-permute-start | bytes 1572872 | tf_op jit(solution)/shard_map/ppermute | solution.py:44

commit v8 on v7

--- a/solution.py
+++ b/solution.py
@@ -96,14 +96,17 @@
 
 
 def by_relation(kinds, rows):
-    parts = [jnp.where(kinds == float(r), rows, 0.0).astype(bf16) for r in range(8)]
+    wide = jnp.broadcast_to(kinds, rows.shape).astype(bf16)
+    parts = [jnp.where(wide == bf16(r), rows, bf16(0)) for r in range(8)]
     return jnp.concatenate(parts, axis=1)
 
 
-def trans_kernel(place, packs, rel, counts, known, trans, source, rel_b):
-    stack = jnp.concatenate([rel[r].astype(bf16) for r in range(8)], axis=1)
-    for r in range(8):
-        rel_b[r] = rel[r].astype(bf16)
+def cast_kernel(rel, rel_b):
+    rel_b[...] = rel[...].astype(bf16)
+
+
+def trans_kernel(place, packs, rel_b, counts, known, trans, source):
+    stack = jnp.concatenate([rel_b[r] for r in range(8)], axis=1)
     ids = lane_ids(512, 256).astype(f32)
     wide = row_ids(place[2], 512)
     for s in range(4):
@@ -111,9 +114,11 @@
         known[s * 8 : (s + 1) * 8, :] = jnp.concatenate([index, index], axis=0)
         column = columns(index)
         hot = (column[:, 0:1] == ids).astype(f32).astype(bf16)
-        rows = dot(hot, packs[s, 0:256, :])
-        source[s * 512 : (s + 1) * 512, :] = rows.astype(bf16)
-        trans[s * 512 : (s + 1) * 512, :] = dot(by_relation(column[:, 1:2], rows), stack, NT).astype(bf16)
+        rows = dot(hot, packs[s, 0:256, :]).astype(bf16)
+        source[s * 512 : (s + 1) * 512, :] = rows
+        for h in range(0, 512, 128):
+            part = by_relation(column[h : h + 128, 1:2], rows[h : h + 128])
+            trans[s * 512 + h : s * 512 + h + 128, :] = dot(part, stack, NT).astype(bf16)
         hits = (column[:, 3:4] == wide).astype(f32)
         counts[s : s + 1, :] = jnp.sum(hits, axis=0, keepdims=True)
     counts[4:8, :] = jnp.zeros((4, 512), f32)
@@ -157,20 +162,28 @@
         g_rows[z] = dot(turned, weight[:, z * 256 : (z + 1) * 256]).T.astype(bf16)
 
 
-def own_kernel(place, g_trans, known, rel_b, own0, *others):
+def own_kernel(place, g_trans, known, rel_b, own0, own1, far):
     sub_ids = lax.broadcasted_iota(jnp.int32, (256, 512), 0).astype(f32)
     stack = rel_b[...].reshape(2048, 256)
     for s in range(4):
         span = place[2] ^ s
         index = known[pl.ds(pl.multiple_of(span * 8, 8), 8), :]
-        grad = g_trans[pl.ds(pl.multiple_of(span * 512, 512), 512), :].astype(f32)
-        total = dot(by_relation(columns(index[0:4])[:, 1:2], grad), stack)
+        grad = g_trans[pl.ds(pl.multiple_of(span * 512, 512), 512), :]
+        kinds = columns(index[0:4])[:, 1:2]
+        parts = [
+            dot(by_relation(kinds[h : h + 128], grad[h : h + 128]), stack).astype(bf16)
+            for h in range(0, 512, 128)
+        ]
         hot = (index[0:1, :] == sub_ids).astype(f32).astype(bf16)
-        mine = dot(hot, total.astype(bf16))
-        if s == 0:
-            own0[...] = mine
+        mine = dot(hot, jnp.concatenate(parts, axis=0))
+        if s < 2:
+            (own0, own1)[s][...] = mine
         else:
-            others[s - 1][...] = mine.astype(bf16)
+            far[s - 2] = mine.astype(bf16)
+
+
+def pass_kernel(own1, came, out):
+    out[...] = (own1[...] + came[1].astype(f32)).astype(bf16)
 
 
 def join_kernel(kept, came, out):
@@ -223,10 +236,9 @@
     return jnp.broadcast_to(row, (128, 256)).T[:, 0:1]
 
 
-def rows_kernel(emb, accum, own0, own1, own2, own3, last, new_emb, new_accum):
-    grad = own0[...] + jnp.concatenate([whole(last, 0, 0), whole(last, 1, 0)], axis=1)
-    for own in (own1, own2, own3):
-        grad = grad + own[...].astype(f32)
+def rows_kernel(emb, accum, own0, far, near, last, new_emb, new_accum):
+    grad = own0[...] + far[0].astype(f32) + near[...].astype(f32)
+    grad = grad + jnp.concatenate([whole(last, 0, 0), whole(last, 1, 0)], axis=1)
     total = to_column(accum[...]) + jnp.mean(grad * grad, axis=1, keepdims=True)
     new_emb[...] = emb[...] - grad * (learn_rate / jnp.sqrt(total))
     new_accum[...] = to_row(total)
@@ -239,14 +251,14 @@
         core, (new_rel, new_accum, block, sem) = place[0], rest
     old = jnp.concatenate([accum[...], accum[...]], axis=0)
     column = jnp.where(core == 0, old[0:8], old[4:12]).T
-    totals = []
+    totals, copies = [], []
     for r in range(4):
         grad = grads[r].astype(f32)
         total = column[:, r : r + 1] + jnp.mean(grad * grad, axis=1, keepdims=True)
         block[r] = rel[4 * core + r] - grad * (learn_rate / jnp.sqrt(total))
         totals.append(total)
-    copy = pltpu.make_async_copy(block, new_rel.at[pl.ds(4 * core, 4)], sem)
-    copy.start()
+        copies.append(pltpu.make_async_copy(block.at[r], new_rel.at[4 * core + r], sem.at[r]))
+        copies[r].start()
     rows = jnp.concatenate(totals + totals, axis=1).T
     if len(rest) == 6:
         first = jnp.concatenate([held[...], held[...]], axis=0)
@@ -255,7 +267,8 @@
         new_accum[...] = jnp.where(core == 0, mixed, turned)
     else:
         new_accum[...] = rows
-    copy.wait()
+    for copy in copies:
+        copy.wait()
 
 
 def update_half(place, relations, rel_accum, grads, before=None):
@@ -266,7 +279,7 @@
         out_shape=(shape((8, 256, 256), f32), shape((8, 256), f32)),
         in_specs=specs,
         out_specs=(ANY, VMEM),
-        scratch_shapes=[pltpu.VMEM((4, 256, 256), f32), pltpu.SemaphoreType.DMA],
+        scratch_shapes=[pltpu.VMEM((4, 256, 256), f32), pltpu.SemaphoreType.DMA((4,))],
         input_output_aliases={4: 0} if before else {},
         compiler_params=pltpu.CompilerParams(vmem_limit_bytes=8 * 1024 * 1024),
         cost_estimate=pl.CostEstimate(flops=0, bytes_accessed=3_000_000, transcendentals=0),
@@ -293,21 +306,24 @@
         ],
     )
     arrived = spread(pieces, DOM)
+    rel_b = call(
+        cast_kernel, shape((8, 256, 256), bf16), 0, (relations,), moved=3_000_000, space=62
+    )
+    rel_b, arrived = lax.optimization_barrier((rel_b, arrived))
     packs = spread(pack, "x")
     routed = call(take_kernel, shape((64, 2, 8, 128), bf16), 1, (matching, arrived), moved=400_000)
     routed, packs = lax.optimization_barrier((routed, packs))
     rows_in = spread(routed.reshape(128, 8, 128), DOM_Z).reshape(64, 2, 8, 128)
-    counts, known, trans, source, rel_b = call(
+    counts, known, trans, source = call(
         trans_kernel,
         (
             shape((8, 512), f32),
             shape((32, 512), f32),
             shape((2048, 256), bf16),
             shape((2048, 256), bf16),
-            shape((8, 256, 256), bf16),
         ),
         1,
-        (place, packs, relations),
+        (place, packs, rel_b),
         flops=2_600_000_000,
         moved=6_000_000,
         space=16,
@@ -335,24 +351,22 @@
     )
     came, g_rows = lax.optimization_barrier((came, g_rows))
     got = spread(call(join_kernel, four, 0, (kept, came), moved=1_500_000), "x")
-    one = shape((256, 256), bf16)
-    own0, *others = call(
+    own0, own1, far = call(
         own_kernel,
-        (shape((256, 256), f32), one, one, one),
+        (shape((256, 256), f32), shape((256, 256), f32), shape((2, 256, 256), bf16)),
         1,
         (place, g_trans, known, rel_b),
         flops=3_000_000_000,
         moved=4_000_000,
         space=16,
     )
-    *others, got = lax.optimization_barrier((*others, got))
-    away = lambda part, k: lax.ppermute(part, "x", [(i, i ^ k) for i in range(4)])
-    others[0], others[1] = away(others[0], 1), away(others[1], 2)
+    far, got = lax.optimization_barrier((far, got))
+    far = lax.ppermute(far, "x", [(i, i ^ 2) for i in range(4)])
     out = call(
         pieces_kernel, shape((64, 2, 3, 4, 128), bf16), 0, (got, g_rows), moved=2_000_000
     )
     mid = spread(out.reshape(128, 3, 4, 128), DOM_Z)
-    *others, mid = lax.optimization_barrier((*others, mid))
+    far, mid = lax.optimization_barrier((far, mid))
     routed_back = call(
         route_kernel,
         shape((64, 2, 2, 4, 128), bf16),
@@ -360,15 +374,16 @@
         (matching, mid.reshape(64, 2, 3, 4, 128)),
         moved=512_000,
     )
-    others[2] = away(others[2], 3)
+    near = call(pass_kernel, shape((256, 256), bf16), 0, (own1, far), moved=500_000)
+    near = lax.ppermute(near, "x", [(i, i ^ 1) for i in range(4)])
     last = spread(routed_back.reshape(128, 2, 4, 128), DOM_Z).reshape(64, 2, 2, 4, 128)
-    others[2], last = lax.optimization_barrier((others[2], last))
+    near, last = lax.optimization_barrier((near, last))
     rel_four = spread(call(rel_kernel, four, 0, (last,), moved=512_000), "x")
     new_embeddings, new_row_accum = call(
         rows_kernel,
         (shape((256, 256), f32), shape((1, 256), f32)),
         0,
-        (embeddings, row_accum.reshape(1, 256), own0, *others, last),
+        (embeddings, row_accum.reshape(1, 256), own0, far, near, last),
         flops=1_000_000,
         moved=1_000_000,
     )

time: 166 us -> 162 us (0.976)
  waiting for transfers between devices: 37.9 us -> 47.6 us
  local copies, waits for them, and re-layouts: 12.3 us -> 4.12 us
  starting transfers between devices: 58.5 us -> 51.6 us
    unnamed x42 -> x22, local copies, waits for them, and re-layouts: 12.3 us -> 4.12 us
    ppermute x3 -> x2, starting transfers between devices: 11.1 us -> 4.38 us  [the longest x1 2.2 us: body(): near = lax.ppermute(near, 'x', [(i, i ^ 1) for i in range(4)])]
    all_to_all x6, waiting for transfers between devices: 29.5 us -> 35.4 us  [spread(): return lax.all_to_all(value, axis, split_axis=0, concat_axis=0, tiled=True)]
    ppermute x3 -> x2, waiting for transfers between devices: 7.82 us -> 11.8 us  [the longest x1 8.01 us: body(): far = lax.ppermute(far, 'x', [(i, i ^ 2) for i in range(4)])]
    pallas_call x11 -> x13, Pallas kernels: 24.7 us -> 26.8 us  [call(): pl.pallas_call(kernel, out_shape=outs, in_specs=specs, out_specs=tuple((A...]
  transfers between devices with their start and end apart: 11 -> 10, of which waited for: 8 -> 9; matrix products, arithmetic and copies ran while one was open for 0% -> 0% of each run, Pallas kernels for 10% -> 11%
where the time goes in v8:
time: 162 us; the launch traced here: 161 us
  starting transfers between devices  51.6 us (32%)
  waiting for transfers between devices  47.6 us (29%)
  Pallas kernels  31.7 us (20%)
  blocking collectives  24.7 us (15%)
  local copies, waits for them, and re-layouts  4.12 us (3%)
    all_to_all x6, starting transfers between devices, spread(): return lax.all_to_all(value, axis, split_axis=0, concat_axis=0, tiled=True)  38.8 us
    all_to_all x6, waiting for transfers between devices, spread(): return lax.all_to_all(value, axis, split_axis=0, concat_axis=0, tiled=True)  35.4 us
    pallas_call x13, Pallas kernels, call(): pl.pallas_call(kernel, out_shape=outs, in_specs=specs, out_specs=tuple((A...  26.8 us
    all_to_all x1, blocking collectives, spread(): return lax.all_to_all(value, axis, split_axis=0, concat_axis=0, tiled=True)  24.7 us
    ppermute x2, starting transfers between devices, swap(): return lax.ppermute(value, axis, [(0, 1), (1, 0)])  8.38 us
    ppermute x1, waiting for transfers between devices, body(): far = lax.ppermute(far, 'x', [(i, i ^ 2) for i in range(4)])  8.01 us
    pallas_call x2, Pallas kernels, update_half(): pl.pallas_call(update_kernel, out_shape=(shape((8, 256, 256), f32), shape...  4.89 us
    unnamed x22, local copies, waits for them, and re-layouts  4.12 us
  transfers between devices with their start and end apart: 10, of which 9 were waited for; matrix products, arithmetic and copies ran while one was open for 0% of the time, Pallas kernels for 11%

profile of v8, /device:TPU:1, one launch (start us, length us, event | category | flops | bytes accessed | tf_op | source)
XLA Modules:
  0.0 160.7 jit_solution(1367881384359585577)
XLA Ops:
  0.6 1.9 %shard_map.121 = (bf16[64,8,128]{2,1,0:T(8,128)(2,1)}, bf16[4,272,256]{2,1,0:T(8,128)(2,1)}) custom-call(f32[256,256]{1,0:T(8,128)} %emb.3, s32[1,512]{1,0:T(1,128)} %bitcast.19, s32[1,512]{1,0:T(1,128)} %bitcast.20, s32[1,512]{1,0:T(1,128)} %bitcast.21, s32[1,512]{1,0:T(1,128)} %neg.1), custom_call_target="tpu_custom_call" | custom-call | bytes 800000 | tf_op jit(solution)/shard_map/pallas_call | solution.py:32
  2.5 24.7 %all_to_all.35.arrived = bf16[64,8,128]{2,1,0:T(8,128)(2,1)S(1)} all-to-all(bf16[64,8,128]{2,1,0:T(8,128)(2,1)} %get-tuple-element.37), channel_id=1, replica_groups=mesh['zlo'=4,'y'=8,'core'=2,'zhi'=2,'x'=4] {'zlo','y','core'}, dimensions={0} | all-to-all | bytes 262144 | tf_op jit(solution)/shard_map/all_to_all | solution.py:48
  27.2 4.1 %all-to-all-start.1 = ((bf16[4,272,256]{2,1,0:T(8,128)(2,1)}), bf16[4,272,256]{2,1,0:T(8,128)(2,1)S(1)}, u32[]{:S(2)}, u32[]{:S(2)}) async-start(bf16[4,272,256]{2,1,0:T(8,128)(2,1)} %get-tuple-element.39), calls=%async_computation.1 | async-start | bytes 1114112 | tf_op jit(solution)/shard_map/all_to_all | solution.py:48
  31.4 2.7 %shard_map.120.rel_b = bf16[8,256,256]{2,1,0:T(8,128)(2,1)} custom-call(f32[8,256,256]{2,1,0:T(8,128)} %rel.5), custom_call_target="tpu_custom_call" | custom-call | bytes 3000000 | tf_op jit(solution)/shard_map/pallas_call | solution.py:32
  34.0 0.0 copy-done.7
  34.0 1.3 shard_map.122
  35.3 5.3 %all-to-all-done.1.packs = bf16[4,272,256]{2,1,0:T(8,128)(2,1)S(1)} async-done(((bf16[4,272,256]{2,1,0:T(8,128)(2,1)}), bf16[4,272,256]{2,1,0:T(8,128)(2,1)S(1)}, u32[]{:S(2)}, u32[]{:S(2)}) %all-to-all-start.1) | async-done | bytes 557088 | tf_op jit(solution)/shard_map/all_to_all | solution.py:48
  40.6 12.3 %all-to-all-start.2 = ((bf16[128,8,128]{2,1,0:T(8,128)(2,1)}), bf16[128,8,128]{2,1,0:T(8,128)(2,1)S(1)}, u32[]{:S(2)}, u32[]{:S(2)}) async-start(bf16[128,8,128]{2,1,0:T(8,128)(2,1)} %bitcast.7), calls=%async_computation.2 | async-start | bytes 524288 | tf_op jit(solution)/shard_map/all_to_all | solution.py:48
  52.9 0.1 pad_add_fusion.place
  53.0 1.2 copy-done.1
  54.2 6.0 %shard_map.123 = (f32[8,512]{1,0:T(8,128)S(1)}, f32[32,512]{1,0:T(8,128)S(1)}, bf16[2048,256]{1,0:T(8,128)(2,1)S(1)}, bf16[2048,256]{1,0:T(8,128)(2,1)S(1)}) custom-call(s32[3]{0:T(128)S(1)} %pad_add_fusion.place, bf16[4,272,256]{2,1,0:T(8,128)(2,1)S(1)} %all-to-all-done.1.packs, bf16[8,256,256]{2,1,0:T(8,128)(2,1)S(1)} %copy-done.1), custom_call_target="tpu_custom_call" | custom-call | flops 2600000000 | bytes 6000000 | tf_op jit(solution)/shard_map/pallas_call | solution.py:32
  60.2 6.8 %all-to-all-done.2 = bf16[128,8,128]{2,1,0:T(8,128)(2,1)S(1)} async-done(((bf16[128,8,128]{2,1,0:T(8,128)(2,1)}), bf16[128,8,128]{2,1,0:T(8,128)(2,1)S(1)}, u32[]{:S(2)}, u32[]{:S(2)}) %all-to-all-start.2) | async-done | bytes 262176 | tf_op jit(solution)/shard_map/all_to_all | solution.py:48
  67.0 4.9 %shard_map.124 = (bf16[2048,512]{1,0:T(8,128)(2,1)S(1)}, bf16[2048,256]{1,0:T(8,128)(2,1)S(1)}, bf16[4,256,256]{2,1,0:T(8,128)(2,1)S(1)}, bf16[4,256,256]{2,1,0:T(8,128)(2,1)S(1)}) custom-call(s32[3]{0:T(128)S(1)} %pad_add_fusion.place, bf16[64,2,8,128]{3,2,1,0:T(8,128)(2,1)S(1)} %bitcast.17, f32[8,512]{1,0:T(8,128)S(1)} %get-tuple-element.43.counts, ...), custom_call_target="tpu_custom_call" | custom-call | flops 3200000000 | bytes 6000000 | tf_op jit(solution)/shard_map/pallas_call | solution.py:32
  71.9 0.0 copy-start.9
  71.9 3.7 %collective-permute-start = (bf16[4,256,256]{2,1,0:T(8,128)(2,1)S(1)}, bf16[4,256,256]{2,1,0:T(8,128)(2,1)S(1)}, u32[]{:S(2)}, u32[]{:S(2)}) collective-permute-start(bf16[4,256,256]{2,1,0:T(8,128)(2,1)S(1)} %get-tuple-element.51), channel_id=1, source_target_pairs={{0,8},{8,0},{1,9},{9,1},{2,10},{10,2},{3,11},{11,3},{4,12},{12,4},... | collective-permute-start | bytes 1572872 | tf_op jit(solution)/shard_map/ppermute | solution.py:44
  75.6 0.9 shard_map.126.g_rows
  76.5 0.0 copy-done.9
  76.5 0.0 copy-start.2
  76.5 0.4 collective-permute-done.came
  76.9 0.9 shard_map.127
  77.9 3.5 %all-to-all-start.3 = ((bf16[4,256,256]{2,1,0:T(8,128)(2,1)}), bf16[4,256,256]{2,1,0:T(8,128)(2,1)S(1)}, u32[]{:S(2)}, u32[]{:S(2)}) async-start(bf16[4,256,256]{2,1,0:T(8,128)(2,1)} %shard_map.127), calls=%async_computation.3 | async-start | bytes 1048576 | tf_op jit(solution)/shard_map/all_to_all | solution.py:48
  81.3 0.0 copy-done.2
  81.4 0.0 copy-start.10
  81.4 1.2 copy-done.10
  82.6 3.9 %shard_map.125 = (f32[256,256]{1,0:T(8,128)S(1)}, f32[256,256]{1,0:T(8,128)S(1)}, bf16[2,256,256]{2,1,0:T(8,128)(2,1)S(1)}) custom-call(s32[3]{0:T(128)S(1)} %pad_add_fusion.place, bf16[2048,256]{1,0:T(8,128)(2,1)S(1)} %copy-done.10, f32[32,512]{1,0:T(8,128)S(1)} %get-tuple-element.44.known, bf16[8,256,256]{2,1,0:T(8,128)(2,1)S(1)} %copy-done.2), custom_call_target="tpu_custom_call" | custom-call | flops 3000000000 | bytes 4000000 | tf_op jit(solution)/shard_map/pallas_call | solution.py:32
  86.5 0.0 copy-start.4
  86.5 0.7 copy-done.4
  87.2 3.4 %all-to-all-done.3.got = bf16[4,256,256]{2,1,0:T(8,128)(2,1)S(1)} async-done(((bf16[4,256,256]{2,1,0:T(8,128)(2,1)}), bf16[4,256,256]{2,1,0:T(8,128)(2,1)S(1)}, u32[]{:S(2)}, u32[]{:S(2)}) %all-to-all-start.3) | async-done | bytes 524320 | tf_op jit(solution)/shard_map/all_to_all | solution.py:48
  90.5 0.9 shard_map.128
  91.5 6.5 %all-to-all-start.4 = ((bf16[128,3,4,128]{3,2,1,0:T(4,128)(2,1)}), bf16[128,3,4,128]{3,2,1,0:T(4,128)(2,1)S(1)}, u32[]{:S(2)}, u32[]{:S(2)}) async-start(bf16[128,3,4,128]{3,2,1,0:T(4,128)(2,1)} %bitcast.9), calls=%async_computation.4 | async-start | bytes 786432 | tf_op jit(solution)/shard_map/all_to_all | solution.py:48
  98.0 2.2 %collective-permute-start.1 = (bf16[2,256,256]{2,1,0:T(8,128)(2,1)S(1)}, bf16[2,256,256]{2,1,0:T(8,128)(2,1)S(1)}, u32[]{:S(2)}, u32[]{:S(2)}) collective-permute-start(bf16[2,256,256]{2,1,0:T(8,128)(2,1)S(1)} %get-tuple-element.54), channel_id=1, source_target_pairs={{0,2},{1,3},{2,0},{3,1},{4,6},{5,7},{6,4},{7,5},{8,10},{9,11},{10,... | collective-permute-start | bytes 786440 | tf_op jit(solution)/shard_map/ppermute | solution.py:364
  100.2 8.0 %collective-permute-done.1.came.far = bf16[2,256,256]{2,1,0:T(8,128)(2,1)S(1)} collective-permute-done((bf16[2,256,256]{2,1,0:T(8,128)(2,1)S(1)}, bf16[2,256,256]{2,1,0:T(8,128)(2,1)S(1)}, u32[]{:S(2)}, u32[]{:S(2)}) %collective-permute-start.1) | collective-permute-done | bytes 262176 | tf_op jit(solution)/shard_map/ppermute | solution.py:364
  108.2 6.2 %all-to-all-done.4 = bf16[128,3,4,128]{3,2,1,0:T(4,128)(2,1)S(1)} async-done(((bf16[128,3,4,128]{3,2,1,0:T(4,128)(2,1)}), bf16[128,3,4,128]{3,2,1,0:T(4,128)(2,1)S(1)}, u32[]{:S(2)}, u32[]{:S(2)}) %all-to-all-start.4) | async-done | bytes 393248 | tf_op jit(solution)/shard_map/all_to_all | solution.py:48
  114.4 1.5 shard_map.130
  115.9 8.9 %all-to-all-start.5 = ((bf16[128,2,4,128]{3,2,1,0:T(4,128)(2,1)}), bf16[128,2,4,128]{3,2,1,0:T(4,128)(2,1)S(1)}, u32[]{:S(2)}, u32[]{:S(2)}) async-start(bf16[128,2,4,128]{3,2,1,0:T(4,128)(2,1)} %bitcast.11), calls=%async_computation.5 | async-start | bytes 524288 | tf_op jit(solution)/shard_map/all_to_all | solution.py:48
  124.9 2.2 %collective-permute-start.2 = (bf16[256,256]{1,0:T(8,128)(2,1)S(1)}, bf16[256,256]{1,0:T(8,128)(2,1)S(1)}, u32[]{:S(2)}, u32[]{:S(2)}) collective-permute-start(bf16[256,256]{1,0:T(8,128)(2,1)S(1)} %shard_map.129), channel_id=1, source_target_pairs={{0,1},{1,0},{2,3},{3,2},{4,5},{5,4},{6,7},{7,6},{8,9},{9,8},{10,11... | collective-permute-start | bytes 393224 | tf_op jit(solution)/shard_map/ppermute | solution.py:378
  127.1 3.8 %collective-permute-done.2.near = bf16[256,256]{1,0:T(8,128)(2,1)S(1)} collective-permute-done((bf16[256,256]{1,0:T(8,128)(2,1)S(1)}, bf16[256,256]{1,0:T(8,128)(2,1)S(1)}, u32[]{:S(2)}, u32[]{:S(2)}) %collective-permute-start.2) | collective-permute-done | bytes 131104 | tf_op jit(solution)/shard_map/ppermute | solution.py:378
  130.9 8.1 %all-to-all-done.5 = bf16[128,2,4,128]{3,2,1,0:T(4,128)(2,1)S(1)} async-done(((bf16[128,2,4,128]{3,2,1,0:T(4,128)(2,1)}), bf16[128,2,4,128]{3,2,1,0:T(4,128)(2,1)S(1)}, u32[]{:S(2)}, u32[]{:S(2)}) %all-to-all-start.5) | async-done | bytes 262176 | tf_op jit(solution)/shard_map/all_to_all | solution.py:48
  139.0 0.9 shard_map.132
  139.8 3.5 %all-to-all-start.6 = ((bf16[4,256,256]{2,1,0:T(8,128)(2,1)}), bf16[4,256,256]{2,1,0:T(8,128)(2,1)S(1)}, u32[]{:S(2)}, u32[]{:S(2)}) async-start(bf16[4,256,256]{2,1,0:T(8,128)(2,1)} %shard_map.132), calls=%async_computation.6 | async-start | bytes 1048576 | tf_op jit(solution)/shard_map/all_to_all | solution.py:48
  143.3 0.0 copy-start.5
  143.3 0.9 copy-done.5
  144.3 1.0 shard_map.131
  145.3 5.6 %all-to-all-done.6.grads = bf16[4,256,256]{2,1,0:T(8,128)(2,1)S(1)} async-done(((bf16[4,256,256]{2,1,0:T(8,128)(2,1)}), bf16[4,256,256]{2,1,0:T(8,128)(2,1)S(1)}, u32[]{:S(2)}, u32[]{:S(2)}) %all-to-all-start.6) | async-done | bytes 524320 | tf_op jit(solution)/shard_map/all_to_all | solution.py:48
  150.9 4.7 %collective-permute-start.3 = (bf16[4,256,256]{2,1,0:T(8,128)(2,1)S(1)}, bf16[4,256,256]{2,1,0:T(8,128)(2,1)S(1)}, u32[]{:S(2)}, u32[]{:S(2)}) collective-permute-start(bf16[4,256,256]{2,1,0:T(8,128)(2,1)S(1)} %all-to-all-done.6.grads), channel_id=1, source_target_pairs={{0,8},{8,0},{1,9},{9,1},{2,10},{10,2},{3,11},{11,3},{4,12},{12,4},... | collective-permute-start | bytes 1572872 | tf_op jit(solution)/shard_map/ppermute | solution.py:44
  155.6 2.2 %shard_map.133 = (f32[8,256,256]{2,1,0:T(8,128)}, f32[8,256]{1,0:T(8,128)S(1)}) custom-call(s32[3]{0:T(128)S(1)} %pad_add_fusion.place, f32[8,256,256]{2,1,0:T(8,128)S(1)} %copy-done, f32[8,256]{1,0:T(8,128)S(1)} %copy-done.6, bf16[4,256,256]{2,1,0:T(8,128)(2,1)S(1)} %all-to-all-done.6.grads), custom_call_target="tpu_custom_call" | custom-call | bytes 3000000 | tf_op jit(solution)/shard_map/pallas_call | solution.py:277
  157.8 0.0 collective-permute-done.3.grads
  157.8 2.7 %shard_map.134 = (f32[8,256,256]{2,1,0:T(8,128)}, f32[8,256]{1,0:T(8,128)}) custom-call(s32[3]{0:T(128)S(1)} %pad_add_fusion.place, f32[8,256,256]{2,1,0:T(8,128)S(1)} %copy-done, f32[8,256]{1,0:T(8,128)S(1)} %copy-done.6, bf16[4,256,256]{2,1,0:T(8,128)(2,1)S(1)} %collective-permute-done.3.grads, ...), custom_call_target="tpu_custom_call", output_to_operand_aliasing={{0}: (4, {})} | custom-call | bytes 3000000 | tf_op jit(solution)/shard_map/pallas_call | solution.py:277
  (11 shorter events, 0.0 us)
Async XLA Ops:
  27.2 6.8 %copy-start.7 = (s32[64]{0:T(128)S(1)}, s32[64]{0:T(128)}, u32[]{:S(2)}) copy-start(s32[64]{0:T(128)} %matching.3) | copy-start | bytes 772
  27.2 13.4 %all-to-all-start.1 = ((bf16[4,272,256]{2,1,0:T(8,128)(2,1)}), bf16[4,272,256]{2,1,0:T(8,128)(2,1)S(1)}, u32[]{:S(2)}, u32[]{:S(2)}) async-start(bf16[4,272,256]{2,1,0:T(8,128)(2,1)} %get-tuple-element.39), calls=%async_computation.1 | async-start | bytes 1114112 | tf_op jit(solution)/shard_map/all_to_all | solution.py:48
  40.6 26.4 %all-to-all-start.2 = ((bf16[128,8,128]{2,1,0:T(8,128)(2,1)}), bf16[128,8,128]{2,1,0:T(8,128)(2,1)S(1)}, u32[]{:S(2)}, u32[]{:S(2)}) async-start(bf16[128,8,128]{2,1,0:T(8,128)(2,1)} %bitcast.7), calls=%async_computation.2 | async-start | bytes 524288 | tf_op jit(solution)/shard_map/all_to_all | solution.py:48
  53.0 1.2 copy-start.1
  71.9 4.6 %copy-start.9 = (bf16[2048,256]{1,0:T(8,128)(2,1)}, bf16[2048,256]{1,0:T(8,128)(2,1)S(1)}, u32[]{:S(2)}) copy-start(bf16[2048,256]{1,0:T(8,128)(2,1)S(1)} %get-tuple-element.47.g_trans) | copy-start | bytes 3145732
  71.9 5.0 %collective-permute-start = (bf16[4,256,256]{2,1,0:T(8,128)(2,1)S(1)}, bf16[4,256,256]{2,1,0:T(8,128)(2,1)S(1)}, u32[]{:S(2)}, u32[]{:S(2)}) collective-permute-start(bf16[4,256,256]{2,1,0:T(8,128)(2,1)S(1)} %get-tuple-element.51), channel_id=1, source_target_pairs={{0,8},{8,0},{1,9},{9,1},{2,10},{10,2},{3,11},{11,3},{4,12},{12,4},... | collective-permute-start | bytes 1572872 | tf_op jit(solution)/shard_map/ppermute | solution.py:44
  76.5 4.8 %copy-start.2 = (bf16[8,256,256]{2,1,0:T(8,128)(2,1)S(1)}, bf16[8,256,256]{2,1,0:T(8,128)(2,1)}, u32[]{:S(2)}) copy-start(bf16[8,256,256]{2,1,0:T(8,128)(2,1)} %shard_map.120.rel_b) | copy-start | bytes 3145732
  77.9 12.7 %all-to-all-start.3 = ((bf16[4,256,256]{2,1,0:T(8,128)(2,1)}), bf16[4,256,256]{2,1,0:T(8,128)(2,1)S(1)}, u32[]{:S(2)}, u32[]{:S(2)}) async-start(bf16[4,256,256]{2,1,0:T(8,128)(2,1)} %shard_map.127), calls=%async_computation.3 | async-start | bytes 1048576 | tf_op jit(solution)/shard_map/all_to_all | solution.py:48
  81.4 1.2 copy-start.10
  86.5 0.7 copy-start.4
  91.4 51.9 %copy-start.3 = (f32[256,256]{1,0:T(8,128)S(1)}, f32[256,256]{1,0:T(8,128)}, u32[]{:S(2)}) copy-start(f32[256,256]{1,0:T(8,128)} %emb.3) | copy-start | bytes 786436
  91.5 51.9 %copy-start.8 = (f32[256]{0:T(256)S(1)}, f32[256]{0:T(256)}, u32[]{:S(2)}) copy-start(f32[256]{0:T(256)} %param.10) | copy-start | bytes 3076
  91.5 23.0 %all-to-all-start.4 = ((bf16[128,3,4,128]{3,2,1,0:T(4,128)(2,1)}), bf16[128,3,4,128]{3,2,1,0:T(4,128)(2,1)S(1)}, u32[]{:S(2)}, u32[]{:S(2)}) async-start(bf16[128,3,4,128]{3,2,1,0:T(4,128)(2,1)} %bitcast.9), calls=%async_computation.4 | async-start | bytes 786432 | tf_op jit(solution)/shard_map/all_to_all | solution.py:48
  98.0 10.2 %collective-permute-start.1 = (bf16[2,256,256]{2,1,0:T(8,128)(2,1)S(1)}, bf16[2,256,256]{2,1,0:T(8,128)(2,1)S(1)}, u32[]{:S(2)}, u32[]{:S(2)}) collective-permute-start(bf16[2,256,256]{2,1,0:T(8,128)(2,1)S(1)} %get-tuple-element.54), channel_id=1, source_target_pairs={{0,2},{1,3},{2,0},{3,1},{4,6},{5,7},{6,4},{7,5},{8,10},{9,11},{10,... | collective-permute-start | bytes 786440 | tf_op jit(solution)/shard_map/ppermute | solution.py:364
  115.9 39.7 %copy-start = (f32[8,256,256]{2,1,0:T(8,128)S(1)}, f32[8,256,256]{2,1,0:T(8,128)}, u32[]{:S(2)}) copy-start(f32[8,256,256]{2,1,0:T(8,128)} %rel.5) | copy-start | bytes 6291460
  115.9 39.7 %copy-start.6 = (f32[8,256]{1,0:T(8,128)S(1)}, f32[8,256]{1,0:T(8,128)}, u32[]{:S(2)}) copy-start(f32[8,256]{1,0:T(8,128)} %accum.3) | copy-start | bytes 24580
  115.9 23.0 %all-to-all-start.5 = ((bf16[128,2,4,128]{3,2,1,0:T(4,128)(2,1)}), bf16[128,2,4,128]{3,2,1,0:T(4,128)(2,1)S(1)}, u32[]{:S(2)}, u32[]{:S(2)}) async-start(bf16[128,2,4,128]{3,2,1,0:T(4,128)(2,1)} %bitcast.11), calls=%async_computation.5 | async-start | bytes 524288 | tf_op jit(solution)/shard_map/all_to_all | solution.py:48
  124.9 6.0 %collective-permute-start.2 = (bf16[256,256]{1,0:T(8,128)(2,1)S(1)}, bf16[256,256]{1,0:T(8,128)(2,1)S(1)}, u32[]{:S(2)}, u32[]{:S(2)}) collective-permute-start(bf16[256,256]{1,0:T(8,128)(2,1)S(1)} %shard_map.129), channel_id=1, source_target_pairs={{0,1},{1,0},{2,3},{3,2},{4,5},{5,4},{6,7},{7,6},{8,9},{9,8},{10,11... | collective-permute-start | bytes 393224 | tf_op jit(solution)/shard_map/ppermute | solution.py:378
  139.8 11.1 %all-to-all-start.6 = ((bf16[4,256,256]{2,1,0:T(8,128)(2,1)}), bf16[4,256,256]{2,1,0:T(8,128)(2,1)S(1)}, u32[]{:S(2)}, u32[]{:S(2)}) async-start(bf16[4,256,256]{2,1,0:T(8,128)(2,1)} %shard_map.132), calls=%async_computation.6 | async-start | bytes 1048576 | tf_op jit(solution)/shard_map/all_to_all | solution.py:48
  143.3 1.0 copy-start.5
  150.9 6.9 %collective-permute-start.3 = (bf16[4,256,256]{2,1,0:T(8,128)(2,1)S(1)}, bf16[4,256,256]{2,1,0:T(8,128)(2,1)S(1)}, u32[]{:S(2)}, u32[]{:S(2)}) collective-permute-start(bf16[4,256,256]{2,1,0:T(8,128)(2,1)S(1)} %all-to-all-done.6.grads), channel_id=1, source_target_pairs={{0,8},{8,0},{1,9},{9,1},{2,10},{10,2},{3,11},{11,3},{4,12},{12,4},... | collective-permute-start | bytes 1572872 | tf_op jit(solution)/shard_map/ppermute | solution.py:44

commit v9 on v8

--- a/solution.py
+++ b/solution.py
@@ -33,7 +33,7 @@
         kernel,
         out_shape=outs,
         in_specs=specs,
-        out_specs=tuple(ANY if k in far_outs else VMEM for k in range(len(outs))) if many else VMEM,
+        out_specs=tuple(ANY if k in far_outs else VMEM for k in range(len(outs))) if many else (ANY if far_outs else VMEM),
         scratch_shapes=list(scratch),
         compiler_params=pltpu.CompilerParams(vmem_limit_bytes=space * 1024 * 1024),
         cost_estimate=pl.CostEstimate(flops=flops, bytes_accessed=moved, transcendentals=0),
@@ -60,10 +60,8 @@
     high = wide // 256
     low = (wide - high * 256).astype(f32)
     both = jnp.concatenate([high.astype(f32), low], axis=0)
-    index_b = jnp.concatenate([both[:, :256], both[:, 256:]], axis=0).astype(bf16)
-    for k in range(4):
-        pack[k, 256:272, :] = index_b
-        pack[k, 0:256, :] = rows[...].astype(bf16)
+    pack[256:272, :] = jnp.concatenate([both[:, :256], both[:, 256:]], axis=0).astype(bf16)
+    pack[0:256, :] = rows[...].astype(bf16)
     for h in range(2):
         half = rows[:, h * 128 : (h + 1) * 128]
         pieces[h * 32 : (h + 1) * 32] = half.reshape(32, 8, 128).astype(bf16)
@@ -101,74 +99,84 @@
     return jnp.concatenate(parts, axis=1)
 
 
-def cast_kernel(rel, rel_b):
-    rel_b[...] = rel[...].astype(bf16)
-
-
-def trans_kernel(place, packs, rel_b, counts, known, trans, source):
+def cast_kernel(rel, rel_b, wide, narrow, sems):
+    taken = [pltpu.make_async_copy(rel.at[r], wide.at[r], sems.at[r]) for r in range(8)]
+    given = [pltpu.make_async_copy(narrow.at[r], rel_b.at[r], sems.at[8 + r]) for r in range(8)]
+    for copy in taken:
+        copy.start()
+    for r in range(8):
+        taken[r].wait()
+        narrow[r] = wide[r].astype(bf16)
+        given[r].start()
+    for copy in given:
+        copy.wait()
+
+
+def trans_kernel(place, pack0, pack1, rel_b, counts, known, trans, source):
     stack = jnp.concatenate([rel_b[r] for r in range(8)], axis=1)
     ids = lane_ids(512, 256).astype(f32)
     wide = row_ids(place[2], 512)
-    for s in range(4):
-        index = indices(packs[s, 256:272, :])
+    for s, pack in enumerate((pack0, pack1)):
+        index = indices(pack[256:272, :])
         known[s * 8 : (s + 1) * 8, :] = jnp.concatenate([index, index], axis=0)
         column = columns(index)
         hot = (column[:, 0:1] == ids).astype(f32).astype(bf16)
-        rows = dot(hot, packs[s, 0:256, :]).astype(bf16)
+        rows = dot(hot, pack[0:256, :]).astype(bf16)
         source[s * 512 : (s + 1) * 512, :] = rows
-        for h in range(0, 512, 128):
-            part = by_relation(column[h : h + 128, 1:2], rows[h : h + 128])
-            trans[s * 512 + h : s * 512 + h + 128, :] = dot(part, stack, NT).astype(bf16)
+        part = by_relation(column[:, 1:2], rows)
+        trans[s * 512 : (s + 1) * 512, :] = dot(part, stack, NT).astype(bf16)
         hits = (column[:, 3:4] == wide).astype(f32)
         counts[s : s + 1, :] = jnp.sum(hits, axis=0, keepdims=True)
-    counts[4:8, :] = jnp.zeros((4, 512), f32)
+    counts[2:8, :] = jnp.zeros((6, 512), f32)
 
 
 def score_kernel(
-    place, rows_in, counts, known, trans, source, weight, g_trans, kept, given, rows
+    place, rows_in, counts0, counts1, known0, known1, trans0, trans1, source0, source1,
+    weight, g_trans, kept, given, rows
 ):
     core = place[0]
     for z in range(2):
         both = rows_in[:, z].reshape(2, 256, 128)
         rows[z * 256 : (z + 1) * 256, :] = jnp.concatenate([both[0], both[1]], axis=1)
-    index = [known[s * 8 : s * 8 + 4, :] for s in range(4)]
+    index = [known[s * 8 : s * 8 + 4, :] for known in (known0, known1) for s in range(2)]
     ids = row_ids(place[2], 256)
     for b in range(8):
         s = b // 2
         column = columns(index[s])[(b % 2) * 256 : (b % 2 + 1) * 256]
         span = slice(b * 256, (b + 1) * 256)
-        score = dot(trans[span, :], rows[...], NT)
+        trans = (trans0, trans1)[b // 4][(b % 4) * 256 : (b % 4 + 1) * 256, :]
+        score = dot(trans, rows[...], NT)
         sig = 1.0 / (1.0 + jnp.exp(-score))
-        count = counts[s : s + 1, :]
+        count = (counts0, counts1)[s // 2][s % 2 : s % 2 + 1, :]
         hit = column[:, 2:3] == ids
         part = jnp.where(hit, (count + 1.0) * sig - 1.0, count * sig).astype(bf16)
         weight[span, :] = part
         g_trans[span, :] = dot(part, rows[...]).astype(bf16)
     turned = g_trans[...].astype(f32).T
     kinds = jnp.concatenate([part[1:2] for part in index], axis=1)
+    source = jnp.concatenate([source0[...], source1[...]], axis=0)
     for r in range(8):
         wanted = r + 4 * core if r < 4 else r - 4 * core
         masked = jnp.where(kinds == wanted.astype(f32), turned, 0.0).astype(bf16)
-        grad = dot(masked, source[...]).astype(bf16)
+        grad = dot(masked, source).astype(bf16)
         if r < 4:
             kept[r] = grad
         else:
             given[r - 4] = grad
 
 
-def partner_kernel(weight, trans, g_rows):
-    turned = trans[...].astype(f32).T.astype(bf16)
+def partner_kernel(weight, trans0, trans1, g_rows):
+    turned = jnp.concatenate([t[...].astype(f32).T.astype(bf16) for t in (trans0, trans1)], axis=1)
     for z in range(2):
         g_rows[z] = dot(turned, weight[:, z * 256 : (z + 1) * 256]).T.astype(bf16)
 
 
-def own_kernel(place, g_trans, known, rel_b, own0, own1, far):
+def own_kernel(g_trans, known0, known1, rel_b, own0, own1, far):
     sub_ids = lax.broadcasted_iota(jnp.int32, (256, 512), 0).astype(f32)
     stack = rel_b[...].reshape(2048, 256)
     for s in range(4):
-        span = place[2] ^ s
-        index = known[pl.ds(pl.multiple_of(span * 8, 8), 8), :]
-        grad = g_trans[pl.ds(pl.multiple_of(span * 512, 512), 512), :]
+        index = (known0, known1)[s // 2][(s % 2) * 8 : (s % 2 + 1) * 8, :]
+        grad = g_trans[s * 512 : (s + 1) * 512, :]
         kinds = columns(index[0:4])[:, 1:2]
         parts = [
             dot(by_relation(kinds[h : h + 128], grad[h : h + 128]), stack).astype(bf16)
@@ -293,7 +301,7 @@
     line = lambda v: v.reshape(1, 512)
     pieces, pack = call(
         first_kernel,
-        (shape((64, 8, 128), bf16), shape((4, 272, 256), bf16)),
+        (shape((64, 8, 128), bf16), shape((272, 256), bf16)),
         0,
         (embeddings, line(src_rows), line(rel_ids), line(dst_rows), line(neg_rows)),
         moved=800_000,
@@ -307,33 +315,46 @@
     )
     arrived = spread(pieces, DOM)
     rel_b = call(
-        cast_kernel, shape((8, 256, 256), bf16), 0, (relations,), moved=3_000_000, space=62
-    )
-    rel_b, arrived = lax.optimization_barrier((rel_b, arrived))
-    packs = spread(pack, "x")
+        cast_kernel,
+        shape((8, 256, 256), bf16),
+        0,
+        (relations,),
+        moved=3_000_000,
+        far=(0,),
+        far_outs=(0,),
+        scratch=[
+            pltpu.VMEM((8, 256, 256), f32),
+            pltpu.VMEM((8, 256, 256), bf16),
+            pltpu.SemaphoreType.DMA((16,)),
+        ],
+        space=62,
+    )
+    packs = [pack] + [
+        lax.ppermute(pack, "x", [(i, i ^ k) for i in range(4)]) for k in range(1, 4)
+    ]
+    packs[1], rel_b, arrived = lax.optimization_barrier((packs[1], rel_b, arrived))
     routed = call(take_kernel, shape((64, 2, 8, 128), bf16), 1, (matching, arrived), moved=400_000)
-    routed, packs = lax.optimization_barrier((routed, packs))
     rows_in = spread(routed.reshape(128, 8, 128), DOM_Z).reshape(64, 2, 8, 128)
-    counts, known, trans, source = call(
-        trans_kernel,
-        (
-            shape((8, 512), f32),
-            shape((32, 512), f32),
-            shape((2048, 256), bf16),
-            shape((2048, 256), bf16),
-        ),
-        1,
-        (place, packs, rel_b),
-        flops=2_600_000_000,
-        moved=6_000_000,
-        space=16,
-    )
+    block = shape((1024, 256), bf16)
+    halves = [
+        call(
+            trans_kernel,
+            (shape((8, 512), f32), shape((16, 512), f32), block, block),
+            1,
+            (place, packs[k], packs[k + 1], rel_b),
+            flops=1_300_000_000,
+            moved=3_000_000,
+            space=16,
+        )
+        for k in (0, 2)
+    ]
+    counts, known, trans, source = zip(*halves)
     four = shape((4, 256, 256), bf16)
     weight, g_trans, kept, given = call(
         score_kernel,
         (shape((2048, 512), bf16), shape((2048, 256), bf16), four, four),
         1,
-        (place, rows_in, counts, known, trans, source),
+        (place, rows_in, *counts, *known, *trans, *source),
         flops=3_200_000_000,
         moved=6_000_000,
         scratch=[pltpu.VMEM((512, 256), bf16)],
@@ -344,7 +365,7 @@
         partner_kernel,
         shape((2, 256, 256), bf16),
         0,
-        (weight, trans),
+        (weight, *trans),
         flops=1_500_000_000,
         moved=4_000_000,
         space=16,
@@ -354,8 +375,8 @@
     own0, own1, far = call(
         own_kernel,
         (shape((256, 256), f32), shape((256, 256), f32), shape((2, 256, 256), bf16)),
-        1,
-        (place, g_trans, known, rel_b),
+        0,
+        (g_trans, *known, rel_b),
         flops=3_000_000_000,
         moved=4_000_000,
         space=16,

time: 162 us -> 161 us (level)
  starting transfers between devices: 51.6 us -> 80.3 us
  blocking collectives: 24.7 us -> 0 us
  waiting for transfers between devices: 47.6 us -> 41.2 us
  local copies, waits for them, and re-layouts: 4.12 us -> 7.77 us
  Pallas kernels: 31.7 us -> 29.3 us
    all_to_all x1 -> x0, blocking collectives: 24.7 us -> none  [spread(): return lax.all_to_all(value, axis, split_axis=0, concat_axis=0, tiled=True)]
    all_to_all x6, starting transfers between devices: 38.8 us -> 57.2 us  [spread(): return lax.all_to_all(value, axis, split_axis=0, concat_axis=0, tiled=True)]
    ppermute x0 -> x3, starting transfers between devices: none -> 10.1 us  [body(): lax.ppermute(pack, 'x', [(i, i ^ k) for i in range(4)])]
    all_to_all x6, waiting for transfers between devices: 35.4 us -> 26.6 us  [spread(): return lax.all_to_all(value, axis, split_axis=0, concat_axis=0, tiled=True)]
    unnamed x22 -> x32, local copies, waits for them, and re-layouts: 4.12 us -> 7.77 us
    pallas_call x13 -> x14, Pallas kernels: 26.8 us -> 24.4 us  [call(): pl.pallas_call(kernel, out_shape=outs, in_specs=specs, out_specs=tuple((A...]
    ppermute x0 -> x3, waiting for transfers between devices: none -> 2.13 us  [body(): lax.ppermute(pack, 'x', [(i, i ^ k) for i in range(4)])]
  transfers between devices with their start and end apart: 10 -> 13, of which waited for: 9 -> 10; matrix products, arithmetic and copies ran while one was open for 0% -> 0% of each run, Pallas kernels for 11% -> 9%
where the time goes in v9:
time: 161 us; the launch traced here: 160 us
  starting transfers between devices  80.3 us (50%)
  waiting for transfers between devices  41.2 us (26%)
  Pallas kernels  29.3 us (18%)
  local copies, waits for them, and re-layouts  7.77 us (5%)
    all_to_all x6, starting transfers between devices, spread(): return lax.all_to_all(value, axis, split_axis=0, concat_axis=0, tiled=True)  57.2 us
    all_to_all x6, waiting for transfers between devices, spread(): return lax.all_to_all(value, axis, split_axis=0, concat_axis=0, tiled=True)  26.6 us
    pallas_call x14, Pallas kernels, call(): pl.pallas_call(kernel, out_shape=outs, in_specs=specs, out_specs=tuple((A...  24.4 us
    ppermute x3, starting transfers between devices, body(): lax.ppermute(pack, 'x', [(i, i ^ k) for i in range(4)])  10.1 us
    ppermute x2, starting transfers between devices, swap(): return lax.ppermute(value, axis, [(0, 1), (1, 0)])  8.65 us
    ppermute x1, waiting for transfers between devices, body(): far = lax.ppermute(far, 'x', [(i, i ^ 2) for i in range(4)])  8.12 us
    unnamed x32, local copies, waits for them, and re-layouts  7.77 us
    pallas_call x2, Pallas kernels, update_half(): pl.pallas_call(update_kernel, out_shape=(shape((8, 256, 256), f32), shape...  4.89 us
  transfers between devices with their start and end apart: 13, of which 10 were waited for; matrix products, arithmetic and copies ran while one was open for 0% of the time, Pallas kernels for 9%

profile of v9, /device:TPU:1, one launch (start us, length us, event | category | flops | bytes accessed | tf_op | source)
XLA Modules:
  0.0 159.8 jit_solution(3358916544045944882)
XLA Ops:
  0.6 1.7 %shard_map.120 = (bf16[64,8,128]{2,1,0:T(8,128)(2,1)}, bf16[272,256]{1,0:T(8,128)(2,1)}) custom-call(f32[256,256]{1,0:T(8,128)} %emb.3, s32[1,512]{1,0:T(1,128)} %bitcast.19, s32[1,512]{1,0:T(1,128)} %bitcast.20, s32[1,512]{1,0:T(1,128)} %bitcast.21, s32[1,512]{1,0:T(1,128)} %neg.1), custom_call_target="tpu_custom_call" | custom-call | bytes 800000 | tf_op jit(solution)/shard_map/pallas_call | solution.py:32
  2.4 14.6 %all-to-all-start = ((bf16[64,8,128]{2,1,0:T(8,128)(2,1)}), bf16[64,8,128]{2,1,0:T(8,128)(2,1)S(1)}, u32[]{:S(2)}, u32[]{:S(2)}) async-start(bf16[64,8,128]{2,1,0:T(8,128)(2,1)} %get-tuple-element.41), calls=%async_computation | async-start | bytes 262144 | tf_op jit(solution)/shard_map/all_to_all | solution.py:48
  17.0 3.3 %collective-permute-start = (bf16[272,256]{1,0:T(8,128)(2,1)}, bf16[272,256]{1,0:T(8,128)(2,1)S(1)}, u32[]{:S(2)}, u32[]{:S(2)}) collective-permute-start(bf16[272,256]{1,0:T(8,128)(2,1)} %get-tuple-element.40.pack0), channel_id=1, source_target_pairs={{0,1},{1,0},{2,3},{3,2},{4,5},{5,4},{6,7},{7,6},{8,9},{9,8},{10,11... | collective-permute-start | bytes 417800 | tf_op jit(solution)/shard_map/ppermute | solution.py:333
  20.3 2.3 %shard_map.121.rel_b = bf16[8,256,256]{2,1,0:T(8,128)(2,1)} custom-call(f32[8,256,256]{2,1,0:T(8,128)} %rel.5), custom_call_target="tpu_custom_call" | custom-call | bytes 3000000 | tf_op jit(solution)/shard_map/pallas_call | solution.py:32
  22.6 1.4 collective-permute-done.pack1
  24.0 3.0 %all-to-all-done.arrived = bf16[64,8,128]{2,1,0:T(8,128)(2,1)S(1)} async-done(((bf16[64,8,128]{2,1,0:T(8,128)(2,1)}), bf16[64,8,128]{2,1,0:T(8,128)(2,1)S(1)}, u32[]{:S(2)}, u32[]{:S(2)}) %all-to-all-start) | async-done | bytes 131104 | tf_op jit(solution)/shard_map/all_to_all | solution.py:48
  27.1 1.3 shard_map.122
  28.4 12.5 %all-to-all-start.1 = ((bf16[128,8,128]{2,1,0:T(8,128)(2,1)}), bf16[128,8,128]{2,1,0:T(8,128)(2,1)S(1)}, u32[]{:S(2)}, u32[]{:S(2)}) async-start(bf16[128,8,128]{2,1,0:T(8,128)(2,1)} %bitcast.7), calls=%async_computation.1 | async-start | bytes 524288 | tf_op jit(solution)/shard_map/all_to_all | solution.py:48
  40.9 4.4 %collective-permute-start.2 = (bf16[272,256]{1,0:T(8,128)(2,1)S(1)}, bf16[272,256]{1,0:T(8,128)(2,1)S(1)}, u32[]{:S(2)}, u32[]{:S(2)}) collective-permute-start(bf16[272,256]{1,0:T(8,128)(2,1)S(1)} %copy-done.9), channel_id=1, source_target_pairs={{0,3},{1,2},{2,1},{3,0},{4,7},{5,6},{6,5},{7,4},{8,11},{9,10},{10,... | collective-permute-start | bytes 417800 | tf_op jit(solution)/shard_map/ppermute | solution.py:333
  45.2 2.4 %collective-permute-start.1 = (bf16[272,256]{1,0:T(8,128)(2,1)S(1)}, bf16[272,256]{1,0:T(8,128)(2,1)S(1)}, u32[]{:S(2)}, u32[]{:S(2)}) collective-permute-start(bf16[272,256]{1,0:T(8,128)(2,1)S(1)} %copy-done.9), channel_id=1, source_target_pairs={{0,2},{1,3},{2,0},{3,1},{4,6},{5,7},{6,4},{7,5},{8,10},{9,11},{10,... | collective-permute-start | bytes 417800 | tf_op jit(solution)/shard_map/ppermute | solution.py:333
  47.7 0.1 pad_add_fusion.place
  47.8 1.2 copy-done.1
  49.0 2.4 %shard_map.123 = (f32[8,512]{1,0:T(8,128)S(1)}, f32[16,512]{1,0:T(8,128)S(1)}, bf16[1024,256]{1,0:T(8,128)(2,1)S(1)}, bf16[1024,256]{1,0:T(8,128)(2,1)S(1)}) custom-call(s32[3]{0:T(128)S(1)} %pad_add_fusion.place, bf16[272,256]{1,0:T(8,128)(2,1)S(1)} %copy-done.9, bf16[272,256]{1,0:T(8,128)(2,1)S(1)} %collective-permute-done.pack1, ...), custom_call_target="tpu_custom_call" | custom-call | flops 1300000000 | bytes 3000000 | tf_op jit(solution)/shard_map/pallas_call | solution.py:32
  51.4 0.8 copy-done.10
  52.2 0.7 collective-permute-done.1.pack0
  52.9 2.4 %shard_map.124 = (f32[8,512]{1,0:T(8,128)S(1)}, f32[16,512]{1,0:T(8,128)S(1)}, bf16[1024,256]{1,0:T(8,128)(2,1)S(1)}, bf16[1024,256]{1,0:T(8,128)(2,1)S(1)}) custom-call(s32[3]{0:T(128)S(1)} %pad_add_fusion.place, bf16[272,256]{1,0:T(8,128)(2,1)S(1)} %collective-permute-done.1.pack0, bf16[272,256]{1,0:T(8,128)(2,1)S(1)} %collective-permute-done.2.pack1, ...), custom_call_target="tpu_custom_call" | custom-call | flops 1300000000 | bytes 3000000 | tf_op jit(solution)/shard_map/pallas_call | solution.py:32
  55.2 0.0 copy-start.12
  55.2 0.8 copy-done.12
  56.0 1.0 copy-done.11
  57.1 1.0 copy-done.13
  58.1 4.9 %shard_map.125 = (bf16[2048,512]{1,0:T(8,128)(2,1)S(1)}, bf16[2048,256]{1,0:T(8,128)(2,1)S(1)}, bf16[4,256,256]{2,1,0:T(8,128)(2,1)S(1)}, bf16[4,256,256]{2,1,0:T(8,128)(2,1)S(1)}) custom-call(s32[3]{0:T(128)S(1)} %pad_add_fusion.place, bf16[64,2,8,128]{3,2,1,0:T(8,128)(2,1)S(1)} %bitcast.17, f32[8,512]{1,0:T(8,128)S(1)} %get-tuple-element.45.counts0, ...), custom_call_target="tpu_custom_call" | custom-call | flops 3200000000 | bytes 6000000 | tf_op jit(solution)/shard_map/pallas_call | solution.py:32
  63.1 3.9 %collective-permute-start.3 = (bf16[4,256,256]{2,1,0:T(8,128)(2,1)S(1)}, bf16[4,256,256]{2,1,0:T(8,128)(2,1)S(1)}, u32[]{:S(2)}, u32[]{:S(2)}) collective-permute-start(bf16[4,256,256]{2,1,0:T(8,128)(2,1)S(1)} %get-tuple-element.57), channel_id=1, source_target_pairs={{0,8},{8,0},{1,9},{9,1},{2,10},{10,2},{3,11},{11,3},{4,12},{12,4},... | collective-permute-start | bytes 1572872 | tf_op jit(solution)/shard_map/ppermute | solution.py:44
  67.0 0.9 shard_map.127.g_rows
  67.9 0.6 collective-permute-done.3.came
  68.5 0.9 shard_map.128
  69.4 3.6 %all-to-all-start.2 = ((bf16[4,256,256]{2,1,0:T(8,128)(2,1)}), bf16[4,256,256]{2,1,0:T(8,128)(2,1)S(1)}, u32[]{:S(2)}, u32[]{:S(2)}) async-start(bf16[4,256,256]{2,1,0:T(8,128)(2,1)} %shard_map.128), calls=%async_computation.2 | async-start | bytes 1048576 | tf_op jit(solution)/shard_map/all_to_all | solution.py:48
  73.1 1.2 copy-done.15
  74.3 3.3 %shard_map.126 = (f32[256,256]{1,0:T(8,128)S(1)}, f32[256,256]{1,0:T(8,128)S(1)}, bf16[2,256,256]{2,1,0:T(8,128)(2,1)S(1)}) custom-call(bf16[2048,256]{1,0:T(8,128)(2,1)S(1)} %copy-done.15, f32[16,512]{1,0:T(8,128)S(1)} %get-tuple-element.47.known0, f32[16,512]{1,0:T(8,128)S(1)} %get-tuple-element.48.known1, bf16[8,256,256]{2,1,0:T(8,128)(2,1)S(1)} %copy-done.2), custom_call_target="tpu_custom_call" | custom-call | flops 3000000000 | bytes 4000000 | tf_op jit(solution)/shard_map/pallas_call | solution.py:32
  77.6 0.7 copy-done.4
  78.3 3.8 %all-to-all-done.2.got = bf16[4,256,256]{2,1,0:T(8,128)(2,1)S(1)} async-done(((bf16[4,256,256]{2,1,0:T(8,128)(2,1)}), bf16[4,256,256]{2,1,0:T(8,128)(2,1)S(1)}, u32[]{:S(2)}, u32[]{:S(2)}) %all-to-all-start.2) | async-done | bytes 524320 | tf_op jit(solution)/shard_map/all_to_all | solution.py:48
  82.1 0.9 shard_map.129
  83.0 14.2 %all-to-all-start.3 = ((bf16[128,3,4,128]{3,2,1,0:T(4,128)(2,1)}), bf16[128,3,4,128]{3,2,1,0:T(4,128)(2,1)S(1)}, u32[]{:S(2)}, u32[]{:S(2)}) async-start(bf16[128,3,4,128]{3,2,1,0:T(4,128)(2,1)} %bitcast.9), calls=%async_computation.3 | async-start | bytes 786432 | tf_op jit(solution)/shard_map/all_to_all | solution.py:48
  97.2 2.2 %collective-permute-start.4 = (bf16[2,256,256]{2,1,0:T(8,128)(2,1)S(1)}, bf16[2,256,256]{2,1,0:T(8,128)(2,1)S(1)}, u32[]{:S(2)}, u32[]{:S(2)}) collective-permute-start(bf16[2,256,256]{2,1,0:T(8,128)(2,1)S(1)} %get-tuple-element.60), channel_id=1, source_target_pairs={{0,2},{1,3},{2,0},{3,1},{4,6},{5,7},{6,4},{7,5},{8,10},{9,11},{10,... | collective-permute-start | bytes 786440 | tf_op jit(solution)/shard_map/ppermute | solution.py:385
  99.4 8.1 %collective-permute-done.4.came.far = bf16[2,256,256]{2,1,0:T(8,128)(2,1)S(1)} collective-permute-done((bf16[2,256,256]{2,1,0:T(8,128)(2,1)S(1)}, bf16[2,256,256]{2,1,0:T(8,128)(2,1)S(1)}, u32[]{:S(2)}, u32[]{:S(2)}) %collective-permute-start.4) | collective-permute-done | bytes 262176 | tf_op jit(solution)/shard_map/ppermute | solution.py:385
  107.5 6.1 %all-to-all-done.3 = bf16[128,3,4,128]{3,2,1,0:T(4,128)(2,1)S(1)} async-done(((bf16[128,3,4,128]{3,2,1,0:T(4,128)(2,1)}), bf16[128,3,4,128]{3,2,1,0:T(4,128)(2,1)S(1)}, u32[]{:S(2)}, u32[]{:S(2)}) %all-to-all-start.3) | async-done | bytes 393248 | tf_op jit(solution)/shard_map/all_to_all | solution.py:48
  113.6 1.5 shard_map.131
  115.1 8.9 %all-to-all-start.4 = ((bf16[128,2,4,128]{3,2,1,0:T(4,128)(2,1)}), bf16[128,2,4,128]{3,2,1,0:T(4,128)(2,1)S(1)}, u32[]{:S(2)}, u32[]{:S(2)}) async-start(bf16[128,2,4,128]{3,2,1,0:T(4,128)(2,1)} %bitcast.11), calls=%async_computation.4 | async-start | bytes 524288 | tf_op jit(solution)/shard_map/all_to_all | solution.py:48
  124.0 2.2 %collective-permute-start.5 = (bf16[256,256]{1,0:T(8,128)(2,1)S(1)}, bf16[256,256]{1,0:T(8,128)(2,1)S(1)}, u32[]{:S(2)}, u32[]{:S(2)}) collective-permute-start(bf16[256,256]{1,0:T(8,128)(2,1)S(1)} %shard_map.130), channel_id=1, source_target_pairs={{0,1},{1,0},{2,3},{3,2},{4,5},{5,4},{6,7},{7,6},{8,9},{9,8},{10,11... | collective-permute-start | bytes 393224 | tf_op jit(solution)/shard_map/ppermute | solution.py:399
  126.2 3.8 %collective-permute-done.5.near = bf16[256,256]{1,0:T(8,128)(2,1)S(1)} collective-permute-done((bf16[256,256]{1,0:T(8,128)(2,1)S(1)}, bf16[256,256]{1,0:T(8,128)(2,1)S(1)}, u32[]{:S(2)}, u32[]{:S(2)}) %collective-permute-start.5) | collective-permute-done | bytes 131104 | tf_op jit(solution)/shard_map/ppermute | solution.py:399
  130.0 8.1 %all-to-all-done.4 = bf16[128,2,4,128]{3,2,1,0:T(4,128)(2,1)S(1)} async-done(((bf16[128,2,4,128]{3,2,1,0:T(4,128)(2,1)}), bf16[128,2,4,128]{3,2,1,0:T(4,128)(2,1)S(1)}, u32[]{:S(2)}, u32[]{:S(2)}) %all-to-all-start.4) | async-done | bytes 262176 | tf_op jit(solution)/shard_map/all_to_all | solution.py:48
  138.1 0.9 shard_map.133
  139.0 3.5 %all-to-all-start.5 = ((bf16[4,256,256]{2,1,0:T(8,128)(2,1)}), bf16[4,256,256]{2,1,0:T(8,128)(2,1)S(1)}, u32[]{:S(2)}, u32[]{:S(2)}) async-start(bf16[4,256,256]{2,1,0:T(8,128)(2,1)} %shard_map.133), calls=%async_computation.5 | async-start | bytes 1048576 | tf_op jit(solution)/shard_map/all_to_all | solution.py:48
  142.5 0.9 copy-done.5
  143.4 1.0 shard_map.132
  144.4 5.6 %all-to-all-done.5.grads = bf16[4,256,256]{2,1,0:T(8,128)(2,1)S(1)} async-done(((bf16[4,256,256]{2,1,0:T(8,128)(2,1)}), bf16[4,256,256]{2,1,0:T(8,128)(2,1)S(1)}, u32[]{:S(2)}, u32[]{:S(2)}) %all-to-all-start.5) | async-done | bytes 524320 | tf_op jit(solution)/shard_map/all_to_all | solution.py:48
  150.0 4.7 %collective-permute-start.6 = (bf16[4,256,256]{2,1,0:T(8,128)(2,1)S(1)}, bf16[4,256,256]{2,1,0:T(8,128)(2,1)S(1)}, u32[]{:S(2)}, u32[]{:S(2)}) collective-permute-start(bf16[4,256,256]{2,1,0:T(8,128)(2,1)S(1)} %all-to-all-done.5.grads), channel_id=1, source_target_pairs={{0,8},{8,0},{1,9},{9,1},{2,10},{10,2},{3,11},{11,3},{4,12},{12,4},... | collective-permute-start | bytes 1572872 | tf_op jit(solution)/shard_map/ppermute | solution.py:44
  154.8 2.2 %shard_map.134 = (f32[8,256,256]{2,1,0:T(8,128)}, f32[8,256]{1,0:T(8,128)S(1)}) custom-call(s32[3]{0:T(128)S(1)} %pad_add_fusion.place, f32[8,256,256]{2,1,0:T(8,128)S(1)} %copy-done, f32[8,256]{1,0:T(8,128)S(1)} %copy-done.6, bf16[4,256,256]{2,1,0:T(8,128)(2,1)S(1)} %all-to-all-done.5.grads), custom_call_target="tpu_custom_call" | custom-call | bytes 3000000 | tf_op jit(solution)/shard_map/pallas_call | solution.py:285
  156.9 2.7 %shard_map.135 = (f32[8,256,256]{2,1,0:T(8,128)}, f32[8,256]{1,0:T(8,128)}) custom-call(s32[3]{0:T(128)S(1)} %pad_add_fusion.place, f32[8,256,256]{2,1,0:T(8,128)S(1)} %copy-done, f32[8,256]{1,0:T(8,128)S(1)} %copy-done.6, bf16[4,256,256]{2,1,0:T(8,128)(2,1)S(1)} %collective-permute-done.6.grads, ...), custom_call_target="tpu_custom_call", output_to_operand_aliasing={{0}: (4, {})} | custom-call | bytes 3000000 | tf_op jit(solution)/shard_map/pallas_call | solution.py:285
  (27 shorter events, 0.1 us)
Async XLA Ops:
  0.6 26.4 %copy-start.7 = (s32[64]{0:T(128)S(1)}, s32[64]{0:T(128)}, u32[]{:S(2)}) copy-start(s32[64]{0:T(128)} %matching.3) | copy-start | bytes 772
  2.4 24.7 %all-to-all-start = ((bf16[64,8,128]{2,1,0:T(8,128)(2,1)}), bf16[64,8,128]{2,1,0:T(8,128)(2,1)S(1)}, u32[]{:S(2)}, u32[]{:S(2)}) async-start(bf16[64,8,128]{2,1,0:T(8,128)(2,1)} %get-tuple-element.41), calls=%async_computation | async-start | bytes 262144 | tf_op jit(solution)/shard_map/all_to_all | solution.py:48
  17.0 23.9 %copy-start.9 = (bf16[272,256]{1,0:T(8,128)(2,1)S(1)}, bf16[272,256]{1,0:T(8,128)(2,1)}, u32[]{:S(2)}) copy-start(bf16[272,256]{1,0:T(8,128)(2,1)} %get-tuple-element.40.pack0) | copy-start | bytes 417796
  17.0 7.0 %collective-permute-start = (bf16[272,256]{1,0:T(8,128)(2,1)}, bf16[272,256]{1,0:T(8,128)(2,1)S(1)}, u32[]{:S(2)}, u32[]{:S(2)}) collective-permute-start(bf16[272,256]{1,0:T(8,128)(2,1)} %get-tuple-element.40.pack0), channel_id=1, source_target_pairs={{0,1},{1,0},{2,3},{3,2},{4,5},{5,4},{6,7},{7,6},{8,9},{9,8},{10,11... | collective-permute-start | bytes 417800 | tf_op jit(solution)/shard_map/ppermute | solution.py:333
  28.4 27.6 %all-to-all-start.1 = ((bf16[128,8,128]{2,1,0:T(8,128)(2,1)}), bf16[128,8,128]{2,1,0:T(8,128)(2,1)S(1)}, u32[]{:S(2)}, u32[]{:S(2)}) async-start(bf16[128,8,128]{2,1,0:T(8,128)(2,1)} %bitcast.7), calls=%async_computation.1 | async-start | bytes 524288 | tf_op jit(solution)/shard_map/all_to_all | solution.py:48
  40.9 11.3 %collective-permute-start.2 = (bf16[272,256]{1,0:T(8,128)(2,1)S(1)}, bf16[272,256]{1,0:T(8,128)(2,1)S(1)}, u32[]{:S(2)}, u32[]{:S(2)}) collective-permute-start(bf16[272,256]{1,0:T(8,128)(2,1)S(1)} %copy-done.9), channel_id=1, source_target_pairs={{0,3},{1,2},{2,1},{3,0},{4,7},{5,6},{6,5},{7,4},{8,11},{9,10},{10,... | collective-permute-start | bytes 417800 | tf_op jit(solution)/shard_map/ppermute | solution.py:333
  45.2 7.6 %collective-permute-start.1 = (bf16[272,256]{1,0:T(8,128)(2,1)S(1)}, bf16[272,256]{1,0:T(8,128)(2,1)S(1)}, u32[]{:S(2)}, u32[]{:S(2)}) collective-permute-start(bf16[272,256]{1,0:T(8,128)(2,1)S(1)} %copy-done.9), channel_id=1, source_target_pairs={{0,2},{1,3},{2,0},{3,1},{4,6},{5,7},{6,4},{7,5},{8,10},{9,11},{10,... | collective-permute-start | bytes 417800 | tf_op jit(solution)/shard_map/ppermute | solution.py:333
  47.8 1.2 copy-start.1
  49.0 3.9 %copy-start.2 = (bf16[8,256,256]{2,1,0:T(8,128)(2,1)S(1)}, bf16[8,256,256]{2,1,0:T(8,128)(2,1)}, u32[]{:S(2)}) copy-start(bf16[8,256,256]{2,1,0:T(8,128)(2,1)} %shard_map.121.rel_b) | copy-start | bytes 3145732
  51.4 0.8 copy-start.10
  55.2 0.8 copy-start.12
  56.0 1.0 copy-start.11
  57.1 1.0 copy-start.13
  63.1 4.9 %copy-start.14 = (bf16[2048,256]{1,0:T(8,128)(2,1)}, bf16[2048,256]{1,0:T(8,128)(2,1)S(1)}, u32[]{:S(2)}) copy-start(bf16[2048,256]{1,0:T(8,128)(2,1)S(1)} %get-tuple-element.53.g_trans) | copy-start | bytes 3145732
  63.1 5.5 %collective-permute-start.3 = (bf16[4,256,256]{2,1,0:T(8,128)(2,1)S(1)}, bf16[4,256,256]{2,1,0:T(8,128)(2,1)S(1)}, u32[]{:S(2)}, u32[]{:S(2)}) collective-permute-start(bf16[4,256,256]{2,1,0:T(8,128)(2,1)S(1)} %get-tuple-element.57), channel_id=1, source_target_pairs={{0,8},{8,0},{1,9},{9,1},{2,10},{10,2},{3,11},{11,3},{4,12},{12,4},... | collective-permute-start | bytes 1572872 | tf_op jit(solution)/shard_map/ppermute | solution.py:44
  69.4 12.7 %all-to-all-start.2 = ((bf16[4,256,256]{2,1,0:T(8,128)(2,1)}), bf16[4,256,256]{2,1,0:T(8,128)(2,1)S(1)}, u32[]{:S(2)}, u32[]{:S(2)}) async-start(bf16[4,256,256]{2,1,0:T(8,128)(2,1)} %shard_map.128), calls=%async_computation.2 | async-start | bytes 1048576 | tf_op jit(solution)/shard_map/all_to_all | solution.py:48
  73.1 1.2 copy-start.15
  77.6 0.7 copy-start.4
  83.0 59.4 %copy-start.3 = (f32[256,256]{1,0:T(8,128)S(1)}, f32[256,256]{1,0:T(8,128)}, u32[]{:S(2)}) copy-start(f32[256,256]{1,0:T(8,128)} %emb.3) | copy-start | bytes 786436
  83.0 59.5 %copy-start.8 = (f32[256]{0:T(256)S(1)}, f32[256]{0:T(256)}, u32[]{:S(2)}) copy-start(f32[256]{0:T(256)} %param.10) | copy-start | bytes 3076
  83.0 30.6 %all-to-all-start.3 = ((bf16[128,3,4,128]{3,2,1,0:T(4,128)(2,1)}), bf16[128,3,4,128]{3,2,1,0:T(4,128)(2,1)S(1)}, u32[]{:S(2)}, u32[]{:S(2)}) async-start(bf16[128,3,4,128]{3,2,1,0:T(4,128)(2,1)} %bitcast.9), calls=%async_computation.3 | async-start | bytes 786432 | tf_op jit(solution)/shard_map/all_to_all | solution.py:48
  97.2 10.3 %collective-permute-start.4 = (bf16[2,256,256]{2,1,0:T(8,128)(2,1)S(1)}, bf16[2,256,256]{2,1,0:T(8,128)(2,1)S(1)}, u32[]{:S(2)}, u32[]{:S(2)}) collective-permute-start(bf16[2,256,256]{2,1,0:T(8,128)(2,1)S(1)} %get-tuple-element.60), channel_id=1, source_target_pairs={{0,2},{1,3},{2,0},{3,1},{4,6},{5,7},{6,4},{7,5},{8,10},{9,11},{10,... | collective-permute-start | bytes 786440 | tf_op jit(solution)/shard_map/ppermute | solution.py:385
  115.1 39.6 %copy-start = (f32[8,256,256]{2,1,0:T(8,128)S(1)}, f32[8,256,256]{2,1,0:T(8,128)}, u32[]{:S(2)}) copy-start(f32[8,256,256]{2,1,0:T(8,128)} %rel.5) | copy-start | bytes 6291460
  115.1 39.6 %copy-start.6 = (f32[8,256]{1,0:T(8,128)S(1)}, f32[8,256]{1,0:T(8,128)}, u32[]{:S(2)}) copy-start(f32[8,256]{1,0:T(8,128)} %accum.3) | copy-start | bytes 24580
  115.1 23.0 %all-to-all-start.4 = ((bf16[128,2,4,128]{3,2,1,0:T(4,128)(2,1)}), bf16[128,2,4,128]{3,2,1,0:T(4,128)(2,1)S(1)}, u32[]{:S(2)}, u32[]{:S(2)}) async-start(bf16[128,2,4,128]{3,2,1,0:T(4,128)(2,1)} %bitcast.11), calls=%async_computation.4 | async-start | bytes 524288 | tf_op jit(solution)/shard_map/all_to_all | solution.py:48
  124.0 6.0 %collective-permute-start.5 = (bf16[256,256]{1,0:T(8,128)(2,1)S(1)}, bf16[256,256]{1,0:T(8,128)(2,1)S(1)}, u32[]{:S(2)}, u32[]{:S(2)}) collective-permute-start(bf16[256,256]{1,0:T(8,128)(2,1)S(1)} %shard_map.130), channel_id=1, source_target_pairs={{0,1},{1,0},{2,3},{3,2},{4,5},{5,4},{6,7},{7,6},{8,9},{9,8},{10,11... | collective-permute-start | bytes 393224 | tf_op jit(solution)/shard_map/ppermute | solution.py:399
  139.0 11.1 %all-to-all-start.5 = ((bf16[4,256,256]{2,1,0:T(8,128)(2,1)}), bf16[4,256,256]{2,1,0:T(8,128)(2,1)S(1)}, u32[]{:S(2)}, u32[]{:S(2)}) async-start(bf16[4,256,256]{2,1,0:T(8,128)(2,1)} %shard_map.133), calls=%async_computation.5 | async-start | bytes 1048576 | tf_op jit(solution)/shard_map/all_to_all | solution.py:48
  142.5 1.0 copy-start.5
  150.0 6.9 %collective-permute-start.6 = (bf16[4,256,256]{2,1,0:T(8,128)(2,1)S(1)}, bf16[4,256,256]{2,1,0:T(8,128)(2,1)S(1)}, u32[]{:S(2)}, u32[]{:S(2)}) collective-permute-start(bf16[4,256,256]{2,1,0:T(8,128)(2,1)S(1)} %all-to-all-done.5.grads), channel_id=1, source_target_pairs={{0,8},{8,0},{1,9},{9,1},{2,10},{10,2},{3,11},{11,3},{4,12},{12,4},... | collective-permute-start | bytes 1572872 | tf_op jit(solution)/shard_map/ppermute | solution.py:44

commit v10 on v9

--- a/solution.py
+++ b/solution.py
@@ -112,53 +112,64 @@
         copy.wait()
 
 
+def span_work(x, pack, stack):
+    index = indices(pack[256:272, :])
+    column = columns(index)
+    hot = (column[:, 0:1] == lane_ids(512, 256).astype(f32)).astype(f32).astype(bf16)
+    rows = dot(hot, pack[0:256, :]).astype(bf16)
+    turned = dot(by_relation(column[:, 1:2], rows), stack, NT).astype(bf16)
+    hits = (column[:, 3:4] == row_ids(x, 512)).astype(f32)
+    return index, rows, turned, jnp.sum(hits, axis=0, keepdims=True)
+
+
 def trans_kernel(place, pack0, pack1, rel_b, counts, known, trans, source):
     stack = jnp.concatenate([rel_b[r] for r in range(8)], axis=1)
-    ids = lane_ids(512, 256).astype(f32)
-    wide = row_ids(place[2], 512)
     for s, pack in enumerate((pack0, pack1)):
-        index = indices(pack[256:272, :])
+        index, rows, turned, count = span_work(place[2], pack, stack)
         known[s * 8 : (s + 1) * 8, :] = jnp.concatenate([index, index], axis=0)
-        column = columns(index)
-        hot = (column[:, 0:1] == ids).astype(f32).astype(bf16)
-        rows = dot(hot, pack[0:256, :]).astype(bf16)
         source[s * 512 : (s + 1) * 512, :] = rows
-        part = by_relation(column[:, 1:2], rows)
-        trans[s * 512 : (s + 1) * 512, :] = dot(part, stack, NT).astype(bf16)
-        hits = (column[:, 3:4] == wide).astype(f32)
-        counts[s : s + 1, :] = jnp.sum(hits, axis=0, keepdims=True)
+        trans[s * 512 : (s + 1) * 512, :] = turned
+        counts[s : s + 1, :] = count
     counts[2:8, :] = jnp.zeros((6, 512), f32)
 
 
 def score_kernel(
-    place, rows_in, counts0, counts1, known0, known1, trans0, trans1, source0, source1,
-    weight, g_trans, kept, given, rows
+    place, rows_in, pack2, pack3, rel_b, counts, known, trans, source,
+    weight, g_trans, kept, given, known1, trans1, rows, source1
 ):
     core = place[0]
     for z in range(2):
         both = rows_in[:, z].reshape(2, 256, 128)
         rows[z * 256 : (z + 1) * 256, :] = jnp.concatenate([both[0], both[1]], axis=1)
-    index = [known[s * 8 : s * 8 + 4, :] for known in (known0, known1) for s in range(2)]
+    index = [known[s * 8 : s * 8 + 4, :] for s in range(2)]
+    count = [counts[s : s + 1, :] for s in range(2)]
+    stack = jnp.concatenate([rel_b[r] for r in range(8)], axis=1)
+    for s, pack in enumerate((pack2, pack3)):
+        one, away, turned, many = span_work(place[2], pack, stack)
+        known1[s * 8 : (s + 1) * 8, :] = jnp.concatenate([one, one], axis=0)
+        source1[s * 512 : (s + 1) * 512, :] = away
+        trans1[s * 512 : (s + 1) * 512, :] = turned
+        index.append(one)
+        count.append(many)
     ids = row_ids(place[2], 256)
     for b in range(8):
         s = b // 2
         column = columns(index[s])[(b % 2) * 256 : (b % 2 + 1) * 256]
         span = slice(b * 256, (b + 1) * 256)
-        trans = (trans0, trans1)[b // 4][(b % 4) * 256 : (b % 4 + 1) * 256, :]
-        score = dot(trans, rows[...], NT)
+        turned = (trans, trans1)[b // 4][(b % 4) * 256 : (b % 4 + 1) * 256, :]
+        score = dot(turned, rows[...], NT)
         sig = 1.0 / (1.0 + jnp.exp(-score))
-        count = (counts0, counts1)[s // 2][s % 2 : s % 2 + 1, :]
         hit = column[:, 2:3] == ids
-        part = jnp.where(hit, (count + 1.0) * sig - 1.0, count * sig).astype(bf16)
+        part = jnp.where(hit, (count[s] + 1.0) * sig - 1.0, count[s] * sig).astype(bf16)
         weight[span, :] = part
         g_trans[span, :] = dot(part, rows[...]).astype(bf16)
     turned = g_trans[...].astype(f32).T
     kinds = jnp.concatenate([part[1:2] for part in index], axis=1)
-    source = jnp.concatenate([source0[...], source1[...]], axis=0)
+    every = jnp.concatenate([source[...], source1[...]], axis=0)
     for r in range(8):
         wanted = r + 4 * core if r < 4 else r - 4 * core
         masked = jnp.where(kinds == wanted.astype(f32), turned, 0.0).astype(bf16)
-        grad = dot(masked, source).astype(bf16)
+        grad = dot(masked, every).astype(bf16)
         if r < 4:
             kept[r] = grad
         else:
@@ -336,36 +347,33 @@
     routed = call(take_kernel, shape((64, 2, 8, 128), bf16), 1, (matching, arrived), moved=400_000)
     rows_in = spread(routed.reshape(128, 8, 128), DOM_Z).reshape(64, 2, 8, 128)
     block = shape((1024, 256), bf16)
-    halves = [
-        call(
-            trans_kernel,
-            (shape((8, 512), f32), shape((16, 512), f32), block, block),
-            1,
-            (place, packs[k], packs[k + 1], rel_b),
-            flops=1_300_000_000,
-            moved=3_000_000,
-            space=16,
-        )
-        for k in (0, 2)
-    ]
-    counts, known, trans, source = zip(*halves)
+    known_shape = shape((16, 512), f32)
+    counts, known0, trans0, source0 = call(
+        trans_kernel,
+        (shape((8, 512), f32), known_shape, block, block),
+        1,
+        (place, packs[0], packs[1], rel_b),
+        flops=1_300_000_000,
+        moved=3_000_000,
+        space=16,
+    )
     four = shape((4, 256, 256), bf16)
-    weight, g_trans, kept, given = call(
+    weight, g_trans, kept, given, known1, trans1 = call(
         score_kernel,
-        (shape((2048, 512), bf16), shape((2048, 256), bf16), four, four),
+        (shape((2048, 512), bf16), shape((2048, 256), bf16), four, four, known_shape, block),
         1,
-        (place, rows_in, *counts, *known, *trans, *source),
-        flops=3_200_000_000,
+        (place, rows_in, packs[2], packs[3], rel_b, counts, known0, trans0, source0),
+        flops=4_500_000_000,
         moved=6_000_000,
-        scratch=[pltpu.VMEM((512, 256), bf16)],
-        space=20,
+        scratch=[pltpu.VMEM((512, 256), bf16), pltpu.VMEM((1024, 256), bf16)],
+        space=28,
     )
     came = swap(given, "core")
     g_rows = call(
         partner_kernel,
         shape((2, 256, 256), bf16),
         0,
-        (weight, *trans),
+        (weight, trans0, trans1),
         flops=1_500_000_000,
         moved=4_000_000,
         space=16,
@@ -376,7 +384,7 @@
         own_kernel,
         (shape((256, 256), f32), shape((256, 256), f32), shape((2, 256, 256), bf16)),
         0,
-        (g_trans, *known, rel_b),
+        (g_trans, known0, known1, rel_b),
         flops=3_000_000_000,
         moved=4_000_000,
         space=16,

time: 161 us -> 157 us (0.975)
  local copies, waits for them, and re-layouts: 7.77 us -> 4.13 us
  waiting for transfers between devices: 41.2 us -> 44 us
  starting transfers between devices: 80.3 us -> 78.3 us
    unnamed x32 -> x24, local copies, waits for them, and re-layouts: 7.77 us -> 4.13 us
    all_to_all x6, waiting for transfers between devices: 26.6 us -> 28.6 us  [spread(): return lax.all_to_all(value, axis, split_axis=0, concat_axis=0, tiled=True)]
    pallas_call x14 -> x13, Pallas kernels: 24.4 us -> 24 us  [call(): pl.pallas_call(kernel, out_shape=outs, in_specs=specs, out_specs=tuple((A...]
  transfers between devices with their start and end apart: 13 -> 13, of which waited for: 10 -> 11; matrix products, arithmetic and copies ran while one was open for 0% -> 0% of each run, Pallas kernels for 9% -> 8%
where the time goes in v10:
time: 157 us; the launch traced here: 156 us
  starting transfers between devices  78.3 us (50%)
  waiting for transfers between devices  44 us (28%)
  Pallas kernels  28.8 us (18%)
  local copies, waits for them, and re-layouts  4.13 us (3%)
    all_to_all x6, starting transfers between devices, spread(): return lax.all_to_all(value, axis, split_axis=0, concat_axis=0, tiled=True)  55.7 us
    all_to_all x6, waiting for transfers between devices, spread(): return lax.all_to_all(value, axis, split_axis=0, concat_axis=0, tiled=True)  28.6 us
    pallas_call x13, Pallas kernels, call(): pl.pallas_call(kernel, out_shape=outs, in_specs=specs, out_specs=tuple((A...  24 us
    ppermute x3, starting transfers between devices, body(): lax.ppermute(pack, 'x', [(i, i ^ k) for i in range(4)])  10.1 us
    ppermute x2, starting transfers between devices, swap(): return lax.ppermute(value, axis, [(0, 1), (1, 0)])  8.2 us
    ppermute x1, waiting for transfers between devices, body(): far = lax.ppermute(far, 'x', [(i, i ^ 2) for i in range(4)])  8.12 us
    pallas_call x2, Pallas kernels, update_half(): pl.pallas_call(update_kernel, out_shape=(shape((8, 256, 256), f32), shape...  4.89 us
    unnamed x24, local copies, waits for them, and re-layouts  4.13 us
  transfers between devices with their start and end apart: 13, of which 11 were waited for; matrix products, arithmetic and copies ran while one was open for 0% of the time, Pallas kernels for 8%

profile of v10, /device:TPU:1, one launch (start us, length us, event | category | flops | bytes accessed | tf_op | source)
XLA Modules:
  0.0 156.5 jit_solution(11015529163763636219)
XLA Ops:
  0.6 1.7 %shard_map.120 = (bf16[64,8,128]{2,1,0:T(8,128)(2,1)}, bf16[272,256]{1,0:T(8,128)(2,1)}) custom-call(f32[256,256]{1,0:T(8,128)} %emb.3, s32[1,512]{1,0:T(1,128)} %bitcast.19, s32[1,512]{1,0:T(1,128)} %bitcast.20, s32[1,512]{1,0:T(1,128)} %bitcast.21, s32[1,512]{1,0:T(1,128)} %neg.1), custom_call_target="tpu_custom_call" | custom-call | bytes 800000 | tf_op jit(solution)/shard_map/pallas_call | solution.py:32
  2.4 14.6 %all-to-all-start = ((bf16[64,8,128]{2,1,0:T(8,128)(2,1)}), bf16[64,8,128]{2,1,0:T(8,128)(2,1)S(1)}, u32[]{:S(2)}, u32[]{:S(2)}) async-start(bf16[64,8,128]{2,1,0:T(8,128)(2,1)} %get-tuple-element.39), calls=%async_computation | async-start | bytes 262144 | tf_op jit(solution)/shard_map/all_to_all | solution.py:48
  17.0 3.3 %collective-permute-start = (bf16[272,256]{1,0:T(8,128)(2,1)}, bf16[272,256]{1,0:T(8,128)(2,1)S(1)}, u32[]{:S(2)}, u32[]{:S(2)}) collective-permute-start(bf16[272,256]{1,0:T(8,128)(2,1)} %get-tuple-element.38.pack0), channel_id=1, source_target_pairs={{0,1},{1,0},{2,3},{3,2},{4,5},{5,4},{6,7},{7,6},{8,9},{9,8},{10,11... | collective-permute-start | bytes 417800 | tf_op jit(solution)/shard_map/ppermute | solution.py:344
  20.3 2.3 %shard_map.121.rel_b = bf16[8,256,256]{2,1,0:T(8,128)(2,1)} custom-call(f32[8,256,256]{2,1,0:T(8,128)} %rel.5), custom_call_target="tpu_custom_call" | custom-call | bytes 3000000 | tf_op jit(solution)/shard_map/pallas_call | solution.py:32
  22.6 1.4 collective-permute-done.pack1
  24.0 3.0 %all-to-all-done.arrived = bf16[64,8,128]{2,1,0:T(8,128)(2,1)S(1)} async-done(((bf16[64,8,128]{2,1,0:T(8,128)(2,1)}), bf16[64,8,128]{2,1,0:T(8,128)(2,1)S(1)}, u32[]{:S(2)}, u32[]{:S(2)}) %all-to-all-start) | async-done | bytes 131104 | tf_op jit(solution)/shard_map/all_to_all | solution.py:48
  27.1 1.3 shard_map.122
  28.4 12.5 %all-to-all-start.1 = ((bf16[128,8,128]{2,1,0:T(8,128)(2,1)}), bf16[128,8,128]{2,1,0:T(8,128)(2,1)S(1)}, u32[]{:S(2)}, u32[]{:S(2)}) async-start(bf16[128,8,128]{2,1,0:T(8,128)(2,1)} %bitcast.7), calls=%async_computation.1 | async-start | bytes 524288 | tf_op jit(solution)/shard_map/all_to_all | solution.py:48
  40.9 4.4 %collective-permute-start.2 = (bf16[272,256]{1,0:T(8,128)(2,1)S(1)}, bf16[272,256]{1,0:T(8,128)(2,1)S(1)}, u32[]{:S(2)}, u32[]{:S(2)}) collective-permute-start(bf16[272,256]{1,0:T(8,128)(2,1)S(1)} %copy-done.9), channel_id=1, source_target_pairs={{0,3},{1,2},{2,1},{3,0},{4,7},{5,6},{6,5},{7,4},{8,11},{9,10},{10,... | collective-permute-start | bytes 417800 | tf_op jit(solution)/shard_map/ppermute | solution.py:344
  45.2 2.4 %collective-permute-start.1 = (bf16[272,256]{1,0:T(8,128)(2,1)S(1)}, bf16[272,256]{1,0:T(8,128)(2,1)S(1)}, u32[]{:S(2)}, u32[]{:S(2)}) collective-permute-start(bf16[272,256]{1,0:T(8,128)(2,1)S(1)} %copy-done.9), channel_id=1, source_target_pairs={{0,2},{1,3},{2,0},{3,1},{4,6},{5,7},{6,4},{7,5},{8,10},{9,11},{10,... | collective-permute-start | bytes 417800 | tf_op jit(solution)/shard_map/ppermute | solution.py:344
  47.7 0.1 pad_add_fusion.place
  47.8 1.2 copy-done.1
  49.0 2.4 %shard_map.123 = (f32[8,512]{1,0:T(8,128)S(1)}, f32[16,512]{1,0:T(8,128)S(1)}, bf16[1024,256]{1,0:T(8,128)(2,1)S(1)}, bf16[1024,256]{1,0:T(8,128)(2,1)S(1)}) custom-call(s32[3]{0:T(128)S(1)} %pad_add_fusion.place, bf16[272,256]{1,0:T(8,128)(2,1)S(1)} %copy-done.9, bf16[272,256]{1,0:T(8,128)(2,1)S(1)} %collective-permute-done.pack1, ...), custom_call_target="tpu_custom_call" | custom-call | flops 1300000000 | bytes 3000000 | tf_op jit(solution)/shard_map/pallas_call | solution.py:32
  51.4 0.0 collective-permute-done.2.pack3
  51.4 1.5 collective-permute-done.1.pack2
  52.8 2.1 %all-to-all-done.1 = bf16[128,8,128]{2,1,0:T(8,128)(2,1)S(1)} async-done(((bf16[128,8,128]{2,1,0:T(8,128)(2,1)}), bf16[128,8,128]{2,1,0:T(8,128)(2,1)S(1)}, u32[]{:S(2)}, u32[]{:S(2)}) %all-to-all-start.1) | async-done | bytes 262176 | tf_op jit(solution)/shard_map/all_to_all | solution.py:48
  54.9 6.8 %shard_map.124 = (bf16[2048,512]{1,0:T(8,128)(2,1)S(1)}, bf16[2048,256]{1,0:T(8,128)(2,1)S(1)}, bf16[4,256,256]{2,1,0:T(8,128)(2,1)S(1)}, bf16[4,256,256]{2,1,0:...) custom-call(s32[3]{0:T(128)S(1)} %pad_add_fusion.place, bf16[64,2,8,128]{3,2,1,0:T(8,128)(2,1)S(1)} %bitcast.17, ...), custom_call_target="tpu_custom_call" | custom-call | flops 4499999744 | bytes 6000000 | tf_op jit(solution)/shard_map/pallas_call | solution.py:32
  61.8 0.0 copy-start.10
  61.8 3.5 %collective-permute-start.3 = (bf16[4,256,256]{2,1,0:T(8,128)(2,1)S(1)}, bf16[4,256,256]{2,1,0:T(8,128)(2,1)S(1)}, u32[]{:S(2)}, u32[]{:S(2)}) collective-permute-start(bf16[4,256,256]{2,1,0:T(8,128)(2,1)S(1)} %get-tuple-element.52), channel_id=1, source_target_pairs={{0,8},{8,0},{1,9},{9,1},{2,10},{10,2},{3,11},{11,3},{4,12},{12,4},... | collective-permute-start | bytes 1572872 | tf_op jit(solution)/shard_map/ppermute | solution.py:44
  65.3 0.9 shard_map.126.g_rows
  66.2 0.6 collective-permute-done.3.came
  66.8 0.9 shard_map.127
  67.7 4.0 %all-to-all-start.2 = ((bf16[4,256,256]{2,1,0:T(8,128)(2,1)}), bf16[4,256,256]{2,1,0:T(8,128)(2,1)S(1)}, u32[]{:S(2)}, u32[]{:S(2)}) async-start(bf16[4,256,256]{2,1,0:T(8,128)(2,1)} %shard_map.127), calls=%async_computation.2 | async-start | bytes 1048576 | tf_op jit(solution)/shard_map/all_to_all | solution.py:48
  71.8 1.2 copy-done.11
  73.0 3.3 %shard_map.125 = (f32[256,256]{1,0:T(8,128)S(1)}, f32[256,256]{1,0:T(8,128)S(1)}, bf16[2,256,256]{2,1,0:T(8,128)(2,1)S(1)}) custom-call(bf16[2048,256]{1,0:T(8,128)(2,1)S(1)} %copy-done.11, f32[16,512]{1,0:T(8,128)S(1)} %get-tuple-element.44.known.known0, f32[16,512]{1,0:T(8,128)S(1)} %get-tuple-element.48.known1, bf16[8,256,256]{2,1,0:T(8,128)(2,1)S(1)} %copy-done.2), custom_call_target="tpu_custom_call" | custom-call | flops 3000000000 | bytes 4000000 | tf_op jit(solution)/shard_map/pallas_call | solution.py:32
  76.3 0.0 copy-start.4
  76.3 0.7 copy-done.4
  77.0 3.7 %all-to-all-done.2.got = bf16[4,256,256]{2,1,0:T(8,128)(2,1)S(1)} async-done(((bf16[4,256,256]{2,1,0:T(8,128)(2,1)}), bf16[4,256,256]{2,1,0:T(8,128)(2,1)S(1)}, u32[]{:S(2)}, u32[]{:S(2)}) %all-to-all-start.2) | async-done | bytes 524320 | tf_op jit(solution)/shard_map/all_to_all | solution.py:48
  80.7 0.9 shard_map.128
  81.6 12.3 %all-to-all-start.3 = ((bf16[128,3,4,128]{3,2,1,0:T(4,128)(2,1)}), bf16[128,3,4,128]{3,2,1,0:T(4,128)(2,1)S(1)}, u32[]{:S(2)}, u32[]{:S(2)}) async-start(bf16[128,3,4,128]{3,2,1,0:T(4,128)(2,1)} %bitcast.9), calls=%async_computation.3 | async-start | bytes 786432 | tf_op jit(solution)/shard_map/all_to_all | solution.py:48
  93.9 2.2 %collective-permute-start.4 = (bf16[2,256,256]{2,1,0:T(8,128)(2,1)S(1)}, bf16[2,256,256]{2,1,0:T(8,128)(2,1)S(1)}, u32[]{:S(2)}, u32[]{:S(2)}) collective-permute-start(bf16[2,256,256]{2,1,0:T(8,128)(2,1)S(1)} %get-tuple-element.56), channel_id=1, source_target_pairs={{0,2},{1,3},{2,0},{3,1},{4,6},{5,7},{6,4},{7,5},{8,10},{9,11},{10,... | collective-permute-start | bytes 786440 | tf_op jit(solution)/shard_map/ppermute | solution.py:393
  96.1 8.1 %collective-permute-done.4.came.far = bf16[2,256,256]{2,1,0:T(8,128)(2,1)S(1)} collective-permute-done((bf16[2,256,256]{2,1,0:T(8,128)(2,1)S(1)}, bf16[2,256,256]{2,1,0:T(8,128)(2,1)S(1)}, u32[]{:S(2)}, u32[]{:S(2)}) %collective-permute-start.4) | collective-permute-done | bytes 262176 | tf_op jit(solution)/shard_map/ppermute | solution.py:393
  104.2 6.1 %all-to-all-done.3 = bf16[128,3,4,128]{3,2,1,0:T(4,128)(2,1)S(1)} async-done(((bf16[128,3,4,128]{3,2,1,0:T(4,128)(2,1)}), bf16[128,3,4,128]{3,2,1,0:T(4,128)(2,1)S(1)}, u32[]{:S(2)}, u32[]{:S(2)}) %all-to-all-start.3) | async-done | bytes 393248 | tf_op jit(solution)/shard_map/all_to_all | solution.py:48
  110.3 1.5 shard_map.130
  111.8 8.9 %all-to-all-start.4 = ((bf16[128,2,4,128]{3,2,1,0:T(4,128)(2,1)}), bf16[128,2,4,128]{3,2,1,0:T(4,128)(2,1)S(1)}, u32[]{:S(2)}, u32[]{:S(2)}) async-start(bf16[128,2,4,128]{3,2,1,0:T(4,128)(2,1)} %bitcast.11), calls=%async_computation.4 | async-start | bytes 524288 | tf_op jit(solution)/shard_map/all_to_all | solution.py:48
  120.7 2.2 %collective-permute-start.5 = (bf16[256,256]{1,0:T(8,128)(2,1)S(1)}, bf16[256,256]{1,0:T(8,128)(2,1)S(1)}, u32[]{:S(2)}, u32[]{:S(2)}) collective-permute-start(bf16[256,256]{1,0:T(8,128)(2,1)S(1)} %shard_map.129), channel_id=1, source_target_pairs={{0,1},{1,0},{2,3},{3,2},{4,5},{5,4},{6,7},{7,6},{8,9},{9,8},{10,11... | collective-permute-start | bytes 393224 | tf_op jit(solution)/shard_map/ppermute | solution.py:407
  122.9 3.8 %collective-permute-done.5.near = bf16[256,256]{1,0:T(8,128)(2,1)S(1)} collective-permute-done((bf16[256,256]{1,0:T(8,128)(2,1)S(1)}, bf16[256,256]{1,0:T(8,128)(2,1)S(1)}, u32[]{:S(2)}, u32[]{:S(2)}) %collective-permute-start.5) | collective-permute-done | bytes 131104 | tf_op jit(solution)/shard_map/ppermute | solution.py:407
  126.7 8.1 %all-to-all-done.4 = bf16[128,2,4,128]{3,2,1,0:T(4,128)(2,1)S(1)} async-done(((bf16[128,2,4,128]{3,2,1,0:T(4,128)(2,1)}), bf16[128,2,4,128]{3,2,1,0:T(4,128)(2,1)S(1)}, u32[]{:S(2)}, u32[]{:S(2)}) %all-to-all-start.4) | async-done | bytes 262176 | tf_op jit(solution)/shard_map/all_to_all | solution.py:48
  134.8 0.9 shard_map.132
  135.6 3.5 %all-to-all-start.5 = ((bf16[4,256,256]{2,1,0:T(8,128)(2,1)}), bf16[4,256,256]{2,1,0:T(8,128)(2,1)S(1)}, u32[]{:S(2)}, u32[]{:S(2)}) async-start(bf16[4,256,256]{2,1,0:T(8,128)(2,1)} %shard_map.132), calls=%async_computation.5 | async-start | bytes 1048576 | tf_op jit(solution)/shard_map/all_to_all | solution.py:48
  139.1 0.0 copy-start.5
  139.1 0.9 copy-done.5
  140.1 1.0 shard_map.131
  141.1 5.6 %all-to-all-done.5.grads = bf16[4,256,256]{2,1,0:T(8,128)(2,1)S(1)} async-done(((bf16[4,256,256]{2,1,0:T(8,128)(2,1)}), bf16[4,256,256]{2,1,0:T(8,128)(2,1)S(1)}, u32[]{:S(2)}, u32[]{:S(2)}) %all-to-all-start.5) | async-done | bytes 524320 | tf_op jit(solution)/shard_map/all_to_all | solution.py:48
  146.7 4.7 %collective-permute-start.6 = (bf16[4,256,256]{2,1,0:T(8,128)(2,1)S(1)}, bf16[4,256,256]{2,1,0:T(8,128)(2,1)S(1)}, u32[]{:S(2)}, u32[]{:S(2)}) collective-permute-start(bf16[4,256,256]{2,1,0:T(8,128)(2,1)S(1)} %all-to-all-done.5.grads), channel_id=1, source_target_pairs={{0,8},{8,0},{1,9},{9,1},{2,10},{10,2},{3,11},{11,3},{4,12},{12,4},... | collective-permute-start | bytes 1572872 | tf_op jit(solution)/shard_map/ppermute | solution.py:44
  151.4 2.2 %shard_map.133 = (f32[8,256,256]{2,1,0:T(8,128)}, f32[8,256]{1,0:T(8,128)S(1)}) custom-call(s32[3]{0:T(128)S(1)} %pad_add_fusion.place, f32[8,256,256]{2,1,0:T(8,128)S(1)} %copy-done, f32[8,256]{1,0:T(8,128)S(1)} %copy-done.6, bf16[4,256,256]{2,1,0:T(8,128)(2,1)S(1)} %all-to-all-done.5.grads), custom_call_target="tpu_custom_call" | custom-call | bytes 3000000 | tf_op jit(solution)/shard_map/pallas_call | solution.py:296
  153.6 0.0 collective-permute-done.6.grads
  153.6 2.7 %shard_map.134 = (f32[8,256,256]{2,1,0:T(8,128)}, f32[8,256]{1,0:T(8,128)}) custom-call(s32[3]{0:T(128)S(1)} %pad_add_fusion.place, f32[8,256,256]{2,1,0:T(8,128)S(1)} %copy-done, f32[8,256]{1,0:T(8,128)S(1)} %copy-done.6, bf16[4,256,256]{2,1,0:T(8,128)(2,1)S(1)} %collective-permute-done.6.grads, ...), custom_call_target="tpu_custom_call", output_to_operand_aliasing={{0}: (4, {})} | custom-call | bytes 3000000 | tf_op jit(solution)/shard_map/pallas_call | solution.py:296
  (18 shorter events, 0.1 us)
Async XLA Ops:
  0.6 26.4 %copy-start.7 = (s32[64]{0:T(128)S(1)}, s32[64]{0:T(128)}, u32[]{:S(2)}) copy-start(s32[64]{0:T(128)} %matching.3) | copy-start | bytes 772
  2.4 24.7 %all-to-all-start = ((bf16[64,8,128]{2,1,0:T(8,128)(2,1)}), bf16[64,8,128]{2,1,0:T(8,128)(2,1)S(1)}, u32[]{:S(2)}, u32[]{:S(2)}) async-start(bf16[64,8,128]{2,1,0:T(8,128)(2,1)} %get-tuple-element.39), calls=%async_computation | async-start | bytes 262144 | tf_op jit(solution)/shard_map/all_to_all | solution.py:48
  17.0 23.9 %copy-start.9 = (bf16[272,256]{1,0:T(8,128)(2,1)S(1)}, bf16[272,256]{1,0:T(8,128)(2,1)}, u32[]{:S(2)}) copy-start(bf16[272,256]{1,0:T(8,128)(2,1)} %get-tuple-element.38.pack0) | copy-start | bytes 417796
  17.0 7.0 %collective-permute-start = (bf16[272,256]{1,0:T(8,128)(2,1)}, bf16[272,256]{1,0:T(8,128)(2,1)S(1)}, u32[]{:S(2)}, u32[]{:S(2)}) collective-permute-start(bf16[272,256]{1,0:T(8,128)(2,1)} %get-tuple-element.38.pack0), channel_id=1, source_target_pairs={{0,1},{1,0},{2,3},{3,2},{4,5},{5,4},{6,7},{7,6},{8,9},{9,8},{10,11... | collective-permute-start | bytes 417800 | tf_op jit(solution)/shard_map/ppermute | solution.py:344
  28.4 26.6 %all-to-all-start.1 = ((bf16[128,8,128]{2,1,0:T(8,128)(2,1)}), bf16[128,8,128]{2,1,0:T(8,128)(2,1)S(1)}, u32[]{:S(2)}, u32[]{:S(2)}) async-start(bf16[128,8,128]{2,1,0:T(8,128)(2,1)} %bitcast.7), calls=%async_computation.1 | async-start | bytes 524288 | tf_op jit(solution)/shard_map/all_to_all | solution.py:48
  40.9 10.5 %collective-permute-start.2 = (bf16[272,256]{1,0:T(8,128)(2,1)S(1)}, bf16[272,256]{1,0:T(8,128)(2,1)S(1)}, u32[]{:S(2)}, u32[]{:S(2)}) collective-permute-start(bf16[272,256]{1,0:T(8,128)(2,1)S(1)} %copy-done.9), channel_id=1, source_target_pairs={{0,3},{1,2},{2,1},{3,0},{4,7},{5,6},{6,5},{7,4},{8,11},{9,10},{10,... | collective-permute-start | bytes 417800 | tf_op jit(solution)/shard_map/ppermute | solution.py:344
  45.2 7.6 %collective-permute-start.1 = (bf16[272,256]{1,0:T(8,128)(2,1)S(1)}, bf16[272,256]{1,0:T(8,128)(2,1)S(1)}, u32[]{:S(2)}, u32[]{:S(2)}) collective-permute-start(bf16[272,256]{1,0:T(8,128)(2,1)S(1)} %copy-done.9), channel_id=1, source_target_pairs={{0,2},{1,3},{2,0},{3,1},{4,6},{5,7},{6,4},{7,5},{8,10},{9,11},{10,... | collective-permute-start | bytes 417800 | tf_op jit(solution)/shard_map/ppermute | solution.py:344
  47.8 1.2 copy-start.1
  49.0 6.0 %copy-start.2 = (bf16[8,256,256]{2,1,0:T(8,128)(2,1)S(1)}, bf16[8,256,256]{2,1,0:T(8,128)(2,1)}, u32[]{:S(2)}) copy-start(bf16[8,256,256]{2,1,0:T(8,128)(2,1)} %shard_map.121.rel_b) | copy-start | bytes 3145732
  61.8 4.4 %copy-start.10 = (bf16[2048,256]{1,0:T(8,128)(2,1)}, bf16[2048,256]{1,0:T(8,128)(2,1)S(1)}, u32[]{:S(2)}) copy-start(bf16[2048,256]{1,0:T(8,128)(2,1)S(1)} %get-tuple-element.47.g_trans) | copy-start | bytes 3145732
  61.8 5.0 %collective-permute-start.3 = (bf16[4,256,256]{2,1,0:T(8,128)(2,1)S(1)}, bf16[4,256,256]{2,1,0:T(8,128)(2,1)S(1)}, u32[]{:S(2)}, u32[]{:S(2)}) collective-permute-start(bf16[4,256,256]{2,1,0:T(8,128)(2,1)S(1)} %get-tuple-element.52), channel_id=1, source_target_pairs={{0,8},{8,0},{1,9},{9,1},{2,10},{10,2},{3,11},{11,3},{4,12},{12,4},... | collective-permute-start | bytes 1572872 | tf_op jit(solution)/shard_map/ppermute | solution.py:44
  67.7 12.9 %all-to-all-start.2 = ((bf16[4,256,256]{2,1,0:T(8,128)(2,1)}), bf16[4,256,256]{2,1,0:T(8,128)(2,1)S(1)}, u32[]{:S(2)}, u32[]{:S(2)}) async-start(bf16[4,256,256]{2,1,0:T(8,128)(2,1)} %shard_map.127), calls=%async_computation.2 | async-start | bytes 1048576 | tf_op jit(solution)/shard_map/all_to_all | solution.py:48
  71.7 1.2 copy-start.11
  76.3 0.7 copy-start.4
  81.6 57.5 %copy-start.3 = (f32[256,256]{1,0:T(8,128)S(1)}, f32[256,256]{1,0:T(8,128)}, u32[]{:S(2)}) copy-start(f32[256,256]{1,0:T(8,128)} %emb.3) | copy-start | bytes 786436
  81.6 57.5 %copy-start.8 = (f32[256]{0:T(256)S(1)}, f32[256]{0:T(256)}, u32[]{:S(2)}) copy-start(f32[256]{0:T(256)} %param.10) | copy-start | bytes 3076
  81.6 28.7 %all-to-all-start.3 = ((bf16[128,3,4,128]{3,2,1,0:T(4,128)(2,1)}), bf16[128,3,4,128]{3,2,1,0:T(4,128)(2,1)S(1)}, u32[]{:S(2)}, u32[]{:S(2)}) async-start(bf16[128,3,4,128]{3,2,1,0:T(4,128)(2,1)} %bitcast.9), calls=%async_computation.3 | async-start | bytes 786432 | tf_op jit(solution)/shard_map/all_to_all | solution.py:48
  93.9 10.3 %collective-permute-start.4 = (bf16[2,256,256]{2,1,0:T(8,128)(2,1)S(1)}, bf16[2,256,256]{2,1,0:T(8,128)(2,1)S(1)}, u32[]{:S(2)}, u32[]{:S(2)}) collective-permute-start(bf16[2,256,256]{2,1,0:T(8,128)(2,1)S(1)} %get-tuple-element.56), channel_id=1, source_target_pairs={{0,2},{1,3},{2,0},{3,1},{4,6},{5,7},{6,4},{7,5},{8,10},{9,11},{10,... | collective-permute-start | bytes 786440 | tf_op jit(solution)/shard_map/ppermute | solution.py:393
  111.8 39.6 %copy-start = (f32[8,256,256]{2,1,0:T(8,128)S(1)}, f32[8,256,256]{2,1,0:T(8,128)}, u32[]{:S(2)}) copy-start(f32[8,256,256]{2,1,0:T(8,128)} %rel.5) | copy-start | bytes 6291460
  111.8 39.6 %copy-start.6 = (f32[8,256]{1,0:T(8,128)S(1)}, f32[8,256]{1,0:T(8,128)}, u32[]{:S(2)}) copy-start(f32[8,256]{1,0:T(8,128)} %accum.3) | copy-start | bytes 24580
  111.8 23.0 %all-to-all-start.4 = ((bf16[128,2,4,128]{3,2,1,0:T(4,128)(2,1)}), bf16[128,2,4,128]{3,2,1,0:T(4,128)(2,1)S(1)}, u32[]{:S(2)}, u32[]{:S(2)}) async-start(bf16[128,2,4,128]{3,2,1,0:T(4,128)(2,1)} %bitcast.11), calls=%async_computation.4 | async-start | bytes 524288 | tf_op jit(solution)/shard_map/all_to_all | solution.py:48
  120.7 6.0 %collective-permute-start.5 = (bf16[256,256]{1,0:T(8,128)(2,1)S(1)}, bf16[256,256]{1,0:T(8,128)(2,1)S(1)}, u32[]{:S(2)}, u32[]{:S(2)}) collective-permute-start(bf16[256,256]{1,0:T(8,128)(2,1)S(1)} %shard_map.129), channel_id=1, source_target_pairs={{0,1},{1,0},{2,3},{3,2},{4,5},{5,4},{6,7},{7,6},{8,9},{9,8},{10,11... | collective-permute-start | bytes 393224 | tf_op jit(solution)/shard_map/ppermute | solution.py:407
  135.6 11.1 %all-to-all-start.5 = ((bf16[4,256,256]{2,1,0:T(8,128)(2,1)}), bf16[4,256,256]{2,1,0:T(8,128)(2,1)S(1)}, u32[]{:S(2)}, u32[]{:S(2)}) async-start(bf16[4,256,256]{2,1,0:T(8,128)(2,1)} %shard_map.132), calls=%async_computation.5 | async-start | bytes 1048576 | tf_op jit(solution)/shard_map/all_to_all | solution.py:48
  139.1 1.0 copy-start.5
  146.7 6.9 %collective-permute-start.6 = (bf16[4,256,256]{2,1,0:T(8,128)(2,1)S(1)}, bf16[4,256,256]{2,1,0:T(8,128)(2,1)S(1)}, u32[]{:S(2)}, u32[]{:S(2)}) collective-permute-start(bf16[4,256,256]{2,1,0:T(8,128)(2,1)S(1)} %all-to-all-done.5.grads), channel_id=1, source_target_pairs={{0,8},{8,0},{1,9},{9,1},{2,10},{10,2},{3,11},{11,3},{4,12},{12,4},... | collective-permute-start | bytes 1572872 | tf_op jit(solution)/shard_map/ppermute | solution.py:44

commit v11 on v10

--- a/solution.py
+++ b/solution.py
@@ -389,13 +389,12 @@
         moved=4_000_000,
         space=16,
     )
-    far, got = lax.optimization_barrier((far, got))
-    far = lax.ppermute(far, "x", [(i, i ^ 2) for i in range(4)])
     out = call(
         pieces_kernel, shape((64, 2, 3, 4, 128), bf16), 0, (got, g_rows), moved=2_000_000
     )
     mid = spread(out.reshape(128, 3, 4, 128), DOM_Z)
     far, mid = lax.optimization_barrier((far, mid))
+    far = lax.ppermute(far, "x", [(i, i ^ 2) for i in range(4)])
     routed_back = call(
         route_kernel,
         shape((64, 2, 2, 4, 128), bf16),
@@ -403,10 +402,10 @@
         (matching, mid.reshape(64, 2, 3, 4, 128)),
         moved=512_000,
     )
+    last = spread(routed_back.reshape(128, 2, 4, 128), DOM_Z).reshape(64, 2, 2, 4, 128)
+    far, last = lax.optimization_barrier((far, last))
     near = call(pass_kernel, shape((256, 256), bf16), 0, (own1, far), moved=500_000)
     near = lax.ppermute(near, "x", [(i, i ^ 1) for i in range(4)])
-    last = spread(routed_back.reshape(128, 2, 4, 128), DOM_Z).reshape(64, 2, 2, 4, 128)
-    near, last = lax.optimization_barrier((near, last))
     rel_four = spread(call(rel_kernel, four, 0, (last,), moved=512_000), "x")
     new_embeddings, new_row_accum = call(
         rows_kernel,

time: 157 us -> 157 us (level)
  blocking collectives: 0 us -> 12.4 us
  waiting for transfers between devices: 44 us -> 35.2 us
  starting transfers between devices: 78.3 us -> 73.6 us
  local copies, waits for them, and re-layouts: 4.13 us -> 5.78 us
    all_to_all x0 -> x1, blocking collectives: none -> 12.4 us  [spread(): return lax.all_to_all(value, axis, split_axis=0, concat_axis=0, tiled=True)]
    all_to_all x6 -> x5, waiting for transfers between devices: 28.6 us -> 19.4 us  [spread(): return lax.all_to_all(value, axis, split_axis=0, concat_axis=0, tiled=True)]
    all_to_all x6 -> x5, starting transfers between devices: 55.7 us -> 49.5 us  [spread(): return lax.all_to_all(value, axis, split_axis=0, concat_axis=0, tiled=True)]
    unnamed x24 -> x28, local copies, waits for them, and re-layouts: 4.13 us -> 5.78 us
  transfers between devices with their start and end apart: 13 -> 12, of which waited for: 11 -> 9; matrix products, arithmetic and copies ran while one was open for 0% -> 0% of each run, Pallas kernels for 8% -> 8%
where the time goes in v11:
time: 157 us; the launch traced here: 156 us
  starting transfers between devices  73.6 us (47%)
  waiting for transfers between devices  35.2 us (22%)
  Pallas kernels  28.4 us (18%)
  blocking collectives  12.4 us (8%)
  local copies, waits for them, and re-layouts  5.78 us (4%)
    all_to_all x5, starting transfers between devices, spread(): return lax.all_to_all(value, axis, split_axis=0, concat_axis=0, tiled=True)  49.5 us
    pallas_call x13, Pallas kernels, call(): pl.pallas_call(kernel, out_shape=outs, in_specs=specs, out_specs=tuple((A...  23.4 us
    all_to_all x5, waiting for transfers between devices, spread(): return lax.all_to_all(value, axis, split_axis=0, concat_axis=0, tiled=True)  19.4 us
    all_to_all x1, blocking collectives, spread(): return lax.all_to_all(value, axis, split_axis=0, concat_axis=0, tiled=True)  12.4 us
    ppermute x3, starting transfers between devices, body(): lax.ppermute(pack, 'x', [(i, i ^ k) for i in range(4)])  10.1 us
    ppermute x2, starting transfers between devices, swap(): return lax.ppermute(value, axis, [(0, 1), (1, 0)])  8.22 us
    ppermute x1, waiting for transfers between devices, body(): far = lax.ppermute(far, 'x', [(i, i ^ 2) for i in range(4)])  7.75 us
    unnamed x28, local copies, waits for them, and re-layouts  5.78 us
  transfers between devices with their start and end apart: 12, of which 9 were waited for; matrix products, arithmetic and copies ran while one was open for 0% of the time, Pallas kernels for 8%

profile of v11, /device:TPU:1, one launch (start us, length us, event | category | flops | bytes accessed | tf_op | source)
XLA Modules:
  0.0 156.5 jit_solution(4371070455124710142)
XLA Ops:
  0.6 1.7 %shard_map.120 = (bf16[64,8,128]{2,1,0:T(8,128)(2,1)}, bf16[272,256]{1,0:T(8,128)(2,1)}) custom-call(f32[256,256]{1,0:T(8,128)} %emb.3, s32[1,512]{1,0:T(1,128)} %bitcast.19, s32[1,512]{1,0:T(1,128)} %bitcast.20, s32[1,512]{1,0:T(1,128)} %bitcast.21, s32[1,512]{1,0:T(1,128)} %neg.1), custom_call_target="tpu_custom_call" | custom-call | bytes 800000 | tf_op jit(solution)/shard_map/pallas_call | solution.py:32
  2.4 14.6 %all-to-all-start = ((bf16[64,8,128]{2,1,0:T(8,128)(2,1)}), bf16[64,8,128]{2,1,0:T(8,128)(2,1)S(1)}, u32[]{:S(2)}, u32[]{:S(2)}) async-start(bf16[64,8,128]{2,1,0:T(8,128)(2,1)} %get-tuple-element.37), calls=%async_computation | async-start | bytes 262144 | tf_op jit(solution)/shard_map/all_to_all | solution.py:48
  17.0 3.3 %collective-permute-start = (bf16[272,256]{1,0:T(8,128)(2,1)}, bf16[272,256]{1,0:T(8,128)(2,1)S(1)}, u32[]{:S(2)}, u32[]{:S(2)}) collective-permute-start(bf16[272,256]{1,0:T(8,128)(2,1)} %get-tuple-element.36.pack0), channel_id=1, source_target_pairs={{0,1},{1,0},{2,3},{3,2},{4,5},{5,4},{6,7},{7,6},{8,9},{9,8},{10,11... | collective-permute-start | bytes 417800 | tf_op jit(solution)/shard_map/ppermute | solution.py:344
  20.3 2.3 %shard_map.121.rel_b = bf16[8,256,256]{2,1,0:T(8,128)(2,1)} custom-call(f32[8,256,256]{2,1,0:T(8,128)} %rel.5), custom_call_target="tpu_custom_call" | custom-call | bytes 3000000 | tf_op jit(solution)/shard_map/pallas_call | solution.py:32
  22.6 1.4 collective-permute-done.pack1
  24.0 3.0 %all-to-all-done.arrived = bf16[64,8,128]{2,1,0:T(8,128)(2,1)S(1)} async-done(((bf16[64,8,128]{2,1,0:T(8,128)(2,1)}), bf16[64,8,128]{2,1,0:T(8,128)(2,1)S(1)}, u32[]{:S(2)}, u32[]{:S(2)}) %all-to-all-start) | async-done | bytes 131104 | tf_op jit(solution)/shard_map/all_to_all | solution.py:48
  27.1 1.3 shard_map.122
  28.4 12.5 %all-to-all-start.1 = ((bf16[128,8,128]{2,1,0:T(8,128)(2,1)}), bf16[128,8,128]{2,1,0:T(8,128)(2,1)S(1)}, u32[]{:S(2)}, u32[]{:S(2)}) async-start(bf16[128,8,128]{2,1,0:T(8,128)(2,1)} %bitcast.7), calls=%async_computation.1 | async-start | bytes 524288 | tf_op jit(solution)/shard_map/all_to_all | solution.py:48
  40.9 4.4 %collective-permute-start.2 = (bf16[272,256]{1,0:T(8,128)(2,1)S(1)}, bf16[272,256]{1,0:T(8,128)(2,1)S(1)}, u32[]{:S(2)}, u32[]{:S(2)}) collective-permute-start(bf16[272,256]{1,0:T(8,128)(2,1)S(1)} %copy-done.11), channel_id=1, source_target_pairs={{0,3},{1,2},{2,1},{3,0},{4,7},{5,6},{6,5},{7,4},{8,11},{9,10},{10,... | collective-permute-start | bytes 417800 | tf_op jit(solution)/shard_map/ppermute | solution.py:344
  45.2 2.4 %collective-permute-start.1 = (bf16[272,256]{1,0:T(8,128)(2,1)S(1)}, bf16[272,256]{1,0:T(8,128)(2,1)S(1)}, u32[]{:S(2)}, u32[]{:S(2)}) collective-permute-start(bf16[272,256]{1,0:T(8,128)(2,1)S(1)} %copy-done.11), channel_id=1, source_target_pairs={{0,2},{1,3},{2,0},{3,1},{4,6},{5,7},{6,4},{7,5},{8,10},{9,11},{10,... | collective-permute-start | bytes 417800 | tf_op jit(solution)/shard_map/ppermute | solution.py:344
  47.7 0.1 pad_add_fusion.place
  47.8 1.2 copy-done.1
  49.0 2.4 %shard_map.123 = (f32[8,512]{1,0:T(8,128)S(1)}, f32[16,512]{1,0:T(8,128)S(1)}, bf16[1024,256]{1,0:T(8,128)(2,1)S(1)}, bf16[1024,256]{1,0:T(8,128)(2,1)S(1)}) custom-call(s32[3]{0:T(128)S(1)} %pad_add_fusion.place, bf16[272,256]{1,0:T(8,128)(2,1)S(1)} %copy-done.11, bf16[272,256]{1,0:T(8,128)(2,1)S(1)} %collective-permute-done.pack1, ...), custom_call_target="tpu_custom_call" | custom-call | flops 1300000000 | bytes 3000000 | tf_op jit(solution)/shard_map/pallas_call | solution.py:32
  51.4 0.0 collective-permute-done.2.pack3
  51.4 1.5 collective-permute-done.1.pack2
  52.8 2.1 %all-to-all-done.1 = bf16[128,8,128]{2,1,0:T(8,128)(2,1)S(1)} async-done(((bf16[128,8,128]{2,1,0:T(8,128)(2,1)}), bf16[128,8,128]{2,1,0:T(8,128)(2,1)S(1)}, u32[]{:S(2)}, u32[]{:S(2)}) %all-to-all-start.1) | async-done | bytes 262176 | tf_op jit(solution)/shard_map/all_to_all | solution.py:48
  54.9 6.9 %shard_map.124 = (bf16[2048,512]{1,0:T(8,128)(2,1)S(1)}, bf16[2048,256]{1,0:T(8,128)(2,1)S(1)}, bf16[4,256,256]{2,1,0:T(8,128)(2,1)S(1)}, bf16[4,256,256]{2,1,0:...) custom-call(s32[3]{0:T(128)S(1)} %pad_add_fusion.place, bf16[64,2,8,128]{3,2,1,0:T(8,128)(2,1)S(1)} %bitcast.17, ...), custom_call_target="tpu_custom_call" | custom-call | flops 4499999744 | bytes 6000000 | tf_op jit(solution)/shard_map/pallas_call | solution.py:32
  61.8 0.0 copy-start.12
  61.8 3.5 %collective-permute-start.3 = (bf16[4,256,256]{2,1,0:T(8,128)(2,1)S(1)}, bf16[4,256,256]{2,1,0:T(8,128)(2,1)S(1)}, u32[]{:S(2)}, u32[]{:S(2)}) collective-permute-start(bf16[4,256,256]{2,1,0:T(8,128)(2,1)S(1)} %get-tuple-element.50), channel_id=1, source_target_pairs={{0,8},{8,0},{1,9},{9,1},{2,10},{10,2},{3,11},{11,3},{4,12},{12,4},... | collective-permute-start | bytes 1572872 | tf_op jit(solution)/shard_map/ppermute | solution.py:44
  65.4 0.9 shard_map.126.g_rows
  66.2 0.6 collective-permute-done.3.came
  66.9 0.1 shard_map.127
  67.0 12.4 %all_to_all.30.got = bf16[4,256,256]{2,1,0:T(8,128)(2,1)S(1)} all-to-all(bf16[4,256,256]{2,1,0:T(8,128)(2,1)S(1)} %shard_map.127), channel_id=1, replica_groups=mesh['zlo'=4,'y'=8,'core'=2,'zhi'=2,'x'=4] {'x'}, dimensions={0} | all-to-all | bytes 1048576 | tf_op jit(solution)/shard_map/all_to_all | solution.py:48
  79.4 0.9 shard_map.128
  80.3 11.8 %all-to-all-start.3 = ((bf16[128,3,4,128]{3,2,1,0:T(4,128)(2,1)}), bf16[128,3,4,128]{3,2,1,0:T(4,128)(2,1)S(1)}, u32[]{:S(2)}, u32[]{:S(2)}) async-start(bf16[128,3,4,128]{3,2,1,0:T(4,128)(2,1)} %bitcast.9), calls=%async_computation.3 | async-start | bytes 786432 | tf_op jit(solution)/shard_map/all_to_all | solution.py:48
  92.1 0.0 copy-start.13
  92.1 1.2 copy-done.13
  93.4 3.5 %shard_map.125 = (f32[256,256]{1,0:T(8,128)S(1)}, f32[256,256]{1,0:T(8,128)S(1)}, bf16[2,256,256]{2,1,0:T(8,128)(2,1)S(1)}) custom-call(bf16[2048,256]{1,0:T(8,128)(2,1)S(1)} %copy-done.13, f32[16,512]{1,0:T(8,128)S(1)} %get-tuple-element.42.known.known0, f32[16,512]{1,0:T(8,128)S(1)} %get-tuple-element.46.known1, bf16[8,256,256]{2,1,0:T(8,128)(2,1)S(1)} %copy-done.2), custom_call_target="tpu_custom_call" | custom-call | flops 3000000000 | bytes 4000000 | tf_op jit(solution)/shard_map/pallas_call | solution.py:32
  96.9 0.7 copy-done.4
  97.6 0.7 copy-done.6
  98.3 10.2 %all-to-all-done.3 = bf16[128,3,4,128]{3,2,1,0:T(4,128)(2,1)S(1)} async-done(((bf16[128,3,4,128]{3,2,1,0:T(4,128)(2,1)}), bf16[128,3,4,128]{3,2,1,0:T(4,128)(2,1)S(1)}, u32[]{:S(2)}, u32[]{:S(2)}) %all-to-all-start.3) | async-done | bytes 393248 | tf_op jit(solution)/shard_map/all_to_all | solution.py:48
  108.5 1.5 shard_map.129
  110.0 7.2 %all-to-all-start.4 = ((bf16[128,2,4,128]{3,2,1,0:T(4,128)(2,1)}), bf16[128,2,4,128]{3,2,1,0:T(4,128)(2,1)S(1)}, u32[]{:S(2)}, u32[]{:S(2)}) async-start(bf16[128,2,4,128]{3,2,1,0:T(4,128)(2,1)} %bitcast.11), calls=%async_computation.4 | async-start | bytes 524288 | tf_op jit(solution)/shard_map/all_to_all | solution.py:48
  117.2 2.4 %collective-permute-start.4 = (bf16[2,256,256]{2,1,0:T(8,128)(2,1)S(1)}, bf16[2,256,256]{2,1,0:T(8,128)(2,1)S(1)}, u32[]{:S(2)}, u32[]{:S(2)}) collective-permute-start(bf16[2,256,256]{2,1,0:T(8,128)(2,1)S(1)} %get-tuple-element.55), channel_id=1, source_target_pairs={{0,2},{1,3},{2,0},{3,1},{4,6},{5,7},{6,4},{7,5},{8,10},{9,11},{10,... | collective-permute-start | bytes 786440 | tf_op jit(solution)/shard_map/ppermute | solution.py:397
  119.7 7.7 %collective-permute-done.4.came.far = bf16[2,256,256]{2,1,0:T(8,128)(2,1)S(1)} collective-permute-done((bf16[2,256,256]{2,1,0:T(8,128)(2,1)S(1)}, bf16[2,256,256]{2,1,0:T(8,128)(2,1)S(1)}, u32[]{:S(2)}, u32[]{:S(2)}) %collective-permute-start.4) | collective-permute-done | bytes 262176 | tf_op jit(solution)/shard_map/ppermute | solution.py:397
  127.4 4.0 %all-to-all-done.4 = bf16[128,2,4,128]{3,2,1,0:T(4,128)(2,1)S(1)} async-done(((bf16[128,2,4,128]{3,2,1,0:T(4,128)(2,1)}), bf16[128,2,4,128]{3,2,1,0:T(4,128)(2,1)S(1)}, u32[]{:S(2)}, u32[]{:S(2)}) %all-to-all-start.4) | async-done | bytes 262176 | tf_op jit(solution)/shard_map/all_to_all | solution.py:48
  131.4 0.9 shard_map.132
  132.3 3.5 %all-to-all-start.5 = ((bf16[4,256,256]{2,1,0:T(8,128)(2,1)}), bf16[4,256,256]{2,1,0:T(8,128)(2,1)S(1)}, u32[]{:S(2)}, u32[]{:S(2)}) async-start(bf16[4,256,256]{2,1,0:T(8,128)(2,1)} %shard_map.132), calls=%async_computation.5 | async-start | bytes 1048576 | tf_op jit(solution)/shard_map/all_to_all | solution.py:48
  135.8 0.9 copy-done.5
  136.8 3.3 %collective-permute-start.5 = (bf16[256,256]{1,0:T(8,128)(2,1)S(1)}, bf16[256,256]{1,0:T(8,128)(2,1)S(1)}, u32[]{:S(2)}, u32[]{:S(2)}) collective-permute-start(bf16[256,256]{1,0:T(8,128)(2,1)S(1)} %shard_map.130), channel_id=1, source_target_pairs={{0,1},{1,0},{2,3},{3,2},{4,5},{5,4},{6,7},{7,6},{8,9},{9,8},{10,11... | collective-permute-start | bytes 393224 | tf_op jit(solution)/shard_map/ppermute | solution.py:408
  140.1 4.6 %collective-permute-done.5.near = bf16[256,256]{1,0:T(8,128)(2,1)S(1)} collective-permute-done((bf16[256,256]{1,0:T(8,128)(2,1)S(1)}, bf16[256,256]{1,0:T(8,128)(2,1)S(1)}, u32[]{:S(2)}, u32[]{:S(2)}) %collective-permute-start.5) | collective-permute-done | bytes 131104 | tf_op jit(solution)/shard_map/ppermute | solution.py:408
  144.7 0.9 copy-done.7
  145.6 1.0 shard_map.131
  146.6 0.0 all-to-all-done.5.grads
  146.6 4.7 %collective-permute-start.6 = (bf16[4,256,256]{2,1,0:T(8,128)(2,1)S(1)}, bf16[4,256,256]{2,1,0:T(8,128)(2,1)S(1)}, u32[]{:S(2)}, u32[]{:S(2)}) collective-permute-start(bf16[4,256,256]{2,1,0:T(8,128)(2,1)S(1)} %all-to-all-done.5.grads), channel_id=1, source_target_pairs={{0,8},{8,0},{1,9},{9,1},{2,10},{10,2},{3,11},{11,3},{4,12},{12,4},... | collective-permute-start | bytes 1572872 | tf_op jit(solution)/shard_map/ppermute | solution.py:44
  151.4 2.2 %shard_map.133 = (f32[8,256,256]{2,1,0:T(8,128)}, f32[8,256]{1,0:T(8,128)S(1)}) custom-call(s32[3]{0:T(128)S(1)} %pad_add_fusion.place, f32[8,256,256]{2,1,0:T(8,128)S(1)} %copy-done, f32[8,256]{1,0:T(8,128)S(1)} %copy-done.8, bf16[4,256,256]{2,1,0:T(8,128)(2,1)S(1)} %all-to-all-done.5.grads), custom_call_target="tpu_custom_call" | custom-call | bytes 3000000 | tf_op jit(solution)/shard_map/pallas_call | solution.py:296
  153.5 0.0 collective-permute-done.6.grads
  153.5 2.8 %shard_map.134 = (f32[8,256,256]{2,1,0:T(8,128)}, f32[8,256]{1,0:T(8,128)}) custom-call(s32[3]{0:T(128)S(1)} %pad_add_fusion.place, f32[8,256,256]{2,1,0:T(8,128)S(1)} %copy-done, f32[8,256]{1,0:T(8,128)S(1)} %copy-done.8, bf16[4,256,256]{2,1,0:T(8,128)(2,1)S(1)} %collective-permute-done.6.grads, ...), custom_call_target="tpu_custom_call", output_to_operand_aliasing={{0}: (4, {})} | custom-call | bytes 3000000 | tf_op jit(solution)/shard_map/pallas_call | solution.py:296
  (21 shorter events, 0.1 us)
Async XLA Ops:
  0.6 26.4 %copy-start.9 = (s32[64]{0:T(128)S(1)}, s32[64]{0:T(128)}, u32[]{:S(2)}) copy-start(s32[64]{0:T(128)} %matching.3) | copy-start | bytes 772
  2.4 24.7 %all-to-all-start = ((bf16[64,8,128]{2,1,0:T(8,128)(2,1)}), bf16[64,8,128]{2,1,0:T(8,128)(2,1)S(1)}, u32[]{:S(2)}, u32[]{:S(2)}) async-start(bf16[64,8,128]{2,1,0:T(8,128)(2,1)} %get-tuple-element.37), calls=%async_computation | async-start | bytes 262144 | tf_op jit(solution)/shard_map/all_to_all | solution.py:48
  17.0 23.9 %copy-start.11 = (bf16[272,256]{1,0:T(8,128)(2,1)S(1)}, bf16[272,256]{1,0:T(8,128)(2,1)}, u32[]{:S(2)}) copy-start(bf16[272,256]{1,0:T(8,128)(2,1)} %get-tuple-element.36.pack0) | copy-start | bytes 417796
  17.0 7.0 %collective-permute-start = (bf16[272,256]{1,0:T(8,128)(2,1)}, bf16[272,256]{1,0:T(8,128)(2,1)S(1)}, u32[]{:S(2)}, u32[]{:S(2)}) collective-permute-start(bf16[272,256]{1,0:T(8,128)(2,1)} %get-tuple-element.36.pack0), channel_id=1, source_target_pairs={{0,1},{1,0},{2,3},{3,2},{4,5},{5,4},{6,7},{7,6},{8,9},{9,8},{10,11... | collective-permute-start | bytes 417800 | tf_op jit(solution)/shard_map/ppermute | solution.py:344
  28.4 26.6 %all-to-all-start.1 = ((bf16[128,8,128]{2,1,0:T(8,128)(2,1)}), bf16[128,8,128]{2,1,0:T(8,128)(2,1)S(1)}, u32[]{:S(2)}, u32[]{:S(2)}) async-start(bf16[128,8,128]{2,1,0:T(8,128)(2,1)} %bitcast.7), calls=%async_computation.1 | async-start | bytes 524288 | tf_op jit(solution)/shard_map/all_to_all | solution.py:48
  40.9 10.5 %collective-permute-start.2 = (bf16[272,256]{1,0:T(8,128)(2,1)S(1)}, bf16[272,256]{1,0:T(8,128)(2,1)S(1)}, u32[]{:S(2)}, u32[]{:S(2)}) collective-permute-start(bf16[272,256]{1,0:T(8,128)(2,1)S(1)} %copy-done.11), channel_id=1, source_target_pairs={{0,3},{1,2},{2,1},{3,0},{4,7},{5,6},{6,5},{7,4},{8,11},{9,10},{10,... | collective-permute-start | bytes 417800 | tf_op jit(solution)/shard_map/ppermute | solution.py:344
  45.2 7.6 %collective-permute-start.1 = (bf16[272,256]{1,0:T(8,128)(2,1)S(1)}, bf16[272,256]{1,0:T(8,128)(2,1)S(1)}, u32[]{:S(2)}, u32[]{:S(2)}) collective-permute-start(bf16[272,256]{1,0:T(8,128)(2,1)S(1)} %copy-done.11), channel_id=1, source_target_pairs={{0,2},{1,3},{2,0},{3,1},{4,6},{5,7},{6,4},{7,5},{8,10},{9,11},{10,... | collective-permute-start | bytes 417800 | tf_op jit(solution)/shard_map/ppermute | solution.py:344
  47.8 1.2 copy-start.1
  49.0 6.0 %copy-start.2 = (bf16[8,256,256]{2,1,0:T(8,128)(2,1)S(1)}, bf16[8,256,256]{2,1,0:T(8,128)(2,1)}, u32[]{:S(2)}) copy-start(bf16[8,256,256]{2,1,0:T(8,128)(2,1)} %shard_map.121.rel_b) | copy-start | bytes 3145732
  61.8 4.4 %copy-start.12 = (bf16[2048,256]{1,0:T(8,128)(2,1)}, bf16[2048,256]{1,0:T(8,128)(2,1)S(1)}, u32[]{:S(2)}) copy-start(bf16[2048,256]{1,0:T(8,128)(2,1)S(1)} %get-tuple-element.45.g_trans) | copy-start | bytes 3145732
  61.8 5.0 %collective-permute-start.3 = (bf16[4,256,256]{2,1,0:T(8,128)(2,1)S(1)}, bf16[4,256,256]{2,1,0:T(8,128)(2,1)S(1)}, u32[]{:S(2)}, u32[]{:S(2)}) collective-permute-start(bf16[4,256,256]{2,1,0:T(8,128)(2,1)S(1)} %get-tuple-element.50), channel_id=1, source_target_pairs={{0,8},{8,0},{1,9},{9,1},{2,10},{10,2},{3,11},{11,3},{4,12},{12,4},... | collective-permute-start | bytes 1572872 | tf_op jit(solution)/shard_map/ppermute | solution.py:44
  80.3 28.2 %all-to-all-start.3 = ((bf16[128,3,4,128]{3,2,1,0:T(4,128)(2,1)}), bf16[128,3,4,128]{3,2,1,0:T(4,128)(2,1)S(1)}, u32[]{:S(2)}, u32[]{:S(2)}) async-start(bf16[128,3,4,128]{3,2,1,0:T(4,128)(2,1)} %bitcast.9), calls=%async_computation.3 | async-start | bytes 786432 | tf_op jit(solution)/shard_map/all_to_all | solution.py:48
  92.1 1.2 copy-start.13
  96.9 0.7 copy-start.4
  97.6 0.7 copy-start.6
  98.3 46.4 %copy-start.3 = (f32[256,256]{1,0:T(8,128)S(1)}, f32[256,256]{1,0:T(8,128)}, u32[]{:S(2)}) copy-start(f32[256,256]{1,0:T(8,128)} %emb.3) | copy-start | bytes 786436
  98.3 46.4 %copy-start.10 = (f32[256]{0:T(256)S(1)}, f32[256]{0:T(256)}, u32[]{:S(2)}) copy-start(f32[256]{0:T(256)} %param.10) | copy-start | bytes 3076
  110.0 41.3 %copy-start = (f32[8,256,256]{2,1,0:T(8,128)S(1)}, f32[8,256,256]{2,1,0:T(8,128)}, u32[]{:S(2)}) copy-start(f32[8,256,256]{2,1,0:T(8,128)} %rel.5) | copy-start | bytes 6291460
  110.0 41.3 %copy-start.8 = (f32[8,256]{1,0:T(8,128)S(1)}, f32[8,256]{1,0:T(8,128)}, u32[]{:S(2)}) copy-start(f32[8,256]{1,0:T(8,128)} %accum.3) | copy-start | bytes 24580
  110.0 21.4 %all-to-all-start.4 = ((bf16[128,2,4,128]{3,2,1,0:T(4,128)(2,1)}), bf16[128,2,4,128]{3,2,1,0:T(4,128)(2,1)S(1)}, u32[]{:S(2)}, u32[]{:S(2)}) async-start(bf16[128,2,4,128]{3,2,1,0:T(4,128)(2,1)} %bitcast.11), calls=%async_computation.4 | async-start | bytes 524288 | tf_op jit(solution)/shard_map/all_to_all | solution.py:48
  117.2 10.2 %collective-permute-start.4 = (bf16[2,256,256]{2,1,0:T(8,128)(2,1)S(1)}, bf16[2,256,256]{2,1,0:T(8,128)(2,1)S(1)}, u32[]{:S(2)}, u32[]{:S(2)}) collective-permute-start(bf16[2,256,256]{2,1,0:T(8,128)(2,1)S(1)} %get-tuple-element.55), channel_id=1, source_target_pairs={{0,2},{1,3},{2,0},{3,1},{4,6},{5,7},{6,4},{7,5},{8,10},{9,11},{10,... | collective-permute-start | bytes 786440 | tf_op jit(solution)/shard_map/ppermute | solution.py:397
  132.3 14.3 %all-to-all-start.5 = ((bf16[4,256,256]{2,1,0:T(8,128)(2,1)}), bf16[4,256,256]{2,1,0:T(8,128)(2,1)S(1)}, u32[]{:S(2)}, u32[]{:S(2)}) async-start(bf16[4,256,256]{2,1,0:T(8,128)(2,1)} %shard_map.132), calls=%async_computation.5 | async-start | bytes 1048576 | tf_op jit(solution)/shard_map/all_to_all | solution.py:48
  135.8 1.0 copy-start.5
  136.8 7.9 %collective-permute-start.5 = (bf16[256,256]{1,0:T(8,128)(2,1)S(1)}, bf16[256,256]{1,0:T(8,128)(2,1)S(1)}, u32[]{:S(2)}, u32[]{:S(2)}) collective-permute-start(bf16[256,256]{1,0:T(8,128)(2,1)S(1)} %shard_map.130), channel_id=1, source_target_pairs={{0,1},{1,0},{2,3},{3,2},{4,5},{5,4},{6,7},{7,6},{8,9},{9,8},{10,11... | collective-permute-start | bytes 393224 | tf_op jit(solution)/shard_map/ppermute | solution.py:408
  144.7 1.0 copy-start.7
  146.6 6.9 %collective-permute-start.6 = (bf16[4,256,256]{2,1,0:T(8,128)(2,1)S(1)}, bf16[4,256,256]{2,1,0:T(8,128)(2,1)S(1)}, u32[]{:S(2)}, u32[]{:S(2)}) collective-permute-start(bf16[4,256,256]{2,1,0:T(8,128)(2,1)S(1)} %all-to-all-done.5.grads), channel_id=1, source_target_pairs={{0,8},{8,0},{1,9},{9,1},{2,10},{10,2},{3,11},{11,3},{4,12},{12,4},... | collective-permute-start | bytes 1572872 | tf_op jit(solution)/shard_map/ppermute | solution.py:44

commit v12 on v11

--- a/solution.py
+++ b/solution.py
@@ -182,7 +182,7 @@
         g_rows[z] = dot(turned, weight[:, z * 256 : (z + 1) * 256]).T.astype(bf16)
 
 
-def own_kernel(g_trans, known0, known1, rel_b, own0, own1, far):
+def own_kernel(g_trans, known0, known1, rel_b, *owns):
     sub_ids = lax.broadcasted_iota(jnp.int32, (256, 512), 0).astype(f32)
     stack = rel_b[...].reshape(2048, 256)
     for s in range(4):
@@ -195,14 +195,7 @@
         ]
         hot = (index[0:1, :] == sub_ids).astype(f32).astype(bf16)
         mine = dot(hot, jnp.concatenate(parts, axis=0))
-        if s < 2:
-            (own0, own1)[s][...] = mine
-        else:
-            far[s - 2] = mine.astype(bf16)
-
-
-def pass_kernel(own1, came, out):
-    out[...] = (own1[...] + came[1].astype(f32)).astype(bf16)
+        owns[s][...] = mine.astype(owns[s].dtype)
 
 
 def join_kernel(kept, came, out):
@@ -255,8 +248,10 @@
     return jnp.broadcast_to(row, (128, 256)).T[:, 0:1]
 
 
-def rows_kernel(emb, accum, own0, far, near, last, new_emb, new_accum):
-    grad = own0[...] + far[0].astype(f32) + near[...].astype(f32)
+def rows_kernel(emb, accum, own0, own1, own2, own3, last, new_emb, new_accum):
+    grad = own0[...]
+    for own in (own1, own2, own3):
+        grad = grad + own[...].astype(f32)
     grad = grad + jnp.concatenate([whole(last, 0, 0), whole(last, 1, 0)], axis=1)
     total = to_column(accum[...]) + jnp.mean(grad * grad, axis=1, keepdims=True)
     new_emb[...] = emb[...] - grad * (learn_rate / jnp.sqrt(total))
@@ -380,21 +375,24 @@
     )
     came, g_rows = lax.optimization_barrier((came, g_rows))
     got = spread(call(join_kernel, four, 0, (kept, came), moved=1_500_000), "x")
-    own0, own1, far = call(
+    one = shape((256, 256), bf16)
+    owns = call(
         own_kernel,
-        (shape((256, 256), f32), shape((256, 256), f32), shape((2, 256, 256), bf16)),
+        (shape((256, 256), f32), one, one, one),
         0,
         (g_trans, known0, known1, rel_b),
         flops=3_000_000_000,
         moved=4_000_000,
         space=16,
     )
+    away = lambda part, k: lax.ppermute(part, "x", [(i, i ^ k) for i in range(4)])
+    first = away(owns[1], 1)
     out = call(
         pieces_kernel, shape((64, 2, 3, 4, 128), bf16), 0, (got, g_rows), moved=2_000_000
     )
     mid = spread(out.reshape(128, 3, 4, 128), DOM_Z)
-    far, mid = lax.optimization_barrier((far, mid))
-    far = lax.ppermute(far, "x", [(i, i ^ 2) for i in range(4)])
+    first, *others, mid = lax.optimization_barrier((first, *owns[2:], mid))
+    others = [away(part, k) for k, part in enumerate(others, 2)]
     routed_back = call(
         route_kernel,
         shape((64, 2, 2, 4, 128), bf16),
@@ -403,15 +401,13 @@
         moved=512_000,
     )
     last = spread(routed_back.reshape(128, 2, 4, 128), DOM_Z).reshape(64, 2, 2, 4, 128)
-    far, last = lax.optimization_barrier((far, last))
-    near = call(pass_kernel, shape((256, 256), bf16), 0, (own1, far), moved=500_000)
-    near = lax.ppermute(near, "x", [(i, i ^ 1) for i in range(4)])
+    *others, last = lax.optimization_barrier((*others, last))
     rel_four = spread(call(rel_kernel, four, 0, (last,), moved=512_000), "x")
     new_embeddings, new_row_accum = call(
         rows_kernel,
         (shape((256, 256), f32), shape((1, 256), f32)),
         0,
-        (embeddings, row_accum.reshape(1, 256), own0, far, near, last),
+        (embeddings, row_accum.reshape(1, 256), owns[0], first, *others, last),
         flops=1_000_000,
         moved=1_000_000,
     )

time: 157 us -> 155 us (0.987)
  starting transfers between devices: 73.6 us -> 77.3 us
  waiting for transfers between devices: 35.2 us -> 31.7 us
  local copies, waits for them, and re-layouts: 5.78 us -> 3.08 us
    ppermute x2 -> x3, waiting for transfers between devices: 12.3 us -> 7.88 us  [body(): lax.ppermute(part, 'x', [(i, i ^ k) for i in range(4)])]
    ppermute x2 -> x3, starting transfers between devices: 5.78 us -> 8.82 us  [body(): lax.ppermute(part, 'x', [(i, i ^ k) for i in range(4)])]
    unnamed x28, local copies, waits for them, and re-layouts: 5.78 us -> 3.08 us
    pallas_call x13 -> x12, Pallas kernels: 23.4 us -> 23.1 us  [call(): pl.pallas_call(kernel, out_shape=outs, in_specs=specs, out_specs=tuple((A...]
  transfers between devices with their start and end apart: 12 -> 13, of which waited for: 9 -> 11; matrix products, arithmetic and copies ran while one was open for 0% -> 0% of each run, Pallas kernels for 8% -> 8%
where the time goes in v12:
time: 155 us; the launch traced here: 154 us
  starting transfers between devices  77.3 us (50%)
  waiting for transfers between devices  31.7 us (20%)
  Pallas kernels  28 us (18%)
  blocking collectives  12.6 us (8%)
  local copies, waits for them, and re-layouts  3.08 us (2%)
    all_to_all x5, starting transfers between devices, spread(): return lax.all_to_all(value, axis, split_axis=0, concat_axis=0, tiled=True)  50.2 us
    pallas_call x12, Pallas kernels, call(): pl.pallas_call(kernel, out_shape=outs, in_specs=specs, out_specs=tuple((A...  23.1 us
    all_to_all x5, waiting for transfers between devices, spread(): return lax.all_to_all(value, axis, split_axis=0, concat_axis=0, tiled=True)  20.3 us
    all_to_all x1, blocking collectives, spread(): return lax.all_to_all(value, axis, split_axis=0, concat_axis=0, tiled=True)  12.6 us
    ppermute x3, starting transfers between devices, body(): lax.ppermute(pack, 'x', [(i, i ^ k) for i in range(4)])  10.1 us
    ppermute x3, starting transfers between devices, body(): lax.ppermute(part, 'x', [(i, i ^ k) for i in range(4)])  8.82 us
    ppermute x2, starting transfers between devices, swap(): return lax.ppermute(value, axis, [(0, 1), (1, 0)])  8.2 us
    ppermute x3, waiting for transfers between devices, body(): lax.ppermute(part, 'x', [(i, i ^ k) for i in range(4)])  7.88 us
  transfers between devices with their start and end apart: 13, of which 11 were waited for; matrix products, arithmetic and copies ran while one was open for 0% of the time, Pallas kernels for 8%

profile of v12, /device:TPU:1, one launch (start us, length us, event | category | flops | bytes accessed | tf_op | source)
XLA Modules:
  0.0 153.8 jit_solution(13649724994314530086)
XLA Ops:
  0.6 1.7 %shard_map.120 = (bf16[64,8,128]{2,1,0:T(8,128)(2,1)}, bf16[272,256]{1,0:T(8,128)(2,1)}) custom-call(f32[256,256]{1,0:T(8,128)} %emb.3, s32[1,512]{1,0:T(1,128)} %bitcast.19, s32[1,512]{1,0:T(1,128)} %bitcast.20, s32[1,512]{1,0:T(1,128)} %bitcast.21, s32[1,512]{1,0:T(1,128)} %neg.1), custom_call_target="tpu_custom_call" | custom-call | bytes 800000 | tf_op jit(solution)/shard_map/pallas_call | solution.py:32
  2.4 14.6 %all-to-all-start = ((bf16[64,8,128]{2,1,0:T(8,128)(2,1)}), bf16[64,8,128]{2,1,0:T(8,128)(2,1)S(1)}, u32[]{:S(2)}, u32[]{:S(2)}) async-start(bf16[64,8,128]{2,1,0:T(8,128)(2,1)} %get-tuple-element.41), calls=%async_computation | async-start | bytes 262144 | tf_op jit(solution)/shard_map/all_to_all | solution.py:48
  17.0 3.3 %collective-permute-start = (bf16[272,256]{1,0:T(8,128)(2,1)}, bf16[272,256]{1,0:T(8,128)(2,1)S(1)}, u32[]{:S(2)}, u32[]{:S(2)}) collective-permute-start(bf16[272,256]{1,0:T(8,128)(2,1)} %get-tuple-element.40.pack0), channel_id=1, source_target_pairs={{0,1},{1,0},{2,3},{3,2},{4,5},{5,4},{6,7},{7,6},{8,9},{9,8},{10,11... | collective-permute-start | bytes 417800 | tf_op jit(solution)/shard_map/ppermute | solution.py:339
  20.3 2.3 %shard_map.121.rel_b = bf16[8,256,256]{2,1,0:T(8,128)(2,1)} custom-call(f32[8,256,256]{2,1,0:T(8,128)} %rel.5), custom_call_target="tpu_custom_call" | custom-call | bytes 3000000 | tf_op jit(solution)/shard_map/pallas_call | solution.py:32
  22.6 1.4 collective-permute-done.pack1
  24.0 3.0 %all-to-all-done.arrived = bf16[64,8,128]{2,1,0:T(8,128)(2,1)S(1)} async-done(((bf16[64,8,128]{2,1,0:T(8,128)(2,1)}), bf16[64,8,128]{2,1,0:T(8,128)(2,1)S(1)}, u32[]{:S(2)}, u32[]{:S(2)}) %all-to-all-start) | async-done | bytes 131104 | tf_op jit(solution)/shard_map/all_to_all | solution.py:48
  27.1 1.3 shard_map.122
  28.4 12.5 %all-to-all-start.1 = ((bf16[128,8,128]{2,1,0:T(8,128)(2,1)}), bf16[128,8,128]{2,1,0:T(8,128)(2,1)S(1)}, u32[]{:S(2)}, u32[]{:S(2)}) async-start(bf16[128,8,128]{2,1,0:T(8,128)(2,1)} %bitcast.7), calls=%async_computation.1 | async-start | bytes 524288 | tf_op jit(solution)/shard_map/all_to_all | solution.py:48
  40.9 4.4 %collective-permute-start.2 = (bf16[272,256]{1,0:T(8,128)(2,1)S(1)}, bf16[272,256]{1,0:T(8,128)(2,1)S(1)}, u32[]{:S(2)}, u32[]{:S(2)}) collective-permute-start(bf16[272,256]{1,0:T(8,128)(2,1)S(1)} %copy-done.11), channel_id=1, source_target_pairs={{0,3},{1,2},{2,1},{3,0},{4,7},{5,6},{6,5},{7,4},{8,11},{9,10},{10,... | collective-permute-start | bytes 417800 | tf_op jit(solution)/shard_map/ppermute | solution.py:339
  45.2 2.4 %collective-permute-start.1 = (bf16[272,256]{1,0:T(8,128)(2,1)S(1)}, bf16[272,256]{1,0:T(8,128)(2,1)S(1)}, u32[]{:S(2)}, u32[]{:S(2)}) collective-permute-start(bf16[272,256]{1,0:T(8,128)(2,1)S(1)} %copy-done.11), channel_id=1, source_target_pairs={{0,2},{1,3},{2,0},{3,1},{4,6},{5,7},{6,4},{7,5},{8,10},{9,11},{10,... | collective-permute-start | bytes 417800 | tf_op jit(solution)/shard_map/ppermute | solution.py:339
  47.7 0.1 pad_add_fusion.place
  47.8 1.2 copy-done.1
  49.0 2.4 %shard_map.123 = (f32[8,512]{1,0:T(8,128)S(1)}, f32[16,512]{1,0:T(8,128)S(1)}, bf16[1024,256]{1,0:T(8,128)(2,1)S(1)}, bf16[1024,256]{1,0:T(8,128)(2,1)S(1)}) custom-call(s32[3]{0:T(128)S(1)} %pad_add_fusion.place, bf16[272,256]{1,0:T(8,128)(2,1)S(1)} %copy-done.11, bf16[272,256]{1,0:T(8,128)(2,1)S(1)} %collective-permute-done.pack1, ...), custom_call_target="tpu_custom_call" | custom-call | flops 1300000000 | bytes 3000000 | tf_op jit(solution)/shard_map/pallas_call | solution.py:32
  51.4 0.0 collective-permute-done.2.pack3
  51.4 1.5 collective-permute-done.1.pack2
  52.8 2.1 %all-to-all-done.1 = bf16[128,8,128]{2,1,0:T(8,128)(2,1)S(1)} async-done(((bf16[128,8,128]{2,1,0:T(8,128)(2,1)}), bf16[128,8,128]{2,1,0:T(8,128)(2,1)S(1)}, u32[]{:S(2)}, u32[]{:S(2)}) %all-to-all-start.1) | async-done | bytes 262176 | tf_op jit(solution)/shard_map/all_to_all | solution.py:48
  54.9 6.7 %shard_map.124 = (bf16[2048,512]{1,0:T(8,128)(2,1)S(1)}, bf16[2048,256]{1,0:T(8,128)(2,1)S(1)}, bf16[4,256,256]{2,1,0:T(8,128)(2,1)S(1)}, bf16[4,256,256]{2,1,0:...) custom-call(s32[3]{0:T(128)S(1)} %pad_add_fusion.place, bf16[64,2,8,128]{3,2,1,0:T(8,128)(2,1)S(1)} %bitcast.17, ...), custom_call_target="tpu_custom_call" | custom-call | flops 4499999744 | bytes 6000000 | tf_op jit(solution)/shard_map/pallas_call | solution.py:32
  61.7 0.0 copy-start.12
  61.7 3.5 %collective-permute-start.4 = (bf16[4,256,256]{2,1,0:T(8,128)(2,1)S(1)}, bf16[4,256,256]{2,1,0:T(8,128)(2,1)S(1)}, u32[]{:S(2)}, u32[]{:S(2)}) collective-permute-start(bf16[4,256,256]{2,1,0:T(8,128)(2,1)S(1)} %get-tuple-element.56), channel_id=1, source_target_pairs={{0,8},{8,0},{1,9},{9,1},{2,10},{10,2},{3,11},{11,3},{4,12},{12,4},... | collective-permute-start | bytes 1572872 | tf_op jit(solution)/shard_map/ppermute | solution.py:44
  65.2 0.9 shard_map.126.g_rows
  66.1 0.6 collective-permute-done.4.came
  66.7 0.1 shard_map.127
  66.9 12.6 %all_to_all.30.got = bf16[4,256,256]{2,1,0:T(8,128)(2,1)S(1)} all-to-all(bf16[4,256,256]{2,1,0:T(8,128)(2,1)S(1)} %shard_map.127), channel_id=1, replica_groups=mesh['zlo'=4,'y'=8,'core'=2,'zhi'=2,'x'=4] {'x'}, dimensions={0} | all-to-all | bytes 1048576 | tf_op jit(solution)/shard_map/all_to_all | solution.py:48
  79.4 0.9 shard_map.128
  80.3 11.8 %all-to-all-start.3 = ((bf16[128,3,4,128]{3,2,1,0:T(4,128)(2,1)}), bf16[128,3,4,128]{3,2,1,0:T(4,128)(2,1)S(1)}, u32[]{:S(2)}, u32[]{:S(2)}) async-start(bf16[128,3,4,128]{3,2,1,0:T(4,128)(2,1)} %bitcast.9), calls=%async_computation.3 | async-start | bytes 786432 | tf_op jit(solution)/shard_map/all_to_all | solution.py:48
  92.1 3.3 %shard_map.125 = (f32[256,256]{1,0:T(8,128)S(1)}, bf16[256,256]{1,0:T(8,128)(2,1)S(1)}, bf16[256,256]{1,0:T(8,128)(2,1)S(1)}, bf16[256,256]{1,0:T(8,128)(2,1)S(1)}) custom-call(bf16[2048,256]{1,0:T(8,128)(2,1)S(1)} %copy-done.13, f32[16,512]{1,0:T(8,128)S(1)} %get-tuple-element.46.known.known0, f32[16,512]{1,0:T(8,128)S(1)} %get-tuple-element.50.known1, ...), custom_call_target="tpu_custom_call" | custom-call | flops 3000000000 | bytes 4000000 | tf_op jit(solution)/shard_map/pallas_call | solution.py:32
  95.4 0.0 copy-start.3
  95.5 0.0 copy-start.10
  95.5 2.3 %collective-permute-start.3 = (bf16[256,256]{1,0:T(8,128)(2,1)S(1)}, bf16[256,256]{1,0:T(8,128)(2,1)S(1)}, u32[]{:S(2)}, u32[]{:S(2)}) collective-permute-start(bf16[256,256]{1,0:T(8,128)(2,1)S(1)} %get-tuple-element.52), channel_id=1, source_target_pairs={{0,1},{1,0},{2,3},{3,2},{4,5},{5,4},{6,7},{7,6},{8,9},{9,8},{10,11... | collective-permute-start | bytes 393224 | tf_op jit(solution)/shard_map/ppermute | solution.py:388
  97.8 3.8 %collective-permute-done.3.own1 = bf16[256,256]{1,0:T(8,128)(2,1)S(1)} collective-permute-done((bf16[256,256]{1,0:T(8,128)(2,1)S(1)}, bf16[256,256]{1,0:T(8,128)(2,1)S(1)}, u32[]{:S(2)}, u32[]{:S(2)}) %collective-permute-start.3) | collective-permute-done | bytes 131104 | tf_op jit(solution)/shard_map/ppermute | solution.py:388
  101.6 6.9 %all-to-all-done.3 = bf16[128,3,4,128]{3,2,1,0:T(4,128)(2,1)S(1)} async-done(((bf16[128,3,4,128]{3,2,1,0:T(4,128)(2,1)}), bf16[128,3,4,128]{3,2,1,0:T(4,128)(2,1)S(1)}, u32[]{:S(2)}, u32[]{:S(2)}) %all-to-all-start.3) | async-done | bytes 393248 | tf_op jit(solution)/shard_map/all_to_all | solution.py:48
  108.5 1.5 shard_map.129
  110.1 7.9 %all-to-all-start.4 = ((bf16[128,2,4,128]{3,2,1,0:T(4,128)(2,1)}), bf16[128,2,4,128]{3,2,1,0:T(4,128)(2,1)S(1)}, u32[]{:S(2)}, u32[]{:S(2)}) async-start(bf16[128,2,4,128]{3,2,1,0:T(4,128)(2,1)} %bitcast.11), calls=%async_computation.4 | async-start | bytes 524288 | tf_op jit(solution)/shard_map/all_to_all | solution.py:48
  117.9 2.5 %collective-permute-start.5 = (bf16[256,256]{1,0:T(8,128)(2,1)S(1)}, bf16[256,256]{1,0:T(8,128)(2,1)S(1)}, u32[]{:S(2)}, u32[]{:S(2)}) collective-permute-start(bf16[256,256]{1,0:T(8,128)(2,1)S(1)} %get-tuple-element.62), channel_id=1, source_target_pairs={{0,2},{1,3},{2,0},{3,1},{4,6},{5,7},{6,4},{7,5},{8,10},{9,11},{10,... | collective-permute-start | bytes 393224 | tf_op jit(solution)/shard_map/ppermute | solution.py:388
  120.5 4.0 %collective-permute-start.6 = (bf16[256,256]{1,0:T(8,128)(2,1)S(1)}, bf16[256,256]{1,0:T(8,128)(2,1)S(1)}, u32[]{:S(2)}, u32[]{:S(2)}) collective-permute-start(bf16[256,256]{1,0:T(8,128)(2,1)S(1)} %get-tuple-element.63), channel_id=1, source_target_pairs={{0,3},{1,2},{2,1},{3,0},{4,7},{5,6},{6,5},{7,4},{8,11},{9,10},{10,... | collective-permute-start | bytes 393224 | tf_op jit(solution)/shard_map/ppermute | solution.py:388
  124.5 1.0 collective-permute-done.5.own2
  125.5 3.1 %collective-permute-done.6.own3 = bf16[256,256]{1,0:T(8,128)(2,1)S(1)} collective-permute-done((bf16[256,256]{1,0:T(8,128)(2,1)S(1)}, bf16[256,256]{1,0:T(8,128)(2,1)S(1)}, u32[]{:S(2)}, u32[]{:S(2)}) %collective-permute-start.6) | collective-permute-done | bytes 131104 | tf_op jit(solution)/shard_map/ppermute | solution.py:388
  128.5 3.5 %all-to-all-done.4 = bf16[128,2,4,128]{3,2,1,0:T(4,128)(2,1)S(1)} async-done(((bf16[128,2,4,128]{3,2,1,0:T(4,128)(2,1)}), bf16[128,2,4,128]{3,2,1,0:T(4,128)(2,1)S(1)}, u32[]{:S(2)}, u32[]{:S(2)}) %all-to-all-start.4) | async-done | bytes 262176 | tf_op jit(solution)/shard_map/all_to_all | solution.py:48
  132.1 0.9 shard_map.131
  132.9 3.5 %all-to-all-start.5 = ((bf16[4,256,256]{2,1,0:T(8,128)(2,1)}), bf16[4,256,256]{2,1,0:T(8,128)(2,1)S(1)}, u32[]{:S(2)}, u32[]{:S(2)}) async-start(bf16[4,256,256]{2,1,0:T(8,128)(2,1)} %shard_map.131), calls=%async_computation.5 | async-start | bytes 1048576 | tf_op jit(solution)/shard_map/all_to_all | solution.py:48
  136.4 0.9 copy-done.5
  137.3 0.9 copy-done.7
  138.2 1.0 shard_map.130
  139.2 4.8 %all-to-all-done.5.grads = bf16[4,256,256]{2,1,0:T(8,128)(2,1)S(1)} async-done(((bf16[4,256,256]{2,1,0:T(8,128)(2,1)}), bf16[4,256,256]{2,1,0:T(8,128)(2,1)S(1)}, u32[]{:S(2)}, u32[]{:S(2)}) %all-to-all-start.5) | async-done | bytes 524320 | tf_op jit(solution)/shard_map/all_to_all | solution.py:48
  144.0 4.7 %collective-permute-start.7 = (bf16[4,256,256]{2,1,0:T(8,128)(2,1)S(1)}, bf16[4,256,256]{2,1,0:T(8,128)(2,1)S(1)}, u32[]{:S(2)}, u32[]{:S(2)}) collective-permute-start(bf16[4,256,256]{2,1,0:T(8,128)(2,1)S(1)} %all-to-all-done.5.grads), channel_id=1, source_target_pairs={{0,8},{8,0},{1,9},{9,1},{2,10},{10,2},{3,11},{11,3},{4,12},{12,4},... | collective-permute-start | bytes 1572872 | tf_op jit(solution)/shard_map/ppermute | solution.py:44
  148.7 2.2 %shard_map.132 = (f32[8,256,256]{2,1,0:T(8,128)}, f32[8,256]{1,0:T(8,128)S(1)}) custom-call(s32[3]{0:T(128)S(1)} %pad_add_fusion.place, f32[8,256,256]{2,1,0:T(8,128)S(1)} %copy-done, f32[8,256]{1,0:T(8,128)S(1)} %copy-done.8, bf16[4,256,256]{2,1,0:T(8,128)(2,1)S(1)} %all-to-all-done.5.grads), custom_call_target="tpu_custom_call" | custom-call | bytes 3000000 | tf_op jit(solution)/shard_map/pallas_call | solution.py:291
  150.9 0.0 collective-permute-done.7.grads
  150.9 2.7 %shard_map.133 = (f32[8,256,256]{2,1,0:T(8,128)}, f32[8,256]{1,0:T(8,128)}) custom-call(s32[3]{0:T(128)S(1)} %pad_add_fusion.place, f32[8,256,256]{2,1,0:T(8,128)S(1)} %copy-done, f32[8,256]{1,0:T(8,128)S(1)} %copy-done.8, bf16[4,256,256]{2,1,0:T(8,128)(2,1)S(1)} %collective-permute-done.7.grads, ...), custom_call_target="tpu_custom_call", output_to_operand_aliasing={{0}: (4, {})} | custom-call | bytes 3000000 | tf_op jit(solution)/shard_map/pallas_call | solution.py:291
  (22 shorter events, 0.0 us)
Async XLA Ops:
  0.6 26.4 %copy-start.9 = (s32[64]{0:T(128)S(1)}, s32[64]{0:T(128)}, u32[]{:S(2)}) copy-start(s32[64]{0:T(128)} %matching.3) | copy-start | bytes 772
  2.4 24.7 %all-to-all-start = ((bf16[64,8,128]{2,1,0:T(8,128)(2,1)}), bf16[64,8,128]{2,1,0:T(8,128)(2,1)S(1)}, u32[]{:S(2)}, u32[]{:S(2)}) async-start(bf16[64,8,128]{2,1,0:T(8,128)(2,1)} %get-tuple-element.41), calls=%async_computation | async-start | bytes 262144 | tf_op jit(solution)/shard_map/all_to_all | solution.py:48
  17.0 23.9 %copy-start.11 = (bf16[272,256]{1,0:T(8,128)(2,1)S(1)}, bf16[272,256]{1,0:T(8,128)(2,1)}, u32[]{:S(2)}) copy-start(bf16[272,256]{1,0:T(8,128)(2,1)} %get-tuple-element.40.pack0) | copy-start | bytes 417796
  17.0 7.0 %collective-permute-start = (bf16[272,256]{1,0:T(8,128)(2,1)}, bf16[272,256]{1,0:T(8,128)(2,1)S(1)}, u32[]{:S(2)}, u32[]{:S(2)}) collective-permute-start(bf16[272,256]{1,0:T(8,128)(2,1)} %get-tuple-element.40.pack0), channel_id=1, source_target_pairs={{0,1},{1,0},{2,3},{3,2},{4,5},{5,4},{6,7},{7,6},{8,9},{9,8},{10,11... | collective-permute-start | bytes 417800 | tf_op jit(solution)/shard_map/ppermute | solution.py:339
  28.4 26.6 %all-to-all-start.1 = ((bf16[128,8,128]{2,1,0:T(8,128)(2,1)}), bf16[128,8,128]{2,1,0:T(8,128)(2,1)S(1)}, u32[]{:S(2)}, u32[]{:S(2)}) async-start(bf16[128,8,128]{2,1,0:T(8,128)(2,1)} %bitcast.7), calls=%async_computation.1 | async-start | bytes 524288 | tf_op jit(solution)/shard_map/all_to_all | solution.py:48
  40.9 10.5 %collective-permute-start.2 = (bf16[272,256]{1,0:T(8,128)(2,1)S(1)}, bf16[272,256]{1,0:T(8,128)(2,1)S(1)}, u32[]{:S(2)}, u32[]{:S(2)}) collective-permute-start(bf16[272,256]{1,0:T(8,128)(2,1)S(1)} %copy-done.11), channel_id=1, source_target_pairs={{0,3},{1,2},{2,1},{3,0},{4,7},{5,6},{6,5},{7,4},{8,11},{9,10},{10,... | collective-permute-start | bytes 417800 | tf_op jit(solution)/shard_map/ppermute | solution.py:339
  45.2 7.6 %collective-permute-start.1 = (bf16[272,256]{1,0:T(8,128)(2,1)S(1)}, bf16[272,256]{1,0:T(8,128)(2,1)S(1)}, u32[]{:S(2)}, u32[]{:S(2)}) collective-permute-start(bf16[272,256]{1,0:T(8,128)(2,1)S(1)} %copy-done.11), channel_id=1, source_target_pairs={{0,2},{1,3},{2,0},{3,1},{4,6},{5,7},{6,4},{7,5},{8,10},{9,11},{10,... | collective-permute-start | bytes 417800 | tf_op jit(solution)/shard_map/ppermute | solution.py:339
  47.8 1.2 copy-start.1
  49.0 6.0 %copy-start.2 = (bf16[8,256,256]{2,1,0:T(8,128)(2,1)S(1)}, bf16[8,256,256]{2,1,0:T(8,128)(2,1)}, u32[]{:S(2)}) copy-start(bf16[8,256,256]{2,1,0:T(8,128)(2,1)} %shard_map.121.rel_b) | copy-start | bytes 3145732
  61.7 4.4 %copy-start.12 = (bf16[2048,256]{1,0:T(8,128)(2,1)}, bf16[2048,256]{1,0:T(8,128)(2,1)S(1)}, u32[]{:S(2)}) copy-start(bf16[2048,256]{1,0:T(8,128)(2,1)S(1)} %get-tuple-element.49.g_trans) | copy-start | bytes 3145732
  61.7 5.0 %collective-permute-start.4 = (bf16[4,256,256]{2,1,0:T(8,128)(2,1)S(1)}, bf16[4,256,256]{2,1,0:T(8,128)(2,1)S(1)}, u32[]{:S(2)}, u32[]{:S(2)}) collective-permute-start(bf16[4,256,256]{2,1,0:T(8,128)(2,1)S(1)} %get-tuple-element.56), channel_id=1, source_target_pairs={{0,8},{8,0},{1,9},{9,1},{2,10},{10,2},{3,11},{11,3},{4,12},{12,4},... | collective-permute-start | bytes 1572872 | tf_op jit(solution)/shard_map/ppermute | solution.py:44
  66.7 25.4 %copy-start.13 = (bf16[2048,256]{1,0:T(8,128)(2,1)S(1)}, bf16[2048,256]{1,0:T(8,128)(2,1)}, u32[]{:S(2)}) copy-start(bf16[2048,256]{1,0:T(8,128)(2,1)} %copy-done.12) | copy-start | bytes 3145732
  80.3 28.2 %all-to-all-start.3 = ((bf16[128,3,4,128]{3,2,1,0:T(4,128)(2,1)}), bf16[128,3,4,128]{3,2,1,0:T(4,128)(2,1)S(1)}, u32[]{:S(2)}, u32[]{:S(2)}) async-start(bf16[128,3,4,128]{3,2,1,0:T(4,128)(2,1)} %bitcast.9), calls=%async_computation.3 | async-start | bytes 786432 | tf_op jit(solution)/shard_map/all_to_all | solution.py:48
  95.4 41.0 %copy-start.3 = (f32[256,256]{1,0:T(8,128)S(1)}, f32[256,256]{1,0:T(8,128)}, u32[]{:S(2)}) copy-start(f32[256,256]{1,0:T(8,128)} %emb.3) | copy-start | bytes 786436
  95.5 41.0 %copy-start.10 = (f32[256]{0:T(256)S(1)}, f32[256]{0:T(256)}, u32[]{:S(2)}) copy-start(f32[256]{0:T(256)} %param.10) | copy-start | bytes 3076
  95.5 6.1 %collective-permute-start.3 = (bf16[256,256]{1,0:T(8,128)(2,1)S(1)}, bf16[256,256]{1,0:T(8,128)(2,1)S(1)}, u32[]{:S(2)}, u32[]{:S(2)}) collective-permute-start(bf16[256,256]{1,0:T(8,128)(2,1)S(1)} %get-tuple-element.52), channel_id=1, source_target_pairs={{0,1},{1,0},{2,3},{3,2},{4,5},{5,4},{6,7},{7,6},{8,9},{9,8},{10,11... | collective-permute-start | bytes 393224 | tf_op jit(solution)/shard_map/ppermute | solution.py:388
  108.5 40.2 %copy-start = (f32[8,256,256]{2,1,0:T(8,128)S(1)}, f32[8,256,256]{2,1,0:T(8,128)}, u32[]{:S(2)}) copy-start(f32[8,256,256]{2,1,0:T(8,128)} %rel.5) | copy-start | bytes 6291460
  108.5 40.2 %copy-start.8 = (f32[8,256]{1,0:T(8,128)S(1)}, f32[8,256]{1,0:T(8,128)}, u32[]{:S(2)}) copy-start(f32[8,256]{1,0:T(8,128)} %accum.3) | copy-start | bytes 24580
  110.1 22.0 %all-to-all-start.4 = ((bf16[128,2,4,128]{3,2,1,0:T(4,128)(2,1)}), bf16[128,2,4,128]{3,2,1,0:T(4,128)(2,1)S(1)}, u32[]{:S(2)}, u32[]{:S(2)}) async-start(bf16[128,2,4,128]{3,2,1,0:T(4,128)(2,1)} %bitcast.11), calls=%async_computation.4 | async-start | bytes 524288 | tf_op jit(solution)/shard_map/all_to_all | solution.py:48
  117.9 7.5 %collective-permute-start.5 = (bf16[256,256]{1,0:T(8,128)(2,1)S(1)}, bf16[256,256]{1,0:T(8,128)(2,1)S(1)}, u32[]{:S(2)}, u32[]{:S(2)}) collective-permute-start(bf16[256,256]{1,0:T(8,128)(2,1)S(1)} %get-tuple-element.62), channel_id=1, source_target_pairs={{0,2},{1,3},{2,0},{3,1},{4,6},{5,7},{6,4},{7,5},{8,10},{9,11},{10,... | collective-permute-start | bytes 393224 | tf_op jit(solution)/shard_map/ppermute | solution.py:388
  120.5 8.1 %collective-permute-start.6 = (bf16[256,256]{1,0:T(8,128)(2,1)S(1)}, bf16[256,256]{1,0:T(8,128)(2,1)S(1)}, u32[]{:S(2)}, u32[]{:S(2)}) collective-permute-start(bf16[256,256]{1,0:T(8,128)(2,1)S(1)} %get-tuple-element.63), channel_id=1, source_target_pairs={{0,3},{1,2},{2,1},{3,0},{4,7},{5,6},{6,5},{7,4},{8,11},{9,10},{10,... | collective-permute-start | bytes 393224 | tf_op jit(solution)/shard_map/ppermute | solution.py:388
  125.5 7.5 %copy-start.4 = (bf16[256,256]{1,0:T(8,128)(2,1)}, bf16[256,256]{1,0:T(8,128)(2,1)S(1)}, u32[]{:S(2)}) copy-start(bf16[256,256]{1,0:T(8,128)(2,1)S(1)} %collective-permute-done.5.own2) | copy-start | bytes 393220
  128.5 4.4 %copy-start.6 = (bf16[256,256]{1,0:T(8,128)(2,1)}, bf16[256,256]{1,0:T(8,128)(2,1)S(1)}, u32[]{:S(2)}) copy-start(bf16[256,256]{1,0:T(8,128)(2,1)S(1)} %collective-permute-done.6.own3) | copy-start | bytes 393220
  132.9 11.1 %all-to-all-start.5 = ((bf16[4,256,256]{2,1,0:T(8,128)(2,1)}), bf16[4,256,256]{2,1,0:T(8,128)(2,1)S(1)}, u32[]{:S(2)}, u32[]{:S(2)}) async-start(bf16[4,256,256]{2,1,0:T(8,128)(2,1)} %shard_map.131), calls=%async_computation.5 | async-start | bytes 1048576 | tf_op jit(solution)/shard_map/all_to_all | solution.py:48
  136.4 0.9 copy-start.5
  137.3 0.9 copy-start.7
  144.0 6.9 %collective-permute-start.7 = (bf16[4,256,256]{2,1,0:T(8,128)(2,1)S(1)}, bf16[4,256,256]{2,1,0:T(8,128)(2,1)S(1)}, u32[]{:S(2)}, u32[]{:S(2)}) collective-permute-start(bf16[4,256,256]{2,1,0:T(8,128)(2,1)S(1)} %all-to-all-done.5.grads), channel_id=1, source_target_pairs={{0,8},{8,0},{1,9},{9,1},{2,10},{10,2},{3,11},{11,3},{4,12},{12,4},... | collective-permute-start | bytes 1572872 | tf_op jit(solution)/shard_map/ppermute | solution.py:44

commit v13 on v12

--- a/solution.py
+++ b/solution.py
@@ -198,17 +198,18 @@
         owns[s][...] = mine.astype(owns[s].dtype)
 
 
-def join_kernel(kept, came, out):
-    for k in range(4):
-        out[k] = (kept[k].astype(f32) + came[k].astype(f32)).astype(bf16)
-
-
-def pieces_kernel(got, g_rows, out):
+def join_kernel(place, kept, came, *outs):
+    for k, out in enumerate(outs):
+        target = place[2] ^ k
+        out[...] = (kept[target].astype(f32) + came[target].astype(f32)).astype(bf16)
+
+
+def pieces_kernel(got0, got1, got2, got3, g_rows, out):
     for h in range(2):
         half = slice(h * 128, (h + 1) * 128)
-        rel = got[0, :, half].astype(f32)
-        for k in range(1, 4):
-            rel = rel + got[k, :, half].astype(f32)
+        rel = got0[:, half].astype(f32)
+        for got in (got1, got2, got3):
+            rel = rel + got[:, half].astype(f32)
         for p, part in enumerate((g_rows[0, :, half].astype(f32), g_rows[1, :, half].astype(f32), rel)):
             tiles = part.reshape(32, 8, 128)
             for z in range(2):
@@ -374,8 +375,10 @@
         space=16,
     )
     came, g_rows = lax.optimization_barrier((came, g_rows))
-    got = spread(call(join_kernel, four, 0, (kept, came), moved=1_500_000), "x")
     one = shape((256, 256), bf16)
+    away = lambda part, k: lax.ppermute(part, "x", [(i, i ^ k) for i in range(4)])
+    joined = call(join_kernel, (one,) * 4, 1, (place, kept, came), moved=1_500_000)
+    got = list(joined[:1]) + [away(joined[k], k) for k in range(1, 4)]
     owns = call(
         own_kernel,
         (shape((256, 256), f32), one, one, one),
@@ -385,10 +388,9 @@
         moved=4_000_000,
         space=16,
     )
-    away = lambda part, k: lax.ppermute(part, "x", [(i, i ^ k) for i in range(4)])
     first = away(owns[1], 1)
     out = call(
-        pieces_kernel, shape((64, 2, 3, 4, 128), bf16), 0, (got, g_rows), moved=2_000_000
+        pieces_kernel, shape((64, 2, 3, 4, 128), bf16), 0, (*got, g_rows), moved=2_000_000
     )
     mid = spread(out.reshape(128, 3, 4, 128), DOM_Z)
     first, *others, mid = lax.optimization_barrier((first, *owns[2:], mid))

time: 155 us -> 157 us (1.013)
  blocking collectives: 12.6 us -> 0 us
  starting transfers between devices: 77.3 us -> 87.7 us
  waiting for transfers between devices: 31.7 us -> 35.7 us
    all_to_all x1 -> x0, blocking collectives: 12.6 us -> none  [spread(): return lax.all_to_all(value, axis, split_axis=0, concat_axis=0, tiled=True)]
    ppermute x3 -> x6, starting transfers between devices: 8.82 us -> 19.2 us  [body(): lax.ppermute(part, 'x', [(i, i ^ k) for i in range(4)])]
    ppermute x3 -> x6, waiting for transfers between devices: 7.88 us -> 12 us  [body(): lax.ppermute(part, 'x', [(i, i ^ k) for i in range(4)])]
  transfers between devices with their start and end apart: 13 -> 16, of which waited for: 11 -> 13; matrix products, arithmetic and copies ran while one was open for 0% -> 0% of each run, Pallas kernels for 8% -> 8%
where the time goes in v13:
time: 157 us; the launch traced here: 156 us
  starting transfers between devices  87.7 us (56%)
  waiting for transfers between devices  35.7 us (23%)
  Pallas kernels  28.5 us (18%)
  local copies, waits for them, and re-layouts  3.08 us (2%)
    all_to_all x5, starting transfers between devices, spread(): return lax.all_to_all(value, axis, split_axis=0, concat_axis=0, tiled=True)  50.2 us
    pallas_call x12, Pallas kernels, call(): pl.pallas_call(kernel, out_shape=outs, in_specs=specs, out_specs=tuple((A...  23.6 us
    all_to_all x5, waiting for transfers between devices, spread(): return lax.all_to_all(value, axis, split_axis=0, concat_axis=0, tiled=True)  20.1 us
    ppermute x6, starting transfers between devices, body(): lax.ppermute(part, 'x', [(i, i ^ k) for i in range(4)])  19.2 us
    ppermute x6, waiting for transfers between devices, body(): lax.ppermute(part, 'x', [(i, i ^ k) for i in range(4)])  12 us
    ppermute x3, starting transfers between devices, body(): lax.ppermute(pack, 'x', [(i, i ^ k) for i in range(4)])  10.1 us
    ppermute x2, starting transfers between devices, swap(): return lax.ppermute(value, axis, [(0, 1), (1, 0)])  8.21 us
    pallas_call x2, Pallas kernels, update_half(): pl.pallas_call(update_kernel, out_shape=(shape((8, 256, 256), f32), shape...  4.89 us
  transfers between devices with their start and end apart: 16, of which 13 were waited for; matrix products, arithmetic and copies ran while one was open for 0% of the time, Pallas kernels for 8%

profile of v13, /device:TPU:1, one launch (start us, length us, event | category | flops | bytes accessed | tf_op | source)
XLA Modules:
  0.0 156.2 jit_solution(17581166337763553182)
XLA Ops:
  0.6 1.7 %shard_map.120 = (bf16[64,8,128]{2,1,0:T(8,128)(2,1)}, bf16[272,256]{1,0:T(8,128)(2,1)}) custom-call(f32[256,256]{1,0:T(8,128)} %emb.3, s32[1,512]{1,0:T(1,128)} %bitcast.19, s32[1,512]{1,0:T(1,128)} %bitcast.20, s32[1,512]{1,0:T(1,128)} %bitcast.21, s32[1,512]{1,0:T(1,128)} %neg.1), custom_call_target="tpu_custom_call" | custom-call | bytes 800000 | tf_op jit(solution)/shard_map/pallas_call | solution.py:32
  2.4 14.6 %all-to-all-start = ((bf16[64,8,128]{2,1,0:T(8,128)(2,1)}), bf16[64,8,128]{2,1,0:T(8,128)(2,1)S(1)}, u32[]{:S(2)}, u32[]{:S(2)}) async-start(bf16[64,8,128]{2,1,0:T(8,128)(2,1)} %get-tuple-element.45), calls=%async_computation | async-start | bytes 262144 | tf_op jit(solution)/shard_map/all_to_all | solution.py:48
  17.0 3.3 %collective-permute-start = (bf16[272,256]{1,0:T(8,128)(2,1)}, bf16[272,256]{1,0:T(8,128)(2,1)S(1)}, u32[]{:S(2)}, u32[]{:S(2)}) collective-permute-start(bf16[272,256]{1,0:T(8,128)(2,1)} %get-tuple-element.44.pack0), channel_id=1, source_target_pairs={{0,1},{1,0},{2,3},{3,2},{4,5},{5,4},{6,7},{7,6},{8,9},{9,8},{10,11... | collective-permute-start | bytes 417800 | tf_op jit(solution)/shard_map/ppermute | solution.py:340
  20.3 2.3 %shard_map.121.rel_b = bf16[8,256,256]{2,1,0:T(8,128)(2,1)} custom-call(f32[8,256,256]{2,1,0:T(8,128)} %rel.5), custom_call_target="tpu_custom_call" | custom-call | bytes 3000000 | tf_op jit(solution)/shard_map/pallas_call | solution.py:32
  22.6 1.4 collective-permute-done.pack1
  24.0 3.0 %all-to-all-done.arrived = bf16[64,8,128]{2,1,0:T(8,128)(2,1)S(1)} async-done(((bf16[64,8,128]{2,1,0:T(8,128)(2,1)}), bf16[64,8,128]{2,1,0:T(8,128)(2,1)S(1)}, u32[]{:S(2)}, u32[]{:S(2)}) %all-to-all-start) | async-done | bytes 131104 | tf_op jit(solution)/shard_map/all_to_all | solution.py:48
  27.1 1.3 shard_map.122
  28.4 12.5 %all-to-all-start.1 = ((bf16[128,8,128]{2,1,0:T(8,128)(2,1)}), bf16[128,8,128]{2,1,0:T(8,128)(2,1)S(1)}, u32[]{:S(2)}, u32[]{:S(2)}) async-start(bf16[128,8,128]{2,1,0:T(8,128)(2,1)} %bitcast.7), calls=%async_computation.1 | async-start | bytes 524288 | tf_op jit(solution)/shard_map/all_to_all | solution.py:48
  40.9 4.4 %collective-permute-start.2 = (bf16[272,256]{1,0:T(8,128)(2,1)S(1)}, bf16[272,256]{1,0:T(8,128)(2,1)S(1)}, u32[]{:S(2)}, u32[]{:S(2)}) collective-permute-start(bf16[272,256]{1,0:T(8,128)(2,1)S(1)} %copy-done.11), channel_id=1, source_target_pairs={{0,3},{1,2},{2,1},{3,0},{4,7},{5,6},{6,5},{7,4},{8,11},{9,10},{10,... | collective-permute-start | bytes 417800 | tf_op jit(solution)/shard_map/ppermute | solution.py:340
  45.2 2.4 %collective-permute-start.1 = (bf16[272,256]{1,0:T(8,128)(2,1)S(1)}, bf16[272,256]{1,0:T(8,128)(2,1)S(1)}, u32[]{:S(2)}, u32[]{:S(2)}) collective-permute-start(bf16[272,256]{1,0:T(8,128)(2,1)S(1)} %copy-done.11), channel_id=1, source_target_pairs={{0,2},{1,3},{2,0},{3,1},{4,6},{5,7},{6,4},{7,5},{8,10},{9,11},{10,... | collective-permute-start | bytes 417800 | tf_op jit(solution)/shard_map/ppermute | solution.py:340
  47.7 0.1 pad_add_fusion.place
  47.8 1.2 copy-done.1
  49.0 2.4 %shard_map.123 = (f32[8,512]{1,0:T(8,128)S(1)}, f32[16,512]{1,0:T(8,128)S(1)}, bf16[1024,256]{1,0:T(8,128)(2,1)S(1)}, bf16[1024,256]{1,0:T(8,128)(2,1)S(1)}) custom-call(s32[3]{0:T(128)S(1)} %pad_add_fusion.place, bf16[272,256]{1,0:T(8,128)(2,1)S(1)} %copy-done.11, bf16[272,256]{1,0:T(8,128)(2,1)S(1)} %collective-permute-done.pack1, ...), custom_call_target="tpu_custom_call" | custom-call | flops 1300000000 | bytes 3000000 | tf_op jit(solution)/shard_map/pallas_call | solution.py:32
  51.4 1.5 collective-permute-done.1.pack2
  52.8 2.1 %all-to-all-done.1 = bf16[128,8,128]{2,1,0:T(8,128)(2,1)S(1)} async-done(((bf16[128,8,128]{2,1,0:T(8,128)(2,1)}), bf16[128,8,128]{2,1,0:T(8,128)(2,1)S(1)}, u32[]{:S(2)}, u32[]{:S(2)}) %all-to-all-start.1) | async-done | bytes 262176 | tf_op jit(solution)/shard_map/all_to_all | solution.py:48
  54.9 6.7 %shard_map.124 = (bf16[2048,512]{1,0:T(8,128)(2,1)S(1)}, bf16[2048,256]{1,0:T(8,128)(2,1)S(1)}, bf16[4,256,256]{2,1,0:T(8,128)(2,1)S(1)}, bf16[4,256,256]{2,1,0:...) custom-call(s32[3]{0:T(128)S(1)} %pad_add_fusion.place, bf16[64,2,8,128]{3,2,1,0:T(8,128)(2,1)S(1)} %bitcast.17, ...), custom_call_target="tpu_custom_call" | custom-call | flops 4499999744 | bytes 6000000 | tf_op jit(solution)/shard_map/pallas_call | solution.py:32
  61.7 0.0 copy-start.12
  61.7 3.5 %collective-permute-start.4 = (bf16[4,256,256]{2,1,0:T(8,128)(2,1)S(1)}, bf16[4,256,256]{2,1,0:T(8,128)(2,1)S(1)}, u32[]{:S(2)}, u32[]{:S(2)}) collective-permute-start(bf16[4,256,256]{2,1,0:T(8,128)(2,1)S(1)} %get-tuple-element.60), channel_id=1, source_target_pairs={{0,8},{8,0},{1,9},{9,1},{2,10},{10,2},{3,11},{11,3},{4,12},{12,4},... | collective-permute-start | bytes 1572872 | tf_op jit(solution)/shard_map/ppermute | solution.py:44
  65.2 0.9 shard_map.126.g_rows
  66.1 0.6 collective-permute-done.4.came
  66.7 0.7 shard_map.127
  67.4 3.1 %collective-permute-start.5 = (bf16[256,256]{1,0:T(8,128)(2,1)S(1)}, bf16[256,256]{1,0:T(8,128)(2,1)S(1)}, u32[]{:S(2)}, u32[]{:S(2)}) collective-permute-start(bf16[256,256]{1,0:T(8,128)(2,1)S(1)} %get-tuple-element.65), channel_id=1, source_target_pairs={{0,1},{1,0},{2,3},{3,2},{4,5},{5,4},{6,7},{7,6},{8,9},{9,8},{10,11... | collective-permute-start | bytes 393224 | tf_op jit(solution)/shard_map/ppermute | solution.py:379
  70.5 4.4 %collective-permute-start.6 = (bf16[256,256]{1,0:T(8,128)(2,1)S(1)}, bf16[256,256]{1,0:T(8,128)(2,1)S(1)}, u32[]{:S(2)}, u32[]{:S(2)}) collective-permute-start(bf16[256,256]{1,0:T(8,128)(2,1)S(1)} %get-tuple-element.66), channel_id=1, source_target_pairs={{0,2},{1,3},{2,0},{3,1},{4,6},{5,7},{6,4},{7,5},{8,10},{9,11},{10,... | collective-permute-start | bytes 393224 | tf_op jit(solution)/shard_map/ppermute | solution.py:379
  74.9 2.1 %collective-permute-start.7 = (bf16[256,256]{1,0:T(8,128)(2,1)S(1)}, bf16[256,256]{1,0:T(8,128)(2,1)S(1)}, u32[]{:S(2)}, u32[]{:S(2)}) collective-permute-start(bf16[256,256]{1,0:T(8,128)(2,1)S(1)} %get-tuple-element.67), channel_id=1, source_target_pairs={{0,3},{1,2},{2,1},{3,0},{4,7},{5,6},{6,5},{7,4},{8,11},{9,10},{10,... | collective-permute-start | bytes 393224 | tf_op jit(solution)/shard_map/ppermute | solution.py:379
  77.0 2.0 %collective-permute-done.6.got2 = bf16[256,256]{1,0:T(8,128)(2,1)S(1)} collective-permute-done((bf16[256,256]{1,0:T(8,128)(2,1)S(1)}, bf16[256,256]{1,0:T(8,128)(2,1)S(1)}, u32[]{:S(2)}, u32[]{:S(2)}) %collective-permute-start.6) | collective-permute-done | bytes 131104 | tf_op jit(solution)/shard_map/ppermute | solution.py:379
  79.1 2.8 %collective-permute-done.7.got3 = bf16[256,256]{1,0:T(8,128)(2,1)S(1)} collective-permute-done((bf16[256,256]{1,0:T(8,128)(2,1)S(1)}, bf16[256,256]{1,0:T(8,128)(2,1)S(1)}, u32[]{:S(2)}, u32[]{:S(2)}) %collective-permute-start.7) | collective-permute-done | bytes 131104 | tf_op jit(solution)/shard_map/ppermute | solution.py:379
  81.8 0.9 shard_map.128
  82.7 11.8 %all-to-all-start.2 = ((bf16[128,3,4,128]{3,2,1,0:T(4,128)(2,1)}), bf16[128,3,4,128]{3,2,1,0:T(4,128)(2,1)S(1)}, u32[]{:S(2)}, u32[]{:S(2)}) async-start(bf16[128,3,4,128]{3,2,1,0:T(4,128)(2,1)} %bitcast.9), calls=%async_computation.2 | async-start | bytes 786432 | tf_op jit(solution)/shard_map/all_to_all | solution.py:48
  94.5 3.3 %shard_map.125 = (f32[256,256]{1,0:T(8,128)S(1)}, bf16[256,256]{1,0:T(8,128)(2,1)S(1)}, bf16[256,256]{1,0:T(8,128)(2,1)S(1)}, bf16[256,256]{1,0:T(8,128)(2,1)S(1)}) custom-call(bf16[2048,256]{1,0:T(8,128)(2,1)S(1)} %copy-done.13, f32[16,512]{1,0:T(8,128)S(1)} %get-tuple-element.50.known.known0, f32[16,512]{1,0:T(8,128)S(1)} %get-tuple-element.54.known1, ...), custom_call_target="tpu_custom_call" | custom-call | flops 3000000000 | bytes 4000000 | tf_op jit(solution)/shard_map/pallas_call | solution.py:32
  97.9 2.7 %collective-permute-start.3 = (bf16[256,256]{1,0:T(8,128)(2,1)S(1)}, bf16[256,256]{1,0:T(8,128)(2,1)S(1)}, u32[]{:S(2)}, u32[]{:S(2)}) collective-permute-start(bf16[256,256]{1,0:T(8,128)(2,1)S(1)} %get-tuple-element.56), channel_id=1, source_target_pairs={{0,1},{1,0},{2,3},{3,2},{4,5},{5,4},{6,7},{7,6},{8,9},{9,8},{10,11... | collective-permute-start | bytes 393224 | tf_op jit(solution)/shard_map/ppermute | solution.py:379
  100.6 3.4 %collective-permute-done.3.own1 = bf16[256,256]{1,0:T(8,128)(2,1)S(1)} collective-permute-done((bf16[256,256]{1,0:T(8,128)(2,1)S(1)}, bf16[256,256]{1,0:T(8,128)(2,1)S(1)}, u32[]{:S(2)}, u32[]{:S(2)}) %collective-permute-start.3) | collective-permute-done | bytes 131104 | tf_op jit(solution)/shard_map/ppermute | solution.py:379
  104.0 6.9 %all-to-all-done.2 = bf16[128,3,4,128]{3,2,1,0:T(4,128)(2,1)S(1)} async-done(((bf16[128,3,4,128]{3,2,1,0:T(4,128)(2,1)}), bf16[128,3,4,128]{3,2,1,0:T(4,128)(2,1)S(1)}, u32[]{:S(2)}, u32[]{:S(2)}) %all-to-all-start.2) | async-done | bytes 393248 | tf_op jit(solution)/shard_map/all_to_all | solution.py:48
  110.9 1.5 shard_map.129
  112.4 7.9 %all-to-all-start.3 = ((bf16[128,2,4,128]{3,2,1,0:T(4,128)(2,1)}), bf16[128,2,4,128]{3,2,1,0:T(4,128)(2,1)S(1)}, u32[]{:S(2)}, u32[]{:S(2)}) async-start(bf16[128,2,4,128]{3,2,1,0:T(4,128)(2,1)} %bitcast.11), calls=%async_computation.3 | async-start | bytes 524288 | tf_op jit(solution)/shard_map/all_to_all | solution.py:48
  120.3 3.5 %collective-permute-start.8 = (bf16[256,256]{1,0:T(8,128)(2,1)S(1)}, bf16[256,256]{1,0:T(8,128)(2,1)S(1)}, u32[]{:S(2)}, u32[]{:S(2)}) collective-permute-start(bf16[256,256]{1,0:T(8,128)(2,1)S(1)} %get-tuple-element.70), channel_id=1, source_target_pairs={{0,2},{1,3},{2,0},{3,1},{4,6},{5,7},{6,4},{7,5},{8,10},{9,11},{10,... | collective-permute-start | bytes 393224 | tf_op jit(solution)/shard_map/ppermute | solution.py:379
  123.9 3.4 %collective-permute-start.9 = (bf16[256,256]{1,0:T(8,128)(2,1)S(1)}, bf16[256,256]{1,0:T(8,128)(2,1)S(1)}, u32[]{:S(2)}, u32[]{:S(2)}) collective-permute-start(bf16[256,256]{1,0:T(8,128)(2,1)S(1)} %get-tuple-element.71), channel_id=1, source_target_pairs={{0,3},{1,2},{2,1},{3,0},{4,7},{5,6},{6,5},{7,4},{8,11},{9,10},{10,... | collective-permute-start | bytes 393224 | tf_op jit(solution)/shard_map/ppermute | solution.py:379
  127.2 0.6 collective-permute-done.8.own2
  127.8 3.3 %collective-permute-done.9.own3 = bf16[256,256]{1,0:T(8,128)(2,1)S(1)} collective-permute-done((bf16[256,256]{1,0:T(8,128)(2,1)S(1)}, bf16[256,256]{1,0:T(8,128)(2,1)S(1)}, u32[]{:S(2)}, u32[]{:S(2)}) %collective-permute-start.9) | collective-permute-done | bytes 131104 | tf_op jit(solution)/shard_map/ppermute | solution.py:379
  131.1 3.3 %all-to-all-done.3 = bf16[128,2,4,128]{3,2,1,0:T(4,128)(2,1)S(1)} async-done(((bf16[128,2,4,128]{3,2,1,0:T(4,128)(2,1)}), bf16[128,2,4,128]{3,2,1,0:T(4,128)(2,1)S(1)}, u32[]{:S(2)}, u32[]{:S(2)}) %all-to-all-start.3) | async-done | bytes 262176 | tf_op jit(solution)/shard_map/all_to_all | solution.py:48
  134.4 0.9 shard_map.131
  135.3 3.5 %all-to-all-start.4 = ((bf16[4,256,256]{2,1,0:T(8,128)(2,1)}), bf16[4,256,256]{2,1,0:T(8,128)(2,1)S(1)}, u32[]{:S(2)}, u32[]{:S(2)}) async-start(bf16[4,256,256]{2,1,0:T(8,128)(2,1)} %shard_map.131), calls=%async_computation.4 | async-start | bytes 1048576 | tf_op jit(solution)/shard_map/all_to_all | solution.py:48
  138.8 0.9 copy-done.5
  139.7 0.9 copy-done.7
  140.6 1.0 shard_map.130
  141.6 4.7 %all-to-all-done.4.grads = bf16[4,256,256]{2,1,0:T(8,128)(2,1)S(1)} async-done(((bf16[4,256,256]{2,1,0:T(8,128)(2,1)}), bf16[4,256,256]{2,1,0:T(8,128)(2,1)S(1)}, u32[]{:S(2)}, u32[]{:S(2)}) %all-to-all-start.4) | async-done | bytes 524320 | tf_op jit(solution)/shard_map/all_to_all | solution.py:48
  146.4 4.7 %collective-permute-start.10 = (bf16[4,256,256]{2,1,0:T(8,128)(2,1)S(1)}, bf16[4,256,256]{2,1,0:T(8,128)(2,1)S(1)}, u32[]{:S(2)}, u32[]{:S(2)}) collective-permute-start(bf16[4,256,256]{2,1,0:T(8,128)(2,1)S(1)} %all-to-all-done.4.grads), channel_id=1, source_target_pairs={{0,8},{8,0},{1,9},{9,1},{2,10},{10,2},{3,11},{11,3},{4,12},{12,4},... | collective-permute-start | bytes 1572872 | tf_op jit(solution)/shard_map/ppermute | solution.py:44
  151.1 2.2 %shard_map.132 = (f32[8,256,256]{2,1,0:T(8,128)}, f32[8,256]{1,0:T(8,128)S(1)}) custom-call(s32[3]{0:T(128)S(1)} %pad_add_fusion.place, f32[8,256,256]{2,1,0:T(8,128)S(1)} %copy-done, f32[8,256]{1,0:T(8,128)S(1)} %copy-done.8, bf16[4,256,256]{2,1,0:T(8,128)(2,1)S(1)} %all-to-all-done.4.grads), custom_call_target="tpu_custom_call" | custom-call | bytes 3000000 | tf_op jit(solution)/shard_map/pallas_call | solution.py:292
  153.3 2.7 %shard_map.133 = (f32[8,256,256]{2,1,0:T(8,128)}, f32[8,256]{1,0:T(8,128)}) custom-call(s32[3]{0:T(128)S(1)} %pad_add_fusion.place, f32[8,256,256]{2,1,0:T(8,128)S(1)} %copy-done, f32[8,256]{1,0:T(8,128)S(1)} %copy-done.8, bf16[4,256,256]{2,1,0:T(8,128)(2,1)S(1)} %collective-permute-done.10.grads, ...), custom_call_target="tpu_custom_call", output_to_operand_aliasing={{0}: (4, {})} | custom-call | bytes 3000000 | tf_op jit(solution)/shard_map/pallas_call | solution.py:292
  (27 shorter events, 0.1 us)
Async XLA Ops:
  0.6 26.4 %copy-start.9 = (s32[64]{0:T(128)S(1)}, s32[64]{0:T(128)}, u32[]{:S(2)}) copy-start(s32[64]{0:T(128)} %matching.3) | copy-start | bytes 772
  2.4 24.7 %all-to-all-start = ((bf16[64,8,128]{2,1,0:T(8,128)(2,1)}), bf16[64,8,128]{2,1,0:T(8,128)(2,1)S(1)}, u32[]{:S(2)}, u32[]{:S(2)}) async-start(bf16[64,8,128]{2,1,0:T(8,128)(2,1)} %get-tuple-element.45), calls=%async_computation | async-start | bytes 262144 | tf_op jit(solution)/shard_map/all_to_all | solution.py:48
  17.0 23.9 %copy-start.11 = (bf16[272,256]{1,0:T(8,128)(2,1)S(1)}, bf16[272,256]{1,0:T(8,128)(2,1)}, u32[]{:S(2)}) copy-start(bf16[272,256]{1,0:T(8,128)(2,1)} %get-tuple-element.44.pack0) | copy-start | bytes 417796
  17.0 7.0 %collective-permute-start = (bf16[272,256]{1,0:T(8,128)(2,1)}, bf16[272,256]{1,0:T(8,128)(2,1)S(1)}, u32[]{:S(2)}, u32[]{:S(2)}) collective-permute-start(bf16[272,256]{1,0:T(8,128)(2,1)} %get-tuple-element.44.pack0), channel_id=1, source_target_pairs={{0,1},{1,0},{2,3},{3,2},{4,5},{5,4},{6,7},{7,6},{8,9},{9,8},{10,11... | collective-permute-start | bytes 417800 | tf_op jit(solution)/shard_map/ppermute | solution.py:340
  28.4 26.6 %all-to-all-start.1 = ((bf16[128,8,128]{2,1,0:T(8,128)(2,1)}), bf16[128,8,128]{2,1,0:T(8,128)(2,1)S(1)}, u32[]{:S(2)}, u32[]{:S(2)}) async-start(bf16[128,8,128]{2,1,0:T(8,128)(2,1)} %bitcast.7), calls=%async_computation.1 | async-start | bytes 524288 | tf_op jit(solution)/shard_map/all_to_all | solution.py:48
  40.9 10.5 %collective-permute-start.2 = (bf16[272,256]{1,0:T(8,128)(2,1)S(1)}, bf16[272,256]{1,0:T(8,128)(2,1)S(1)}, u32[]{:S(2)}, u32[]{:S(2)}) collective-permute-start(bf16[272,256]{1,0:T(8,128)(2,1)S(1)} %copy-done.11), channel_id=1, source_target_pairs={{0,3},{1,2},{2,1},{3,0},{4,7},{5,6},{6,5},{7,4},{8,11},{9,10},{10,... | collective-permute-start | bytes 417800 | tf_op jit(solution)/shard_map/ppermute | solution.py:340
  45.2 7.6 %collective-permute-start.1 = (bf16[272,256]{1,0:T(8,128)(2,1)S(1)}, bf16[272,256]{1,0:T(8,128)(2,1)S(1)}, u32[]{:S(2)}, u32[]{:S(2)}) collective-permute-start(bf16[272,256]{1,0:T(8,128)(2,1)S(1)} %copy-done.11), channel_id=1, source_target_pairs={{0,2},{1,3},{2,0},{3,1},{4,6},{5,7},{6,4},{7,5},{8,10},{9,11},{10,... | collective-permute-start | bytes 417800 | tf_op jit(solution)/shard_map/ppermute | solution.py:340
  47.8 1.2 copy-start.1
  49.0 6.0 %copy-start.2 = (bf16[8,256,256]{2,1,0:T(8,128)(2,1)S(1)}, bf16[8,256,256]{2,1,0:T(8,128)(2,1)}, u32[]{:S(2)}) copy-start(bf16[8,256,256]{2,1,0:T(8,128)(2,1)} %shard_map.121.rel_b) | copy-start | bytes 3145732
  61.7 4.4 %copy-start.12 = (bf16[2048,256]{1,0:T(8,128)(2,1)}, bf16[2048,256]{1,0:T(8,128)(2,1)S(1)}, u32[]{:S(2)}) copy-start(bf16[2048,256]{1,0:T(8,128)(2,1)S(1)} %get-tuple-element.53.g_trans) | copy-start | bytes 3145732
  61.7 5.0 %collective-permute-start.4 = (bf16[4,256,256]{2,1,0:T(8,128)(2,1)S(1)}, bf16[4,256,256]{2,1,0:T(8,128)(2,1)S(1)}, u32[]{:S(2)}, u32[]{:S(2)}) collective-permute-start(bf16[4,256,256]{2,1,0:T(8,128)(2,1)S(1)} %get-tuple-element.60), channel_id=1, source_target_pairs={{0,8},{8,0},{1,9},{9,1},{2,10},{10,2},{3,11},{11,3},{4,12},{12,4},... | collective-permute-start | bytes 1572872 | tf_op jit(solution)/shard_map/ppermute | solution.py:44
  66.7 27.8 %copy-start.13 = (bf16[2048,256]{1,0:T(8,128)(2,1)S(1)}, bf16[2048,256]{1,0:T(8,128)(2,1)}, u32[]{:S(2)}) copy-start(bf16[2048,256]{1,0:T(8,128)(2,1)} %copy-done.12) | copy-start | bytes 3145732
  67.4 9.6 %collective-permute-start.5 = (bf16[256,256]{1,0:T(8,128)(2,1)S(1)}, bf16[256,256]{1,0:T(8,128)(2,1)S(1)}, u32[]{:S(2)}, u32[]{:S(2)}) collective-permute-start(bf16[256,256]{1,0:T(8,128)(2,1)S(1)} %get-tuple-element.65), channel_id=1, source_target_pairs={{0,1},{1,0},{2,3},{3,2},{4,5},{5,4},{6,7},{7,6},{8,9},{9,8},{10,11... | collective-permute-start | bytes 393224 | tf_op jit(solution)/shard_map/ppermute | solution.py:379
  70.5 8.5 %collective-permute-start.6 = (bf16[256,256]{1,0:T(8,128)(2,1)S(1)}, bf16[256,256]{1,0:T(8,128)(2,1)S(1)}, u32[]{:S(2)}, u32[]{:S(2)}) collective-permute-start(bf16[256,256]{1,0:T(8,128)(2,1)S(1)} %get-tuple-element.66), channel_id=1, source_target_pairs={{0,2},{1,3},{2,0},{3,1},{4,6},{5,7},{6,4},{7,5},{8,10},{9,11},{10,... | collective-permute-start | bytes 393224 | tf_op jit(solution)/shard_map/ppermute | solution.py:379
  74.9 6.9 %collective-permute-start.7 = (bf16[256,256]{1,0:T(8,128)(2,1)S(1)}, bf16[256,256]{1,0:T(8,128)(2,1)S(1)}, u32[]{:S(2)}, u32[]{:S(2)}) collective-permute-start(bf16[256,256]{1,0:T(8,128)(2,1)S(1)} %get-tuple-element.67), channel_id=1, source_target_pairs={{0,3},{1,2},{2,1},{3,0},{4,7},{5,6},{6,5},{7,4},{8,11},{9,10},{10,... | collective-permute-start | bytes 393224 | tf_op jit(solution)/shard_map/ppermute | solution.py:379
  82.7 28.2 %all-to-all-start.2 = ((bf16[128,3,4,128]{3,2,1,0:T(4,128)(2,1)}), bf16[128,3,4,128]{3,2,1,0:T(4,128)(2,1)S(1)}, u32[]{:S(2)}, u32[]{:S(2)}) async-start(bf16[128,3,4,128]{3,2,1,0:T(4,128)(2,1)} %bitcast.9), calls=%async_computation.2 | async-start | bytes 786432 | tf_op jit(solution)/shard_map/all_to_all | solution.py:48
  97.8 41.0 %copy-start.3 = (f32[256,256]{1,0:T(8,128)S(1)}, f32[256,256]{1,0:T(8,128)}, u32[]{:S(2)}) copy-start(f32[256,256]{1,0:T(8,128)} %emb.3) | copy-start | bytes 786436
  97.8 41.0 %copy-start.10 = (f32[256]{0:T(256)S(1)}, f32[256]{0:T(256)}, u32[]{:S(2)}) copy-start(f32[256]{0:T(256)} %param.10) | copy-start | bytes 3076
  97.9 6.1 %collective-permute-start.3 = (bf16[256,256]{1,0:T(8,128)(2,1)S(1)}, bf16[256,256]{1,0:T(8,128)(2,1)S(1)}, u32[]{:S(2)}, u32[]{:S(2)}) collective-permute-start(bf16[256,256]{1,0:T(8,128)(2,1)S(1)} %get-tuple-element.56), channel_id=1, source_target_pairs={{0,1},{1,0},{2,3},{3,2},{4,5},{5,4},{6,7},{7,6},{8,9},{9,8},{10,11... | collective-permute-start | bytes 393224 | tf_op jit(solution)/shard_map/ppermute | solution.py:379
  110.9 40.2 %copy-start = (f32[8,256,256]{2,1,0:T(8,128)S(1)}, f32[8,256,256]{2,1,0:T(8,128)}, u32[]{:S(2)}) copy-start(f32[8,256,256]{2,1,0:T(8,128)} %rel.5) | copy-start | bytes 6291460
  110.9 40.2 %copy-start.8 = (f32[8,256]{1,0:T(8,128)S(1)}, f32[8,256]{1,0:T(8,128)}, u32[]{:S(2)}) copy-start(f32[8,256]{1,0:T(8,128)} %accum.3) | copy-start | bytes 24580
  112.4 22.0 %all-to-all-start.3 = ((bf16[128,2,4,128]{3,2,1,0:T(4,128)(2,1)}), bf16[128,2,4,128]{3,2,1,0:T(4,128)(2,1)S(1)}, u32[]{:S(2)}, u32[]{:S(2)}) async-start(bf16[128,2,4,128]{3,2,1,0:T(4,128)(2,1)} %bitcast.11), calls=%async_computation.3 | async-start | bytes 524288 | tf_op jit(solution)/shard_map/all_to_all | solution.py:48
  120.3 7.5 %collective-permute-start.8 = (bf16[256,256]{1,0:T(8,128)(2,1)S(1)}, bf16[256,256]{1,0:T(8,128)(2,1)S(1)}, u32[]{:S(2)}, u32[]{:S(2)}) collective-permute-start(bf16[256,256]{1,0:T(8,128)(2,1)S(1)} %get-tuple-element.70), channel_id=1, source_target_pairs={{0,2},{1,3},{2,0},{3,1},{4,6},{5,7},{6,4},{7,5},{8,10},{9,11},{10,... | collective-permute-start | bytes 393224 | tf_op jit(solution)/shard_map/ppermute | solution.py:379
  123.9 7.2 %collective-permute-start.9 = (bf16[256,256]{1,0:T(8,128)(2,1)S(1)}, bf16[256,256]{1,0:T(8,128)(2,1)S(1)}, u32[]{:S(2)}, u32[]{:S(2)}) collective-permute-start(bf16[256,256]{1,0:T(8,128)(2,1)S(1)} %get-tuple-element.71), channel_id=1, source_target_pairs={{0,3},{1,2},{2,1},{3,0},{4,7},{5,6},{6,5},{7,4},{8,11},{9,10},{10,... | collective-permute-start | bytes 393224 | tf_op jit(solution)/shard_map/ppermute | solution.py:379
  127.8 7.5 %copy-start.4 = (bf16[256,256]{1,0:T(8,128)(2,1)}, bf16[256,256]{1,0:T(8,128)(2,1)S(1)}, u32[]{:S(2)}) copy-start(bf16[256,256]{1,0:T(8,128)(2,1)S(1)} %collective-permute-done.8.own2) | copy-start | bytes 393220
  131.1 4.2 %copy-start.6 = (bf16[256,256]{1,0:T(8,128)(2,1)}, bf16[256,256]{1,0:T(8,128)(2,1)S(1)}, u32[]{:S(2)}) copy-start(bf16[256,256]{1,0:T(8,128)(2,1)S(1)} %collective-permute-done.9.own3) | copy-start | bytes 393220
  135.3 11.1 %all-to-all-start.4 = ((bf16[4,256,256]{2,1,0:T(8,128)(2,1)}), bf16[4,256,256]{2,1,0:T(8,128)(2,1)S(1)}, u32[]{:S(2)}, u32[]{:S(2)}) async-start(bf16[4,256,256]{2,1,0:T(8,128)(2,1)} %shard_map.131), calls=%async_computation.4 | async-start | bytes 1048576 | tf_op jit(solution)/shard_map/all_to_all | solution.py:48
  138.8 0.9 copy-start.5
  139.7 0.9 copy-start.7
  146.4 6.9 %collective-permute-start.10 = (bf16[4,256,256]{2,1,0:T(8,128)(2,1)S(1)}, bf16[4,256,256]{2,1,0:T(8,128)(2,1)S(1)}, u32[]{:S(2)}, u32[]{:S(2)}) collective-permute-start(bf16[4,256,256]{2,1,0:T(8,128)(2,1)S(1)} %all-to-all-done.4.grads), channel_id=1, source_target_pairs={{0,8},{8,0},{1,9},{9,1},{2,10},{10,2},{3,11},{11,3},{4,12},{12,4},... | collective-permute-start | bytes 1572872 | tf_op jit(solution)/shard_map/ppermute | solution.py:44

commit v14 on v12

--- a/solution.py
+++ b/solution.py
@@ -48,30 +48,51 @@
     return lax.all_to_all(value, axis, split_axis=0, concat_axis=0, tiled=True)
 
 
-def first_kernel(emb, src, rel, dst, neg, pieces, pack, rows, index, sems):
-    copies = [pltpu.make_async_copy(emb, rows, sems.at[0])]
-    for k, part in enumerate((src, rel, dst, neg)):
-        copies.append(pltpu.make_async_copy(part, index.at[k], sems.at[k + 1]))
-    for copy in copies:
-        copy.start()
-    for copy in copies:
-        copy.wait()
+def copy_out(source, target, sem):
+    copy = pltpu.make_async_copy(source, target, sem)
+    copy.start()
+    return copy
+
+
+def first_kernel(emb, src, rel, dst, neg, pieces_out, pack_out, rows, index, pieces, pack, sems):
+    halves = [
+        copy_out(emb.at[pl.ds(k * 128, 128), :], rows.at[pl.ds(k * 128, 128), :], sems.at[k])
+        for k in range(2)
+    ]
+    parts = [copy_out(part, index.at[k], sems.at[2 + k]) for k, part in enumerate((src, rel, dst, neg))]
+    sent = []
+    for k in range(2):
+        halves[k].wait()
+        block = rows[k * 128 : (k + 1) * 128, :]
+        for h in range(2):
+            span = slice(h * 32 + k * 16, h * 32 + (k + 1) * 16)
+            pieces[span] = block[:, h * 128 : (h + 1) * 128].reshape(16, 8, 128).astype(bf16)
+            place = pl.ds(h * 32 + k * 16, 16)
+            sent.append(copy_out(pieces.at[place], pieces_out.at[place], sems.at[6 + 2 * k + h]))
+        pack[k * 128 : (k + 1) * 128, :] = block.astype(bf16)
+    for part in parts:
+        part.wait()
     wide = jnp.concatenate([index[k] for k in range(4)], axis=0)
     high = wide // 256
     low = (wide - high * 256).astype(f32)
     both = jnp.concatenate([high.astype(f32), low], axis=0)
     pack[256:272, :] = jnp.concatenate([both[:, :256], both[:, 256:]], axis=0).astype(bf16)
-    pack[0:256, :] = rows[...].astype(bf16)
-    for h in range(2):
-        half = rows[:, h * 128 : (h + 1) * 128]
-        pieces[h * 32 : (h + 1) * 32] = half.reshape(32, 8, 128).astype(bf16)
-
-
-def take_kernel(matching, arrived, routed):
-    for d in range(64):
-        piece = arrived[matching[d]]
-        routed[d, 0] = piece
-        routed[d, 1] = piece
+    sent.append(copy_out(pack, pack_out, sems.at[10]))
+    for copy in sent:
+        copy.wait()
+
+
+def take_kernel(matching, arrived, out, routed, sems):
+    sent = []
+    for k in range(4):
+        for d in range(k * 16, (k + 1) * 16):
+            piece = arrived[matching[d]]
+            routed[d, 0] = piece
+            routed[d, 1] = piece
+        span = pl.ds(k * 16, 16)
+        sent.append(copy_out(routed.at[span], out.at[span], sems.at[k]))
+    for copy in sent:
+        copy.wait()
 
 
 def indices(part):
@@ -203,7 +224,8 @@
         out[k] = (kept[k].astype(f32) + came[k].astype(f32)).astype(bf16)
 
 
-def pieces_kernel(got, g_rows, out):
+def pieces_kernel(got, g_rows, out, tiles_out, sems):
+    sent = []
     for h in range(2):
         half = slice(h * 128, (h + 1) * 128)
         rel = got[0, :, half].astype(f32)
@@ -212,19 +234,25 @@
         for p, part in enumerate((g_rows[0, :, half].astype(f32), g_rows[1, :, half].astype(f32), rel)):
             tiles = part.reshape(32, 8, 128)
             for z in range(2):
-                out[h * 32 : (h + 1) * 32, z, p] = tiles[:, z * 4 : (z + 1) * 4].astype(bf16)
+                tiles_out[h * 32 : (h + 1) * 32, z, p] = tiles[:, z * 4 : (z + 1) * 4].astype(bf16)
+        span = pl.ds(h * 32, 32)
+        sent.append(copy_out(tiles_out.at[span], out.at[span], sems.at[h]))
+    for copy in sent:
+        copy.wait()
 
 
 def route_kernel(matching, mid, out):
-    rel = [jnp.zeros((4, 128), f32), jnp.zeros((4, 128), f32)]
-    for d in range(64):
-        rel[d % 2] = rel[d % 2] + (mid[d, 0, 2].astype(f32) + mid[d, 1, 2].astype(f32))
+    parts = mid[:, :, 2].astype(f32).reshape(32, 2, 2, 4, 128)
+    for c in range(2):
+        tail = jnp.sum(jnp.sum(parts[:, c], axis=1), axis=0).astype(bf16)
+        for d in range(c, 64, 2):
+            for z in range(2):
+                out[d, z, 1] = tail
+    rows = (mid[:, 0, 0:2].astype(f32) + mid[:, 1, 0:2].astype(f32)).astype(bf16)
     for d in range(64):
         target = matching[d]
-        tail = jnp.where(target % 2 == 0, rel[0], rel[1]).astype(bf16)
         for z in range(2):
-            out[target, z, 0] = (mid[d, 0, z].astype(f32) + mid[d, 1, z].astype(f32)).astype(bf16)
-            out[target, z, 1] = tail
+            out[target, z, 0] = rows[d, z]
 
 
 def whole(last, h, p):
@@ -233,11 +261,11 @@
     return jnp.concatenate(parts, axis=1).reshape(256, 128)
 
 
-def rel_kernel(last, out):
+def rel_kernel(last, out, held, sems):
     for h in range(2):
-        part = whole(last, h, 1).astype(bf16)
-        for k in range(4):
-            out[k, :, h * 128 : (h + 1) * 128] = part
+        held[:, h * 128 : (h + 1) * 128] = whole(last, h, 1).astype(bf16)
+    for copy in [copy_out(held, out.at[k], sems.at[k]) for k in range(4)]:
+        copy.wait()
 
 
 def to_row(column):
@@ -312,11 +340,14 @@
         (embeddings, line(src_rows), line(rel_ids), line(dst_rows), line(neg_rows)),
         moved=800_000,
         far=(0, 1, 2, 3, 4),
+        far_outs=(0, 1),
         space=62,
         scratch=[
             pltpu.VMEM((256, 256), f32),
             pltpu.VMEM((4, 1, 512), jnp.int32),
-            pltpu.SemaphoreType.DMA((5,)),
+            pltpu.VMEM((64, 8, 128), bf16),
+            pltpu.VMEM((272, 256), bf16),
+            pltpu.SemaphoreType.DMA((11,)),
         ],
     )
     arrived = spread(pieces, DOM)
@@ -339,7 +370,15 @@
         lax.ppermute(pack, "x", [(i, i ^ k) for i in range(4)]) for k in range(1, 4)
     ]
     packs[1], rel_b, arrived = lax.optimization_barrier((packs[1], rel_b, arrived))
-    routed = call(take_kernel, shape((64, 2, 8, 128), bf16), 1, (matching, arrived), moved=400_000)
+    routed = call(
+        take_kernel,
+        shape((64, 2, 8, 128), bf16),
+        1,
+        (matching, arrived),
+        moved=400_000,
+        far_outs=(0,),
+        scratch=[pltpu.VMEM((64, 2, 8, 128), bf16), pltpu.SemaphoreType.DMA((4,))],
+    )
     rows_in = spread(routed.reshape(128, 8, 128), DOM_Z).reshape(64, 2, 8, 128)
     block = shape((1024, 256), bf16)
     known_shape = shape((16, 512), f32)
@@ -388,7 +427,13 @@
     away = lambda part, k: lax.ppermute(part, "x", [(i, i ^ k) for i in range(4)])
     first = away(owns[1], 1)
     out = call(
-        pieces_kernel, shape((64, 2, 3, 4, 128), bf16), 0, (got, g_rows), moved=2_000_000
+        pieces_kernel,
+        shape((64, 2, 3, 4, 128), bf16),
+        0,
+        (got, g_rows),
+        moved=2_000_000,
+        far_outs=(0,),
+        scratch=[pltpu.VMEM((64, 2, 3, 4, 128), bf16), pltpu.SemaphoreType.DMA((2,))],
     )
     mid = spread(out.reshape(128, 3, 4, 128), DOM_Z)
     first, *others, mid = lax.optimization_barrier((first, *owns[2:], mid))
@@ -402,7 +447,17 @@
     )
     last = spread(routed_back.reshape(128, 2, 4, 128), DOM_Z).reshape(64, 2, 2, 4, 128)
     *others, last = lax.optimization_barrier((*others, last))
-    rel_four = spread(call(rel_kernel, four, 0, (last,), moved=512_000), "x")
+    rel_four = spread(call(
+            rel_kernel,
+            four,
+            0,
+            (last,),
+            moved=512_000,
+            far_outs=(0,),
+            scratch=[pltpu.VMEM((256, 256), bf16), pltpu.SemaphoreType.DMA((4,))],
+        ),
+        "x",
+    )
     new_embeddings, new_row_accum = call(
         rows_kernel,
         (shape((256, 256), f32), shape((1, 256), f32)),

time: 155 us -> 155 us (level)
  no operation moved by 1% of the time
where the time goes in v14:
time: 155 us; the launch traced here: 154 us
  starting transfers between devices  77.3 us (50%)
  waiting for transfers between devices  31.7 us (20%)
  Pallas kernels  27.8 us (18%)
  blocking collectives  12.6 us (8%)
  local copies, waits for them, and re-layouts  3.08 us (2%)
    all_to_all x5, starting transfers between devices, spread(): return lax.all_to_all(value, axis, split_axis=0, concat_axis=0, tiled=True)  50.2 us
    pallas_call x12, Pallas kernels, call(): pl.pallas_call(kernel, out_shape=outs, in_specs=specs, out_specs=tuple((A...  22.9 us
    all_to_all x5, waiting for transfers between devices, spread(): return lax.all_to_all(value, axis, split_axis=0, concat_axis=0, tiled=True)  20.3 us
    all_to_all x1, blocking collectives, spread(): return lax.all_to_all(value, axis, split_axis=0, concat_axis=0, tiled=True)  12.6 us
    ppermute x3, starting transfers between devices, body(): lax.ppermute(pack, 'x', [(i, i ^ k) for i in range(4)])  10.1 us
    ppermute x3, starting transfers between devices, body(): lax.ppermute(part, 'x', [(i, i ^ k) for i in range(4)])  8.82 us
    ppermute x2, starting transfers between devices, swap(): return lax.ppermute(value, axis, [(0, 1), (1, 0)])  8.2 us
    ppermute x3, waiting for transfers between devices, body(): lax.ppermute(part, 'x', [(i, i ^ k) for i in range(4)])  7.89 us
  transfers between devices with their start and end apart: 13, of which 11 were waited for; matrix products, arithmetic and copies ran while one was open for 0% of the time, Pallas kernels for 8%

profile of v14, /device:TPU:1, one launch (start us, length us, event | category | flops | bytes accessed | tf_op | source)
XLA Modules:
  0.0 153.7 jit_solution(8846959427935699745)
XLA Ops:
  0.6 1.8 %shard_map.120 = (bf16[64,8,128]{2,1,0:T(8,128)(2,1)}, bf16[272,256]{1,0:T(8,128)(2,1)}) custom-call(f32[256,256]{1,0:T(8,128)} %emb.3, s32[1,512]{1,0:T(1,128)} %bitcast.19, s32[1,512]{1,0:T(1,128)} %bitcast.20, s32[1,512]{1,0:T(1,128)} %bitcast.21, s32[1,512]{1,0:T(1,128)} %neg.1), custom_call_target="tpu_custom_call" | custom-call | bytes 800000 | tf_op jit(solution)/shard_map/pallas_call | solution.py:32
  2.4 14.6 %all-to-all-start = ((bf16[64,8,128]{2,1,0:T(8,128)(2,1)}), bf16[64,8,128]{2,1,0:T(8,128)(2,1)S(1)}, u32[]{:S(2)}, u32[]{:S(2)}) async-start(bf16[64,8,128]{2,1,0:T(8,128)(2,1)} %get-tuple-element.41), calls=%async_computation | async-start | bytes 262144 | tf_op jit(solution)/shard_map/all_to_all | solution.py:48
  17.0 3.3 %collective-permute-start = (bf16[272,256]{1,0:T(8,128)(2,1)}, bf16[272,256]{1,0:T(8,128)(2,1)S(1)}, u32[]{:S(2)}, u32[]{:S(2)}) collective-permute-start(bf16[272,256]{1,0:T(8,128)(2,1)} %get-tuple-element.40.pack0), channel_id=1, source_target_pairs={{0,1},{1,0},{2,3},{3,2},{4,5},{5,4},{6,7},{7,6},{8,9},{9,8},{10,11... | collective-permute-start | bytes 417800 | tf_op jit(solution)/shard_map/ppermute | solution.py:370
  20.3 2.3 %shard_map.121.rel_b = bf16[8,256,256]{2,1,0:T(8,128)(2,1)} custom-call(f32[8,256,256]{2,1,0:T(8,128)} %rel.5), custom_call_target="tpu_custom_call" | custom-call | bytes 3000000 | tf_op jit(solution)/shard_map/pallas_call | solution.py:32
  22.6 1.4 collective-permute-done.pack1
  24.0 3.0 %all-to-all-done.arrived = bf16[64,8,128]{2,1,0:T(8,128)(2,1)S(1)} async-done(((bf16[64,8,128]{2,1,0:T(8,128)(2,1)}), bf16[64,8,128]{2,1,0:T(8,128)(2,1)S(1)}, u32[]{:S(2)}, u32[]{:S(2)}) %all-to-all-start) | async-done | bytes 131104 | tf_op jit(solution)/shard_map/all_to_all | solution.py:48
  27.1 1.3 shard_map.122
  28.4 12.5 %all-to-all-start.1 = ((bf16[128,8,128]{2,1,0:T(8,128)(2,1)}), bf16[128,8,128]{2,1,0:T(8,128)(2,1)S(1)}, u32[]{:S(2)}, u32[]{:S(2)}) async-start(bf16[128,8,128]{2,1,0:T(8,128)(2,1)} %bitcast.7), calls=%async_computation.1 | async-start | bytes 524288 | tf_op jit(solution)/shard_map/all_to_all | solution.py:48
  40.9 4.4 %collective-permute-start.2 = (bf16[272,256]{1,0:T(8,128)(2,1)S(1)}, bf16[272,256]{1,0:T(8,128)(2,1)S(1)}, u32[]{:S(2)}, u32[]{:S(2)}) collective-permute-start(bf16[272,256]{1,0:T(8,128)(2,1)S(1)} %copy-done.11), channel_id=1, source_target_pairs={{0,3},{1,2},{2,1},{3,0},{4,7},{5,6},{6,5},{7,4},{8,11},{9,10},{10,... | collective-permute-start | bytes 417800 | tf_op jit(solution)/shard_map/ppermute | solution.py:370
  45.3 2.4 %collective-permute-start.1 = (bf16[272,256]{1,0:T(8,128)(2,1)S(1)}, bf16[272,256]{1,0:T(8,128)(2,1)S(1)}, u32[]{:S(2)}, u32[]{:S(2)}) collective-permute-start(bf16[272,256]{1,0:T(8,128)(2,1)S(1)} %copy-done.11), channel_id=1, source_target_pairs={{0,2},{1,3},{2,0},{3,1},{4,6},{5,7},{6,4},{7,5},{8,10},{9,11},{10,... | collective-permute-start | bytes 417800 | tf_op jit(solution)/shard_map/ppermute | solution.py:370
  47.7 0.1 pad_add_fusion.place
  47.8 1.2 copy-done.1
  49.0 2.4 %shard_map.123 = (f32[8,512]{1,0:T(8,128)S(1)}, f32[16,512]{1,0:T(8,128)S(1)}, bf16[1024,256]{1,0:T(8,128)(2,1)S(1)}, bf16[1024,256]{1,0:T(8,128)(2,1)S(1)}) custom-call(s32[3]{0:T(128)S(1)} %pad_add_fusion.place, bf16[272,256]{1,0:T(8,128)(2,1)S(1)} %copy-done.11, bf16[272,256]{1,0:T(8,128)(2,1)S(1)} %collective-permute-done.pack1, ...), custom_call_target="tpu_custom_call" | custom-call | flops 1300000000 | bytes 3000000 | tf_op jit(solution)/shard_map/pallas_call | solution.py:32
  51.4 0.0 collective-permute-done.2.pack3
  51.4 1.5 collective-permute-done.1.pack2
  52.9 2.1 %all-to-all-done.1 = bf16[128,8,128]{2,1,0:T(8,128)(2,1)S(1)} async-done(((bf16[128,8,128]{2,1,0:T(8,128)(2,1)}), bf16[128,8,128]{2,1,0:T(8,128)(2,1)S(1)}, u32[]{:S(2)}, u32[]{:S(2)}) %all-to-all-start.1) | async-done | bytes 262176 | tf_op jit(solution)/shard_map/all_to_all | solution.py:48
  55.0 6.7 %shard_map.124 = (bf16[2048,512]{1,0:T(8,128)(2,1)S(1)}, bf16[2048,256]{1,0:T(8,128)(2,1)S(1)}, bf16[4,256,256]{2,1,0:T(8,128)(2,1)S(1)}, bf16[4,256,256]{2,1,0:...) custom-call(s32[3]{0:T(128)S(1)} %pad_add_fusion.place, bf16[64,2,8,128]{3,2,1,0:T(8,128)(2,1)S(1)} %bitcast.17, ...), custom_call_target="tpu_custom_call" | custom-call | flops 4499999744 | bytes 6000000 | tf_op jit(solution)/shard_map/pallas_call | solution.py:32
  61.7 0.0 copy-start.12
  61.7 3.5 %collective-permute-start.4 = (bf16[4,256,256]{2,1,0:T(8,128)(2,1)S(1)}, bf16[4,256,256]{2,1,0:T(8,128)(2,1)S(1)}, u32[]{:S(2)}, u32[]{:S(2)}) collective-permute-start(bf16[4,256,256]{2,1,0:T(8,128)(2,1)S(1)} %get-tuple-element.56), channel_id=1, source_target_pairs={{0,8},{8,0},{1,9},{9,1},{2,10},{10,2},{3,11},{11,3},{4,12},{12,4},... | collective-permute-start | bytes 1572872 | tf_op jit(solution)/shard_map/ppermute | solution.py:44
  65.2 0.9 shard_map.126.g_rows
  66.1 0.6 collective-permute-done.4.came
  66.7 0.1 shard_map.127
  66.9 12.6 %all_to_all.30.got = bf16[4,256,256]{2,1,0:T(8,128)(2,1)S(1)} all-to-all(bf16[4,256,256]{2,1,0:T(8,128)(2,1)S(1)} %shard_map.127), channel_id=1, replica_groups=mesh['zlo'=4,'y'=8,'core'=2,'zhi'=2,'x'=4] {'x'}, dimensions={0} | all-to-all | bytes 1048576 | tf_op jit(solution)/shard_map/all_to_all | solution.py:48
  79.4 0.9 shard_map.128
  80.3 11.8 %all-to-all-start.3 = ((bf16[128,3,4,128]{3,2,1,0:T(4,128)(2,1)}), bf16[128,3,4,128]{3,2,1,0:T(4,128)(2,1)S(1)}, u32[]{:S(2)}, u32[]{:S(2)}) async-start(bf16[128,3,4,128]{3,2,1,0:T(4,128)(2,1)} %bitcast.9), calls=%async_computation.3 | async-start | bytes 786432 | tf_op jit(solution)/shard_map/all_to_all | solution.py:48
  92.1 3.3 %shard_map.125 = (f32[256,256]{1,0:T(8,128)S(1)}, bf16[256,256]{1,0:T(8,128)(2,1)S(1)}, bf16[256,256]{1,0:T(8,128)(2,1)S(1)}, bf16[256,256]{1,0:T(8,128)(2,1)S(1)}) custom-call(bf16[2048,256]{1,0:T(8,128)(2,1)S(1)} %copy-done.13, f32[16,512]{1,0:T(8,128)S(1)} %get-tuple-element.46.known.known0, f32[16,512]{1,0:T(8,128)S(1)} %get-tuple-element.50.known1, ...), custom_call_target="tpu_custom_call" | custom-call | flops 3000000000 | bytes 4000000 | tf_op jit(solution)/shard_map/pallas_call | solution.py:32
  95.4 0.0 copy-start.3
  95.5 0.0 copy-start.10
  95.5 2.3 %collective-permute-start.3 = (bf16[256,256]{1,0:T(8,128)(2,1)S(1)}, bf16[256,256]{1,0:T(8,128)(2,1)S(1)}, u32[]{:S(2)}, u32[]{:S(2)}) collective-permute-start(bf16[256,256]{1,0:T(8,128)(2,1)S(1)} %get-tuple-element.52), channel_id=1, source_target_pairs={{0,1},{1,0},{2,3},{3,2},{4,5},{5,4},{6,7},{7,6},{8,9},{9,8},{10,11... | collective-permute-start | bytes 393224 | tf_op jit(solution)/shard_map/ppermute | solution.py:427
  97.8 3.8 %collective-permute-done.3.own1 = bf16[256,256]{1,0:T(8,128)(2,1)S(1)} collective-permute-done((bf16[256,256]{1,0:T(8,128)(2,1)S(1)}, bf16[256,256]{1,0:T(8,128)(2,1)S(1)}, u32[]{:S(2)}, u32[]{:S(2)}) %collective-permute-start.3) | collective-permute-done | bytes 131104 | tf_op jit(solution)/shard_map/ppermute | solution.py:427
  101.6 6.9 %all-to-all-done.3 = bf16[128,3,4,128]{3,2,1,0:T(4,128)(2,1)S(1)} async-done(((bf16[128,3,4,128]{3,2,1,0:T(4,128)(2,1)}), bf16[128,3,4,128]{3,2,1,0:T(4,128)(2,1)S(1)}, u32[]{:S(2)}, u32[]{:S(2)}) %all-to-all-start.3) | async-done | bytes 393248 | tf_op jit(solution)/shard_map/all_to_all | solution.py:48
  108.5 1.4 shard_map.129
  109.9 7.9 %all-to-all-start.4 = ((bf16[128,2,4,128]{3,2,1,0:T(4,128)(2,1)}), bf16[128,2,4,128]{3,2,1,0:T(4,128)(2,1)S(1)}, u32[]{:S(2)}, u32[]{:S(2)}) async-start(bf16[128,2,4,128]{3,2,1,0:T(4,128)(2,1)} %bitcast.11), calls=%async_computation.4 | async-start | bytes 524288 | tf_op jit(solution)/shard_map/all_to_all | solution.py:48
  117.8 2.5 %collective-permute-start.5 = (bf16[256,256]{1,0:T(8,128)(2,1)S(1)}, bf16[256,256]{1,0:T(8,128)(2,1)S(1)}, u32[]{:S(2)}, u32[]{:S(2)}) collective-permute-start(bf16[256,256]{1,0:T(8,128)(2,1)S(1)} %get-tuple-element.62), channel_id=1, source_target_pairs={{0,2},{1,3},{2,0},{3,1},{4,6},{5,7},{6,4},{7,5},{8,10},{9,11},{10,... | collective-permute-start | bytes 393224 | tf_op jit(solution)/shard_map/ppermute | solution.py:427
  120.4 4.0 %collective-permute-start.6 = (bf16[256,256]{1,0:T(8,128)(2,1)S(1)}, bf16[256,256]{1,0:T(8,128)(2,1)S(1)}, u32[]{:S(2)}, u32[]{:S(2)}) collective-permute-start(bf16[256,256]{1,0:T(8,128)(2,1)S(1)} %get-tuple-element.63), channel_id=1, source_target_pairs={{0,3},{1,2},{2,1},{3,0},{4,7},{5,6},{6,5},{7,4},{8,11},{9,10},{10,... | collective-permute-start | bytes 393224 | tf_op jit(solution)/shard_map/ppermute | solution.py:427
  124.4 1.0 collective-permute-done.5.own2
  125.4 3.1 %collective-permute-done.6.own3 = bf16[256,256]{1,0:T(8,128)(2,1)S(1)} collective-permute-done((bf16[256,256]{1,0:T(8,128)(2,1)S(1)}, bf16[256,256]{1,0:T(8,128)(2,1)S(1)}, u32[]{:S(2)}, u32[]{:S(2)}) %collective-permute-start.6) | collective-permute-done | bytes 131104 | tf_op jit(solution)/shard_map/ppermute | solution.py:427
  128.4 3.5 %all-to-all-done.4 = bf16[128,2,4,128]{3,2,1,0:T(4,128)(2,1)S(1)} async-done(((bf16[128,2,4,128]{3,2,1,0:T(4,128)(2,1)}), bf16[128,2,4,128]{3,2,1,0:T(4,128)(2,1)S(1)}, u32[]{:S(2)}, u32[]{:S(2)}) %all-to-all-start.4) | async-done | bytes 262176 | tf_op jit(solution)/shard_map/all_to_all | solution.py:48
  131.9 0.9 shard_map.131
  132.8 3.5 %all-to-all-start.5 = ((bf16[4,256,256]{2,1,0:T(8,128)(2,1)}), bf16[4,256,256]{2,1,0:T(8,128)(2,1)S(1)}, u32[]{:S(2)}, u32[]{:S(2)}) async-start(bf16[4,256,256]{2,1,0:T(8,128)(2,1)} %shard_map.131), calls=%async_computation.5 | async-start | bytes 1048576 | tf_op jit(solution)/shard_map/all_to_all | solution.py:48
  136.4 0.9 copy-done.5
  137.3 0.9 copy-done.7
  138.2 1.0 shard_map.130
  139.2 4.8 %all-to-all-done.5.grads = bf16[4,256,256]{2,1,0:T(8,128)(2,1)S(1)} async-done(((bf16[4,256,256]{2,1,0:T(8,128)(2,1)}), bf16[4,256,256]{2,1,0:T(8,128)(2,1)S(1)}, u32[]{:S(2)}, u32[]{:S(2)}) %all-to-all-start.5) | async-done | bytes 524320 | tf_op jit(solution)/shard_map/all_to_all | solution.py:48
  143.9 4.7 %collective-permute-start.7 = (bf16[4,256,256]{2,1,0:T(8,128)(2,1)S(1)}, bf16[4,256,256]{2,1,0:T(8,128)(2,1)S(1)}, u32[]{:S(2)}, u32[]{:S(2)}) collective-permute-start(bf16[4,256,256]{2,1,0:T(8,128)(2,1)S(1)} %all-to-all-done.5.grads), channel_id=1, source_target_pairs={{0,8},{8,0},{1,9},{9,1},{2,10},{10,2},{3,11},{11,3},{4,12},{12,4},... | collective-permute-start | bytes 1572872 | tf_op jit(solution)/shard_map/ppermute | solution.py:44
  148.7 2.2 %shard_map.132 = (f32[8,256,256]{2,1,0:T(8,128)}, f32[8,256]{1,0:T(8,128)S(1)}) custom-call(s32[3]{0:T(128)S(1)} %pad_add_fusion.place, f32[8,256,256]{2,1,0:T(8,128)S(1)} %copy-done, f32[8,256]{1,0:T(8,128)S(1)} %copy-done.8, bf16[4,256,256]{2,1,0:T(8,128)(2,1)S(1)} %all-to-all-done.5.grads), custom_call_target="tpu_custom_call" | custom-call | bytes 3000000 | tf_op jit(solution)/shard_map/pallas_call | solution.py:319
  150.8 0.0 collective-permute-done.7.grads
  150.8 2.7 %shard_map.133 = (f32[8,256,256]{2,1,0:T(8,128)}, f32[8,256]{1,0:T(8,128)}) custom-call(s32[3]{0:T(128)S(1)} %pad_add_fusion.place, f32[8,256,256]{2,1,0:T(8,128)S(1)} %copy-done, f32[8,256]{1,0:T(8,128)S(1)} %copy-done.8, bf16[4,256,256]{2,1,0:T(8,128)(2,1)S(1)} %collective-permute-done.7.grads, ...), custom_call_target="tpu_custom_call", output_to_operand_aliasing={{0}: (4, {})} | custom-call | bytes 3000000 | tf_op jit(solution)/shard_map/pallas_call | solution.py:319
  (22 shorter events, 0.0 us)
Async XLA Ops:
  0.6 26.5 %copy-start.9 = (s32[64]{0:T(128)S(1)}, s32[64]{0:T(128)}, u32[]{:S(2)}) copy-start(s32[64]{0:T(128)} %matching.3) | copy-start | bytes 772
  2.4 24.7 %all-to-all-start = ((bf16[64,8,128]{2,1,0:T(8,128)(2,1)}), bf16[64,8,128]{2,1,0:T(8,128)(2,1)S(1)}, u32[]{:S(2)}, u32[]{:S(2)}) async-start(bf16[64,8,128]{2,1,0:T(8,128)(2,1)} %get-tuple-element.41), calls=%async_computation | async-start | bytes 262144 | tf_op jit(solution)/shard_map/all_to_all | solution.py:48
  17.0 23.9 %copy-start.11 = (bf16[272,256]{1,0:T(8,128)(2,1)S(1)}, bf16[272,256]{1,0:T(8,128)(2,1)}, u32[]{:S(2)}) copy-start(bf16[272,256]{1,0:T(8,128)(2,1)} %get-tuple-element.40.pack0) | copy-start | bytes 417796
  17.0 7.0 %collective-permute-start = (bf16[272,256]{1,0:T(8,128)(2,1)}, bf16[272,256]{1,0:T(8,128)(2,1)S(1)}, u32[]{:S(2)}, u32[]{:S(2)}) collective-permute-start(bf16[272,256]{1,0:T(8,128)(2,1)} %get-tuple-element.40.pack0), channel_id=1, source_target_pairs={{0,1},{1,0},{2,3},{3,2},{4,5},{5,4},{6,7},{7,6},{8,9},{9,8},{10,11... | collective-permute-start | bytes 417800 | tf_op jit(solution)/shard_map/ppermute | solution.py:370
  28.4 26.6 %all-to-all-start.1 = ((bf16[128,8,128]{2,1,0:T(8,128)(2,1)}), bf16[128,8,128]{2,1,0:T(8,128)(2,1)S(1)}, u32[]{:S(2)}, u32[]{:S(2)}) async-start(bf16[128,8,128]{2,1,0:T(8,128)(2,1)} %bitcast.7), calls=%async_computation.1 | async-start | bytes 524288 | tf_op jit(solution)/shard_map/all_to_all | solution.py:48
  40.9 10.5 %collective-permute-start.2 = (bf16[272,256]{1,0:T(8,128)(2,1)S(1)}, bf16[272,256]{1,0:T(8,128)(2,1)S(1)}, u32[]{:S(2)}, u32[]{:S(2)}) collective-permute-start(bf16[272,256]{1,0:T(8,128)(2,1)S(1)} %copy-done.11), channel_id=1, source_target_pairs={{0,3},{1,2},{2,1},{3,0},{4,7},{5,6},{6,5},{7,4},{8,11},{9,10},{10,... | collective-permute-start | bytes 417800 | tf_op jit(solution)/shard_map/ppermute | solution.py:370
  45.3 7.6 %collective-permute-start.1 = (bf16[272,256]{1,0:T(8,128)(2,1)S(1)}, bf16[272,256]{1,0:T(8,128)(2,1)S(1)}, u32[]{:S(2)}, u32[]{:S(2)}) collective-permute-start(bf16[272,256]{1,0:T(8,128)(2,1)S(1)} %copy-done.11), channel_id=1, source_target_pairs={{0,2},{1,3},{2,0},{3,1},{4,6},{5,7},{6,4},{7,5},{8,10},{9,11},{10,... | collective-permute-start | bytes 417800 | tf_op jit(solution)/shard_map/ppermute | solution.py:370
  47.8 1.2 copy-start.1
  49.0 6.0 %copy-start.2 = (bf16[8,256,256]{2,1,0:T(8,128)(2,1)S(1)}, bf16[8,256,256]{2,1,0:T(8,128)(2,1)}, u32[]{:S(2)}) copy-start(bf16[8,256,256]{2,1,0:T(8,128)(2,1)} %shard_map.121.rel_b) | copy-start | bytes 3145732
  61.7 4.4 %copy-start.12 = (bf16[2048,256]{1,0:T(8,128)(2,1)}, bf16[2048,256]{1,0:T(8,128)(2,1)S(1)}, u32[]{:S(2)}) copy-start(bf16[2048,256]{1,0:T(8,128)(2,1)S(1)} %get-tuple-element.49.g_trans) | copy-start | bytes 3145732
  61.7 5.0 %collective-permute-start.4 = (bf16[4,256,256]{2,1,0:T(8,128)(2,1)S(1)}, bf16[4,256,256]{2,1,0:T(8,128)(2,1)S(1)}, u32[]{:S(2)}, u32[]{:S(2)}) collective-permute-start(bf16[4,256,256]{2,1,0:T(8,128)(2,1)S(1)} %get-tuple-element.56), channel_id=1, source_target_pairs={{0,8},{8,0},{1,9},{9,1},{2,10},{10,2},{3,11},{11,3},{4,12},{12,4},... | collective-permute-start | bytes 1572872 | tf_op jit(solution)/shard_map/ppermute | solution.py:44
  66.7 25.4 %copy-start.13 = (bf16[2048,256]{1,0:T(8,128)(2,1)S(1)}, bf16[2048,256]{1,0:T(8,128)(2,1)}, u32[]{:S(2)}) copy-start(bf16[2048,256]{1,0:T(8,128)(2,1)} %copy-done.12) | copy-start | bytes 3145732
  80.3 28.2 %all-to-all-start.3 = ((bf16[128,3,4,128]{3,2,1,0:T(4,128)(2,1)}), bf16[128,3,4,128]{3,2,1,0:T(4,128)(2,1)S(1)}, u32[]{:S(2)}, u32[]{:S(2)}) async-start(bf16[128,3,4,128]{3,2,1,0:T(4,128)(2,1)} %bitcast.9), calls=%async_computation.3 | async-start | bytes 786432 | tf_op jit(solution)/shard_map/all_to_all | solution.py:48
  95.4 40.9 %copy-start.3 = (f32[256,256]{1,0:T(8,128)S(1)}, f32[256,256]{1,0:T(8,128)}, u32[]{:S(2)}) copy-start(f32[256,256]{1,0:T(8,128)} %emb.3) | copy-start | bytes 786436
  95.5 40.9 %copy-start.10 = (f32[256]{0:T(256)S(1)}, f32[256]{0:T(256)}, u32[]{:S(2)}) copy-start(f32[256]{0:T(256)} %param.10) | copy-start | bytes 3076
  95.5 6.1 %collective-permute-start.3 = (bf16[256,256]{1,0:T(8,128)(2,1)S(1)}, bf16[256,256]{1,0:T(8,128)(2,1)S(1)}, u32[]{:S(2)}, u32[]{:S(2)}) collective-permute-start(bf16[256,256]{1,0:T(8,128)(2,1)S(1)} %get-tuple-element.52), channel_id=1, source_target_pairs={{0,1},{1,0},{2,3},{3,2},{4,5},{5,4},{6,7},{7,6},{8,9},{9,8},{10,11... | collective-permute-start | bytes 393224 | tf_op jit(solution)/shard_map/ppermute | solution.py:427
  108.5 40.1 %copy-start = (f32[8,256,256]{2,1,0:T(8,128)S(1)}, f32[8,256,256]{2,1,0:T(8,128)}, u32[]{:S(2)}) copy-start(f32[8,256,256]{2,1,0:T(8,128)} %rel.5) | copy-start | bytes 6291460
  108.5 40.1 %copy-start.8 = (f32[8,256]{1,0:T(8,128)S(1)}, f32[8,256]{1,0:T(8,128)}, u32[]{:S(2)}) copy-start(f32[8,256]{1,0:T(8,128)} %accum.3) | copy-start | bytes 24580
  109.9 22.0 %all-to-all-start.4 = ((bf16[128,2,4,128]{3,2,1,0:T(4,128)(2,1)}), bf16[128,2,4,128]{3,2,1,0:T(4,128)(2,1)S(1)}, u32[]{:S(2)}, u32[]{:S(2)}) async-start(bf16[128,2,4,128]{3,2,1,0:T(4,128)(2,1)} %bitcast.11), calls=%async_computation.4 | async-start | bytes 524288 | tf_op jit(solution)/shard_map/all_to_all | solution.py:48
  117.8 7.5 %collective-permute-start.5 = (bf16[256,256]{1,0:T(8,128)(2,1)S(1)}, bf16[256,256]{1,0:T(8,128)(2,1)S(1)}, u32[]{:S(2)}, u32[]{:S(2)}) collective-permute-start(bf16[256,256]{1,0:T(8,128)(2,1)S(1)} %get-tuple-element.62), channel_id=1, source_target_pairs={{0,2},{1,3},{2,0},{3,1},{4,6},{5,7},{6,4},{7,5},{8,10},{9,11},{10,... | collective-permute-start | bytes 393224 | tf_op jit(solution)/shard_map/ppermute | solution.py:427
  120.4 8.1 %collective-permute-start.6 = (bf16[256,256]{1,0:T(8,128)(2,1)S(1)}, bf16[256,256]{1,0:T(8,128)(2,1)S(1)}, u32[]{:S(2)}, u32[]{:S(2)}) collective-permute-start(bf16[256,256]{1,0:T(8,128)(2,1)S(1)} %get-tuple-element.63), channel_id=1, source_target_pairs={{0,3},{1,2},{2,1},{3,0},{4,7},{5,6},{6,5},{7,4},{8,11},{9,10},{10,... | collective-permute-start | bytes 393224 | tf_op jit(solution)/shard_map/ppermute | solution.py:427
  125.4 7.5 %copy-start.4 = (bf16[256,256]{1,0:T(8,128)(2,1)}, bf16[256,256]{1,0:T(8,128)(2,1)S(1)}, u32[]{:S(2)}) copy-start(bf16[256,256]{1,0:T(8,128)(2,1)S(1)} %collective-permute-done.5.own2) | copy-start | bytes 393220
  128.4 4.4 %copy-start.6 = (bf16[256,256]{1,0:T(8,128)(2,1)}, bf16[256,256]{1,0:T(8,128)(2,1)S(1)}, u32[]{:S(2)}) copy-start(bf16[256,256]{1,0:T(8,128)(2,1)S(1)} %collective-permute-done.6.own3) | copy-start | bytes 393220
  132.8 11.1 %all-to-all-start.5 = ((bf16[4,256,256]{2,1,0:T(8,128)(2,1)}), bf16[4,256,256]{2,1,0:T(8,128)(2,1)S(1)}, u32[]{:S(2)}, u32[]{:S(2)}) async-start(bf16[4,256,256]{2,1,0:T(8,128)(2,1)} %shard_map.131), calls=%async_computation.5 | async-start | bytes 1048576 | tf_op jit(solution)/shard_map/all_to_all | solution.py:48
  136.4 0.9 copy-start.5
  137.3 0.9 copy-start.7
  143.9 6.9 %collective-permute-start.7 = (bf16[4,256,256]{2,1,0:T(8,128)(2,1)S(1)}, bf16[4,256,256]{2,1,0:T(8,128)(2,1)S(1)}, u32[]{:S(2)}, u32[]{:S(2)}) collective-permute-start(bf16[4,256,256]{2,1,0:T(8,128)(2,1)S(1)} %all-to-all-done.5.grads), channel_id=1, source_target_pairs={{0,8},{8,0},{1,9},{9,1},{2,10},{10,2},{3,11},{11,3},{4,12},{12,4},... | collective-permute-start | bytes 1572872 | tf_op jit(solution)/shard_map/ppermute | solution.py:44

commit v15 on v12

--- a/solution.py
+++ b/solution.py
@@ -135,9 +135,8 @@
 
 def score_kernel(
     place, rows_in, pack2, pack3, rel_b, counts, known, trans, source,
-    weight, g_trans, kept, given, known1, trans1, rows, source1
+    weight, g_trans, given, known1, trans1, source1, rows
 ):
-    core = place[0]
     for z in range(2):
         both = rows_in[:, z].reshape(2, 256, 128)
         rows[z * 256 : (z + 1) * 256, :] = jnp.concatenate([both[0], both[1]], axis=1)
@@ -163,23 +162,26 @@
         part = jnp.where(hit, (count[s] + 1.0) * sig - 1.0, count[s] * sig).astype(bf16)
         weight[span, :] = part
         g_trans[span, :] = dot(part, rows[...]).astype(bf16)
+    relation_part(1 - place[0], g_trans, index, source, source1, given)
+
+
+def relation_part(core, g_trans, index, source0, source1, out):
     turned = g_trans[...].astype(f32).T
     kinds = jnp.concatenate([part[1:2] for part in index], axis=1)
-    every = jnp.concatenate([source[...], source1[...]], axis=0)
-    for r in range(8):
-        wanted = r + 4 * core if r < 4 else r - 4 * core
-        masked = jnp.where(kinds == wanted.astype(f32), turned, 0.0).astype(bf16)
-        grad = dot(masked, every).astype(bf16)
-        if r < 4:
-            kept[r] = grad
-        else:
-            given[r - 4] = grad
-
-
-def partner_kernel(weight, trans0, trans1, g_rows):
+    every = jnp.concatenate([source0[...], source1[...]], axis=0)
+    for r in range(4):
+        masked = jnp.where(kinds == (r + 4 * core).astype(f32), turned, 0.0).astype(bf16)
+        out[r] = dot(masked, every).astype(bf16)
+
+
+def partner_kernel(
+    place, weight, trans0, trans1, g_trans, known0, known1, source0, source1, g_rows, kept
+):
     turned = jnp.concatenate([t[...].astype(f32).T.astype(bf16) for t in (trans0, trans1)], axis=1)
     for z in range(2):
         g_rows[z] = dot(turned, weight[:, z * 256 : (z + 1) * 256]).T.astype(bf16)
+    index = [known[s * 8 : s * 8 + 4, :] for known in (known0, known1) for s in range(2)]
+    relation_part(place[0], g_trans, index, source0, source1, kept)
 
 
 def own_kernel(g_trans, known0, known1, rel_b, *owns):
@@ -353,23 +355,23 @@
         space=16,
     )
     four = shape((4, 256, 256), bf16)
-    weight, g_trans, kept, given, known1, trans1 = call(
+    weight, g_trans, given, known1, trans1, source1 = call(
         score_kernel,
-        (shape((2048, 512), bf16), shape((2048, 256), bf16), four, four, known_shape, block),
+        (shape((2048, 512), bf16), shape((2048, 256), bf16), four, known_shape, block, block),
         1,
         (place, rows_in, packs[2], packs[3], rel_b, counts, known0, trans0, source0),
         flops=4_500_000_000,
         moved=6_000_000,
-        scratch=[pltpu.VMEM((512, 256), bf16), pltpu.VMEM((1024, 256), bf16)],
+        scratch=[pltpu.VMEM((512, 256), bf16)],
         space=28,
     )
     came = swap(given, "core")
-    g_rows = call(
+    g_rows, kept = call(
         partner_kernel,
-        shape((2, 256, 256), bf16),
-        0,
-        (weight, trans0, trans1),
-        flops=1_500_000_000,
+        (shape((2, 256, 256), bf16), four),
+        1,
+        (place, weight, trans0, trans1, g_trans, known0, known1, source0, source1),
+        flops=2_500_000_000,
         moved=4_000_000,
         space=16,
     )

time: 155 us -> 155 us (level)
    unnamed x28 -> x36, local copies, waits for them, and re-layouts: 3.08 us -> 3.1 us
  transfers between devices with their start and end apart: 13 -> 13, of which waited for: 11 -> 10; matrix products, arithmetic and copies ran while one was open for 0% -> 0% of each run, Pallas kernels for 8% -> 9%
where the time goes in v15:
time: 155 us; the launch traced here: 154 us
  starting transfers between devices  76.6 us (49%)
  waiting for transfers between devices  31.1 us (20%)
  Pallas kernels  28.4 us (18%)
  blocking collectives  13.3 us (9%)
  local copies, waits for them, and re-layouts  3.1 us (2%)
    all_to_all x5, starting transfers between devices, spread(): return lax.all_to_all(value, axis, split_axis=0, concat_axis=0, tiled=True)  49.5 us
    pallas_call x12, Pallas kernels, call(): pl.pallas_call(kernel, out_shape=outs, in_specs=specs, out_specs=tuple((A...  23.5 us
    all_to_all x5, waiting for transfers between devices, spread(): return lax.all_to_all(value, axis, split_axis=0, concat_axis=0, tiled=True)  20.3 us
    all_to_all x1, blocking collectives, spread(): return lax.all_to_all(value, axis, split_axis=0, concat_axis=0, tiled=True)  13.3 us
    ppermute x3, starting transfers between devices, body(): lax.ppermute(pack, 'x', [(i, i ^ k) for i in range(4)])  10.1 us
    ppermute x3, starting transfers between devices, body(): lax.ppermute(part, 'x', [(i, i ^ k) for i in range(4)])  8.82 us
    ppermute x2, starting transfers between devices, swap(): return lax.ppermute(value, axis, [(0, 1), (1, 0)])  8.2 us
    ppermute x3, waiting for transfers between devices, body(): lax.ppermute(part, 'x', [(i, i ^ k) for i in range(4)])  7.88 us
  transfers between devices with their start and end apart: 13, of which 10 were waited for; matrix products, arithmetic and copies ran while one was open for 0% of the time, Pallas kernels for 9%

profile of v15, /device:TPU:1, one launch (start us, length us, event | category | flops | bytes accessed | tf_op | source)
XLA Modules:
  0.0 153.7 jit_solution(2551031589495879120)
XLA Ops:
  0.6 1.7 %shard_map.120 = (bf16[64,8,128]{2,1,0:T(8,128)(2,1)}, bf16[272,256]{1,0:T(8,128)(2,1)}) custom-call(f32[256,256]{1,0:T(8,128)} %emb.3, s32[1,512]{1,0:T(1,128)} %bitcast.19, s32[1,512]{1,0:T(1,128)} %bitcast.20, s32[1,512]{1,0:T(1,128)} %bitcast.21, s32[1,512]{1,0:T(1,128)} %neg.1), custom_call_target="tpu_custom_call" | custom-call | bytes 800000 | tf_op jit(solution)/shard_map/pallas_call | solution.py:32
  2.4 14.6 %all-to-all-start = ((bf16[64,8,128]{2,1,0:T(8,128)(2,1)}), bf16[64,8,128]{2,1,0:T(8,128)(2,1)S(1)}, u32[]{:S(2)}, u32[]{:S(2)}) async-start(bf16[64,8,128]{2,1,0:T(8,128)(2,1)} %get-tuple-element.43), calls=%async_computation | async-start | bytes 262144 | tf_op jit(solution)/shard_map/all_to_all | solution.py:48
  17.0 3.3 %collective-permute-start = (bf16[272,256]{1,0:T(8,128)(2,1)}, bf16[272,256]{1,0:T(8,128)(2,1)S(1)}, u32[]{:S(2)}, u32[]{:S(2)}) collective-permute-start(bf16[272,256]{1,0:T(8,128)(2,1)} %get-tuple-element.42.pack0), channel_id=1, source_target_pairs={{0,1},{1,0},{2,3},{3,2},{4,5},{5,4},{6,7},{7,6},{8,9},{9,8},{10,11... | collective-permute-start | bytes 417800 | tf_op jit(solution)/shard_map/ppermute | solution.py:341
  20.3 2.3 %shard_map.121.rel_b = bf16[8,256,256]{2,1,0:T(8,128)(2,1)} custom-call(f32[8,256,256]{2,1,0:T(8,128)} %rel.5), custom_call_target="tpu_custom_call" | custom-call | bytes 3000000 | tf_op jit(solution)/shard_map/pallas_call | solution.py:32
  22.6 1.4 collective-permute-done.pack1
  24.0 3.0 %all-to-all-done.arrived = bf16[64,8,128]{2,1,0:T(8,128)(2,1)S(1)} async-done(((bf16[64,8,128]{2,1,0:T(8,128)(2,1)}), bf16[64,8,128]{2,1,0:T(8,128)(2,1)S(1)}, u32[]{:S(2)}, u32[]{:S(2)}) %all-to-all-start) | async-done | bytes 131104 | tf_op jit(solution)/shard_map/all_to_all | solution.py:48
  27.1 1.3 shard_map.122
  28.4 12.5 %all-to-all-start.1 = ((bf16[128,8,128]{2,1,0:T(8,128)(2,1)}), bf16[128,8,128]{2,1,0:T(8,128)(2,1)S(1)}, u32[]{:S(2)}, u32[]{:S(2)}) async-start(bf16[128,8,128]{2,1,0:T(8,128)(2,1)} %bitcast.7), calls=%async_computation.1 | async-start | bytes 524288 | tf_op jit(solution)/shard_map/all_to_all | solution.py:48
  40.9 4.4 %collective-permute-start.2 = (bf16[272,256]{1,0:T(8,128)(2,1)S(1)}, bf16[272,256]{1,0:T(8,128)(2,1)S(1)}, u32[]{:S(2)}, u32[]{:S(2)}) collective-permute-start(bf16[272,256]{1,0:T(8,128)(2,1)S(1)} %copy-done.11), channel_id=1, source_target_pairs={{0,3},{1,2},{2,1},{3,0},{4,7},{5,6},{6,5},{7,4},{8,11},{9,10},{10,... | collective-permute-start | bytes 417800 | tf_op jit(solution)/shard_map/ppermute | solution.py:341
  45.2 2.4 %collective-permute-start.1 = (bf16[272,256]{1,0:T(8,128)(2,1)S(1)}, bf16[272,256]{1,0:T(8,128)(2,1)S(1)}, u32[]{:S(2)}, u32[]{:S(2)}) collective-permute-start(bf16[272,256]{1,0:T(8,128)(2,1)S(1)} %copy-done.11), channel_id=1, source_target_pairs={{0,2},{1,3},{2,0},{3,1},{4,6},{5,7},{6,4},{7,5},{8,10},{9,11},{10,... | collective-permute-start | bytes 417800 | tf_op jit(solution)/shard_map/ppermute | solution.py:341
  47.7 0.1 pad_add_fusion.place
  47.8 1.2 copy-done.1
  49.0 2.4 %shard_map.123 = (f32[8,512]{1,0:T(8,128)S(1)}, f32[16,512]{1,0:T(8,128)S(1)}, bf16[1024,256]{1,0:T(8,128)(2,1)S(1)}, bf16[1024,256]{1,0:T(8,128)(2,1)S(1)}) custom-call(s32[3]{0:T(128)S(1)} %pad_add_fusion.place, bf16[272,256]{1,0:T(8,128)(2,1)S(1)} %copy-done.11, bf16[272,256]{1,0:T(8,128)(2,1)S(1)} %collective-permute-done.pack1, ...), custom_call_target="tpu_custom_call" | custom-call | flops 1300000000 | bytes 3000000 | tf_op jit(solution)/shard_map/pallas_call | solution.py:32
  51.4 1.4 collective-permute-done.1.pack2
  52.8 2.1 %all-to-all-done.1 = bf16[128,8,128]{2,1,0:T(8,128)(2,1)S(1)} async-done(((bf16[128,8,128]{2,1,0:T(8,128)(2,1)}), bf16[128,8,128]{2,1,0:T(8,128)(2,1)S(1)}, u32[]{:S(2)}, u32[]{:S(2)}) %all-to-all-start.1) | async-done | bytes 262176 | tf_op jit(solution)/shard_map/all_to_all | solution.py:48
  54.9 5.6 %shard_map.124 = (bf16[2048,512]{1,0:T(8,128)(2,1)S(1)}, bf16[2048,256]{1,0:T(8,128)(2,1)S(1)}, bf16[4,256,256]{2,1,0:T(8,128)(2,1)S(1)}, f32[16,512]{1,0:T(8,12...) custom-call(s32[3]{0:T(128)S(1)} %pad_add_fusion.place, bf16[64,2,8,128]{3,2,1,0:T(8,128)(2,1)S(1)} %bitcast.17, ...), custom_call_target="tpu_custom_call" | custom-call | flops 4499999744 | bytes 6000000 | tf_op jit(solution)/shard_map/pallas_call | solution.py:32
  60.6 0.0 copy-start.12
  60.6 0.0 copy-start.16
  60.6 3.5 %collective-permute-start.4 = (bf16[4,256,256]{2,1,0:T(8,128)(2,1)S(1)}, bf16[4,256,256]{2,1,0:T(8,128)(2,1)S(1)}, u32[]{:S(2)}, u32[]{:S(2)}) collective-permute-start(bf16[4,256,256]{2,1,0:T(8,128)(2,1)S(1)} %get-tuple-element.61), channel_id=1, source_target_pairs={{0,8},{8,0},{1,9},{9,1},{2,10},{10,2},{3,11},{11,3},{4,12},{12,4},... | collective-permute-start | bytes 1572872 | tf_op jit(solution)/shard_map/ppermute | solution.py:44
  64.1 2.4 %shard_map.126 = (bf16[2,256,256]{2,1,0:T(8,128)(2,1)S(1)}, bf16[4,256,256]{2,1,0:T(8,128)(2,1)S(1)}) custom-call(s32[3]{0:T(128)S(1)} %pad_add_fusion.place, bf16[2048,512]{1,0:T(8,128)(2,1)S(1)} %get-tuple-element.57.weight, bf16[1024,256]{1,0:T(8,128)(2,1)S(1)} %get-tuple-element.49.trans.trans0, bf16[1024,256]{1,0:T(8,128)(2,1)S(1)} %get-tuple-element.58.trans1, ...), custom_call_target="tpu_custom_call" | custom-call | flops 2500000000 | bytes 4000000 | tf_op jit(solution)/shard_map/pallas_call | solution.py:32
  66.6 0.0 copy-start.13
  66.6 0.0 copy-start.17
  66.7 0.1 shard_map.127
  66.8 13.3 %all_to_all.30.got = bf16[4,256,256]{2,1,0:T(8,128)(2,1)S(1)} all-to-all(bf16[4,256,256]{2,1,0:T(8,128)(2,1)S(1)} %shard_map.127), channel_id=1, replica_groups=mesh['zlo'=4,'y'=8,'core'=2,'zhi'=2,'x'=4] {'x'}, dimensions={0} | all-to-all | bytes 1048576 | tf_op jit(solution)/shard_map/all_to_all | solution.py:48
  80.1 0.9 shard_map.128
  81.0 11.1 %all-to-all-start.3 = ((bf16[128,3,4,128]{3,2,1,0:T(4,128)(2,1)}), bf16[128,3,4,128]{3,2,1,0:T(4,128)(2,1)S(1)}, u32[]{:S(2)}, u32[]{:S(2)}) async-start(bf16[128,3,4,128]{3,2,1,0:T(4,128)(2,1)} %bitcast.9), calls=%async_computation.3 | async-start | bytes 786432 | tf_op jit(solution)/shard_map/all_to_all | solution.py:48
  92.1 3.3 %shard_map.125 = (f32[256,256]{1,0:T(8,128)S(1)}, bf16[256,256]{1,0:T(8,128)(2,1)S(1)}, bf16[256,256]{1,0:T(8,128)(2,1)S(1)}, bf16[256,256]{1,0:T(8,128)(2,1)S(1)}) custom-call(bf16[2048,256]{1,0:T(8,128)(2,1)S(1)} %copy-done.13, f32[16,512]{1,0:T(8,128)S(1)} %copy-done.15, f32[16,512]{1,0:T(8,128)S(1)} %copy-done.17, bf16[8,256,256]{2,1,0:T(8,128)(2,1)S(1)} %copy-done.2), custom_call_target="tpu_custom_call" | custom-call | flops 3000000000 | bytes 4000000 | tf_op jit(solution)/shard_map/pallas_call | solution.py:32
  95.4 0.0 copy-start.3
  95.4 0.0 copy-start.10
  95.4 2.3 %collective-permute-start.3 = (bf16[256,256]{1,0:T(8,128)(2,1)S(1)}, bf16[256,256]{1,0:T(8,128)(2,1)S(1)}, u32[]{:S(2)}, u32[]{:S(2)}) collective-permute-start(bf16[256,256]{1,0:T(8,128)(2,1)S(1)} %get-tuple-element.54), channel_id=1, source_target_pairs={{0,1},{1,0},{2,3},{3,2},{4,5},{5,4},{6,7},{7,6},{8,9},{9,8},{10,11... | collective-permute-start | bytes 393224 | tf_op jit(solution)/shard_map/ppermute | solution.py:390
  97.7 3.8 %collective-permute-done.3.own1 = bf16[256,256]{1,0:T(8,128)(2,1)S(1)} collective-permute-done((bf16[256,256]{1,0:T(8,128)(2,1)S(1)}, bf16[256,256]{1,0:T(8,128)(2,1)S(1)}, u32[]{:S(2)}, u32[]{:S(2)}) %collective-permute-start.3) | collective-permute-done | bytes 131104 | tf_op jit(solution)/shard_map/ppermute | solution.py:390
  101.5 6.9 %all-to-all-done.3 = bf16[128,3,4,128]{3,2,1,0:T(4,128)(2,1)S(1)} async-done(((bf16[128,3,4,128]{3,2,1,0:T(4,128)(2,1)}), bf16[128,3,4,128]{3,2,1,0:T(4,128)(2,1)S(1)}, u32[]{:S(2)}, u32[]{:S(2)}) %all-to-all-start.3) | async-done | bytes 393248 | tf_op jit(solution)/shard_map/all_to_all | solution.py:48
  108.4 1.5 shard_map.129
  110.0 7.9 %all-to-all-start.4 = ((bf16[128,2,4,128]{3,2,1,0:T(4,128)(2,1)}), bf16[128,2,4,128]{3,2,1,0:T(4,128)(2,1)S(1)}, u32[]{:S(2)}, u32[]{:S(2)}) async-start(bf16[128,2,4,128]{3,2,1,0:T(4,128)(2,1)} %bitcast.11), calls=%async_computation.4 | async-start | bytes 524288 | tf_op jit(solution)/shard_map/all_to_all | solution.py:48
  117.9 2.5 %collective-permute-start.5 = (bf16[256,256]{1,0:T(8,128)(2,1)S(1)}, bf16[256,256]{1,0:T(8,128)(2,1)S(1)}, u32[]{:S(2)}, u32[]{:S(2)}) collective-permute-start(bf16[256,256]{1,0:T(8,128)(2,1)S(1)} %get-tuple-element.66), channel_id=1, source_target_pairs={{0,2},{1,3},{2,0},{3,1},{4,6},{5,7},{6,4},{7,5},{8,10},{9,11},{10,... | collective-permute-start | bytes 393224 | tf_op jit(solution)/shard_map/ppermute | solution.py:390
  120.4 4.0 %collective-permute-start.6 = (bf16[256,256]{1,0:T(8,128)(2,1)S(1)}, bf16[256,256]{1,0:T(8,128)(2,1)S(1)}, u32[]{:S(2)}, u32[]{:S(2)}) collective-permute-start(bf16[256,256]{1,0:T(8,128)(2,1)S(1)} %get-tuple-element.67), channel_id=1, source_target_pairs={{0,3},{1,2},{2,1},{3,0},{4,7},{5,6},{6,5},{7,4},{8,11},{9,10},{10,... | collective-permute-start | bytes 393224 | tf_op jit(solution)/shard_map/ppermute | solution.py:390
  124.4 1.0 collective-permute-done.5.own2
  125.4 3.1 %collective-permute-done.6.own3 = bf16[256,256]{1,0:T(8,128)(2,1)S(1)} collective-permute-done((bf16[256,256]{1,0:T(8,128)(2,1)S(1)}, bf16[256,256]{1,0:T(8,128)(2,1)S(1)}, u32[]{:S(2)}, u32[]{:S(2)}) %collective-permute-start.6) | collective-permute-done | bytes 131104 | tf_op jit(solution)/shard_map/ppermute | solution.py:390
  128.5 3.5 %all-to-all-done.4 = bf16[128,2,4,128]{3,2,1,0:T(4,128)(2,1)S(1)} async-done(((bf16[128,2,4,128]{3,2,1,0:T(4,128)(2,1)}), bf16[128,2,4,128]{3,2,1,0:T(4,128)(2,1)S(1)}, u32[]{:S(2)}, u32[]{:S(2)}) %all-to-all-start.4) | async-done | bytes 262176 | tf_op jit(solution)/shard_map/all_to_all | solution.py:48
  132.0 0.9 shard_map.131
  132.8 3.5 %all-to-all-start.5 = ((bf16[4,256,256]{2,1,0:T(8,128)(2,1)}), bf16[4,256,256]{2,1,0:T(8,128)(2,1)S(1)}, u32[]{:S(2)}, u32[]{:S(2)}) async-start(bf16[4,256,256]{2,1,0:T(8,128)(2,1)} %shard_map.131), calls=%async_computation.5 | async-start | bytes 1048576 | tf_op jit(solution)/shard_map/all_to_all | solution.py:48
  136.4 0.9 copy-done.5
  137.2 0.9 copy-done.7
  138.2 1.0 shard_map.130
  139.2 4.8 %all-to-all-done.5.grads = bf16[4,256,256]{2,1,0:T(8,128)(2,1)S(1)} async-done(((bf16[4,256,256]{2,1,0:T(8,128)(2,1)}), bf16[4,256,256]{2,1,0:T(8,128)(2,1)S(1)}, u32[]{:S(2)}, u32[]{:S(2)}) %all-to-all-start.5) | async-done | bytes 524320 | tf_op jit(solution)/shard_map/all_to_all | solution.py:48
  143.9 4.7 %collective-permute-start.7 = (bf16[4,256,256]{2,1,0:T(8,128)(2,1)S(1)}, bf16[4,256,256]{2,1,0:T(8,128)(2,1)S(1)}, u32[]{:S(2)}, u32[]{:S(2)}) collective-permute-start(bf16[4,256,256]{2,1,0:T(8,128)(2,1)S(1)} %all-to-all-done.5.grads), channel_id=1, source_target_pairs={{0,8},{8,0},{1,9},{9,1},{2,10},{10,2},{3,11},{11,3},{4,12},{12,4},... | collective-permute-start | bytes 1572872 | tf_op jit(solution)/shard_map/ppermute | solution.py:44
  148.6 2.2 %shard_map.132 = (f32[8,256,256]{2,1,0:T(8,128)}, f32[8,256]{1,0:T(8,128)S(1)}) custom-call(s32[3]{0:T(128)S(1)} %pad_add_fusion.place, f32[8,256,256]{2,1,0:T(8,128)S(1)} %copy-done, f32[8,256]{1,0:T(8,128)S(1)} %copy-done.8, bf16[4,256,256]{2,1,0:T(8,128)(2,1)S(1)} %all-to-all-done.5.grads), custom_call_target="tpu_custom_call" | custom-call | bytes 3000000 | tf_op jit(solution)/shard_map/pallas_call | solution.py:293
  150.8 2.7 %shard_map.133 = (f32[8,256,256]{2,1,0:T(8,128)}, f32[8,256]{1,0:T(8,128)}) custom-call(s32[3]{0:T(128)S(1)} %pad_add_fusion.place, f32[8,256,256]{2,1,0:T(8,128)S(1)} %copy-done, f32[8,256]{1,0:T(8,128)S(1)} %copy-done.8, bf16[4,256,256]{2,1,0:T(8,128)(2,1)S(1)} %collective-permute-done.7.grads, ...), custom_call_target="tpu_custom_call", output_to_operand_aliasing={{0}: (4, {})} | custom-call | bytes 3000000 | tf_op jit(solution)/shard_map/pallas_call | solution.py:293
  (30 shorter events, 0.1 us)
Async XLA Ops:
  0.6 26.4 %copy-start.9 = (s32[64]{0:T(128)S(1)}, s32[64]{0:T(128)}, u32[]{:S(2)}) copy-start(s32[64]{0:T(128)} %matching.3) | copy-start | bytes 772
  2.4 24.7 %all-to-all-start = ((bf16[64,8,128]{2,1,0:T(8,128)(2,1)}), bf16[64,8,128]{2,1,0:T(8,128)(2,1)S(1)}, u32[]{:S(2)}, u32[]{:S(2)}) async-start(bf16[64,8,128]{2,1,0:T(8,128)(2,1)} %get-tuple-element.43), calls=%async_computation | async-start | bytes 262144 | tf_op jit(solution)/shard_map/all_to_all | solution.py:48
  17.0 23.9 %copy-start.11 = (bf16[272,256]{1,0:T(8,128)(2,1)S(1)}, bf16[272,256]{1,0:T(8,128)(2,1)}, u32[]{:S(2)}) copy-start(bf16[272,256]{1,0:T(8,128)(2,1)} %get-tuple-element.42.pack0) | copy-start | bytes 417796
  17.0 7.0 %collective-permute-start = (bf16[272,256]{1,0:T(8,128)(2,1)}, bf16[272,256]{1,0:T(8,128)(2,1)S(1)}, u32[]{:S(2)}, u32[]{:S(2)}) collective-permute-start(bf16[272,256]{1,0:T(8,128)(2,1)} %get-tuple-element.42.pack0), channel_id=1, source_target_pairs={{0,1},{1,0},{2,3},{3,2},{4,5},{5,4},{6,7},{7,6},{8,9},{9,8},{10,11... | collective-permute-start | bytes 417800 | tf_op jit(solution)/shard_map/ppermute | solution.py:341
  28.4 26.6 %all-to-all-start.1 = ((bf16[128,8,128]{2,1,0:T(8,128)(2,1)}), bf16[128,8,128]{2,1,0:T(8,128)(2,1)S(1)}, u32[]{:S(2)}, u32[]{:S(2)}) async-start(bf16[128,8,128]{2,1,0:T(8,128)(2,1)} %bitcast.7), calls=%async_computation.1 | async-start | bytes 524288 | tf_op jit(solution)/shard_map/all_to_all | solution.py:48
  40.9 10.5 %collective-permute-start.2 = (bf16[272,256]{1,0:T(8,128)(2,1)S(1)}, bf16[272,256]{1,0:T(8,128)(2,1)S(1)}, u32[]{:S(2)}, u32[]{:S(2)}) collective-permute-start(bf16[272,256]{1,0:T(8,128)(2,1)S(1)} %copy-done.11), channel_id=1, source_target_pairs={{0,3},{1,2},{2,1},{3,0},{4,7},{5,6},{6,5},{7,4},{8,11},{9,10},{10,... | collective-permute-start | bytes 417800 | tf_op jit(solution)/shard_map/ppermute | solution.py:341
  45.2 7.6 %collective-permute-start.1 = (bf16[272,256]{1,0:T(8,128)(2,1)S(1)}, bf16[272,256]{1,0:T(8,128)(2,1)S(1)}, u32[]{:S(2)}, u32[]{:S(2)}) collective-permute-start(bf16[272,256]{1,0:T(8,128)(2,1)S(1)} %copy-done.11), channel_id=1, source_target_pairs={{0,2},{1,3},{2,0},{3,1},{4,6},{5,7},{6,4},{7,5},{8,10},{9,11},{10,... | collective-permute-start | bytes 417800 | tf_op jit(solution)/shard_map/ppermute | solution.py:341
  47.8 1.2 copy-start.1
  49.0 6.0 %copy-start.2 = (bf16[8,256,256]{2,1,0:T(8,128)(2,1)S(1)}, bf16[8,256,256]{2,1,0:T(8,128)(2,1)}, u32[]{:S(2)}) copy-start(bf16[8,256,256]{2,1,0:T(8,128)(2,1)} %shard_map.121.rel_b) | copy-start | bytes 3145732
  51.4 12.7 %copy-start.14 = (f32[16,512]{1,0:T(8,128)}, f32[16,512]{1,0:T(8,128)S(1)}, u32[]{:S(2)}) copy-start(f32[16,512]{1,0:T(8,128)S(1)} %get-tuple-element.48.known.known0) | copy-start | bytes 98308
  60.6 6.0 %copy-start.12 = (bf16[2048,256]{1,0:T(8,128)(2,1)}, bf16[2048,256]{1,0:T(8,128)(2,1)S(1)}, u32[]{:S(2)}) copy-start(bf16[2048,256]{1,0:T(8,128)(2,1)S(1)} %get-tuple-element.51.g_trans) | copy-start | bytes 3145732
  60.6 6.0 %copy-start.16 = (f32[16,512]{1,0:T(8,128)}, f32[16,512]{1,0:T(8,128)S(1)}, u32[]{:S(2)}) copy-start(f32[16,512]{1,0:T(8,128)S(1)} %get-tuple-element.52.known1) | copy-start | bytes 98308
  60.6 6.0 %collective-permute-start.4 = (bf16[4,256,256]{2,1,0:T(8,128)(2,1)S(1)}, bf16[4,256,256]{2,1,0:T(8,128)(2,1)S(1)}, u32[]{:S(2)}, u32[]{:S(2)}) collective-permute-start(bf16[4,256,256]{2,1,0:T(8,128)(2,1)S(1)} %get-tuple-element.61), channel_id=1, source_target_pairs={{0,8},{8,0},{1,9},{9,1},{2,10},{10,2},{3,11},{11,3},{4,12},{12,4},... | collective-permute-start | bytes 1572872 | tf_op jit(solution)/shard_map/ppermute | solution.py:44
  66.6 25.4 %copy-start.13 = (bf16[2048,256]{1,0:T(8,128)(2,1)S(1)}, bf16[2048,256]{1,0:T(8,128)(2,1)}, u32[]{:S(2)}) copy-start(bf16[2048,256]{1,0:T(8,128)(2,1)} %copy-done.12) | copy-start | bytes 3145732
  66.6 25.4 %copy-start.15 = (f32[16,512]{1,0:T(8,128)S(1)}, f32[16,512]{1,0:T(8,128)}, u32[]{:S(2)}) copy-start(f32[16,512]{1,0:T(8,128)} %copy-done.14) | copy-start | bytes 98308
  66.6 25.4 %copy-start.17 = (f32[16,512]{1,0:T(8,128)S(1)}, f32[16,512]{1,0:T(8,128)}, u32[]{:S(2)}) copy-start(f32[16,512]{1,0:T(8,128)} %copy-done.16) | copy-start | bytes 98308
  81.0 27.5 %all-to-all-start.3 = ((bf16[128,3,4,128]{3,2,1,0:T(4,128)(2,1)}), bf16[128,3,4,128]{3,2,1,0:T(4,128)(2,1)S(1)}, u32[]{:S(2)}, u32[]{:S(2)}) async-start(bf16[128,3,4,128]{3,2,1,0:T(4,128)(2,1)} %bitcast.9), calls=%async_computation.3 | async-start | bytes 786432 | tf_op jit(solution)/shard_map/all_to_all | solution.py:48
  95.4 41.0 %copy-start.3 = (f32[256,256]{1,0:T(8,128)S(1)}, f32[256,256]{1,0:T(8,128)}, u32[]{:S(2)}) copy-start(f32[256,256]{1,0:T(8,128)} %emb.3) | copy-start | bytes 786436
  95.4 41.0 %copy-start.10 = (f32[256]{0:T(256)S(1)}, f32[256]{0:T(256)}, u32[]{:S(2)}) copy-start(f32[256]{0:T(256)} %param.10) | copy-start | bytes 3076
  95.4 6.1 %collective-permute-start.3 = (bf16[256,256]{1,0:T(8,128)(2,1)S(1)}, bf16[256,256]{1,0:T(8,128)(2,1)S(1)}, u32[]{:S(2)}, u32[]{:S(2)}) collective-permute-start(bf16[256,256]{1,0:T(8,128)(2,1)S(1)} %get-tuple-element.54), channel_id=1, source_target_pairs={{0,1},{1,0},{2,3},{3,2},{4,5},{5,4},{6,7},{7,6},{8,9},{9,8},{10,11... | collective-permute-start | bytes 393224 | tf_op jit(solution)/shard_map/ppermute | solution.py:390
  108.4 40.2 %copy-start = (f32[8,256,256]{2,1,0:T(8,128)S(1)}, f32[8,256,256]{2,1,0:T(8,128)}, u32[]{:S(2)}) copy-start(f32[8,256,256]{2,1,0:T(8,128)} %rel.5) | copy-start | bytes 6291460
  108.4 40.2 %copy-start.8 = (f32[8,256]{1,0:T(8,128)S(1)}, f32[8,256]{1,0:T(8,128)}, u32[]{:S(2)}) copy-start(f32[8,256]{1,0:T(8,128)} %accum.3) | copy-start | bytes 24580
  110.0 22.0 %all-to-all-start.4 = ((bf16[128,2,4,128]{3,2,1,0:T(4,128)(2,1)}), bf16[128,2,4,128]{3,2,1,0:T(4,128)(2,1)S(1)}, u32[]{:S(2)}, u32[]{:S(2)}) async-start(bf16[128,2,4,128]{3,2,1,0:T(4,128)(2,1)} %bitcast.11), calls=%async_computation.4 | async-start | bytes 524288 | tf_op jit(solution)/shard_map/all_to_all | solution.py:48
  117.9 7.5 %collective-permute-start.5 = (bf16[256,256]{1,0:T(8,128)(2,1)S(1)}, bf16[256,256]{1,0:T(8,128)(2,1)S(1)}, u32[]{:S(2)}, u32[]{:S(2)}) collective-permute-start(bf16[256,256]{1,0:T(8,128)(2,1)S(1)} %get-tuple-element.66), channel_id=1, source_target_pairs={{0,2},{1,3},{2,0},{3,1},{4,6},{5,7},{6,4},{7,5},{8,10},{9,11},{10,... | collective-permute-start | bytes 393224 | tf_op jit(solution)/shard_map/ppermute | solution.py:390
  120.4 8.1 %collective-permute-start.6 = (bf16[256,256]{1,0:T(8,128)(2,1)S(1)}, bf16[256,256]{1,0:T(8,128)(2,1)S(1)}, u32[]{:S(2)}, u32[]{:S(2)}) collective-permute-start(bf16[256,256]{1,0:T(8,128)(2,1)S(1)} %get-tuple-element.67), channel_id=1, source_target_pairs={{0,3},{1,2},{2,1},{3,0},{4,7},{5,6},{6,5},{7,4},{8,11},{9,10},{10,... | collective-permute-start | bytes 393224 | tf_op jit(solution)/shard_map/ppermute | solution.py:390
  125.4 7.5 %copy-start.4 = (bf16[256,256]{1,0:T(8,128)(2,1)}, bf16[256,256]{1,0:T(8,128)(2,1)S(1)}, u32[]{:S(2)}) copy-start(bf16[256,256]{1,0:T(8,128)(2,1)S(1)} %collective-permute-done.5.own2) | copy-start | bytes 393220
  128.5 4.4 %copy-start.6 = (bf16[256,256]{1,0:T(8,128)(2,1)}, bf16[256,256]{1,0:T(8,128)(2,1)S(1)}, u32[]{:S(2)}) copy-start(bf16[256,256]{1,0:T(8,128)(2,1)S(1)} %collective-permute-done.6.own3) | copy-start | bytes 393220
  132.8 11.1 %all-to-all-start.5 = ((bf16[4,256,256]{2,1,0:T(8,128)(2,1)}), bf16[4,256,256]{2,1,0:T(8,128)(2,1)S(1)}, u32[]{:S(2)}, u32[]{:S(2)}) async-start(bf16[4,256,256]{2,1,0:T(8,128)(2,1)} %shard_map.131), calls=%async_computation.5 | async-start | bytes 1048576 | tf_op jit(solution)/shard_map/all_to_all | solution.py:48
  136.3 0.9 copy-start.5
  137.2 0.9 copy-start.7
  143.9 6.9 %collective-permute-start.7 = (bf16[4,256,256]{2,1,0:T(8,128)(2,1)S(1)}, bf16[4,256,256]{2,1,0:T(8,128)(2,1)S(1)}, u32[]{:S(2)}, u32[]{:S(2)}) collective-permute-start(bf16[4,256,256]{2,1,0:T(8,128)(2,1)S(1)} %all-to-all-done.5.grads), channel_id=1, source_target_pairs={{0,8},{8,0},{1,9},{9,1},{2,10},{10,2},{3,11},{11,3},{4,12},{12,4},... | collective-permute-start | bytes 1572872 | tf_op jit(solution)/shard_map/ppermute | solution.py:44

commit v16 on v12

--- a/solution.py
+++ b/solution.py
@@ -338,7 +338,7 @@
     packs = [pack] + [
         lax.ppermute(pack, "x", [(i, i ^ k) for i in range(4)]) for k in range(1, 4)
     ]
-    packs[1], rel_b, arrived = lax.optimization_barrier((packs[1], rel_b, arrived))
+    rel_b, arrived = lax.optimization_barrier((rel_b, arrived))
     routed = call(take_kernel, shape((64, 2, 8, 128), bf16), 1, (matching, arrived), moved=400_000)
     rows_in = spread(routed.reshape(128, 8, 128), DOM_Z).reshape(64, 2, 8, 128)
     block = shape((1024, 256), bf16)

time: 155 us -> 156 us (level)
    all_to_all x5, waiting for transfers between devices: 20.3 us -> 22.9 us  [spread(): return lax.all_to_all(value, axis, split_axis=0, concat_axis=0, tiled=True)]
    ppermute x3, waiting for transfers between devices: 2.91 us -> 1.33 us  [body(): lax.ppermute(pack, 'x', [(i, i ^ k) for i in range(4)])]
  transfers between devices with their start and end apart: 13 -> 13, of which waited for: 11 -> 9; matrix products, arithmetic and copies ran while one was open for 0% -> 0% of each run, Pallas kernels for 8% -> 8%
where the time goes in v16:
time: 156 us; the launch traced here: 155 us
  starting transfers between devices  78.5 us (50%)
  waiting for transfers between devices  32.7 us (21%)
  Pallas kernels  28 us (18%)
  blocking collectives  11.5 us (7%)
  local copies, waits for them, and re-layouts  3.08 us (2%)
    all_to_all x5, starting transfers between devices, spread(): return lax.all_to_all(value, axis, split_axis=0, concat_axis=0, tiled=True)  51.4 us
    pallas_call x12, Pallas kernels, call(): pl.pallas_call(kernel, out_shape=outs, in_specs=specs, out_specs=tuple((A...  23.1 us
    all_to_all x5, waiting for transfers between devices, spread(): return lax.all_to_all(value, axis, split_axis=0, concat_axis=0, tiled=True)  22.9 us
    all_to_all x1, blocking collectives, spread(): return lax.all_to_all(value, axis, split_axis=0, concat_axis=0, tiled=True)  11.5 us
    ppermute x3, starting transfers between devices, body(): lax.ppermute(pack, 'x', [(i, i ^ k) for i in range(4)])  9.4 us
    ppermute x2, starting transfers between devices, swap(): return lax.ppermute(value, axis, [(0, 1), (1, 0)])  8.92 us
    ppermute x3, starting transfers between devices, body(): lax.ppermute(part, 'x', [(i, i ^ k) for i in range(4)])  8.82 us
    ppermute x3, waiting for transfers between devices, body(): lax.ppermute(part, 'x', [(i, i ^ k) for i in range(4)])  7.89 us
  transfers between devices with their start and end apart: 13, of which 9 were waited for; matrix products, arithmetic and copies ran while one was open for 0% of the time, Pallas kernels for 8%

profile of v16, /device:TPU:1, one launch (start us, length us, event | category | flops | bytes accessed | tf_op | source)
XLA Modules:
  0.0 155.0 jit_solution(10900419919682182482)
XLA Ops:
  0.6 1.7 %shard_map.121 = (bf16[64,8,128]{2,1,0:T(8,128)(2,1)}, bf16[272,256]{1,0:T(8,128)(2,1)}) custom-call(f32[256,256]{1,0:T(8,128)} %emb.3, s32[1,512]{1,0:T(1,128)} %bitcast.19, s32[1,512]{1,0:T(1,128)} %bitcast.20, s32[1,512]{1,0:T(1,128)} %bitcast.21, s32[1,512]{1,0:T(1,128)} %neg.1), custom_call_target="tpu_custom_call" | custom-call | bytes 800000 | tf_op jit(solution)/shard_map/pallas_call | solution.py:32
  2.4 14.6 %all-to-all-start = ((bf16[64,8,128]{2,1,0:T(8,128)(2,1)}), bf16[64,8,128]{2,1,0:T(8,128)(2,1)S(1)}, u32[]{:S(2)}, u32[]{:S(2)}) async-start(bf16[64,8,128]{2,1,0:T(8,128)(2,1)} %get-tuple-element.39), calls=%async_computation | async-start | bytes 262144 | tf_op jit(solution)/shard_map/all_to_all | solution.py:48
  17.0 2.3 %shard_map.120.rel_b = bf16[8,256,256]{2,1,0:T(8,128)(2,1)} custom-call(f32[8,256,256]{2,1,0:T(8,128)} %rel.5), custom_call_target="tpu_custom_call" | custom-call | bytes 3000000 | tf_op jit(solution)/shard_map/pallas_call | solution.py:32
  19.4 7.7 %all-to-all-done.arrived = bf16[64,8,128]{2,1,0:T(8,128)(2,1)S(1)} async-done(((bf16[64,8,128]{2,1,0:T(8,128)(2,1)}), bf16[64,8,128]{2,1,0:T(8,128)(2,1)S(1)}, u32[]{:S(2)}, u32[]{:S(2)}) %all-to-all-start) | async-done | bytes 131104 | tf_op jit(solution)/shard_map/all_to_all | solution.py:48
  27.1 1.3 shard_map.122
  28.4 11.2 %all-to-all-start.1 = ((bf16[128,8,128]{2,1,0:T(8,128)(2,1)}), bf16[128,8,128]{2,1,0:T(8,128)(2,1)S(1)}, u32[]{:S(2)}, u32[]{:S(2)}) async-start(bf16[128,8,128]{2,1,0:T(8,128)(2,1)} %bitcast.7), calls=%async_computation.1 | async-start | bytes 524288 | tf_op jit(solution)/shard_map/all_to_all | solution.py:48
  39.6 3.1 %collective-permute-start.2 = (bf16[272,256]{1,0:T(8,128)(2,1)S(1)}, bf16[272,256]{1,0:T(8,128)(2,1)S(1)}, u32[]{:S(2)}, u32[]{:S(2)}) collective-permute-start(bf16[272,256]{1,0:T(8,128)(2,1)S(1)} %copy-done.11), channel_id=1, source_target_pairs={{0,1},{1,0},{2,3},{3,2},{4,5},{5,4},{6,7},{7,6},{8,9},{9,8},{10,11... | collective-permute-start | bytes 417800 | tf_op jit(solution)/shard_map/ppermute | solution.py:339
  42.7 3.7 %collective-permute-start.1 = (bf16[272,256]{1,0:T(8,128)(2,1)S(1)}, bf16[272,256]{1,0:T(8,128)(2,1)S(1)}, u32[]{:S(2)}, u32[]{:S(2)}) collective-permute-start(bf16[272,256]{1,0:T(8,128)(2,1)S(1)} %copy-done.11), channel_id=1, source_target_pairs={{0,3},{1,2},{2,1},{3,0},{4,7},{5,6},{6,5},{7,4},{8,11},{9,10},{10,... | collective-permute-start | bytes 417800 | tf_op jit(solution)/shard_map/ppermute | solution.py:339
  46.4 2.6 %collective-permute-start = (bf16[272,256]{1,0:T(8,128)(2,1)S(1)}, bf16[272,256]{1,0:T(8,128)(2,1)S(1)}, u32[]{:S(2)}, u32[]{:S(2)}) collective-permute-start(bf16[272,256]{1,0:T(8,128)(2,1)S(1)} %copy-done.11), channel_id=1, source_target_pairs={{0,2},{1,3},{2,0},{3,1},{4,6},{5,7},{6,4},{7,5},{8,10},{9,11},{10,... | collective-permute-start | bytes 417800 | tf_op jit(solution)/shard_map/ppermute | solution.py:339
  49.0 0.1 pad_add_fusion.place
  49.1 0.0 collective-permute-done.2.pack1
  49.1 1.2 copy-done.1
  50.3 2.4 %shard_map.123 = (f32[8,512]{1,0:T(8,128)S(1)}, f32[16,512]{1,0:T(8,128)S(1)}, bf16[1024,256]{1,0:T(8,128)(2,1)S(1)}, bf16[1024,256]{1,0:T(8,128)(2,1)S(1)}) custom-call(s32[3]{0:T(128)S(1)} %pad_add_fusion.place, bf16[272,256]{1,0:T(8,128)(2,1)S(1)} %copy-done.11, bf16[272,256]{1,0:T(8,128)(2,1)S(1)} %collective-permute-done.2.pack1, ...), custom_call_target="tpu_custom_call" | custom-call | flops 1300000000 | bytes 3000000 | tf_op jit(solution)/shard_map/pallas_call | solution.py:32
  52.7 0.0 collective-permute-done.1.pack3
  52.7 1.3 collective-permute-done.pack2
  54.0 0.0 all-to-all-done.1
  54.0 6.7 %shard_map.124 = (bf16[2048,512]{1,0:T(8,128)(2,1)S(1)}, bf16[2048,256]{1,0:T(8,128)(2,1)S(1)}, bf16[4,256,256]{2,1,0:T(8,128)(2,1)S(1)}, bf16[4,256,256]{2,1,0:...) custom-call(s32[3]{0:T(128)S(1)} %pad_add_fusion.place, bf16[64,2,8,128]{3,2,1,0:T(8,128)(2,1)S(1)} %bitcast.17, ...), custom_call_target="tpu_custom_call" | custom-call | flops 4499999744 | bytes 6000000 | tf_op jit(solution)/shard_map/pallas_call | solution.py:32
  60.8 0.0 copy-start.12
  60.8 4.2 %collective-permute-start.4 = (bf16[4,256,256]{2,1,0:T(8,128)(2,1)S(1)}, bf16[4,256,256]{2,1,0:T(8,128)(2,1)S(1)}, u32[]{:S(2)}, u32[]{:S(2)}) collective-permute-start(bf16[4,256,256]{2,1,0:T(8,128)(2,1)S(1)} %get-tuple-element.54), channel_id=1, source_target_pairs={{0,8},{8,0},{1,9},{9,1},{2,10},{10,2},{3,11},{11,3},{4,12},{12,4},... | collective-permute-start | bytes 1572872 | tf_op jit(solution)/shard_map/ppermute | solution.py:44
  65.0 0.9 shard_map.126.g_rows
  65.9 0.6 collective-permute-done.4.came
  66.5 0.1 shard_map.127
  66.6 11.5 %all_to_all.30.got = bf16[4,256,256]{2,1,0:T(8,128)(2,1)S(1)} all-to-all(bf16[4,256,256]{2,1,0:T(8,128)(2,1)S(1)} %shard_map.127), channel_id=1, replica_groups=mesh['zlo'=4,'y'=8,'core'=2,'zhi'=2,'x'=4] {'x'}, dimensions={0} | all-to-all | bytes 1048576 | tf_op jit(solution)/shard_map/all_to_all | solution.py:48
  78.1 0.9 shard_map.128
  79.0 14.2 %all-to-all-start.3 = ((bf16[128,3,4,128]{3,2,1,0:T(4,128)(2,1)}), bf16[128,3,4,128]{3,2,1,0:T(4,128)(2,1)S(1)}, u32[]{:S(2)}, u32[]{:S(2)}) async-start(bf16[128,3,4,128]{3,2,1,0:T(4,128)(2,1)} %bitcast.9), calls=%async_computation.3 | async-start | bytes 786432 | tf_op jit(solution)/shard_map/all_to_all | solution.py:48
  93.3 3.3 %shard_map.125 = (f32[256,256]{1,0:T(8,128)S(1)}, bf16[256,256]{1,0:T(8,128)(2,1)S(1)}, bf16[256,256]{1,0:T(8,128)(2,1)S(1)}, bf16[256,256]{1,0:T(8,128)(2,1)S(1)}) custom-call(bf16[2048,256]{1,0:T(8,128)(2,1)S(1)} %copy-done.13, f32[16,512]{1,0:T(8,128)S(1)} %get-tuple-element.44.known.known0, f32[16,512]{1,0:T(8,128)S(1)} %get-tuple-element.48.known1, ...), custom_call_target="tpu_custom_call" | custom-call | flops 3000000000 | bytes 4000000 | tf_op jit(solution)/shard_map/pallas_call | solution.py:32
  96.6 0.0 copy-start.3
  96.6 0.0 copy-start.10
  96.6 2.3 %collective-permute-start.3 = (bf16[256,256]{1,0:T(8,128)(2,1)S(1)}, bf16[256,256]{1,0:T(8,128)(2,1)S(1)}, u32[]{:S(2)}, u32[]{:S(2)}) collective-permute-start(bf16[256,256]{1,0:T(8,128)(2,1)S(1)} %get-tuple-element.50), channel_id=1, source_target_pairs={{0,1},{1,0},{2,3},{3,2},{4,5},{5,4},{6,7},{7,6},{8,9},{9,8},{10,11... | collective-permute-start | bytes 393224 | tf_op jit(solution)/shard_map/ppermute | solution.py:388
  99.0 3.8 %collective-permute-done.3.own1 = bf16[256,256]{1,0:T(8,128)(2,1)S(1)} collective-permute-done((bf16[256,256]{1,0:T(8,128)(2,1)S(1)}, bf16[256,256]{1,0:T(8,128)(2,1)S(1)}, u32[]{:S(2)}, u32[]{:S(2)}) %collective-permute-start.3) | collective-permute-done | bytes 131104 | tf_op jit(solution)/shard_map/ppermute | solution.py:388
  102.8 6.9 %all-to-all-done.3 = bf16[128,3,4,128]{3,2,1,0:T(4,128)(2,1)S(1)} async-done(((bf16[128,3,4,128]{3,2,1,0:T(4,128)(2,1)}), bf16[128,3,4,128]{3,2,1,0:T(4,128)(2,1)S(1)}, u32[]{:S(2)}, u32[]{:S(2)}) %all-to-all-start.3) | async-done | bytes 393248 | tf_op jit(solution)/shard_map/all_to_all | solution.py:48
  109.7 1.5 shard_map.129
  111.2 7.9 %all-to-all-start.4 = ((bf16[128,2,4,128]{3,2,1,0:T(4,128)(2,1)}), bf16[128,2,4,128]{3,2,1,0:T(4,128)(2,1)S(1)}, u32[]{:S(2)}, u32[]{:S(2)}) async-start(bf16[128,2,4,128]{3,2,1,0:T(4,128)(2,1)} %bitcast.11), calls=%async_computation.4 | async-start | bytes 524288 | tf_op jit(solution)/shard_map/all_to_all | solution.py:48
  119.1 2.5 %collective-permute-start.5 = (bf16[256,256]{1,0:T(8,128)(2,1)S(1)}, bf16[256,256]{1,0:T(8,128)(2,1)S(1)}, u32[]{:S(2)}, u32[]{:S(2)}) collective-permute-start(bf16[256,256]{1,0:T(8,128)(2,1)S(1)} %get-tuple-element.60), channel_id=1, source_target_pairs={{0,2},{1,3},{2,0},{3,1},{4,6},{5,7},{6,4},{7,5},{8,10},{9,11},{10,... | collective-permute-start | bytes 393224 | tf_op jit(solution)/shard_map/ppermute | solution.py:388
  121.6 4.0 %collective-permute-start.6 = (bf16[256,256]{1,0:T(8,128)(2,1)S(1)}, bf16[256,256]{1,0:T(8,128)(2,1)S(1)}, u32[]{:S(2)}, u32[]{:S(2)}) collective-permute-start(bf16[256,256]{1,0:T(8,128)(2,1)S(1)} %get-tuple-element.61), channel_id=1, source_target_pairs={{0,3},{1,2},{2,1},{3,0},{4,7},{5,6},{6,5},{7,4},{8,11},{9,10},{10,... | collective-permute-start | bytes 393224 | tf_op jit(solution)/shard_map/ppermute | solution.py:388
  125.6 1.0 collective-permute-done.5.own2
  126.6 3.1 %collective-permute-done.6.own3 = bf16[256,256]{1,0:T(8,128)(2,1)S(1)} collective-permute-done((bf16[256,256]{1,0:T(8,128)(2,1)S(1)}, bf16[256,256]{1,0:T(8,128)(2,1)S(1)}, u32[]{:S(2)}, u32[]{:S(2)}) %collective-permute-start.6) | collective-permute-done | bytes 131104 | tf_op jit(solution)/shard_map/ppermute | solution.py:388
  129.7 3.5 %all-to-all-done.4 = bf16[128,2,4,128]{3,2,1,0:T(4,128)(2,1)S(1)} async-done(((bf16[128,2,4,128]{3,2,1,0:T(4,128)(2,1)}), bf16[128,2,4,128]{3,2,1,0:T(4,128)(2,1)S(1)}, u32[]{:S(2)}, u32[]{:S(2)}) %all-to-all-start.4) | async-done | bytes 262176 | tf_op jit(solution)/shard_map/all_to_all | solution.py:48
  133.2 0.9 shard_map.131
  134.1 3.5 %all-to-all-start.5 = ((bf16[4,256,256]{2,1,0:T(8,128)(2,1)}), bf16[4,256,256]{2,1,0:T(8,128)(2,1)S(1)}, u32[]{:S(2)}, u32[]{:S(2)}) async-start(bf16[4,256,256]{2,1,0:T(8,128)(2,1)} %shard_map.131), calls=%async_computation.5 | async-start | bytes 1048576 | tf_op jit(solution)/shard_map/all_to_all | solution.py:48
  137.6 0.9 copy-done.5
  138.5 0.9 copy-done.7
  139.4 1.0 shard_map.130
  140.4 4.8 %all-to-all-done.5.grads = bf16[4,256,256]{2,1,0:T(8,128)(2,1)S(1)} async-done(((bf16[4,256,256]{2,1,0:T(8,128)(2,1)}), bf16[4,256,256]{2,1,0:T(8,128)(2,1)S(1)}, u32[]{:S(2)}, u32[]{:S(2)}) %all-to-all-start.5) | async-done | bytes 524320 | tf_op jit(solution)/shard_map/all_to_all | solution.py:48
  145.2 4.7 %collective-permute-start.7 = (bf16[4,256,256]{2,1,0:T(8,128)(2,1)S(1)}, bf16[4,256,256]{2,1,0:T(8,128)(2,1)S(1)}, u32[]{:S(2)}, u32[]{:S(2)}) collective-permute-start(bf16[4,256,256]{2,1,0:T(8,128)(2,1)S(1)} %all-to-all-done.5.grads), channel_id=1, source_target_pairs={{0,8},{8,0},{1,9},{9,1},{2,10},{10,2},{3,11},{11,3},{4,12},{12,4},... | collective-permute-start | bytes 1572872 | tf_op jit(solution)/shard_map/ppermute | solution.py:44
  149.9 2.2 %shard_map.132 = (f32[8,256,256]{2,1,0:T(8,128)}, f32[8,256]{1,0:T(8,128)S(1)}) custom-call(s32[3]{0:T(128)S(1)} %pad_add_fusion.place, f32[8,256,256]{2,1,0:T(8,128)S(1)} %copy-done, f32[8,256]{1,0:T(8,128)S(1)} %copy-done.8, bf16[4,256,256]{2,1,0:T(8,128)(2,1)S(1)} %all-to-all-done.5.grads), custom_call_target="tpu_custom_call" | custom-call | bytes 3000000 | tf_op jit(solution)/shard_map/pallas_call | solution.py:291
  152.0 0.0 collective-permute-done.7.grads
  152.1 2.7 %shard_map.133 = (f32[8,256,256]{2,1,0:T(8,128)}, f32[8,256]{1,0:T(8,128)}) custom-call(s32[3]{0:T(128)S(1)} %pad_add_fusion.place, f32[8,256,256]{2,1,0:T(8,128)S(1)} %copy-done, f32[8,256]{1,0:T(8,128)S(1)} %copy-done.8, bf16[4,256,256]{2,1,0:T(8,128)(2,1)S(1)} %collective-permute-done.7.grads, ...), custom_call_target="tpu_custom_call", output_to_operand_aliasing={{0}: (4, {})} | custom-call | bytes 3000000 | tf_op jit(solution)/shard_map/pallas_call | solution.py:291
  (22 shorter events, 0.0 us)
Async XLA Ops:
  0.6 26.4 %copy-start.9 = (s32[64]{0:T(128)S(1)}, s32[64]{0:T(128)}, u32[]{:S(2)}) copy-start(s32[64]{0:T(128)} %matching.3) | copy-start | bytes 772
  2.4 24.7 %all-to-all-start = ((bf16[64,8,128]{2,1,0:T(8,128)(2,1)}), bf16[64,8,128]{2,1,0:T(8,128)(2,1)S(1)}, u32[]{:S(2)}, u32[]{:S(2)}) async-start(bf16[64,8,128]{2,1,0:T(8,128)(2,1)} %get-tuple-element.39), calls=%async_computation | async-start | bytes 262144 | tf_op jit(solution)/shard_map/all_to_all | solution.py:48
  17.0 22.6 %copy-start.11 = (bf16[272,256]{1,0:T(8,128)(2,1)S(1)}, bf16[272,256]{1,0:T(8,128)(2,1)}, u32[]{:S(2)}) copy-start(bf16[272,256]{1,0:T(8,128)(2,1)} %get-tuple-element.41.pack0) | copy-start | bytes 417796
  28.4 25.6 %all-to-all-start.1 = ((bf16[128,8,128]{2,1,0:T(8,128)(2,1)}), bf16[128,8,128]{2,1,0:T(8,128)(2,1)S(1)}, u32[]{:S(2)}, u32[]{:S(2)}) async-start(bf16[128,8,128]{2,1,0:T(8,128)(2,1)} %bitcast.7), calls=%async_computation.1 | async-start | bytes 524288 | tf_op jit(solution)/shard_map/all_to_all | solution.py:48
  39.6 9.5 %collective-permute-start.2 = (bf16[272,256]{1,0:T(8,128)(2,1)S(1)}, bf16[272,256]{1,0:T(8,128)(2,1)S(1)}, u32[]{:S(2)}, u32[]{:S(2)}) collective-permute-start(bf16[272,256]{1,0:T(8,128)(2,1)S(1)} %copy-done.11), channel_id=1, source_target_pairs={{0,1},{1,0},{2,3},{3,2},{4,5},{5,4},{6,7},{7,6},{8,9},{9,8},{10,11... | collective-permute-start | bytes 417800 | tf_op jit(solution)/shard_map/ppermute | solution.py:339
  42.7 10.0 %collective-permute-start.1 = (bf16[272,256]{1,0:T(8,128)(2,1)S(1)}, bf16[272,256]{1,0:T(8,128)(2,1)S(1)}, u32[]{:S(2)}, u32[]{:S(2)}) collective-permute-start(bf16[272,256]{1,0:T(8,128)(2,1)S(1)} %copy-done.11), channel_id=1, source_target_pairs={{0,3},{1,2},{2,1},{3,0},{4,7},{5,6},{6,5},{7,4},{8,11},{9,10},{10,... | collective-permute-start | bytes 417800 | tf_op jit(solution)/shard_map/ppermute | solution.py:339
  46.4 7.6 %collective-permute-start = (bf16[272,256]{1,0:T(8,128)(2,1)S(1)}, bf16[272,256]{1,0:T(8,128)(2,1)S(1)}, u32[]{:S(2)}, u32[]{:S(2)}) collective-permute-start(bf16[272,256]{1,0:T(8,128)(2,1)S(1)} %copy-done.11), channel_id=1, source_target_pairs={{0,2},{1,3},{2,0},{3,1},{4,6},{5,7},{6,4},{7,5},{8,10},{9,11},{10,... | collective-permute-start | bytes 417800 | tf_op jit(solution)/shard_map/ppermute | solution.py:339
  49.1 1.2 copy-start.1
  50.3 3.7 %copy-start.2 = (bf16[8,256,256]{2,1,0:T(8,128)(2,1)S(1)}, bf16[8,256,256]{2,1,0:T(8,128)(2,1)}, u32[]{:S(2)}) copy-start(bf16[8,256,256]{2,1,0:T(8,128)(2,1)} %shard_map.120.rel_b) | copy-start | bytes 3145732
  60.8 5.1 %copy-start.12 = (bf16[2048,256]{1,0:T(8,128)(2,1)}, bf16[2048,256]{1,0:T(8,128)(2,1)S(1)}, u32[]{:S(2)}) copy-start(bf16[2048,256]{1,0:T(8,128)(2,1)S(1)} %get-tuple-element.47.g_trans) | copy-start | bytes 3145732
  60.8 5.7 %collective-permute-start.4 = (bf16[4,256,256]{2,1,0:T(8,128)(2,1)S(1)}, bf16[4,256,256]{2,1,0:T(8,128)(2,1)S(1)}, u32[]{:S(2)}, u32[]{:S(2)}) collective-permute-start(bf16[4,256,256]{2,1,0:T(8,128)(2,1)S(1)} %get-tuple-element.54), channel_id=1, source_target_pairs={{0,8},{8,0},{1,9},{9,1},{2,10},{10,2},{3,11},{11,3},{4,12},{12,4},... | collective-permute-start | bytes 1572872 | tf_op jit(solution)/shard_map/ppermute | solution.py:44
  66.5 26.8 %copy-start.13 = (bf16[2048,256]{1,0:T(8,128)(2,1)S(1)}, bf16[2048,256]{1,0:T(8,128)(2,1)}, u32[]{:S(2)}) copy-start(bf16[2048,256]{1,0:T(8,128)(2,1)} %copy-done.12) | copy-start | bytes 3145732
  79.0 30.6 %all-to-all-start.3 = ((bf16[128,3,4,128]{3,2,1,0:T(4,128)(2,1)}), bf16[128,3,4,128]{3,2,1,0:T(4,128)(2,1)S(1)}, u32[]{:S(2)}, u32[]{:S(2)}) async-start(bf16[128,3,4,128]{3,2,1,0:T(4,128)(2,1)} %bitcast.9), calls=%async_computation.3 | async-start | bytes 786432 | tf_op jit(solution)/shard_map/all_to_all | solution.py:48
  96.6 41.0 %copy-start.3 = (f32[256,256]{1,0:T(8,128)S(1)}, f32[256,256]{1,0:T(8,128)}, u32[]{:S(2)}) copy-start(f32[256,256]{1,0:T(8,128)} %emb.3) | copy-start | bytes 786436
  96.6 41.0 %copy-start.10 = (f32[256]{0:T(256)S(1)}, f32[256]{0:T(256)}, u32[]{:S(2)}) copy-start(f32[256]{0:T(256)} %param.10) | copy-start | bytes 3076
  96.6 6.1 %collective-permute-start.3 = (bf16[256,256]{1,0:T(8,128)(2,1)S(1)}, bf16[256,256]{1,0:T(8,128)(2,1)S(1)}, u32[]{:S(2)}, u32[]{:S(2)}) collective-permute-start(bf16[256,256]{1,0:T(8,128)(2,1)S(1)} %get-tuple-element.50), channel_id=1, source_target_pairs={{0,1},{1,0},{2,3},{3,2},{4,5},{5,4},{6,7},{7,6},{8,9},{9,8},{10,11... | collective-permute-start | bytes 393224 | tf_op jit(solution)/shard_map/ppermute | solution.py:388
  109.7 40.2 %copy-start = (f32[8,256,256]{2,1,0:T(8,128)S(1)}, f32[8,256,256]{2,1,0:T(8,128)}, u32[]{:S(2)}) copy-start(f32[8,256,256]{2,1,0:T(8,128)} %rel.5) | copy-start | bytes 6291460
  109.7 40.2 %copy-start.8 = (f32[8,256]{1,0:T(8,128)S(1)}, f32[8,256]{1,0:T(8,128)}, u32[]{:S(2)}) copy-start(f32[8,256]{1,0:T(8,128)} %accum.3) | copy-start | bytes 24580
  111.2 22.0 %all-to-all-start.4 = ((bf16[128,2,4,128]{3,2,1,0:T(4,128)(2,1)}), bf16[128,2,4,128]{3,2,1,0:T(4,128)(2,1)S(1)}, u32[]{:S(2)}, u32[]{:S(2)}) async-start(bf16[128,2,4,128]{3,2,1,0:T(4,128)(2,1)} %bitcast.11), calls=%async_computation.4 | async-start | bytes 524288 | tf_op jit(solution)/shard_map/all_to_all | solution.py:48
  119.1 7.5 %collective-permute-start.5 = (bf16[256,256]{1,0:T(8,128)(2,1)S(1)}, bf16[256,256]{1,0:T(8,128)(2,1)S(1)}, u32[]{:S(2)}, u32[]{:S(2)}) collective-permute-start(bf16[256,256]{1,0:T(8,128)(2,1)S(1)} %get-tuple-element.60), channel_id=1, source_target_pairs={{0,2},{1,3},{2,0},{3,1},{4,6},{5,7},{6,4},{7,5},{8,10},{9,11},{10,... | collective-permute-start | bytes 393224 | tf_op jit(solution)/shard_map/ppermute | solution.py:388
  121.6 8.1 %collective-permute-start.6 = (bf16[256,256]{1,0:T(8,128)(2,1)S(1)}, bf16[256,256]{1,0:T(8,128)(2,1)S(1)}, u32[]{:S(2)}, u32[]{:S(2)}) collective-permute-start(bf16[256,256]{1,0:T(8,128)(2,1)S(1)} %get-tuple-element.61), channel_id=1, source_target_pairs={{0,3},{1,2},{2,1},{3,0},{4,7},{5,6},{6,5},{7,4},{8,11},{9,10},{10,... | collective-permute-start | bytes 393224 | tf_op jit(solution)/shard_map/ppermute | solution.py:388
  126.6 7.5 %copy-start.4 = (bf16[256,256]{1,0:T(8,128)(2,1)}, bf16[256,256]{1,0:T(8,128)(2,1)S(1)}, u32[]{:S(2)}) copy-start(bf16[256,256]{1,0:T(8,128)(2,1)S(1)} %collective-permute-done.5.own2) | copy-start | bytes 393220
  129.7 4.4 %copy-start.6 = (bf16[256,256]{1,0:T(8,128)(2,1)}, bf16[256,256]{1,0:T(8,128)(2,1)S(1)}, u32[]{:S(2)}) copy-start(bf16[256,256]{1,0:T(8,128)(2,1)S(1)} %collective-permute-done.6.own3) | copy-start | bytes 393220
  134.1 11.1 %all-to-all-start.5 = ((bf16[4,256,256]{2,1,0:T(8,128)(2,1)}), bf16[4,256,256]{2,1,0:T(8,128)(2,1)S(1)}, u32[]{:S(2)}, u32[]{:S(2)}) async-start(bf16[4,256,256]{2,1,0:T(8,128)(2,1)} %shard_map.131), calls=%async_computation.5 | async-start | bytes 1048576 | tf_op jit(solution)/shard_map/all_to_all | solution.py:48
  137.6 0.9 copy-start.5
  138.5 0.9 copy-start.7
  145.2 6.9 %collective-permute-start.7 = (bf16[4,256,256]{2,1,0:T(8,128)(2,1)S(1)}, bf16[4,256,256]{2,1,0:T(8,128)(2,1)S(1)}, u32[]{:S(2)}, u32[]{:S(2)}) collective-permute-start(bf16[4,256,256]{2,1,0:T(8,128)(2,1)S(1)} %all-to-all-done.5.grads), channel_id=1, source_target_pairs={{0,8},{8,0},{1,9},{9,1},{2,10},{10,2},{3,11},{11,3},{4,12},{12,4},... | collective-permute-start | bytes 1572872 | tf_op jit(solution)/shard_map/ppermute | solution.py:44
